TPU v7x, 32 devices: a whole 2x2x4 slice. The times are simulated.
32 devices in a mesh: dp: 8 (over z, y), shard: 4 (over x, core).
Axes of the slice: x: 2, y: 2, z: 4, core: 2. Of those that a mesh axis runs over, the one named last changes fastest.
Arguments:
- tokens: bfloat16 [51200, 512], P(('dp', 'shard')), may hold values from -40 to 40
- cotangent: bfloat16 [51200, 512], P(('dp', 'shard')), may hold values from -5 to 5
- regions: int32 [51200], P(('dp', 'shard')), may hold values from 0 to 3
- validity: int32 [51200], P(('dp', 'shard')), may hold values from 0 to 1
- qkv_weight: bfloat16 [786432], P(('dp', 'shard')), may hold values from -0.25 to 0.25
- proj_weight: bfloat16 [262144], P(('dp', 'shard')), may hold values from -1 to 1
- fc1_weight: bfloat16 [1048576], P(('dp', 'shard')), may hold values from -0.25 to 0.25
- fc2_weight: bfloat16 [1048576], P(('dp', 'shard')), may hold values from -0.125 to 0.125
- vectors: bfloat16 [6144], P(('dp', 'shard')), may hold values from -1.5 to 1.65
- rel_table: float32 [361, 16], replicated, may hold values from -4 to 4
Outputs:
- result: bfloat16 [51200, 512], P(('dp', 'shard'))
- tokens_grad: float32 [51200, 512], P(('dp', 'shard'))
- qkv_grad: float32 [786432], P(('dp', 'shard'))
- proj_grad: float32 [262144], P(('dp', 'shard'))
- fc1_grad: float32 [1048576], P(('dp', 'shard'))
- fc2_grad: float32 [1048576], P(('dp', 'shard'))
- vectors_grad: float32 [6144], P(('dp', 'shard'))
- table_grad: float32 [361, 16], replicated
- stats: float32 [5], replicated
All inputs are finite; a program needn't handle non-finite values.
Results may differ from a plain program's by a relative error of at most 0.011.
Values may be sent and summed in bfloat16 or wider, within the bound.
No kernel may reach another device: no remote copies, remote signals or barrier semaphores. Data moves between devices by JAX's collectives and lax.ppermute only.
A program may use at most 192 MiB of HBM per device.

v0:
```python
import jax
import jax.numpy as jnp
from jax import lax
from jax.sharding import PartitionSpec as P

D = 512
FF = 2048
HEADS = 16
HD = 32
WSIDE = 10
RELN = 361


def layer_norm(values, gain, shift):
    center = values - jnp.mean(values, axis=-1, keepdims=True)
    spread = jnp.mean(center * center, axis=-1, keepdims=True)
    return center * lax.rsqrt(spread + 1e-05) * gain + shift


def gelu_exact(values):
    return jax.nn.gelu(values, approximate=False)


def relative_index(side):
    cells = jnp.arange(side * side, dtype=jnp.int32)
    rows_at = cells // side
    cols_at = cells % side
    offset = (rows_at[:, None] - rows_at[None, :] + side - 1) * (2 * side - 1)
    return (offset + cols_at[:, None] - cols_at[None, :] + side - 1).reshape(-1)


def contract_rows(left, right):
    return lax.dot_general(
        left, right, (((0,), (0,)), ((), ())), preferred_element_type=jnp.float32
    )


def contract_cols(left, right):
    return lax.dot_general(
        left, right, (((1,), (1,)), ((), ())), preferred_element_type=jnp.float32
    )


def masked_scores(queries, keys, position, allowed, factor):
    scores = (
        jnp.einsum("wnhd,wmhd->whnm", queries, keys, preferred_element_type=jnp.float32) * factor
    )
    return jnp.where(allowed, scores + position[None], -1000000000.0)


def shards(
    tokens,
    cotangent,
    regions,
    validity,
    qkv_weight,
    proj_weight,
    fc1_weight,
    fc2_weight,
    vectors,
    rel_table,
):
    cells = WSIDE * WSIDE
    rows = tokens.shape[0]
    windows = rows // cells
    factor = HD ** (-0.5)
    attn_parts = (
        lax.all_gather(qkv_weight, ("dp", "shard"), axis=0, tiled=True),
        lax.all_gather(proj_weight, ("dp", "shard"), axis=0, tiled=True),
        lax.all_gather(vectors, ("dp", "shard"), axis=0, tiled=True),
    )
    mlp_parts = (
        lax.all_gather(fc1_weight, ("dp", "shard"), axis=0, tiled=True),
        lax.all_gather(fc2_weight, ("dp", "shard"), axis=0, tiled=True),
    )
    qkv_full = attn_parts[0].reshape(D, 3 * D)
    proj_full = attn_parts[1].reshape(D, D)
    params = attn_parts[2].astype(jnp.float32)
    gain_one = params[0:D]
    shift_one = params[D : 2 * D]
    query_bias = params[2 * D : 3 * D]
    value_bias = params[3 * D : 4 * D]
    proj_bias = params[4 * D : 5 * D]
    gain_two = params[5 * D : 6 * D]
    shift_two = params[6 * D : 7 * D]
    down_bias = params[7 * D : 8 * D]
    up_bias = params[8 * D : 8 * D + FF]
    one_hot = (relative_index(WSIDE)[:, None] == jnp.arange(RELN, dtype=jnp.int32)[None, :]).astype(
        jnp.float32
    )
    bias_rows = jnp.dot(one_hot, rel_table, precision=lax.Precision.HIGHEST)
    position = bias_rows.reshape(cells, cells, HEADS).transpose(2, 0, 1)
    region_win = regions.reshape(windows, cells)
    valid_win = validity.reshape(windows, cells)
    allowed = (region_win[:, :, None] == region_win[:, None, :]) & (valid_win[:, None, :] == 1)
    allowed = (allowed | jnp.eye(cells, dtype=jnp.bool_)[None])[:, None]
    stream = tokens.astype(jnp.float32)
    normed_f, norm_one_back = jax.vjp(layer_norm, stream, gain_one, shift_one)
    normed = normed_f.astype(jnp.bfloat16)
    mixed = jnp.dot(normed, qkv_full, preferred_element_type=jnp.float32)
    queries = (mixed[:, 0:D] + query_bias).astype(jnp.bfloat16).reshape(windows, cells, HEADS, HD)
    keys = mixed[:, D : 2 * D].astype(jnp.bfloat16).reshape(windows, cells, HEADS, HD)
    values = (
        (mixed[:, 2 * D : 3 * D] + value_bias)
        .astype(jnp.bfloat16)
        .reshape(windows, cells, HEADS, HD)
    )
    scores = masked_scores(queries, keys, position, allowed, factor)
    top_score = jnp.max(scores, axis=-1, keepdims=True)
    log_total = top_score + jnp.log(jnp.sum(jnp.exp(scores - top_score), axis=-1, keepdims=True))
    probs_low = jnp.exp(scores - log_total).astype(jnp.bfloat16)
    attended = jnp.einsum("whnm,wmhd->wnhd", probs_low, values, preferred_element_type=jnp.float32)
    attended = attended.reshape(rows, D).astype(jnp.bfloat16)
    branch = jnp.dot(attended, proj_full, preferred_element_type=jnp.float32) + proj_bias
    middle = stream + branch
    up_full = mlp_parts[0].reshape(D, FF)
    down_full = mlp_parts[1].reshape(FF, D)
    normed_two_f, norm_two_back = jax.vjp(layer_norm, middle, gain_two, shift_two)
    normed_two = normed_two_f.astype(jnp.bfloat16)
    pre_act = jnp.dot(normed_two, up_full, preferred_element_type=jnp.float32) + up_bias
    activ_f, gelu_back = jax.vjp(gelu_exact, pre_act)
    activ = activ_f.astype(jnp.bfloat16)
    second = jnp.dot(activ, down_full, preferred_element_type=jnp.float32) + down_bias
    result = middle + second
    weight = validity.astype(jnp.float32)

    def masked_square(field):
        return jnp.sum(weight * jnp.sum(field * field, axis=-1))

    squares = jnp.stack(
        [
            masked_square(stream),
            masked_square(branch),
            masked_square(middle),
            masked_square(second),
            masked_square(result),
            jnp.sum(weight),
        ]
    )
    square_totals = lax.psum(squares, ("dp", "shard"))
    again_attn = (
        lax.all_gather(qkv_weight, ("dp", "shard"), axis=0, tiled=True),
        lax.all_gather(proj_weight, ("dp", "shard"), axis=0, tiled=True),
    )
    again_mlp = (
        lax.all_gather(fc1_weight, ("dp", "shard"), axis=0, tiled=True),
        lax.all_gather(fc2_weight, ("dp", "shard"), axis=0, tiled=True),
    )
    qkv_back = again_attn[0].reshape(D, 3 * D)
    proj_back = again_attn[1].reshape(D, D)
    up_back = again_mlp[0].reshape(D, FF)
    down_back = again_mlp[1].reshape(FF, D)
    grad_out = cotangent.astype(jnp.float32)
    grad_down = contract_rows(activ, cotangent)
    grad_down_bias = jnp.sum(grad_out, axis=0)
    grad_activ = contract_cols(cotangent, down_back)
    grad_pre = gelu_back(grad_activ)[0].astype(jnp.bfloat16)
    grad_up = contract_rows(normed_two, grad_pre)
    grad_up_bias = jnp.sum(grad_pre, axis=0, dtype=jnp.float32)
    grad_normed_two = contract_cols(grad_pre, up_back)
    grad_middle_part, grad_gain_two, grad_shift_two = norm_two_back(grad_normed_two)
    grad_middle = grad_out + grad_middle_part
    mlp_totals = (
        lax.psum_scatter(grad_up.reshape(-1), ("dp", "shard"), scatter_dimension=0, tiled=True),
        lax.psum_scatter(grad_down.reshape(-1), ("dp", "shard"), scatter_dimension=0, tiled=True),
    )
    grad_branch = grad_middle.astype(jnp.bfloat16)
    grad_proj = contract_rows(attended, grad_branch)
    grad_proj_bias = jnp.sum(grad_branch, axis=0, dtype=jnp.float32)
    grad_attended = (
        contract_cols(grad_branch, proj_back)
        .astype(jnp.bfloat16)
        .reshape(windows, cells, HEADS, HD)
    )
    again_scores = masked_scores(queries, keys, position, allowed, factor)
    probs = jnp.exp(again_scores - log_total)
    probs_back = probs.astype(jnp.bfloat16)
    grad_values = jnp.einsum(
        "whnm,wnhd->wmhd", probs_back, grad_attended, preferred_element_type=jnp.float32
    ).astype(jnp.bfloat16)
    grad_probs = jnp.einsum(
        "wnhd,wmhd->whnm", grad_attended, values, preferred_element_type=jnp.float32
    )
    centered = jnp.sum(grad_probs * probs, axis=-1, keepdims=True)
    grad_scores = (probs * (grad_probs - centered)).astype(jnp.bfloat16)
    score_sums = (
        jnp.sum(grad_scores, axis=0, dtype=jnp.float32)
        .transpose(1, 2, 0)
        .reshape(cells * cells, HEADS)
    )
    grad_table = lax.dot_general(
        one_hot, score_sums, (((0,), (0,)), ((), ())), precision=lax.Precision.HIGHEST
    )
    grad_queries = (
        (
            jnp.einsum("whnm,wmhd->wnhd", grad_scores, keys, preferred_element_type=jnp.float32)
            * factor
        )
        .astype(jnp.bfloat16)
        .reshape(rows, D)
    )
    grad_keys = (
        (
            jnp.einsum("whnm,wnhd->wmhd", grad_scores, queries, preferred_element_type=jnp.float32)
            * factor
        )
        .astype(jnp.bfloat16)
        .reshape(rows, D)
    )
    grad_values = grad_values.reshape(rows, D)
    grad_mixed = jnp.concatenate([grad_queries, grad_keys, grad_values], axis=1)
    grad_qkv = contract_rows(normed, grad_mixed)
    grad_query_bias = jnp.sum(grad_queries, axis=0, dtype=jnp.float32)
    grad_value_bias = jnp.sum(grad_values, axis=0, dtype=jnp.float32)
    grad_normed = contract_cols(grad_mixed, qkv_back)
    grad_in_part, grad_gain_one, grad_shift_one = norm_one_back(grad_normed)
    grad_tokens = grad_middle + grad_in_part
    grad_vectors = jnp.concatenate(
        [
            grad_gain_one,
            grad_shift_one,
            grad_query_bias,
            grad_value_bias,
            grad_proj_bias,
            grad_gain_two,
            grad_shift_two,
            grad_down_bias,
            grad_up_bias,
        ]
    )
    attn_totals = (
        lax.psum_scatter(grad_qkv.reshape(-1), ("dp", "shard"), scatter_dimension=0, tiled=True),
        lax.psum_scatter(grad_proj.reshape(-1), ("dp", "shard"), scatter_dimension=0, tiled=True),
        lax.psum_scatter(grad_vectors, ("dp", "shard"), scatter_dimension=0, tiled=True),
    )
    table_total = lax.psum(grad_table, ("dp", "shard"))
    stats = jnp.sqrt(square_totals[0:5] / (square_totals[5] * D) + 1e-06)
    return (
        result.astype(jnp.bfloat16),
        grad_tokens,
        attn_totals[0],
        attn_totals[1],
        mlp_totals[0],
        mlp_totals[1],
        attn_totals[2],
        table_total,
        stats,
    )


def solution(mesh):
    in_specs = (
        P(("dp", "shard"), None),
        P(("dp", "shard"), None),
        P(("dp", "shard")),
        P(("dp", "shard")),
        P(("dp", "shard")),
        P(("dp", "shard")),
        P(("dp", "shard")),
        P(("dp", "shard")),
        P(("dp", "shard")),
        P(),
    )
    out_specs = (
        P(("dp", "shard"), None),
        P(("dp", "shard"), None),
        P(("dp", "shard")),
        P(("dp", "shard")),
        P(("dp", "shard")),
        P(("dp", "shard")),
        P(("dp", "shard")),
        P(),
        P(),
    )
    return jax.shard_map(shards, mesh=mesh, in_specs=in_specs, out_specs=out_specs, check_vma=False)
```

profile of v0, /device:TPU:0, one launch (start us, length us, event | category | flops | bytes accessed | tf_op | source)
XLA Modules:
  0.0 632.0 jit_solution(228444470786425955)
XLA Ops:
  10.4 42.2 %all-reduce = bf16[6144]{0:T(1024)(128)(2,1)S(1)} all-reduce(bf16[6144]{0:T(1024)(128)(2,1)S(1)} %dynamic-update-slice), channel_id=1, replica_groups=mesh['dp'=8,'shard'=4] {'dp','shard'}, use_global_device_ids=true, to_apply=%add | all-reduce | flops 6144 | bytes 24576
  58.0 6.9 %fusion.1 = f32[10000,16]{0,1:T(8,128)S(1)} fusion(f32[361,16]{0,1:T(8,128)S(1)} %copy-done, s32[10000]{0:T(1024)S(1)} %reshape.274), kind=kOutput, calls=%fused_computation.3 | convolution fusion | flops 696729984 | bytes 703104 | tf_op jit(solution)/shard_map/dot_general | solution.py:91
  66.8 42.5 %all_gather.21 = bf16[262144]{0:T(1024)(128)(2,1)S(1)} all-gather(bf16[8192]{0:T(1024)(128)(2,1)S(1)} %copy-done.42), channel_id=1, replica_groups=mesh['dp'=8,'shard'=4] {'dp','shard'}, dimensions={0}, use_global_device_ids=true | all-gather | bytes 540672 | tf_op jit(solution)/shard_map/all_gather | solution.py:69
  124.8 5.2 reshape.257
  132.8 5.6 reshape.258
  138.4 11.8 %fusion.57 = (f32[16,16,100]{2,1,0:T(8,128)S(1)}, f32[16,16,100,100]{2,3,1,0:T(8,128)}) fusion(f32[16,100,100]{1,2,0:T(8,128)} %copy.58, bf16[16,100,16,32]{1,0,3,2:T(8,128)(2,1)} %reshape.258, bf16[16,100,16,32]{1,0,3,2:T(8,128)(2,1)} %reshape.257, pred[16,100,100]{1,2,0:T(8,128)(4,1)} %and_or_fusion), kind=kOutput, calls=%fused_computation.137 | convolution fusion | flops 174054400 | bytes 14419200 | tf_op jit(solution)/shard_map/wnhd,wmhd->whnm/dot_general | solution.py:46
  150.2 9.2 %exponential_reduce_fusion = f32[16,16,100]{2,1,0:T(8,128)S(1)} fusion(f32[16,16,100,100]{2,3,1,0:T(8,128)} %get-tuple-element.60, f32[16,16,100]{2,1,0:T(8,128)S(1)} %get-tuple-element.59), kind=kLoop, calls=%fused_computation.8 | loop fusion | flops 5094400 | bytes 10444800 | tf_op jit(solution)/shard_map/reduce_sum | solution.py:110
  162.2 5.5 reshape.256
  167.7 8.2 %convert_bitcast_fusion.1 = bf16[16,100,16,32]{1,3,2,0:T(8,128)(2,1)S(1)} fusion(bf16[16,100,16,32]{1,0,3,2:T(8,128)(2,1)} %reshape.256, f32[16,16,100,100]{2,3,1,0:T(8,128)} %get-tuple-element.60, f32[16,16,100]{2,1,0:T(8,128)S(1)} %log_add_fusion), kind=kOutput, calls=%fused_computation.75 | convolution fusion | flops 169779200 | bytes 13619200 | tf_op jit(solution)/shard_map/whnm,wmhd->wnhd/dot_general | solution.py:112
  192.7 35.5 %multiply_convert_fusion.1 = (bf16[1600,2048]{1,0:T(8,128)(2,1)}, f32[1600,2048]{1,0:T(8,128)}, f32[1600,2048]{1,0:T(8,128)}) fusion(f32[2048]{0:T(1024)S(1)} %slice.67, bf16[512,2048]{1,0:T(8,128)(2,1)} %reshape.261, f32[1600,512]{1,0:T(8,128)S(1)} %copy-done.10, f32[512]{0:T(512)S(1)} %get-tuple-element.53, f32[512]{0:T(512)S(1)} %get-tuple-element.52, ...), kind=kOutput, calls=%fused_computation.13 | convolution fusion | flops 3575808000 | bytes 38167040 | tf_op jit(solution)/shard_map/dot_general | solution.py:120
  232.5 17.6 %convert_reduce_fusion.1 = (f32[2048]{0:T(1024)S(1)}, bf16[1600,2048]{1,0:T(8,128)(2,1)}) fusion(f32[1600,2048]{1,0:T(8,128)} %get-tuple-element.42, bf16[1600,512]{1,0:T(8,128)(2,1)} %param.11, bf16[2048,512]{1,0:T(8,128)(2,1)} %reshape.262, f32[1600,2048]{1,0:T(8,128)} %get-tuple-element.61, f32[2048]{0:T(1024)S(1)} %slice.67), kind=kOutput, calls=%fused_computation.11 | convolution fusion | flops 3411146752 | bytes 36519936 | tf_op jit(solution)/shard_map/dot_general | solution.py:39
  250.1 6.0 fusion.58
  256.2 6.4 %multiply_reduce_fusion.1 = (f32[1600]{0:T(1024)S(1)}, f32[1600]{0:T(1024)S(1)}, f32[1600]{0:T(1024)S(1)}, f32[512]{0:T(512)S(1)}, f32[512]{0:T(512)S(1)}, /*index=5*/f32[1600]{0:T(1024)S(1)}, bf16[1600,512]{1,0:T(8,128)(2,1)}) fusion(f32[1600,512]{1,0:T(8,128)S(1)} %copy-done.10, f32[1600,512]{1,0:T(8,128)S(1)} %fusion.58, f32[512]{0:T(512)S(1)} %get-tuple-element.52, ...), kind=kOutput, calls=%fused_computation.60 | convolution fusion | flops 3369362432 | bytes 16889344 | tf_op jit(solution)/shard_map/dot_general | solution.py:123
  271.7 6.8 %reshape.263 = bf16[16,100,16,32]{1,0,3,2:T(8,128)(2,1)} reshape(bf16[1600,512]{0,1:T(8,128)(2,1)} %copy.62) | data formatting | bytes 3276800 | tf_op jit(solution)/shard_map/reshape | solution.py:173
  278.5 9.4 %convert_reduce_fusion.3 = (f32[16,32]{1,0:T(8,128)S(1)}, bf16[16,100,16,32]{1,3,2,0:T(8,128)(2,1)S(1)}) fusion(f32[16,16,100,100]{2,3,1,0:T(8,128)} %get-tuple-element.60, f32[16,16,100]{2,1,0:T(8,128)S(1)} %copy-done.19, bf16[16,100,16,32]{1,0,3,2:T(8,128)(2,1)} %reshape.263), kind=kOutput, calls=%fused_computation.40 | convolution fusion | flops 171417088 | bytes 13621248 | tf_op jit(solution)/shard_map/whnm,wnhd->wmhd/dot_general | solution.py:178
  287.9 10.4 %multiply_reduce_fusion = (f32[16,16,100]{2,1,0:T(8,128)S(1)}, f32[16,16,100,100]{2,3,1,0:T(8,128)}) fusion(f32[16,16,100,100]{2,3,1,0:T(8,128)} %get-tuple-element.60, f32[16,16,100]{2,1,0:T(8,128)S(1)} %copy-done.19, bf16[16,100,16,32]{1,0,3,2:T(8,128)(2,1)S(1)} %copy-done.5, bf16[16,100,16,32]{1,0,3,2:T(8,128)(2,1)S(1)} %copy-done.6), kind=kOutput, calls=%fused_computation.6 | convolution fusion | flops 171494400 | bytes 23961600 | tf_op jit(solution)/shard_map/wnhd,wmhd->whnm/dot_general | solution.py:181
  298.4 11.9 %convert_reduce_fusion = (f32[16,100,100]{1,2,0:T(8,128)}, bf16[16,16,100,100]{2,3,1,0:T(8,128)(2,1)S(1)}) fusion(f32[16,16,100,100]{2,3,1,0:T(8,128)} %get-tuple-element.63, f32[16,16,100]{2,1,0:T(8,128)S(1)} %get-tuple-element.62, f32[16,16,100,100]{2,3,1,0:T(8,128)} %get-tuple-element.60, f32[16,16,100]{2,1,0:T(8,128)S(1)} %copy-done.19), kind=kLoop, calls=%fused_computation.4 | loop fusion | flops 15200000 | bytes 26444800 | tf_op jit(solution)/shard_map/reduce_sum | solution.py:187
  318.7 9.1 %convolution_bitcast_fusion.1 = f32[64,16,8,128]{3,2,1,0:T(8,128)} fusion(bf16[1600,2048]{1,0:T(8,128)(2,1)} %get-tuple-element.70, f32[1600,512]{1,0:T(8,128)S(1)} %copy-done.12, f32[512]{0:T(512)S(1)} %get-tuple-element.53, f32[512]{0:T(512)S(1)} %get-tuple-element.52, f32[1600]{0:T(1024)S(1)} %fusion.44, f32[1600]{0:T(1024)S(1)} %broadcast_multiply_fusion), kind=kOutput, calls=%fused_computation.73 | convolution fusion | flops 3359539200 | bytes 14041600 | tf_op jit(solution)/shard_map/dot_general | solution.py:33
  329.9 5.7 convolution_bitcast_fusion
  362.6 5.2 copy.80
  371.8 5.4 fusion.45
  394.3 8.7 %fusion.51 = (f32[512]{0:T(512)S(1)}, f32[1600]{0:T(1024)S(1)}, f32[1600]{0:T(1024)S(1)}, f32[1600,512]{1,0:T(8,128)}) fusion(f32[512]{0:T(512)S(1)} %copy-done.41, f32[1600]{0:T(1024)S(1)} %copy-done.31, bf16[1600,512]{1,0:T(8,128)(2,1)} %param.10, bf16[1600,1536]{0,1:T(8,128)(2,1)} %copy-done.28, bf16[512,1536]{1,0:T(8,128)(2,1)} %copy-done.26), kind=kOutput, calls=%fused_computation.133 | convolution fusion | flops 2523132416 | bytes 11426560 | tf_op jit(solution)/shard_map/dot_general | solution.py:39
  422.0 39.9 %all-reduce.6 = (f32[6144]{0:T(1024)S(1)}, f32[361,16]{0,1:T(8,128)}, f32[6]{0:T(128)S(1)}) all-reduce(f32[6144]{0:T(1024)S(1)} %constant_dynamic-update-slice_fusion.6, f32[361,16]{0,1:T(8,128)S(1)} %fusion, f32[6]{0:T(128)S(1)} %stack.27), channel_id=6, replica_groups=mesh['dp'=8,'shard'=4] {'dp','shard'}, use_global_device_ids=true, to_apply=%region_24.25.clone | all-reduce | flops 11926 | bytes 95408
  464.3 154.6 %all-reduce.10.cloned.1.call-done = (f32[786432]{0:T(1024)}, f32[262144]{0:T(1024)}, f32[1048576]{0:T(1024)}, f32[1048576]{0:T(1024)}) async-done(((f32[786432]{0:T(1024)}, f32[262144]{0:T(1024)}, f32[1048576]{0:T(1024)}, f32[1048576]{0:T(1024)}), (f32[786432]{0:T(1024)}, f32[262144]{0:T(1024)}, f32[1048576]{0:T(1024)}, f32[1048576]{0:T(1024)})) %all-reduce.10.cloned.1.call-update) | async-done | bytes 12582928
  (198 shorter events, 146.6 us)
Async XLA Ops:
  7.2 50.7 %copy-start = (f32[361,16]{0,1:T(8,128)S(1)}, f32[361,16]{0,1:T(8,128)}, u32[]{:S(2)}) copy-start(f32[361,16]{0,1:T(8,128)} %param.19) | copy-start | bytes 69316
  7.2 104.5 %all-gather.4.cloned.1.call-start = ((), (), s32[]{:S(2)}) async-start(), calls=%async_computation | async-start | bytes 1622016 | tf_op jit(solution)/shard_map/all_gather | solution.py:68
  7.9 180.4 %all-gather.6.cloned.1.call-start = ((), (), s32[]{:S(2)}) async-start(), calls=%async_computation.1 | async-start | bytes 2162688 | tf_op jit(solution)/shard_map/all_gather | solution.py:73
  8.7 219.5 %all-gather.8.cloned.1.call-start = ((), (), s32[]{:S(2)}) async-start(), calls=%async_computation.2 | async-start | bytes 2162688 | tf_op jit(solution)/shard_map/all_gather | solution.py:74
  9.4 609.5 %all-reduce.10.cloned.1.call-start = ((), (), s32[]{:S(2)}) async-start(), calls=%async_computation.3 | async-start | bytes 25165824
  53.1 62.0 %copy-start.40 = (f32[512]{0:T(512)}, f32[512]{0:T(512)S(1)}, u32[]{:S(2)}) copy-start(f32[512]{0:T(512)S(1)} %get-tuple-element.57) | copy-start | bytes 6148
  53.1 62.0 %copy-start.45 = (f32[512]{0:T(512)}, f32[512]{0:T(512)S(1)}, u32[]{:S(2)}) copy-start(f32[512]{0:T(512)S(1)} %get-tuple-element.58) | copy-start | bytes 6148
  55.0 60.2 %copy-start.30 = (f32[1600]{0:T(1024)}, f32[1600]{0:T(1024)S(1)}, u32[]{:S(2)}) copy-start(f32[1600]{0:T(1024)S(1)} %broadcast_multiply_fusion.1) | copy-start | bytes 19204
  57.1 58.0 %copy-start.34 = (f32[1600]{0:T(1024)}, f32[1600]{0:T(1024)S(1)}, u32[]{:S(2)}) copy-start(f32[1600]{0:T(1024)S(1)} %fusion.43) | copy-start | bytes 19204
  58.0 8.7 %copy-start.38 = (s32[1600]{0:T(1024)S(1)}, s32[1600]{0:T(1024)}, u32[]{:S(2)}) copy-start(s32[1600]{0:T(1024)} %param.13) | copy-start | bytes 19204
  58.0 8.8 %copy-start.42 = (bf16[8192]{0:T(1024)(128)(2,1)S(1)}, bf16[8192]{0:T(1024)(128)(2,1)}, u32[]{:S(2)}) copy-start(bf16[8192]{0:T(1024)(128)(2,1)} %param.15) | copy-start | bytes 49156
  65.3 49.8 %copy-start.2 = (bf16[1600,512]{1,0:T(8,128)(2,1)S(1)}, bf16[1600,512]{1,0:T(8,128)(2,1)}, u32[]{:S(2)}) copy-start(bf16[1600,512]{1,0:T(8,128)(2,1)} %param.10) | copy-start | bytes 4915204
  232.5 17.6 %copy-start.21 = (bf16[512,2048]{1,0:T(8,128)(2,1)S(1)}, bf16[512,2048]{1,0:T(8,128)(2,1)}, u32[]{:S(2)}) copy-start(bf16[512,2048]{1,0:T(8,128)(2,1)} %reshape.261) | copy-start | bytes 6291460
  268.1 10.4 %copy-start.19 = (f32[16,16,100]{2,1,0:T(8,128)S(1)}, f32[16,16,100]{2,1,0:T(8,128)}, u32[]{:S(2)}) copy-start(f32[16,16,100]{2,1,0:T(8,128)} %copy-done.18) | copy-start | bytes 307204
  278.5 9.4 %copy-start.5 = (bf16[16,100,16,32]{1,0,3,2:T(8,128)(2,1)S(1)}, bf16[16,100,16,32]{1,0,3,2:T(8,128)(2,1)}, u32[]{:S(2)}) copy-start(bf16[16,100,16,32]{1,0,3,2:T(8,128)(2,1)} %reshape.256) | copy-start | bytes 4915204
  278.5 9.4 %copy-start.6 = (bf16[16,100,16,32]{1,0,3,2:T(8,128)(2,1)S(1)}, bf16[16,100,16,32]{1,0,3,2:T(8,128)(2,1)}, u32[]{:S(2)}) copy-start(bf16[16,100,16,32]{1,0,3,2:T(8,128)(2,1)} %reshape.263) | copy-start | bytes 4915204
  298.4 11.9 %copy-start.13 = (bf16[16,100,16,32]{1,0,3,2:T(8,128)(2,1)S(1)}, bf16[16,100,16,32]{1,0,3,2:T(8,128)(2,1)}, u32[]{:S(2)}) copy-start(bf16[16,100,16,32]{1,0,3,2:T(8,128)(2,1)} %reshape.257) | copy-start | bytes 4915204
  315.0 14.9 %slice-start = ((s8[6553600]{0:T(1024)(128)(4,1)}), s8[4194304]{0:T(1024)(128)(4,1)S(1)}, s32[]{:S(2)}) async-start(s8[6553600]{0:T(1024)(128)(4,1)} %bitcast.83), calls=%async_computation.4 | async-start | bytes 8388608
  318.7 9.2 %copy-start.23 = (bf16[1600,512]{0,1:T(8,128)(2,1)S(1)}, bf16[1600,512]{0,1:T(8,128)(2,1)}, u32[]{:S(2)}) copy-start(bf16[1600,512]{0,1:T(8,128)(2,1)} %copy-done.22) | copy-start | bytes 4915204
  318.7 9.2 %copy-start.25 = (bf16[1600,512]{1,0:T(8,128)(2,1)S(1)}, bf16[1600,512]{1,0:T(8,128)(2,1)}, u32[]{:S(2)}) copy-start(bf16[1600,512]{1,0:T(8,128)(2,1)} %copy-done.24) | copy-start | bytes 4915204
  318.7 11.2 %slice-start.1 = ((s8[6553600]{0:T(1024)(128)(4,1)}), s8[2359296]{0:T(1024)(128)(4,1)S(1)}, s32[]{:S(2)}) async-start(s8[6553600]{0:T(1024)(128)(4,1)} %bitcast.83), calls=%async_computation.5 | async-start | bytes 4718592
  394.3 8.7 %copy-start.43 = (f32[1600]{0:T(1024)S(1)}, f32[1600]{0:T(1024)}, u32[]{:S(2)}) copy-start(f32[1600]{0:T(1024)} %get-tuple-element.48) | copy-start | bytes 19204
  394.3 13.3 %copy-start.33 = (f32[1600]{0:T(1024)S(1)}, f32[1600]{0:T(1024)}, u32[]{:S(2)}) copy-start(f32[1600]{0:T(1024)} %copy-done.32) | copy-start | bytes 19204
  411.8 213.1 %copy-start.1 = (f32[361,16]{0,1:T(8,128)S(1)}, f32[361,16]{0,1:T(8,128)}, u32[]{:S(2)}) copy-start(f32[361,16]{0,1:T(8,128)} %param.19) | copy-start | bytes 69316
  (31 other events, 132.9 us)
Sparse Core Ops, SparseCore 0:
  10.9 57.6 all-gather.3
  71.4 55.8 all-gather.5
  130.2 55.2 all-gather.7
  389.5 229.2 all-reduce.9
where the time goes:
time: 640 us; the launch traced here: 632 us
  matrix products  165 us (26%)
  waiting for transfers between devices  157 us (25%)
  local copies, waits for them, and re-layouts  127 us (20%)
  blocking collectives  125 us (20%)
  other arithmetic  42.1 us (7%)
  between operations  15.8 us (2%)
    unnamed x5, waiting for transfers between devices  157 us
    unnamed x2, blocking collectives  82.1 us
    all_gather x1, blocking collectives, shards(): lax.all_gather(proj_weight, ('dp', 'shard'), axis=0, tiled=True)  42.5 us
    dot_general x1, matrix products, shards(): jnp.dot(normed_two, up_full, preferred_element_type=jnp.float32) + up_bias  35.5 us
    dot_general x4, matrix products, contract_cols(): lax.dot_general(left, right, (((1,), (1,)), ((), ())), preferred_element_...  34.5 us
    unnamed x122, local copies, waits for them, and re-layouts  29.3 us
    dot_general x4, matrix products, contract_rows(): lax.dot_general(left, right, (((0,), (0,)), ((), ())), preferred_element_...  22.2 us
  transfers between devices with their start and end apart: 4, of which 1 were waited for; matrix products, arithmetic and copies ran while one was open for 26% of the time, Pallas kernels for 0%

commit v1 on v0

v1 whole, which is shorter than its diff:
```python
import functools

import jax
import jax.numpy as jnp
from jax import lax
from jax.experimental import pallas as pl
from jax.experimental.pallas import tpu as pltpu
from jax.sharding import PartitionSpec as P

D = 512
FF = 2048
HEADS = 16
HD = 32
WSIDE = 10
RELN = 361
CELLS = WSIDE * WSIDE
GW = 4
GR = GW * CELLS
KP = 112
LANES = 128
GL = GW * LANES
RP = 384
AXES = ("dp", "shard")
LOG2E = 1.4426950408889634
NEG = -1e9
RT2 = 0.7071067811865476
PHI = 0.3989422804014327
f32 = jnp.float32
bf16 = jnp.bfloat16
sds = jax.ShapeDtypeStruct


def nn(a, b):
    return lax.dot_general(a, b, (((1,), (0,)), ((), ())), preferred_element_type=f32)


def nt(a, b):
    return lax.dot_general(a, b, (((1,), (1,)), ((), ())), preferred_element_type=f32)


def whole(shape):
    return pl.BlockSpec(shape, lambda i: (0,) * len(shape))


def params(mib):
    return pltpu.CompilerParams(vmem_limit_bytes=mib * 2**20)


def bit_groups(count):
    bits = count.bit_length() - 1
    groups = [(0,)]
    at = 1
    while at < bits:
        groups.append(tuple(range(at, min(at + 2, bits))))
        at += 2
    return groups


def masks_of(group):
    return [sum(((v >> k) & 1) << b for k, b in enumerate(group)) for v in range(1, 1 << len(group))]


def swap(x, mask, count):
    return lax.ppermute(x, AXES, [(i, i ^ mask) for i in range(count)])


def place_of(rel, groups):
    pos = 0
    for g in groups:
        pos = pos * (1 << len(g)) + ((rel >> g[0]) & ((1 << len(g)) - 1))
    return pos


def gather_pieces(x, groups, count):
    cur = x[None]
    rels = [0]
    for g in groups[:1:-1]:
        ms = masks_of(g)
        cur = jnp.concatenate([cur] + [swap(cur, m, count) for m in ms], axis=0)
        rels = [r ^ m for m in [0] + ms for r in rels]
    pieces = [(rels, cur)]
    if len(groups) > 1:
        for m in masks_of(groups[1]):
            pieces.append(([r ^ m for r in rels], swap(cur, m, count)))
    for rs, arr in list(pieces):
        pieces.append(([r ^ 1 for r in rs], swap(arr, 1, count)))
    return pieces


def natural_order(pieces, me, count):
    rels = [r for rs, _ in pieces for r in rs]
    where = [0] * count
    for k, r in enumerate(rels):
        where[r] = k
    both = jnp.concatenate([a for _, a in pieces], axis=0)
    return jnp.take(both, jnp.asarray(where, jnp.int32)[jnp.arange(count) ^ me], axis=0)


def scatter_sum(pk, groups, count):
    half = count // 2
    cur = pk[:half].astype(f32) + swap(pk[half:], 1, count).astype(f32)
    for g in groups[1:]:
        ms = masks_of(g)
        n = cur.shape[0] // (len(ms) + 1)
        parts = [swap(cur[(k + 1) * n : (k + 2) * n].astype(bf16), m, count).astype(f32) for k, m in enumerate(ms)]
        cur = cur[:n]
        for part in parts:
            cur = cur + part
    return cur[0]


def total(x, groups, count):
    for g in groups:
        got = [x] + [swap(x, m, count) for m in masks_of(g)]
        while len(got) > 1:
            got = [got[k] + got[k + 1] for k in range(0, len(got), 2)]
        x = got[0]
    return x


def attn_fwd_body(me_ref, x_ref, rowv_ref, colv_ref, mask_ref, bias_ref, *refs, plan, rpd):
    pieces = refs[: len(plan)]
    (oT_ref, o_ref, qT_ref, kT_ref, v_ref, pT_ref, h1T_ref, w_ref) = refs[len(plan) : len(plan) + 8]
    wT, xs, h1p, kn, vT, osc, sem = refs[len(plan) + 8 :]

    @pl.when(pl.program_id(0) == 0)
    def _():
        copies = []
        for ref, rels in zip(pieces, plan):
            if rels is None:
                copies.append(pltpu.make_async_copy(ref, w_ref, sem.at[len(copies)]))
                continue
            for t, r in enumerate(rels):
                at = pl.multiple_of((r ^ me_ref[0]) * rpd, rpd)
                copies.append(
                    pltpu.make_async_copy(
                        ref.at[t, :, pl.ds(0, 3 * D)], w_ref.at[pl.ds(at, rpd), :], sem.at[len(copies)]
                    )
                )
        for c in copies:
            c.start()
        for c in copies:
            c.wait()
        for a in range(3 * D // LANES):
            wT[LANES * a : LANES * (a + 1), :] = w_ref[:, LANES * a : LANES * (a + 1)].T

    xs[0:GR, :] = x_ref[...].astype(f32)
    gain = rowv_ref[0:1, :]
    shift = rowv_ref[1:2, :]
    value_bias = rowv_ref[3:4, :]
    rows = lax.broadcasted_iota(jnp.int32, (104, 1), 0)
    for w in range(GW):
        xw = xs[CELLS * w : CELLS * w + 104, :]
        c = xw - jnp.mean(xw, axis=-1, keepdims=True)
        var = jnp.mean(c * c, axis=-1, keepdims=True)
        h = jnp.where(rows < CELLS, c * lax.rsqrt(var + 1e-5) * gain + shift, 0.0)
        h = jnp.concatenate([h, jnp.zeros((LANES - 104, D), f32)], axis=0).astype(bf16)
        h1p[LANES * w : LANES * w + LANES, :] = h
        for a in range(D // LANES):
            h1T_ref[LANES * a : LANES * a + LANES, LANES * w : LANES * w + LANES] = h[:, LANES * a : LANES * a + LANES].T
    h1T_ref[D : D + 16, :] = jnp.ones((16, GL), bf16)
    hp = h1p[...]
    qT_ref[...] = (nt(wT[0:D, :], hp) + colv_ref[:, 0:1]).astype(bf16)
    kT_ref[...] = nt(wT[D : 2 * D, :], hp).astype(bf16)
    vT[...] = (nt(wT[2 * D : 3 * D, :], hp) + colv_ref[:, 1:2]).astype(bf16)
    kn[...] = nn(hp, w_ref[:, D : 2 * D]).astype(bf16)
    v_ref[...] = (nn(hp, w_ref[:, 2 * D : 3 * D]) + value_bias).astype(bf16)
    lane = lax.broadcasted_iota(jnp.int32, (1, LANES), 1) // HD
    factor = HD**-0.5 * LOG2E

    def window(w, carry):
        at = pl.multiple_of(w * LANES, LANES)
        allowed = mask_ref[w]
        for g in range(4):
            kb = kn[pl.ds(at, KP), LANES * g : LANES * g + LANES]
            ks = jnp.concatenate([jnp.where(lane == q, kb, jnp.zeros_like(kb)) for q in range(4)], axis=0)
            s = nn(ks, qT_ref[LANES * g : LANES * g + LANES, pl.ds(at, LANES)])
            for q in range(4):
                h = 4 * g + q
                t = s[KP * q : KP * q + KP] * factor + bias_ref[h] + allowed
                e = jnp.exp2(t - jnp.max(t, axis=0, keepdims=True))
                p = (e * (1.0 / jnp.sum(e, axis=0, keepdims=True))).astype(bf16)
                pT_ref[w, h] = p
                oT_ref[HD * h : HD * h + HD, pl.ds(at, LANES)] = nn(
                    vT[HD * h : HD * h + HD, pl.ds(at, LANES)][:, 0:KP], p
                ).astype(bf16)
        return carry

    lax.fori_loop(0, GW, window, 0)
    for w in range(GW):
        for a in range(D // LANES):
            osc[CELLS * w : CELLS * w + 104, LANES * a : LANES * a + LANES] = (
                oT_ref[LANES * a : LANES * a + LANES, LANES * w : LANES * w + LANES].astype(f32).T[0:104]
            )
    o_ref[...] = osc[0:GR, :].astype(bf16)


def any_specs(n):
    return [pl.BlockSpec(memory_space=pl.ANY)] * n


SMEM = pl.BlockSpec(memory_space=pltpu.SMEM)


def attn_fwd(me, x, rowv, colv, allowed, bias, plan, pieces, rpd):
    n = x.shape[0] // GR
    copies = sum(1 if r is None else len(r) for r in plan)
    rb = pl.BlockSpec((GR, D), lambda i: (i, 0))
    tb = pl.BlockSpec((D, GL), lambda i: (0, i))
    return pl.pallas_call(
        functools.partial(attn_fwd_body, plan=plan, rpd=rpd),
        grid=(n,),
        in_specs=[SMEM, rb, whole((8, D)), whole((D, 2)), pl.BlockSpec((GW, KP, LANES), lambda i: (i, 0, 0)), whole((HEADS, KP, LANES))]
        + any_specs(len(pieces)),
        out_specs=[
            tb,
            rb,
            tb,
            tb,
            pl.BlockSpec((GL, D), lambda i: (i, 0)),
            pl.BlockSpec((GW, HEADS, KP, LANES), lambda i: (i, 0, 0, 0)),
            pl.BlockSpec((D + 16, GL), lambda i: (0, i)),
            whole((D, 3 * D)),
        ],
        out_shape=[
            sds((D, n * GL), bf16),
            sds((n * GR, D), bf16),
            sds((D, n * GL), bf16),
            sds((D, n * GL), bf16),
            sds((n * GL, D), bf16),
            sds((n * GW, HEADS, KP, LANES), bf16),
            sds((D + 16, n * GL), bf16),
            sds((D, 3 * D), bf16),
        ],
        scratch_shapes=[
            pltpu.VMEM((3 * D, D), bf16),
            pltpu.VMEM((GR + 8, D), f32),
            pltpu.VMEM((GL, D), bf16),
            pltpu.VMEM((GL, D), bf16),
            pltpu.VMEM((D, GL), bf16),
            pltpu.VMEM((GR + 8, D), f32),
            pltpu.SemaphoreType.DMA((copies,)),
        ],
        compiler_params=params(56),
        cost_estimate=pl.CostEstimate(flops=8 * 10**9, bytes_accessed=20 * 10**6, transcendentals=4 * 10**6),
        name="attn_fwd",
    )(me, x, rowv, colv, allowed, bias, *pieces)


def mlp_body(me_ref, x_ref, o_ref, g_ref, vld_ref, bf1_ref, rowv_ref, *refs, plan, rows, owners, rpd, groups):
    pieces = refs[: len(plan)]
    (mid_ref, dmid_ref, e_ref, vec_ref, dbf1_ref, sa_ref, p_ref, v_ref) = refs[len(plan) : len(plan) + 8]
    rest = refs[len(plan) + 8 :]
    if owners:
        pk_ref = rest[0]
        rest = rest[1:]
    else:
        dU_ref, dV_ref = rest[:2]
        rest = rest[2:]
    u4, h2, h2T, gp, gT, dh2, es, dus, sem = rest
    j = pl.program_id(0)
    padded = h2.shape[0]
    part = padded // 4
    proj_bias = rowv_ref[4:5, :]
    gain = rowv_ref[5:6, :]
    shift = rowv_ref[6:7, :]

    def copies():
        first, later = [], []
        count = 0
        for ref, rels in zip(pieces, plan):
            if rels is None:
                dst = (p_ref, u4, v_ref)[count]
                (first if count == 0 else later).append(pltpu.make_async_copy(ref, dst, sem.at[count]))
                count += 1
                continue
            for t, r in enumerate(rels):
                owner = r ^ me_ref[0]
                at = pl.ds(pl.multiple_of(owner * rpd, rpd), rpd)
                first.append(pltpu.make_async_copy(ref.at[t, 0], p_ref.at[at, :], sem.at[count]))
                later.append(pltpu.make_async_copy(ref.at[t, pl.ds(1, 4)], u4.at[:, at, :], sem.at[count + 1]))
                later.append(
                    pltpu.make_async_copy(
                        ref.at[t, pl.ds(5, 4)], v_ref.at[pl.ds(pl.multiple_of(owner * 4, 4), 4)], sem.at[count + 2]
                    )
                )
                count += 3
        return first, later

    @pl.when(j == 0)
    def _():
        first, later = copies()
        for c in first + later:
            c.start()
        h2[rows:padded, :] = jnp.zeros((padded - rows, D), bf16)
        gp[rows:padded, :] = jnp.zeros((padded - rows, D), bf16)
        gp[0:rows, :] = g_ref[...]
        for c in first:
            c.wait()

        def block(k, acc):
            at = pl.ds(pl.multiple_of(k * GR, 16), GR)
            a = nn(o_ref[at, :], p_ref[...]) + proj_bias
            acc = acc + jnp.sum(a * a * vld_ref[at, :], axis=0, keepdims=True)
            mid = x_ref[at, :].astype(f32) + a
            mid_ref[at, :] = mid
            c = mid - jnp.mean(mid, axis=-1, keepdims=True)
            var = jnp.mean(c * c, axis=-1, keepdims=True)
            h2[at, :] = (c * lax.rsqrt(var + 1e-5) * gain + shift).astype(bf16)
            return acc

        sa_ref[...] = jnp.broadcast_to(lax.fori_loop(0, rows // GR, block, jnp.zeros((1, D), f32)), (8, D))

        def turn(k, carry):
            at = pl.ds(pl.multiple_of(k * LANES, LANES), LANES)
            for a in range(D // LANES):
                cols = slice(LANES * a, LANES * a + LANES)
                h2T[cols, at] = h2[at, cols].T
                gT[cols, at] = gp[at, cols].T
            return carry

        lax.fori_loop(0, padded // LANES, turn, 0)
        for c in later:
            c.wait()

    up_bias = bf1_ref[...]

    def chunk(k, acc):
        at = pl.ds(pl.multiple_of(k * part, 16), part)
        u = nn(h2[at, :], u4[j]) + up_bias
        de = nt(gp[at, :], v_ref[pl.ds(pl.multiple_of(32 * j, 32), 32)].reshape(512, D))
        cdf = 0.5 * lax.erf(u * RT2) + 0.5
        es[at, :] = (u * cdf).astype(bf16)
        du = (de * (cdf + u * (PHI * jnp.exp2(u * u * (-0.5 * LOG2E))))).astype(bf16)
        dus[at, :] = du
        d = nt(du, u4[j])

        @pl.when(j == 0)
        def _():
            dh2[at, :] = d

        @pl.when(j > 0)
        def _():
            dh2[at, :] += d

        return acc + jnp.sum(du.astype(f32), axis=0, keepdims=True)

    dbf1_ref[...] = lax.fori_loop(0, 4, chunk, jnp.zeros((1, 512), f32))
    e_ref[...] = es[0:rows, :]
    dU = nn(h2T[...], dus[...]).astype(bf16)
    dV = nn(gT[...], es[...]).astype(bf16).T
    if owners:
        me = me_ref[0]
        at = pl.ds(pl.multiple_of(j * rpd, rpd), rpd)
        for k in range(owners):
            pk_ref[place_of(k ^ me, groups), at, :] = dU[rpd * k : rpd * k + rpd]
        per = 512 // (4 * rpd)
        for k in range(per):
            pk_ref[place_of((j * per + k) ^ me, groups), 4 * rpd : 8 * rpd, :] = dV[4 * rpd * k : 4 * rpd * k + 4 * rpd]
    else:
        dU_ref[...] = dU
        dV_ref[...] = dV

    @pl.when(j == pl.num_programs(0) - 1)
    def _():
        def block(k, acc):
            at = pl.ds(pl.multiple_of(k * GR, 16), GR)
            mid = mid_ref[at, :]
            c = mid - jnp.mean(mid, axis=-1, keepdims=True)
            rs = lax.rsqrt(jnp.mean(c * c, axis=-1, keepdims=True) + 1e-5)
            xh = c * rs
            d = dh2[at, :]
            dx = d * gain
            dxx = d * xh
            m1 = jnp.mean(dx, axis=-1, keepdims=True)
            m2 = jnp.mean(dxx * gain, axis=-1, keepdims=True)
            grad = g_ref[at, :].astype(f32)
            dm = grad + (dx - m1 - xh * m2) * rs
            dmid_ref[at, :] = dm
            terms = (dm.astype(bf16).astype(f32), dxx, d, grad)
            return tuple(a + jnp.sum(t, axis=0, keepdims=True) for a, t in zip(acc, terms))

        sums = lax.fori_loop(0, rows // GR, block, (jnp.zeros((1, D), f32),) * 4)
        for q in range(4):
            vec_ref[q : q + 1, :] = sums[q]
        vec_ref[4:8, :] = jnp.zeros((4, D), f32)


def mlp(me, x, o, g, vld, bf1, rowv, plan, pieces, rpd, owners, count, groups):
    rows = x.shape[0]
    padded = -(-rows // LANES) * LANES
    copies = sum(1 if r is None else 3 * len(r) for r in plan)
    rb = whole((rows, D))
    if owners:
        grad_specs = [whole((count, 8 * rpd, 512))]
        grad_shapes = [sds((count, 8 * rpd, 512), bf16)]
    else:
        grad_specs = [pl.BlockSpec((D, 512), lambda j: (0, j)), pl.BlockSpec((512, D), lambda j: (j, 0))]
        grad_shapes = [sds((D, FF), bf16), sds((FF, D), bf16)]
    return pl.pallas_call(
        functools.partial(mlp_body, plan=plan, rows=rows, owners=count if owners else 0, rpd=rpd, groups=groups),
        grid=(FF // 512,),
        in_specs=[SMEM, rb, rb, rb, whole((rows, 1)), pl.BlockSpec((1, 512), lambda j: (0, j)), whole((8, D))]
        + any_specs(len(pieces)),
        out_specs=[rb, rb, pl.BlockSpec((rows, 512), lambda j: (0, j)), whole((8, D)), pl.BlockSpec((1, 512), lambda j: (0, j)), whole((8, D)), whole((D, D)), whole((128, 16, D))]
        + grad_specs,
        out_shape=[sds((rows, D), f32), sds((rows, D), f32), sds((rows, FF), bf16), sds((8, D), f32), sds((1, FF), f32), sds((8, D), f32), sds((D, D), bf16), sds((128, 16, D), bf16)]
        + grad_shapes,
        scratch_shapes=[
            pltpu.VMEM((4, D, 512), bf16),
            pltpu.VMEM((padded, D), bf16),
            pltpu.VMEM((D, padded), bf16),
            pltpu.VMEM((padded, D), bf16),
            pltpu.VMEM((D, padded), bf16),
            pltpu.VMEM((padded, D), f32),
            pltpu.VMEM((padded, 512), bf16),
            pltpu.VMEM((padded, 512), bf16),
            pltpu.SemaphoreType.DMA((copies,)),
        ],
        compiler_params=params(60),
        cost_estimate=pl.CostEstimate(flops=18 * 10**9, bytes_accessed=30 * 10**6, transcendentals=7 * 10**6),
        name="mlp",
    )(me, x, o, g, vld, bf1, rowv, *pieces)


def attn_bwd_body(me_ref, dmid_ref, p_ref, oT_ref, qT_ref, kT_ref, v_ref, pT_ref, h1T_ref, *refs, owners, rpd, groups):
    dmT_ref, acc_ref, vec_ref = refs[:3]
    grads = refs[3:-5]
    xs, dap, doT, dw, dproj = refs[-5:]
    i = pl.program_id(0)

    @pl.when(i == 0)
    def _():
        acc_ref[...] = jnp.zeros_like(acc_ref)
        dw[...] = jnp.zeros_like(dw)
        dproj[...] = jnp.zeros_like(dproj)

    xs[0:GR, :] = dmid_ref[...]
    rows = lax.broadcasted_iota(jnp.int32, (104, 1), 0)
    for w in range(GW):
        d = jnp.where(rows < CELLS, xs[CELLS * w : CELLS * w + 104, :], 0.0)
        dap[LANES * w : LANES * w + LANES, :] = jnp.concatenate([d, jnp.zeros((LANES - 104, D), f32)], axis=0).astype(bf16)
    da = dap[...]
    doT[...] = nt(p_ref[...], da).astype(bf16)
    dproj[...] += nn(oT_ref[...], da)
    lane = lax.broadcasted_iota(jnp.int32, (1, LANES), 1) // HD
    factor = HD**-0.5
    tail = jnp.zeros((HD, LANES - KP), bf16)

    def window(w, carry):
        at = pl.ds(pl.multiple_of(w * LANES, LANES), LANES)
        for g in range(4):
            vb = v_ref[pl.ds(pl.multiple_of(w * LANES, LANES), KP), LANES * g : LANES * g + LANES]
            vs = jnp.concatenate([jnp.where(lane == q, vb, jnp.zeros_like(vb)) for q in range(4)], axis=0)
            dp = nn(vs, doT[LANES * g : LANES * g + LANES, at])
            for q in range(4):
                h = 4 * g + q
                head = slice(HD * h, HD * h + HD)
                p = pT_ref[w, h]
                do = doT[head, at]
                delta = jnp.sum(do.astype(f32) * oT_ref[head, at].astype(f32), axis=0, keepdims=True)
                ds = p.astype(f32) * (dp[KP * q : KP * q + KP] - delta)
                acc_ref[h] += ds
                ds = ds.astype(bf16)
                dmT_ref[head, at] = (nn(kT_ref[head, at][:, 0:KP], ds) * factor).astype(bf16)
                dk = (nt(qT_ref[head, at], ds) * factor).astype(bf16)
                dmT_ref[D + HD * h : D + HD * h + HD, at] = jnp.concatenate([dk, tail], axis=1)
                dv = nt(do, p).astype(bf16)
                dmT_ref[2 * D + HD * h : 2 * D + HD * h + HD, at] = jnp.concatenate([dv, tail], axis=1)
        return carry

    lax.fori_loop(0, GW, window, 0)
    dw[...] += nt(h1T_ref[...], dmT_ref[...])

    @pl.when(i == pl.num_programs(0) - 1)
    def _():
        if owners:
            me = me_ref[0]
            for k in range(owners):
                pos = place_of(k ^ me, groups)
                for q in range(3):
                    grads[0][pos, rpd * q : rpd * q + rpd, :] = dw[rpd * k : rpd * k + rpd, D * q : D * q + D].astype(bf16)
                grads[0][pos, 3 * rpd : 4 * rpd, :] = dproj[rpd * k : rpd * k + rpd, :].astype(bf16)
        else:
            grads[0][...] = dw[0:D, :].astype(bf16)
            grads[1][...] = dproj[...].astype(bf16)
        vec_ref[...] = dw[D : D + 8, :]


def attn_bwd(me, dmid, p, oT, qT, kT, v, pT, h1T, rpd, owners, count, groups):
    n = dmid.shape[0] // GR

    def tb(r):
        return pl.BlockSpec((r, GL), lambda i: (0, i))

    if owners:
        grad_shapes = [sds((count, 4 * rpd, D), bf16)]
    else:
        grad_shapes = [sds((D, 3 * D), bf16), sds((D, D), bf16)]
    return pl.pallas_call(
        functools.partial(attn_bwd_body, owners=count if owners else 0, rpd=rpd, groups=groups),
        grid=(n,),
        in_specs=[SMEM, pl.BlockSpec((GR, D), lambda i: (i, 0)), whole((D, D)), tb(D), tb(D), tb(D), pl.BlockSpec((GL, D), lambda i: (i, 0)), pl.BlockSpec((GW, HEADS, KP, LANES), lambda i: (i, 0, 0, 0)), tb(D + 16)],
        out_specs=[tb(3 * D), whole((HEADS, KP, LANES)), whole((8, 3 * D))] + [whole(s.shape) for s in grad_shapes],
        out_shape=[sds((3 * D, n * GL), bf16), sds((HEADS, KP, LANES), f32), sds((8, 3 * D), f32)] + grad_shapes,
        scratch_shapes=[
            pltpu.VMEM((GR + 8, D), f32),
            pltpu.VMEM((GL, D), bf16),
            pltpu.VMEM((D, GL), bf16),
            pltpu.VMEM((D + 16, 3 * D), f32),
            pltpu.VMEM((D, D), f32),
        ],
        compiler_params=params(60),
        cost_estimate=pl.CostEstimate(flops=15 * 10**9, bytes_accessed=25 * 10**6, transcendentals=0),
        name="attn_bwd",
    )(me, dmid, p, oT, qT, kT, v, pT, h1T)


def grad_in_body(dmT_ref, w_ref, x_ref, dmid_ref, rowv_ref, tg_ref, vec_ref, dsc):
    dT = nn(w_ref[...], dmT_ref[...])
    for w in range(GW):
        for a in range(D // LANES):
            cols = slice(LANES * a, LANES * a + LANES)
            dsc[CELLS * w : CELLS * w + 104, cols] = dT[cols, LANES * w : LANES * w + LANES].T[0:104]
    d = dsc[0:GR, :]
    x = x_ref[...].astype(f32)
    c = x - jnp.mean(x, axis=-1, keepdims=True)
    rs = lax.rsqrt(jnp.mean(c * c, axis=-1, keepdims=True) + 1e-5)
    xh = c * rs
    gain = rowv_ref[0:1, :]
    dx = d * gain
    dxx = d * xh
    m1 = jnp.mean(dx, axis=-1, keepdims=True)
    m2 = jnp.mean(dxx * gain, axis=-1, keepdims=True)
    tg_ref[...] = dmid_ref[...] + (dx - m1 - xh * m2) * rs

    @pl.when(pl.program_id(0) == 0)
    def _():
        vec_ref[...] = jnp.zeros_like(vec_ref)

    vec_ref[0:1, :] += jnp.sum(dxx, axis=0, keepdims=True)
    vec_ref[1:2, :] += jnp.sum(d, axis=0, keepdims=True)


def grad_in(dmT, w, x, dmid, rowv):
    n = x.shape[0] // GR
    rb = pl.BlockSpec((GR, D), lambda i: (i, 0))
    return pl.pallas_call(
        grad_in_body,
        grid=(n,),
        in_specs=[pl.BlockSpec((3 * D, GL), lambda i: (0, i)), whole((D, 3 * D)), rb, rb, whole((8, D))],
        out_specs=[rb, whole((8, D))],
        out_shape=[sds((n * GR, D), f32), sds((8, D), f32)],
        scratch_shapes=[pltpu.VMEM((GR + 8, D), f32)],
        compiler_params=params(40),
        cost_estimate=pl.CostEstimate(flops=4 * 10**9, bytes_accessed=16 * 10**6, transcendentals=0),
        name="grad_in",
    )(dmT, w, x, dmid, rowv)


def finish_body(e_ref, v_ref, mid_ref, x_ref, vld_ref, rowv_ref, sa_ref, res_ref, st_ref):
    f = nn(e_ref[...], v_ref[...].reshape(FF, D)) + rowv_ref[7:8, :]
    mid = mid_ref[...]
    out = mid + f
    res_ref[...] = out.astype(bf16)
    vl = vld_ref[...]
    x = x_ref[...].astype(f32)

    @pl.when(pl.program_id(0) == 0)
    def _():
        st_ref[...] = jnp.zeros_like(st_ref)
        st_ref[1:2, :] = sa_ref[0:1, :]

    for k, t in ((0, x), (2, mid), (3, f), (4, out)):
        st_ref[k : k + 1, :] += jnp.sum(t * t * vl, axis=0, keepdims=True)
    st_ref[5:6, :] += jnp.sum(jnp.broadcast_to(vl, (GR, D)), axis=0, keepdims=True)


def finish(e, v, mid, x, vld, rowv, sa):
    n = x.shape[0] // GR
    rb = pl.BlockSpec((GR, D), lambda i: (i, 0))
    return pl.pallas_call(
        finish_body,
        grid=(n,),
        in_specs=[pl.BlockSpec((GR, FF), lambda i: (i, 0)), whole((128, 16, D)), rb, rb, pl.BlockSpec((GR, 1), lambda i: (i, 0)), whole((8, D)), whole((8, D))],
        out_specs=[rb, whole((8, D))],
        out_shape=[sds((n * GR, D), bf16), sds((8, D), f32)],
        compiler_params=params(40),
        cost_estimate=pl.CostEstimate(flops=3 * 10**9, bytes_accessed=16 * 10**6, transcendentals=0),
        name="finish",
    )(e, v, mid, x, vld, rowv, sa)


def place_code(shape, axis):
    c = lax.broadcasted_iota(jnp.int32, shape, axis)
    return jnp.where(c < CELLS, (2 * WSIDE - 1) * (c // WSIDE) + c % WSIDE, -1000)


def rel_bias_body(t_ref, o_ref):
    t = t_ref[...]
    hi = t.astype(bf16)
    r = t - hi.astype(f32)
    md = r.astype(bf16)
    lo = (r - md.astype(f32)).astype(bf16)
    three = jnp.concatenate([hi, md, lo], axis=0)
    code = place_code((RP, LANES), 1) - lax.broadcasted_iota(jnp.int32, (RP, LANES), 0) + 180

    def step(j, carry):
        hit = jnp.where(code == (2 * WSIDE - 1) * (j // WSIDE) + j % WSIDE, 1.0, 0.0).astype(bf16)
        b = nn(three, hit)
        o_ref[:, pl.ds(j, 1), :] = (b[0:16] + b[16:32] + b[32:48]).reshape(HEADS, 1, LANES)
        return carry

    o_ref[:, CELLS:KP, :] = jnp.zeros((HEADS, KP - CELLS, LANES), f32)
    lax.fori_loop(0, CELLS, step, 0)


def rel_bias(table):
    return pl.pallas_call(
        rel_bias_body,
        out_shape=sds((HEADS, KP, LANES), f32),
        cost_estimate=pl.CostEstimate(flops=6 * 10**9, bytes_accessed=10**6, transcendentals=0),
        name="rel_bias",
    )(table)


def rel_grad_body(a_ref, o_ref):
    code = place_code((LANES, RP), 0) - lax.broadcasted_iota(jnp.int32, (LANES, RP), 1) + 180

    def step(j, acc):
        hit = jnp.where(code == (2 * WSIDE - 1) * (j // WSIDE) + j % WSIDE, 1.0, 0.0).astype(bf16)
        t = a_ref[:, pl.ds(j, 1), :].reshape(HEADS, LANES)
        hi = t.astype(bf16)
        lo = (t - hi.astype(f32)).astype(bf16)
        b = nn(jnp.concatenate([hi, lo], axis=0), hit)
        return acc + b[0:16] + b[16:32]

    o_ref[...] = lax.fori_loop(0, CELLS, step, jnp.zeros((HEADS, RP), f32))


def rel_grad(acc):
    return pl.pallas_call(
        rel_grad_body,
        out_shape=sds((HEADS, RP), f32),
        cost_estimate=pl.CostEstimate(flops=6 * 10**9, bytes_accessed=10**6, transcendentals=0),
        name="rel_grad",
    )(acc)


def shards(tokens, cotangent, regions, validity, qkv_weight, proj_weight, fc1_weight, fc2_weight, vectors, rel_table, *, count, inner):
    rows = tokens.shape[0]
    windows = rows // CELLS
    groups = bit_groups(count)
    rpd = D // count
    direct = rpd % 16 == 0
    me = lax.axis_index("dp") * inner + lax.axis_index("shard")
    me_s = me.astype(jnp.int32).reshape(1)

    vec_pieces = gather_pieces(vectors.reshape(1, -1), groups, count)
    attn_pieces = gather_pieces(qkv_weight.reshape(rpd, 3 * D), groups, count)
    packed = jnp.concatenate(
        [
            proj_weight.reshape(1, rpd, D),
            fc1_weight.reshape(rpd, 4, 512).transpose(1, 0, 2),
            fc2_weight.reshape(4, rpd, D),
        ],
        axis=0,
    )
    mlp_pieces = gather_pieces(packed.reshape(9 * rpd, D), groups, count)
    vec = natural_order(vec_pieces, me, count).reshape(-1).astype(f32)
    rowv = vec[: 8 * D].reshape(8, D)
    colv = rowv[2:4].T
    bf1 = vec[8 * D :].reshape(1, FF)
    if direct:
        attn_plan = [r for r, _ in attn_pieces]
        attn_w = [a for _, a in attn_pieces]
        mlp_plan = [r for r, _ in mlp_pieces]
        mlp_w = [a.reshape(-1, 9, rpd, D) for _, a in mlp_pieces]
    else:
        attn_plan = [None]
        attn_w = [natural_order(attn_pieces, me, count).reshape(D, 3 * D)]
        both = natural_order(mlp_pieces, me, count).reshape(count, 9, rpd, D)
        mlp_plan = [None] * 3
        mlp_w = [both[:, 0].reshape(D, D), both[:, 1:5].transpose(1, 0, 2, 3).reshape(4, D, 512), both[:, 5:].reshape(128, 16, D)]

    bias = rel_bias(jnp.pad(rel_table.T * LOG2E, ((0, 0), (0, RP - RELN))))
    reg = regions.reshape(windows, CELLS)
    val = validity.reshape(windows, CELLS)
    allowed = (reg[:, :, None] == reg[:, None, :]) & (val[:, :, None] == 1)
    allowed = jnp.where(allowed | jnp.eye(CELLS, dtype=jnp.bool_)[None], 0.0, NEG).astype(f32)
    allowed = jnp.pad(allowed, ((0, 0), (0, KP - CELLS), (0, LANES - CELLS)), constant_values=NEG)
    vld = validity.astype(f32).reshape(rows, 1)

    oT, o, qT, kT, v, pT, h1T, w_full = attn_fwd(me_s, tokens, rowv, colv, allowed, bias, attn_plan, attn_w, rpd)
    got = mlp(me_s, tokens, o, cotangent, vld, bf1, rowv, mlp_plan, mlp_w, rpd, direct, count, groups)
    mid, dmid, e, vec_two, dbf1, branch_sq, p_full, v_full = got[:8]
    order = None
    if direct:
        mlp_pk = got[8]
    else:
        blocks = jnp.arange(count)
        where = place_of(blocks, groups)
        order = jnp.zeros((count,), jnp.int32).at[where].set(blocks.astype(jnp.int32)) ^ me
        dU = got[8].reshape(count, rpd, 4, 512).transpose(0, 2, 1, 3).reshape(count, 4 * rpd, 512)
        mlp_pk = jnp.take(jnp.concatenate([dU, got[9].reshape(count, 4 * rpd, D)], axis=1), order, axis=0)
    mlp_sum = scatter_sum(mlp_pk, groups, count)

    got = attn_bwd(me_s, dmid, p_full, oT, qT, kT, v, pT, h1T, rpd, direct, count, groups)
    dmT, score_sums, vec_one = got[:3]
    if direct:
        attn_pk = got[3]
    else:
        dW = got[3].reshape(count, rpd, 3, D).transpose(0, 2, 1, 3).reshape(count, 3 * rpd, D)
        attn_pk = jnp.take(jnp.concatenate([dW, got[4].reshape(count, rpd, D)], axis=1), order, axis=0)
    attn_sum = scatter_sum(attn_pk, groups, count)
    grad_tokens, vec_in = grad_in(dmT, w_full, tokens, dmid, rowv)
    table = rel_grad(score_sums)
    result, squares = finish(e, v_full, mid, tokens, vld, rowv, branch_sq)
    small = jnp.concatenate(
        [
            vec_in[0:2],
            vec_one[0:1, 0:D],
            vec_one[0:1, 2 * D : 3 * D],
            vec_two[0:4],
            dbf1.reshape(4, D),
            table.reshape(-1, D),
            squares,
        ],
        axis=0,
    )
    small = total(small, groups, count)
    length = vectors.shape[0]
    grad_vectors = lax.dynamic_slice(small[:12].reshape(-1), (me * length,), (length,))
    grad_table = small[12:24].reshape(HEADS, RP)[:, :RELN].T
    sums = jnp.sum(small[24:32], axis=1)
    stats = jnp.sqrt(sums[0:5] / sums[5] + 1e-06)
    return (
        result,
        grad_tokens,
        attn_sum[: 3 * rpd].reshape(3, rpd, D).transpose(1, 0, 2).reshape(-1),
        attn_sum[3 * rpd :].reshape(-1),
        mlp_sum[: 4 * rpd].reshape(4, rpd, 512).transpose(1, 0, 2).reshape(-1),
        mlp_sum[4 * rpd :].reshape(-1),
        grad_vectors,
        grad_table,
        stats,
    )


def solution(mesh):
    flat = P(AXES)
    tall = P(AXES, None)
    in_specs = (tall, tall, flat, flat, flat, flat, flat, flat, flat, P())
    out_specs = (tall, tall, flat, flat, flat, flat, flat, P(), P())
    inner = mesh.shape["shard"]
    body = functools.partial(shards, count=mesh.shape["dp"] * inner, inner=inner)
    return jax.shard_map(body, mesh=mesh, in_specs=in_specs, out_specs=out_specs, check_vma=False)
```

time: 640 us -> 333 us (0.52); the launches traced: 632 us -> 332 us
  matrix products: 165 us -> 0 us
  Pallas kernels: 0 us -> 156 us
  blocking collectives: 125 us -> 0 us
  waiting for transfers between devices: 157 us -> 68.1 us
  local copies, waits for them, and re-layouts: 127 us -> 38.9 us
  starting transfers between devices: 0.15 us -> 52.9 us
  other arithmetic: 42.1 us -> 15.7 us
  between operations: 15.8 us -> 1.19 us
    dot_general x20 -> x0, matrix products: 165 us -> none  [the longest x1 35.5 us: shards(): jnp.dot(normed_two, up_full, preferred_element_type=jnp.float32) + up_bias]
    unnamed x5 -> x0, waiting for transfers between devices: 157 us -> none
    pallas_call x0 -> x7, Pallas kernels: none -> 156 us  [the longest x1 44.6 us: mlp(): pl.pallas_call(functools.partial(mlp_body, plan=plan, rows=rows, owners=c...]
    unnamed x2 -> x0, blocking collectives: 82.1 us -> none
    ppermute x0 -> x51, waiting for transfers between devices: none -> 68.1 us  [swap(): return lax.ppermute(x, AXES, [(i, i ^ mask) for i in range(count)])]
    reshape x14 -> x12, local copies, waits for them, and re-layouts: 57.8 us -> 2.79 us  [the longest x1 1.17 us: shards(): vld = validity.astype(f32).reshape(rows, 1)]
    ppermute x0 -> x51, starting transfers between devices: none -> 52.9 us  [swap(): return lax.ppermute(x, AXES, [(i, i ^ mask) for i in range(count)])]
    all_gather x1 -> x0, blocking collectives: 42.5 us -> none  [shards(): lax.all_gather(proj_weight, ('dp', 'shard'), axis=0, tiled=True)]
  transfers between devices with their start and end apart: 4 -> 51, of which waited for: 1 -> 22; matrix products, arithmetic and copies ran while one was open for 26% -> 10% of each run, Pallas kernels for 0% -> 22%
where the time goes in v1:
time: 333 us; the launch traced here: 332 us
  Pallas kernels  156 us (47%)
  waiting for transfers between devices  68.1 us (20%)
  starting transfers between devices  52.9 us (16%)
  local copies, waits for them, and re-layouts  38.9 us (12%)
  other arithmetic  15.7 us (5%)
    ppermute x51, waiting for transfers between devices, swap(): return lax.ppermute(x, AXES, [(i, i ^ mask) for i in range(count)])  68.1 us
    ppermute x51, starting transfers between devices, swap(): return lax.ppermute(x, AXES, [(i, i ^ mask) for i in range(count)])  52.9 us
    pallas_call x1, Pallas kernels, mlp(): pl.pallas_call(functools.partial(mlp_body, plan=plan, rows=rows, owners=c...  44.6 us
    pallas_call x1, Pallas kernels, attn_bwd(): pl.pallas_call(functools.partial(attn_bwd_body, owners=count if owners el...  36.5 us
    pallas_call x1, Pallas kernels, attn_fwd(): pl.pallas_call(functools.partial(attn_fwd_body, plan=plan, rpd=rpd), grid...  24.5 us
    unnamed x68, local copies, waits for them, and re-layouts  18.4 us
    pallas_call x1, Pallas kernels, rel_grad(): pl.pallas_call(rel_grad_body, out_shape=sds((HEADS, RP), f32), cost_estim...  17.9 us
    pallas_call x1, Pallas kernels, rel_bias(): pl.pallas_call(rel_bias_body, out_shape=sds((HEADS, KP, LANES), f32), cos...  17.8 us
  transfers between devices with their start and end apart: 51, of which 22 were waited for; matrix products, arithmetic and copies ran while one was open for 10% of the time, Pallas kernels for 22%

profile of v1, /device:TPU:0, one launch (start us, length us, event | category | flops | bytes accessed | tf_op | source)
XLA Modules:
  0.0 332.4 jit_solution(2288714072456481119)
XLA Ops:
  1.3 3.0 collective-permute-start
  8.8 3.5 %collective-permute-start.11 = (bf16[1,16,1536]{2,1,0:T(8,128)(2,1)S(1)}, bf16[1,16,1536]{2,1,0:T(8,128)(2,1)S(1)}, u32[]{:S(2)}, u32[]{:S(2)}) collective-permute-start(bf16[1,16,1536]{2,1,0:T(8,128)(2,1)S(1)} %broadcast_in_dim_reshape.13), channel_id=1, source_target_pairs={{0,16},{1,17},{2,18},{3,19},{4,20},{5,21},{6,22},{7,23},{8,24},{9,... | collective-permute-start | bytes 147464 | tf_op jit(solution)/shard_map/ppermute | solution.py:64
  16.6 17.8 %rel_bias.1.bias_ref = f32[16,112,128]{2,1,0:T(8,128)} custom-call(f32[16,384]{1,0:T(8,128)} %pad.9.t_ref), custom_call_target="tpu_custom_call" | custom-call | flops 6000000000 | bytes 1000000 | tf_op jit(solution)/shard_map/rel_bias/pallas_call | solution.py:619
  38.9 3.9 %collective-permute-start.22 = (bf16[1,144,512]{2,1,0:T(8,128)(2,1)S(1)}, bf16[1,144,512]{2,1,0:T(8,128)(2,1)S(1)}, u32[]{:S(2)}, u32[]{:S(2)}) collective-permute-start(bf16[1,144,512]{2,1,0:T(8,128)(2,1)S(1)} %bitcast.60), channel_id=1, source_target_pairs={{0,24},{1,25},{2,26},{3,27},{4,28},{5,29},{6,30},{7,31},{8,16},{9,... | collective-permute-start | bytes 442376 | tf_op jit(solution)/shard_map/ppermute | solution.py:64
  58.4 3.5 %collective-permute-done.14.refs_2_ = bf16[4,16,1536]{2,1,0:T(8,128)(2,1)S(1)} collective-permute-done((bf16[4,16,1536]{2,1,0:T(8,128)(2,1)S(1)}, bf16[4,16,1536]{2,1,0:T(8,128)(2,1)S(1)}, u32[]{:S(2)}, u32[]{:S(2)}) %collective-permute-start.14) | collective-permute-done | bytes 196640 | tf_op jit(solution)/shard_map/ppermute | solution.py:64
  67.2 4.5 %collective-permute-done.23 = bf16[4,144,512]{2,1,0:T(8,128)(2,1)S(1)} collective-permute-done((bf16[4,144,512]{2,1,0:T(8,128)(2,1)S(1)}, bf16[4,144,512]{2,1,0:T(8,128)(2,1)S(1)}, u32[]{:S(2)}, u32[]{:S(2)}) %collective-permute-start.23) | collective-permute-done | bytes 589856 | tf_op jit(solution)/shard_map/ppermute | solution.py:64
  71.6 14.7 %collective-permute-done.24 = bf16[4,144,512]{2,1,0:T(8,128)(2,1)S(1)} collective-permute-done((bf16[4,144,512]{2,1,0:T(8,128)(2,1)S(1)}, bf16[4,144,512]{2,1,0:T(8,128)(2,1)S(1)}, u32[]{:S(2)}, u32[]{:S(2)}) %collective-permute-start.24) | collective-permute-done | bytes 589856 | tf_op jit(solution)/shard_map/ppermute | solution.py:64
  86.9 24.5 %attn_fwd.1 = (bf16[512,2048]{1,0:T(8,128)(2,1)}, bf16[1600,512]{1,0:T(8,128)(2,1)}, bf16[512,2048]{1,0:T(8,128)(2,1)}, bf16[512,2048]{1,0:T(8,128)(2,1)}, bf16[...) custom-call(s32[1]{0:T(128)} %bitcast.me_ref, ...), custom_call_target="tpu_custom_call" | custom-call | flops 8000000000 | bytes 20000000 | tf_op jit(solution)/shard_map/attn_fwd/pallas_call | solution.py:210
  113.2 44.6 %mlp.1 = (f32[1600,512]{1,0:T(8,128)}, f32[1600,512]{1,0:T(8,128)}, bf16[1600,2048]{1,0:T(8,128)(2,1)}, f32[8,512]{1,0:T(8,128)}, f32[1,2048]{1,0:T(1,128)}, /*i...) custom-call(s32[1]{0:T(128)} %bitcast.me_ref, ...), custom_call_target="tpu_custom_call" | custom-call | flops 17999998976 | bytes 30000000 | tf_op jit(solution)/shard_map/mlp/pallas_call | solution.py:400
  157.7 36.5 %attn_bwd.1 = (bf16[1536,2048]{1,0:T(8,128)(2,1)}, f32[16,112,128]{2,1,0:T(8,128)}, f32[8,1536]{1,0:T(8,128)}, bf16[32,64,512]{2,1,0:T(8,128)(2,1)}) custom-call(s32[1]{0:T(128)} %bitcast.me_ref, f32[1600,512]{1,0:T(8,128)} %get-tuple-element.40.dmid_ref, bf16[512,512]{1,0:T(8,128)(2,1)} %get-tuple-element.41.p_ref, ...), custom_call_target="tpu_custom_call" | custom-call | flops 15000000512 | bytes 25000000 | tf_op jit(solution)/shard_map/attn_bwd/pallas_call | solution.py:500
  196.6 17.9 %rel_grad.1 = f32[16,384]{1,0:T(8,128)} custom-call(f32[16,112,128]{2,1,0:T(8,128)} %get-tuple-element.57.a_ref), custom_call_target="tpu_custom_call" | custom-call | flops 6000000000 | bytes 1000000 | tf_op jit(solution)/shard_map/rel_grad/pallas_call | solution.py:642
  222.1 7.8 %grad_in.1 = (f32[1600,512]{1,0:T(8,128)}, f32[8,512]{1,0:T(8,128)S(1)}) custom-call(bf16[1536,2048]{1,0:T(8,128)(2,1)S(1)} %copy-done.8, bf16[512,1536]{1,0:T(8,128)(2,1)S(1)} %copy-done.10, bf16[1600,512]{1,0:T(8,128)(2,1)S(1)} %copy-done.4, f32[1600,512]{1,0:T(8,128)S(1)} %copy-done.9, f32[8,512]{1,0:T(8,128)S(1)} %copy-done.6), custom_call_target="tpu_custom_call" | custom-call | flops 4000000000 | bytes 16000000 | tf_op jit(solution)/shard_map/grad_in/pallas_call | solution.py:548
  231.9 2.9 copy-done
  238.9 6.5 %finish.1 = (bf16[1600,512]{1,0:T(8,128)(2,1)}, f32[8,512]{1,0:T(8,128)S(1)}) custom-call(bf16[1600,2048]{1,0:T(8,128)(2,1)S(1)} %copy-done, bf16[128,16,512]{2,1,0:T(8,128)(2,1)S(1)} %copy-done.3, f32[1600,512]{1,0:T(8,128)S(1)} %copy-done.1, bf16[1600,512]{1,0:T(8,128)(2,1)S(1)} %copy-done.5, f32[1600,1]{1,0:T(8,128)S(1)} %copy-done.2, ...), custom_call_target="tpu_custom_call" | custom-call | flops 3000000000 | bytes 16000000 | tf_op jit(solution)/shard_map/finish/pallas_call | solution.py:582
  250.6 3.2 slice.152
  258.3 3.7 %collective-permute-done.49 = f32[32,512]{1,0:T(8,128)S(1)} collective-permute-done((f32[32,512]{1,0:T(8,128)S(1)}, f32[32,512]{1,0:T(8,128)S(1)}, u32[]{:S(2)}, u32[]{:S(2)}) %collective-permute-start.49) | collective-permute-done | bytes 65568 | tf_op jit(solution)/shard_map/ppermute | solution.py:64
  271.1 4.7 %collective-permute-done.33 = bf16[4,64,512]{2,1,0:T(8,128)(2,1)S(1)} collective-permute-done((bf16[4,64,512]{2,1,0:T(8,128)(2,1)S(1)}, bf16[4,64,512]{2,1,0:T(8,128)(2,1)S(1)}, u32[]{:S(2)}, u32[]{:S(2)}) %collective-permute-start.33) | collective-permute-done | bytes 262176 | tf_op jit(solution)/shard_map/ppermute | solution.py:64
  275.8 4.1 %collective-permute-done.32 = bf16[4,64,512]{2,1,0:T(8,128)(2,1)S(1)} collective-permute-done((bf16[4,64,512]{2,1,0:T(8,128)(2,1)S(1)}, bf16[4,64,512]{2,1,0:T(8,128)(2,1)S(1)}, u32[]{:S(2)}, u32[]{:S(2)}) %collective-permute-start.32) | collective-permute-done | bytes 262176 | tf_op jit(solution)/shard_map/ppermute | solution.py:64
  281.6 3.0 collective-permute-start.36
  284.6 5.1 %convert_add_fusion = (f32[16,128,512]{2,1,0:T(8,128)}, bf16[16,128,512]{2,1,0:T(8,128)(2,1)S(1)}) fusion(bf16[16,128,512]{2,1,0:T(8,128)(2,1)} %collective-permute-done.37, bf16[32,128,512]{2,1,0:T(8,128)(2,1)} %get-tuple-element.52), kind=kLoop, calls=%fused_computation.2 | loop fusion | flops 4194304 | bytes 10485760 | tf_op jit(solution)/shard_map/add | solution.py:101
  300.0 5.6 %collective-permute-done.40 = bf16[4,128,512]{2,1,0:T(8,128)(2,1)S(1)} collective-permute-done((bf16[4,128,512]{2,1,0:T(8,128)(2,1)S(1)}, bf16[4,128,512]{2,1,0:T(8,128)(2,1)S(1)}, u32[]{:S(2)}, u32[]{:S(2)}) %collective-permute-start.40) | collective-permute-done | bytes 524320 | tf_op jit(solution)/shard_map/ppermute | solution.py:64
  305.6 9.4 %collective-permute-done.39 = bf16[4,128,512]{2,1,0:T(8,128)(2,1)} collective-permute-done((bf16[4,128,512]{2,1,0:T(8,128)(2,1)S(1)}, bf16[4,128,512]{2,1,0:T(8,128)(2,1)}, u32[]{:S(2)}, u32[]{:S(2)}) %collective-permute-start.39) | collective-permute-done | bytes 524320 | tf_op jit(solution)/shard_map/ppermute | solution.py:64
  322.0 3.3 collective-permute-done.43
  325.2 5.6 %collective-permute-done.42 = bf16[1,128,512]{2,1,0:T(8,128)(2,1)S(1)} collective-permute-done((bf16[1,128,512]{2,1,0:T(8,128)(2,1)S(1)}, bf16[1,128,512]{2,1,0:T(8,128)(2,1)S(1)}, u32[]{:S(2)}, u32[]{:S(2)}) %collective-permute-start.42) | collective-permute-done | bytes 131104 | tf_op jit(solution)/shard_map/ppermute | solution.py:64
  (227 shorter events, 92.2 us)
Async XLA Ops:
  1.3 33.8 %collective-permute-start = (bf16[1,1,192]{2,0,1:T(2,128)(2,1)S(1)}, bf16[1,1,192]{2,0,1:T(2,128)(2,1)S(1)}, u32[]{:S(2)}, u32[]{:S(2)}) collective-permute-start(bf16[1,1,192]{2,0,1:T(2,128)(2,1)S(1)} %broadcast_in_dim_reshape.12), channel_id=1, source_target_pairs={{0,8},{1,9},{2,10},{3,11},{4,12},{5,13},{6,14},{7,15},{8,0},{9,1},... | collective-permute-start | bytes 1160 | tf_op jit(solution)/shard_map/ppermute | solution.py:64
  4.3 30.9 %collective-permute-start.1 = (bf16[1,1,192]{2,0,1:T(2,128)(2,1)S(1)}, bf16[1,1,192]{2,0,1:T(2,128)(2,1)S(1)}, u32[]{:S(2)}, u32[]{:S(2)}) collective-permute-start(bf16[1,1,192]{2,0,1:T(2,128)(2,1)S(1)} %broadcast_in_dim_reshape.12), channel_id=1, source_target_pairs={{0,16},{1,17},{2,18},{3,19},{4,20},{5,21},{6,22},{7,23},{8,24},{9,... | collective-permute-start | bytes 1160 | tf_op jit(solution)/shard_map/ppermute | solution.py:64
  6.9 28.3 %collective-permute-start.2 = (bf16[1,1,192]{2,0,1:T(2,128)(2,1)S(1)}, bf16[1,1,192]{2,0,1:T(2,128)(2,1)S(1)}, u32[]{:S(2)}, u32[]{:S(2)}) collective-permute-start(bf16[1,1,192]{2,0,1:T(2,128)(2,1)S(1)} %broadcast_in_dim_reshape.12), channel_id=1, source_target_pairs={{0,24},{1,25},{2,26},{3,27},{4,28},{5,29},{6,30},{7,31},{8,16},{9,... | collective-permute-start | bytes 1160 | tf_op jit(solution)/shard_map/ppermute | solution.py:64
  7.8 30.7 %collective-permute-start.10 = (bf16[1,16,1536]{2,1,0:T(8,128)(2,1)S(1)}, bf16[1,16,1536]{2,1,0:T(8,128)(2,1)S(1)}, u32[]{:S(2)}, u32[]{:S(2)}) collective-permute-start(bf16[1,16,1536]{2,1,0:T(8,128)(2,1)S(1)} %broadcast_in_dim_reshape.13), channel_id=1, source_target_pairs={{0,8},{1,9},{2,10},{3,11},{4,12},{5,13},{6,14},{7,15},{8,0},{9,1},... | collective-permute-start | bytes 147464 | tf_op jit(solution)/shard_map/ppermute | solution.py:64
  8.8 30.1 %collective-permute-start.11 = (bf16[1,16,1536]{2,1,0:T(8,128)(2,1)S(1)}, bf16[1,16,1536]{2,1,0:T(8,128)(2,1)S(1)}, u32[]{:S(2)}, u32[]{:S(2)}) collective-permute-start(bf16[1,16,1536]{2,1,0:T(8,128)(2,1)S(1)} %broadcast_in_dim_reshape.13), channel_id=1, source_target_pairs={{0,16},{1,17},{2,18},{3,19},{4,20},{5,21},{6,22},{7,23},{8,24},{9,... | collective-permute-start | bytes 147464 | tf_op jit(solution)/shard_map/ppermute | solution.py:64
  38.9 12.6 %collective-permute-start.22 = (bf16[1,144,512]{2,1,0:T(8,128)(2,1)S(1)}, bf16[1,144,512]{2,1,0:T(8,128)(2,1)S(1)}, u32[]{:S(2)}, u32[]{:S(2)}) collective-permute-start(bf16[1,144,512]{2,1,0:T(8,128)(2,1)S(1)} %bitcast.60), channel_id=1, source_target_pairs={{0,24},{1,25},{2,26},{3,27},{4,28},{5,29},{6,30},{7,31},{8,16},{9,... | collective-permute-start | bytes 442376 | tf_op jit(solution)/shard_map/ppermute | solution.py:64
  49.9 12.0 %collective-permute-start.14 = (bf16[4,16,1536]{2,1,0:T(8,128)(2,1)S(1)}, bf16[4,16,1536]{2,1,0:T(8,128)(2,1)S(1)}, u32[]{:S(2)}, u32[]{:S(2)}) collective-permute-start(bf16[4,16,1536]{2,1,0:T(8,128)(2,1)S(1)} %constant_dynamic-update-slice_fusion.refs_0_), channel_id=1, source_target_pairs={{0,4},{1,5},{2,6},{3,7},{4,0},{5,1},{6,2},{7,3},{8,12},{9,13},{10,... | collective-permute-start | bytes 589832 | tf_op jit(solution)/shard_map/ppermute | solution.py:64
  54.7 16.9 %collective-permute-start.23 = (bf16[4,144,512]{2,1,0:T(8,128)(2,1)S(1)}, bf16[4,144,512]{2,1,0:T(8,128)(2,1)S(1)}, u32[]{:S(2)}, u32[]{:S(2)}) collective-permute-start(bf16[4,144,512]{2,1,0:T(8,128)(2,1)S(1)} %pad_maximum_fusion.1), channel_id=1, source_target_pairs={{0,2},{1,3},{2,0},{3,1},{4,6},{5,7},{6,4},{7,5},{8,10},{9,11},{10,... | collective-permute-start | bytes 1769480 | tf_op jit(solution)/shard_map/ppermute | solution.py:64
  56.3 30.0 %collective-permute-start.24 = (bf16[4,144,512]{2,1,0:T(8,128)(2,1)S(1)}, bf16[4,144,512]{2,1,0:T(8,128)(2,1)S(1)}, u32[]{:S(2)}, u32[]{:S(2)}) collective-permute-start(bf16[4,144,512]{2,1,0:T(8,128)(2,1)S(1)} %pad_maximum_fusion.1), channel_id=1, source_target_pairs={{0,4},{1,5},{2,6},{3,7},{4,0},{5,1},{6,2},{7,3},{8,12},{9,13},{10,... | collective-permute-start | bytes 1769480 | tf_op jit(solution)/shard_map/ppermute | solution.py:64
  57.8 28.5 %collective-permute-start.25 = (bf16[4,144,512]{2,1,0:T(8,128)(2,1)S(1)}, bf16[4,144,512]{2,1,0:T(8,128)(2,1)}, u32[]{:S(2)}, u32[]{:S(2)}) collective-permute-start(bf16[4,144,512]{2,1,0:T(8,128)(2,1)S(1)} %pad_maximum_fusion.1), channel_id=1, source_target_pairs={{0,6},{1,7},{2,4},{3,5},{4,2},{5,3},{6,0},{7,1},{8,14},{9,15},{10,... | collective-permute-start | bytes 1769480 | tf_op jit(solution)/shard_map/ppermute | solution.py:64
  63.7 23.2 %collective-permute-start.19 = (bf16[4,16,1536]{2,1,0:T(8,128)(2,1)S(1)}, bf16[4,16,1536]{2,1,0:T(8,128)(2,1)}, u32[]{:S(2)}, u32[]{:S(2)}) collective-permute-start(bf16[4,16,1536]{2,1,0:T(8,128)(2,1)S(1)} %collective-permute-done.15.refs_3_), channel_id=1, source_target_pairs={{0,1},{1,0},{2,3},{3,2},{4,5},{5,4},{6,7},{7,6},{8,9},{9,8},{10,11... | collective-permute-start | bytes 589832 | tf_op jit(solution)/shard_map/ppermute | solution.py:64
  66.9 44.5 %collective-permute-start.26 = (bf16[4,144,512]{2,1,0:T(8,128)(2,1)S(1)}, bf16[4,144,512]{2,1,0:T(8,128)(2,1)S(1)}, u32[]{:S(2)}, u32[]{:S(2)}) collective-permute-start(bf16[4,144,512]{2,1,0:T(8,128)(2,1)S(1)} %pad_maximum_fusion.1), channel_id=1, source_target_pairs={{0,1},{1,0},{2,3},{3,2},{4,5},{5,4},{6,7},{7,6},{8,9},{9,8},{10,11... | collective-permute-start | bytes 1769480 | tf_op jit(solution)/shard_map/ppermute | solution.py:64
  71.6 39.8 %collective-permute-start.27 = (bf16[4,144,512]{2,1,0:T(8,128)(2,1)S(1)}, bf16[4,144,512]{2,1,0:T(8,128)(2,1)S(1)}, u32[]{:S(2)}, u32[]{:S(2)}) collective-permute-start(bf16[4,144,512]{2,1,0:T(8,128)(2,1)S(1)} %collective-permute-done.23), channel_id=1, source_target_pairs={{0,1},{1,0},{2,3},{3,2},{4,5},{5,4},{6,7},{7,6},{8,9},{9,8},{10,11... | collective-permute-start | bytes 1769480 | tf_op jit(solution)/shard_map/ppermute | solution.py:64
  86.3 25.1 %collective-permute-start.28 = (bf16[4,144,512]{2,1,0:T(8,128)(2,1)S(1)}, bf16[4,144,512]{2,1,0:T(8,128)(2,1)S(1)}, u32[]{:S(2)}, u32[]{:S(2)}) collective-permute-start(bf16[4,144,512]{2,1,0:T(8,128)(2,1)S(1)} %collective-permute-done.24), channel_id=1, source_target_pairs={{0,1},{1,0},{2,3},{3,2},{4,5},{5,4},{6,7},{7,6},{8,9},{9,8},{10,11... | collective-permute-start | bytes 1769480 | tf_op jit(solution)/shard_map/ppermute | solution.py:64
  86.3 26.0 %collective-permute-start.29 = (bf16[4,144,512]{2,1,0:T(8,128)(2,1)}, bf16[4,144,512]{2,1,0:T(8,128)(2,1)S(1)}, u32[]{:S(2)}, u32[]{:S(2)}) collective-permute-start(bf16[4,144,512]{2,1,0:T(8,128)(2,1)} %collective-permute-done.25), channel_id=1, source_target_pairs={{0,1},{1,0},{2,3},{3,2},{4,5},{5,4},{6,7},{7,6},{8,9},{9,8},{10,11... | collective-permute-start | bytes 1769480 | tf_op jit(solution)/shard_map/ppermute | solution.py:64
  196.5 67.0 %collective-permute-start.30 = (bf16[16,64,512]{2,1,0:T(8,128)(2,1)}, bf16[16,64,512]{2,1,0:T(8,128)(2,1)}, u32[]{:S(2)}, u32[]{:S(2)}) collective-permute-start(bf16[16,64,512]{2,1,0:T(8,128)(2,1)} %slice.140), channel_id=1, source_target_pairs={{0,1},{1,0},{2,3},{3,2},{4,5},{5,4},{6,7},{7,6},{8,9},{9,8},{10,11... | collective-permute-start | bytes 3145736 | tf_op jit(solution)/shard_map/ppermute | solution.py:64
  253.7 30.8 %collective-permute-start.37 = (bf16[16,128,512]{2,1,0:T(8,128)(2,1)}, bf16[16,128,512]{2,1,0:T(8,128)(2,1)}, u32[]{:S(2)}, u32[]{:S(2)}) collective-permute-start(bf16[16,128,512]{2,1,0:T(8,128)(2,1)} %slice.152), channel_id=1, source_target_pairs={{0,1},{1,0},{2,3},{3,2},{4,5},{5,4},{6,7},{7,6},{8,9},{9,8},{10,11... | collective-permute-start | bytes 6291464 | tf_op jit(solution)/shard_map/ppermute | solution.py:64
  267.8 12.1 %collective-permute-start.32 = (bf16[4,64,512]{2,1,0:T(8,128)(2,1)S(1)}, bf16[4,64,512]{2,1,0:T(8,128)(2,1)S(1)}, u32[]{:S(2)}, u32[]{:S(2)}) collective-permute-start(bf16[4,64,512]{2,1,0:T(8,128)(2,1)S(1)} %get-tuple-element.72), channel_id=1, source_target_pairs={{0,4},{1,5},{2,6},{3,7},{4,0},{5,1},{6,2},{7,3},{8,12},{9,13},{10,... | collective-permute-start | bytes 786440 | tf_op jit(solution)/shard_map/ppermute | solution.py:64
  268.3 12.1 %collective-permute-start.31 = (bf16[4,64,512]{2,1,0:T(8,128)(2,1)S(1)}, bf16[4,64,512]{2,1,0:T(8,128)(2,1)}, u32[]{:S(2)}, u32[]{:S(2)}) collective-permute-start(bf16[4,64,512]{2,1,0:T(8,128)(2,1)S(1)} %get-tuple-element.70), channel_id=1, source_target_pairs={{0,2},{1,3},{2,0},{3,1},{4,6},{5,7},{6,4},{7,5},{8,10},{9,11},{10,... | collective-permute-start | bytes 786440 | tf_op jit(solution)/shard_map/ppermute | solution.py:64
  281.6 12.5 %collective-permute-start.36 = (bf16[1,64,512]{2,1,0:T(8,128)(2,1)S(1)}, bf16[1,64,512]{2,1,0:T(8,128)(2,1)S(1)}, u32[]{:S(2)}, u32[]{:S(2)}) collective-permute-start(bf16[1,64,512]{2,1,0:T(8,128)(2,1)S(1)} %get-tuple-element.79), channel_id=1, source_target_pairs={{0,24},{1,25},{2,26},{3,27},{4,28},{5,29},{6,30},{7,31},{8,16},{9,... | collective-permute-start | bytes 196616 | tf_op jit(solution)/shard_map/ppermute | solution.py:64
  289.8 15.9 %collective-permute-start.40 = (bf16[4,128,512]{2,1,0:T(8,128)(2,1)S(1)}, bf16[4,128,512]{2,1,0:T(8,128)(2,1)S(1)}, u32[]{:S(2)}, u32[]{:S(2)}) collective-permute-start(bf16[4,128,512]{2,1,0:T(8,128)(2,1)S(1)} %get-tuple-element.68), channel_id=1, source_target_pairs={{0,6},{1,7},{2,4},{3,5},{4,2},{5,3},{6,0},{7,1},{8,14},{9,15},{10,... | collective-permute-start | bytes 1572872 | tf_op jit(solution)/shard_map/ppermute | solution.py:64
  290.7 24.3 %collective-permute-start.39 = (bf16[4,128,512]{2,1,0:T(8,128)(2,1)S(1)}, bf16[4,128,512]{2,1,0:T(8,128)(2,1)}, u32[]{:S(2)}, u32[]{:S(2)}) collective-permute-start(bf16[4,128,512]{2,1,0:T(8,128)(2,1)S(1)} %get-tuple-element.69), channel_id=1, source_target_pairs={{0,4},{1,5},{2,6},{3,7},{4,0},{5,1},{6,2},{7,3},{8,12},{9,13},{10,... | collective-permute-start | bytes 1572872 | tf_op jit(solution)/shard_map/ppermute | solution.py:64
  291.7 23.3 %collective-permute-start.38 = (bf16[4,128,512]{2,1,0:T(8,128)(2,1)S(1)}, bf16[4,128,512]{2,1,0:T(8,128)(2,1)}, u32[]{:S(2)}, u32[]{:S(2)}) collective-permute-start(bf16[4,128,512]{2,1,0:T(8,128)(2,1)S(1)} %get-tuple-element.67), channel_id=1, source_target_pairs={{0,2},{1,3},{2,0},{3,1},{4,6},{5,7},{6,4},{7,5},{8,10},{9,11},{10,... | collective-permute-start | bytes 1572872 | tf_op jit(solution)/shard_map/ppermute | solution.py:64
  318.2 12.6 %collective-permute-start.42 = (bf16[1,128,512]{2,1,0:T(8,128)(2,1)S(1)}, bf16[1,128,512]{2,1,0:T(8,128)(2,1)S(1)}, u32[]{:S(2)}, u32[]{:S(2)}) collective-permute-start(bf16[1,128,512]{2,1,0:T(8,128)(2,1)S(1)} %get-tuple-element.75), channel_id=1, source_target_pairs={{0,16},{1,17},{2,18},{3,19},{4,20},{5,21},{6,22},{7,23},{8,24},{9,... | collective-permute-start | bytes 393224 | tf_op jit(solution)/shard_map/ppermute | solution.py:64
  (57 other events, 499.7 us)

commit v2 on v1

--- a/solution.py
+++ b/solution.py
@@ -71,20 +71,26 @@
     return pos
 
 
-def gather_pieces(x, groups, count):
+def after(values, *others):
+    return lax.optimization_barrier((values, others))[0]
+
+
+def gather_upper(x, groups, count):
     cur = x[None]
     rels = [0]
     for g in groups[:1:-1]:
         ms = masks_of(g)
         cur = jnp.concatenate([cur] + [swap(cur, m, count) for m in ms], axis=0)
         rels = [r ^ m for m in [0] + ms for r in rels]
-    pieces = [(rels, cur)]
-    if len(groups) > 1:
-        for m in masks_of(groups[1]):
-            pieces.append(([r ^ m for r in rels], swap(cur, m, count)))
-    for rs, arr in list(pieces):
-        pieces.append(([r ^ 1 for r in rs], swap(arr, 1, count)))
-    return pieces
+    return rels, cur
+
+
+def gather_plane(rels, cur, groups, count):
+    return [(rels, cur)] + [([r ^ m for r in rels], swap(cur, m, count)) for m in masks_of(groups[1])]
+
+
+def gather_core(pieces, count):
+    return pieces + [([r ^ 1 for r in rels], swap(arr, 1, count)) for rels, arr in pieces]
 
 
 def natural_order(pieces, me, count):
@@ -96,17 +102,14 @@
     return jnp.take(both, jnp.asarray(where, jnp.int32)[jnp.arange(count) ^ me], axis=0)
 
 
-def scatter_sum(pk, groups, count):
-    half = count // 2
-    cur = pk[:half].astype(f32) + swap(pk[half:], 1, count).astype(f32)
-    for g in groups[1:]:
-        ms = masks_of(g)
-        n = cur.shape[0] // (len(ms) + 1)
-        parts = [swap(cur[(k + 1) * n : (k + 2) * n].astype(bf16), m, count).astype(f32) for k, m in enumerate(ms)]
-        cur = cur[:n]
-        for part in parts:
-            cur = cur + part
-    return cur[0]
+def split_sum(terms, group):
+    n = terms[0].shape[0] >> len(group)
+    parts = [sum(t[k * n : (k + 1) * n].astype(f32) for t in terms) for k in range(1 << len(group))]
+    return parts[0], [p.astype(bf16) for p in parts[1:]]
+
+
+def send_parts(parts, group, count):
+    return [swap(p, m, count) for p, m in zip(parts, masks_of(group))]
 
 
 def total(x, groups, count):
@@ -118,17 +121,32 @@
     return x
 
 
-def attn_fwd_body(me_ref, x_ref, rowv_ref, colv_ref, mask_ref, bias_ref, *refs, plan, rpd):
+def lay_vectors(raw, per, rowv_ref):
+    unit = LANES // 2
+    each = per // unit
+    low = lax.broadcasted_iota(jnp.int32, (1, LANES), 1) < unit
+
+    def half(c, high):
+        owner, part = divmod(c, each)
+        got = raw[owner, part // 2 : part // 2 + 1, :].astype(f32)
+        return got if part % 2 == high else pltpu.roll(got, unit, 1)
+
+    for m in range((8 * D + FF) // LANES):
+        row, col = divmod(m * LANES, D)
+        rowv_ref[row : row + 1, col : col + LANES] = jnp.where(low, half(2 * m, 0), half(2 * m + 1, 1))
+
+
+def attn_fwd_body(me_ref, x_ref, mask_ref, bias_ref, *refs, plan, rpd, per):
     pieces = refs[: len(plan)]
-    (oT_ref, o_ref, qT_ref, kT_ref, v_ref, pT_ref, h1T_ref, w_ref) = refs[len(plan) : len(plan) + 8]
-    wT, xs, h1p, kn, vT, osc, sem = refs[len(plan) + 8 :]
+    (oT_ref, o_ref, qT_ref, kT_ref, v_ref, pT_ref, h1T_ref, w_ref, rowv_ref) = refs[len(plan) : len(plan) + 9]
+    wT, xs, h1p, kn, vT, osc, colv_ref, raw, sem = refs[len(plan) + 9 :]
 
     @pl.when(pl.program_id(0) == 0)
     def _():
         copies = []
         for ref, rels in zip(pieces, plan):
             if rels is None:
-                copies.append(pltpu.make_async_copy(ref, w_ref, sem.at[len(copies)]))
+                copies.append(pltpu.make_async_copy(ref, (w_ref, rowv_ref)[len(copies)], sem.at[len(copies)]))
                 continue
             for t, r in enumerate(rels):
                 at = pl.multiple_of((r ^ me_ref[0]) * rpd, rpd)
@@ -137,12 +155,20 @@
                         ref.at[t, :, pl.ds(0, 3 * D)], w_ref.at[pl.ds(at, rpd), :], sem.at[len(copies)]
                     )
                 )
+                copies.append(
+                    pltpu.make_async_copy(ref.at[t, :, pl.ds(3 * D, LANES)], raw.at[r ^ me_ref[0]], sem.at[len(copies)])
+                )
         for c in copies:
             c.start()
         for c in copies:
             c.wait()
         for a in range(3 * D // LANES):
             wT[LANES * a : LANES * (a + 1), :] = w_ref[:, LANES * a : LANES * (a + 1)].T
+        if plan[0] is not None:
+            rowv_ref[12:16, :] = jnp.zeros((4, D), f32)
+            lay_vectors(raw, per, rowv_ref)
+        for a in range(D // LANES):
+            colv_ref[LANES * a : LANES * (a + 1), :] = rowv_ref[0:8, LANES * a : LANES * (a + 1)].T
 
     xs[0:GR, :] = x_ref[...].astype(f32)
     gain = rowv_ref[0:1, :]
@@ -160,9 +186,9 @@
             h1T_ref[LANES * a : LANES * a + LANES, LANES * w : LANES * w + LANES] = h[:, LANES * a : LANES * a + LANES].T
     h1T_ref[D : D + 16, :] = jnp.ones((16, GL), bf16)
     hp = h1p[...]
-    qT_ref[...] = (nt(wT[0:D, :], hp) + colv_ref[:, 0:1]).astype(bf16)
+    qT_ref[...] = (nt(wT[0:D, :], hp) + colv_ref[:, 2:3]).astype(bf16)
     kT_ref[...] = nt(wT[D : 2 * D, :], hp).astype(bf16)
-    vT[...] = (nt(wT[2 * D : 3 * D, :], hp) + colv_ref[:, 1:2]).astype(bf16)
+    vT[...] = (nt(wT[2 * D : 3 * D, :], hp) + colv_ref[:, 3:4]).astype(bf16)
     kn[...] = nn(hp, w_ref[:, D : 2 * D]).astype(bf16)
     v_ref[...] = (nn(hp, w_ref[:, 2 * D : 3 * D]) + value_bias).astype(bf16)
     lane = lax.broadcasted_iota(jnp.int32, (1, LANES), 1) // HD
@@ -202,15 +228,15 @@
 SMEM = pl.BlockSpec(memory_space=pltpu.SMEM)
 
 
-def attn_fwd(me, x, rowv, colv, allowed, bias, plan, pieces, rpd):
+def attn_fwd(me, x, allowed, bias, plan, pieces, rpd, per, count):
     n = x.shape[0] // GR
-    copies = sum(1 if r is None else len(r) for r in plan)
+    copies = sum(1 if r is None else 2 * len(r) for r in plan)
     rb = pl.BlockSpec((GR, D), lambda i: (i, 0))
     tb = pl.BlockSpec((D, GL), lambda i: (0, i))
     return pl.pallas_call(
-        functools.partial(attn_fwd_body, plan=plan, rpd=rpd),
+        functools.partial(attn_fwd_body, plan=plan, rpd=rpd, per=per),
         grid=(n,),
-        in_specs=[SMEM, rb, whole((8, D)), whole((D, 2)), pl.BlockSpec((GW, KP, LANES), lambda i: (i, 0, 0)), whole((HEADS, KP, LANES))]
+        in_specs=[SMEM, rb, pl.BlockSpec((GW, KP, LANES), lambda i: (i, 0, 0)), whole((HEADS, KP, LANES))]
         + any_specs(len(pieces)),
         out_specs=[
             tb,
@@ -221,6 +247,7 @@
             pl.BlockSpec((GW, HEADS, KP, LANES), lambda i: (i, 0, 0, 0)),
             pl.BlockSpec((D + 16, GL), lambda i: (0, i)),
             whole((D, 3 * D)),
+            whole((16, D)),
         ],
         out_shape=[
             sds((D, n * GL), bf16),
@@ -231,6 +258,7 @@
             sds((n * GW, HEADS, KP, LANES), bf16),
             sds((D + 16, n * GL), bf16),
             sds((D, 3 * D), bf16),
+            sds((16, D), f32),
         ],
         scratch_shapes=[
             pltpu.VMEM((3 * D, D), bf16),
@@ -239,24 +267,25 @@
             pltpu.VMEM((GL, D), bf16),
             pltpu.VMEM((D, GL), bf16),
             pltpu.VMEM((GR + 8, D), f32),
+            pltpu.VMEM((D, 8), f32),
+            pltpu.VMEM((count, max(rpd, 16), LANES), bf16),
             pltpu.SemaphoreType.DMA((copies,)),
         ],
-        compiler_params=params(56),
-        cost_estimate=pl.CostEstimate(flops=8 * 10**9, bytes_accessed=20 * 10**6, transcendentals=4 * 10**6),
+        compiler_params=params(60),
+        cost_estimate=pl.CostEstimate(flops=10**7, bytes_accessed=10**5, transcendentals=0),
         name="attn_fwd",
-    )(me, x, rowv, colv, allowed, bias, *pieces)
-
-
-def mlp_body(me_ref, x_ref, o_ref, g_ref, vld_ref, bf1_ref, rowv_ref, *refs, plan, rows, owners, rpd, groups):
+    )(me, x, allowed, bias, *pieces)
+
+
+def mlp_body(me_ref, x_ref, o_ref, g_ref, vld_ref, rowv_ref, *refs, plan, rows, owners, rpd, groups):
     pieces = refs[: len(plan)]
     (mid_ref, dmid_ref, e_ref, vec_ref, dbf1_ref, sa_ref, p_ref, v_ref) = refs[len(plan) : len(plan) + 8]
     rest = refs[len(plan) + 8 :]
     if owners:
-        pk_ref = rest[0]
-        rest = rest[1:]
+        keep_ref, send_ref = rest[:2]
     else:
         dU_ref, dV_ref = rest[:2]
-        rest = rest[2:]
+    rest = rest[2:]
     u4, h2, h2T, gp, gT, dh2, es, dus, sem = rest
     j = pl.program_id(0)
     padded = h2.shape[0]
@@ -323,7 +352,7 @@
         for c in later:
             c.wait()
 
-    up_bias = bf1_ref[...]
+    up_bias = rowv_ref[pl.ds(8 + j, 1), :]
 
     def chunk(k, acc):
         at = pl.ds(pl.multiple_of(k * part, 16), part)
@@ -352,11 +381,18 @@
     if owners:
         me = me_ref[0]
         at = pl.ds(pl.multiple_of(j * rpd, rpd), rpd)
-        for k in range(owners):
-            pk_ref[place_of(k ^ me, groups), at, :] = dU[rpd * k : rpd * k + rpd]
         per = 512 // (4 * rpd)
-        for k in range(per):
-            pk_ref[place_of((j * per + k) ^ me, groups), 4 * rpd : 8 * rpd, :] = dV[4 * rpd * k : 4 * rpd * k + 4 * rpd]
+
+        def store(flip):
+            for k in range(owners):
+                to = (keep_ref, send_ref)[(k ^ flip) & 1]
+                to[place_of(k ^ me, groups[1:]), at, :] = dU[rpd * k : rpd * k + rpd]
+            for k in range(per):
+                to = (keep_ref, send_ref)[(k ^ flip) & 1]
+                to[place_of((j * per + k) ^ me, groups[1:]), 4 * rpd : 8 * rpd, :] = dV[4 * rpd * k : 4 * rpd * k + 4 * rpd]
+
+        pl.when(me & 1 == 0)(lambda: store(0))
+        pl.when(me & 1 == 1)(lambda: store(1))
     else:
         dU_ref[...] = dU
         dV_ref[...] = dV
@@ -386,21 +422,21 @@
         vec_ref[4:8, :] = jnp.zeros((4, D), f32)
 
 
-def mlp(me, x, o, g, vld, bf1, rowv, plan, pieces, rpd, owners, count, groups):
+def mlp(me, x, o, g, vld, rowv, plan, pieces, rpd, owners, count, groups):
     rows = x.shape[0]
     padded = -(-rows // LANES) * LANES
     copies = sum(1 if r is None else 3 * len(r) for r in plan)
     rb = whole((rows, D))
     if owners:
-        grad_specs = [whole((count, 8 * rpd, 512))]
-        grad_shapes = [sds((count, 8 * rpd, 512), bf16)]
+        grad_specs = [whole((count // 2, 8 * rpd, 512))] * 2
+        grad_shapes = [sds((count // 2, 8 * rpd, 512), bf16)] * 2
     else:
         grad_specs = [pl.BlockSpec((D, 512), lambda j: (0, j)), pl.BlockSpec((512, D), lambda j: (j, 0))]
         grad_shapes = [sds((D, FF), bf16), sds((FF, D), bf16)]
     return pl.pallas_call(
         functools.partial(mlp_body, plan=plan, rows=rows, owners=count if owners else 0, rpd=rpd, groups=groups),
         grid=(FF // 512,),
-        in_specs=[SMEM, rb, rb, rb, whole((rows, 1)), pl.BlockSpec((1, 512), lambda j: (0, j)), whole((8, D))]
+        in_specs=[SMEM, rb, rb, rb, whole((rows, 1)), whole((16, D))]
         + any_specs(len(pieces)),
         out_specs=[rb, rb, pl.BlockSpec((rows, 512), lambda j: (0, j)), whole((8, D)), pl.BlockSpec((1, 512), lambda j: (0, j)), whole((8, D)), whole((D, D)), whole((128, 16, D))]
         + grad_specs,
@@ -418,9 +454,9 @@
             pltpu.SemaphoreType.DMA((copies,)),
         ],
         compiler_params=params(60),
-        cost_estimate=pl.CostEstimate(flops=18 * 10**9, bytes_accessed=30 * 10**6, transcendentals=7 * 10**6),
+        cost_estimate=pl.CostEstimate(flops=10**7, bytes_accessed=10**5, transcendentals=0),
         name="mlp",
-    )(me, x, o, g, vld, bf1, rowv, *pieces)
+    )(me, x, o, g, vld, rowv, *pieces)
 
 
 def attn_bwd_body(me_ref, dmid_ref, p_ref, oT_ref, qT_ref, kT_ref, v_ref, pT_ref, h1T_ref, *refs, owners, rpd, groups):
@@ -476,11 +512,17 @@
     def _():
         if owners:
             me = me_ref[0]
-            for k in range(owners):
-                pos = place_of(k ^ me, groups)
-                for q in range(3):
-                    grads[0][pos, rpd * q : rpd * q + rpd, :] = dw[rpd * k : rpd * k + rpd, D * q : D * q + D].astype(bf16)
-                grads[0][pos, 3 * rpd : 4 * rpd, :] = dproj[rpd * k : rpd * k + rpd, :].astype(bf16)
+
+            def store(flip):
+                for k in range(owners):
+                    to = grads[(k ^ flip) & 1]
+                    pos = place_of(k ^ me, groups[1:])
+                    for q in range(3):
+                        to[pos, rpd * q : rpd * q + rpd, :] = dw[rpd * k : rpd * k + rpd, D * q : D * q + D].astype(bf16)
+                    to[pos, 3 * rpd : 4 * rpd, :] = dproj[rpd * k : rpd * k + rpd, :].astype(bf16)
+
+            pl.when(me & 1 == 0)(lambda: store(0))
+            pl.when(me & 1 == 1)(lambda: store(1))
         else:
             grads[0][...] = dw[0:D, :].astype(bf16)
             grads[1][...] = dproj[...].astype(bf16)
@@ -494,7 +536,7 @@
         return pl.BlockSpec((r, GL), lambda i: (0, i))
 
     if owners:
-        grad_shapes = [sds((count, 4 * rpd, D), bf16)]
+        grad_shapes = [sds((count // 2, 4 * rpd, D), bf16)] * 2
     else:
         grad_shapes = [sds((D, 3 * D), bf16), sds((D, D), bf16)]
     return pl.pallas_call(
@@ -511,7 +553,7 @@
             pltpu.VMEM((D, D), f32),
         ],
         compiler_params=params(60),
-        cost_estimate=pl.CostEstimate(flops=15 * 10**9, bytes_accessed=25 * 10**6, transcendentals=0),
+        cost_estimate=pl.CostEstimate(flops=10**7, bytes_accessed=10**5, transcendentals=0),
         name="attn_bwd",
     )(me, dmid, p, oT, qT, kT, v, pT, h1T)
 
@@ -548,12 +590,12 @@
     return pl.pallas_call(
         grad_in_body,
         grid=(n,),
-        in_specs=[pl.BlockSpec((3 * D, GL), lambda i: (0, i)), whole((D, 3 * D)), rb, rb, whole((8, D))],
+        in_specs=[pl.BlockSpec((3 * D, GL), lambda i: (0, i)), whole((D, 3 * D)), rb, rb, whole((16, D))],
         out_specs=[rb, whole((8, D))],
         out_shape=[sds((n * GR, D), f32), sds((8, D), f32)],
         scratch_shapes=[pltpu.VMEM((GR + 8, D), f32)],
-        compiler_params=params(40),
-        cost_estimate=pl.CostEstimate(flops=4 * 10**9, bytes_accessed=16 * 10**6, transcendentals=0),
+        compiler_params=params(60),
+        cost_estimate=pl.CostEstimate(flops=10**7, bytes_accessed=10**5, transcendentals=0),
         name="grad_in",
     )(dmT, w, x, dmid, rowv)
 
@@ -582,67 +624,76 @@
     return pl.pallas_call(
         finish_body,
         grid=(n,),
-        in_specs=[pl.BlockSpec((GR, FF), lambda i: (i, 0)), whole((128, 16, D)), rb, rb, pl.BlockSpec((GR, 1), lambda i: (i, 0)), whole((8, D)), whole((8, D))],
+        in_specs=[pl.BlockSpec((GR, FF), lambda i: (i, 0)), whole((128, 16, D)), rb, rb, pl.BlockSpec((GR, 1), lambda i: (i, 0)), whole((16, D)), whole((8, D))],
         out_specs=[rb, whole((8, D))],
         out_shape=[sds((n * GR, D), bf16), sds((8, D), f32)],
-        compiler_params=params(40),
-        cost_estimate=pl.CostEstimate(flops=3 * 10**9, bytes_accessed=16 * 10**6, transcendentals=0),
+        compiler_params=params(60),
+        cost_estimate=pl.CostEstimate(flops=10**7, bytes_accessed=10**5, transcendentals=0),
         name="finish",
     )(e, v, mid, x, vld, rowv, sa)
 
 
-def place_code(shape, axis):
-    c = lax.broadcasted_iota(jnp.int32, shape, axis)
-    return jnp.where(c < CELLS, (2 * WSIDE - 1) * (c // WSIDE) + c % WSIDE, -1000)
+def place_hits(shape, axis, rev=0):
+    c = lax.broadcasted_iota(jnp.int32, shape, 1 - axis)
+    code = jnp.where(c < CELLS, (2 * WSIDE - 1) * (c // WSIDE) + c % WSIDE, -1000)
+    if rev:
+        code = rev - code
+    return jnp.where(code == lax.broadcasted_iota(jnp.int32, shape, axis), 1.0, 0.0).astype(bf16)
 
 
 def rel_bias_body(t_ref, o_ref):
-    t = t_ref[...]
-    hi = t.astype(bf16)
-    r = t - hi.astype(f32)
-    md = r.astype(bf16)
-    lo = (r - md.astype(f32)).astype(bf16)
-    three = jnp.concatenate([hi, md, lo], axis=0)
-    code = place_code((RP, LANES), 1) - lax.broadcasted_iota(jnp.int32, (RP, LANES), 0) + 180
-
-    def step(j, carry):
-        hit = jnp.where(code == (2 * WSIDE - 1) * (j // WSIDE) + j % WSIDE, 1.0, 0.0).astype(bf16)
-        b = nn(three, hit)
-        o_ref[:, pl.ds(j, 1), :] = (b[0:16] + b[16:32] + b[32:48]).reshape(HEADS, 1, LANES)
+    keys = place_hits((KP, 192), 1)
+    queries = place_hits((256, LANES), 0)
+
+    def head(h, carry):
+        row = pltpu.roll(jnp.broadcast_to(t_ref[pl.ds(h, 1), :], (8, RP)), 0, 1, stride=1, stride_axis=0)
+        t = jnp.concatenate([pltpu.roll(row, (8 * k - 180) % RP, 1)[:, 0:256] for k in range(24)], axis=0)
+        hi = t.astype(bf16)
+        r = t - hi.astype(f32)
+        md = r.astype(bf16)
+        lo = (r - md.astype(f32)).astype(bf16)
+        o_ref[h] = sum(nn(nn(keys, part).astype(bf16), queries) for part in (lo, md, hi))
         return carry
 
-    o_ref[:, CELLS:KP, :] = jnp.zeros((HEADS, KP - CELLS, LANES), f32)
-    lax.fori_loop(0, CELLS, step, 0)
+    lax.fori_loop(0, HEADS, head, 0, unroll=8)
 
 
 def rel_bias(table):
     return pl.pallas_call(
         rel_bias_body,
         out_shape=sds((HEADS, KP, LANES), f32),
-        cost_estimate=pl.CostEstimate(flops=6 * 10**9, bytes_accessed=10**6, transcendentals=0),
+        compiler_params=params(60),
+        cost_estimate=pl.CostEstimate(flops=10**7, bytes_accessed=10**5, transcendentals=0),
         name="rel_bias",
     )(table)
 
 
 def rel_grad_body(a_ref, o_ref):
-    code = place_code((LANES, RP), 0) - lax.broadcasted_iota(jnp.int32, (LANES, RP), 1) + 180
-
-    def step(j, acc):
-        hit = jnp.where(code == (2 * WSIDE - 1) * (j // WSIDE) + j % WSIDE, 1.0, 0.0).astype(bf16)
-        t = a_ref[:, pl.ds(j, 1), :].reshape(HEADS, LANES)
-        hi = t.astype(bf16)
-        lo = (t - hi.astype(f32)).astype(bf16)
-        b = nn(jnp.concatenate([hi, lo], axis=0), hit)
-        return acc + b[0:16] + b[16:32]
-
-    o_ref[...] = lax.fori_loop(0, CELLS, step, jnp.zeros((HEADS, RP), f32))
+    keys = place_hits((192, KP), 0, 191)
+    queries = place_hits((LANES, 256), 1)
+    zero = jnp.zeros((8, RP - 256), f32)
+
+    def head(h, carry):
+        a = a_ref[h]
+        hi = a.astype(bf16)
+        lo = (a - hi.astype(f32)).astype(bf16)
+        b = nn(nn(keys, hi).astype(bf16), queries) + nn(nn(keys, lo).astype(bf16), queries)
+        t = jnp.zeros((8, RP), f32)
+        for k in range(24):
+            t = t + pltpu.roll(jnp.concatenate([b[8 * k : 8 * k + 8], zero], axis=1), (8 * k - 11) % RP, 1)
+        t = pltpu.roll(t, 0, 1, stride=1, stride_axis=0)
+        o_ref[pl.ds(h, 1), :] = jnp.sum(t, axis=0, keepdims=True)
+        return carry
+
+    lax.fori_loop(0, HEADS, head, 0, unroll=8)
 
 
 def rel_grad(acc):
     return pl.pallas_call(
         rel_grad_body,
         out_shape=sds((HEADS, RP), f32),
-        cost_estimate=pl.CostEstimate(flops=6 * 10**9, bytes_accessed=10**6, transcendentals=0),
+        compiler_params=params(60),
+        cost_estimate=pl.CostEstimate(flops=10**7, bytes_accessed=10**5, transcendentals=0),
         name="rel_grad",
     )(acc)
 
@@ -656,8 +707,13 @@
     me = lax.axis_index("dp") * inner + lax.axis_index("shard")
     me_s = me.astype(jnp.int32).reshape(1)
 
-    vec_pieces = gather_pieces(vectors.reshape(1, -1), groups, count)
-    attn_pieces = gather_pieces(qkv_weight.reshape(rpd, 3 * D), groups, count)
+    per = vectors.shape[0]
+    if direct:
+        own = jnp.pad(vectors, (0, rpd * LANES - per)).reshape(rpd, LANES)
+        own = jnp.concatenate([qkv_weight.reshape(rpd, 3 * D), own], axis=1)
+    else:
+        own = jnp.concatenate([qkv_weight, vectors]).reshape(1, -1)
+    rels, attn_up = gather_upper(own, groups, count)
     packed = jnp.concatenate(
         [
             proj_weight.reshape(1, rpd, D),
@@ -666,22 +722,17 @@
         ],
         axis=0,
     )
-    mlp_pieces = gather_pieces(packed.reshape(9 * rpd, D), groups, count)
-    vec = natural_order(vec_pieces, me, count).reshape(-1).astype(f32)
-    rowv = vec[: 8 * D].reshape(8, D)
-    colv = rowv[2:4].T
-    bf1 = vec[8 * D :].reshape(1, FF)
+    packed = after(packed.reshape(9 * rpd, D), attn_up)
+    _, mlp_up = gather_upper(packed, groups, count)
+    attn_pieces = gather_core(gather_plane(rels, attn_up, groups, count), count)
+    mlp_pieces = gather_plane(rels, mlp_up, groups, count)
     if direct:
         attn_plan = [r for r, _ in attn_pieces]
         attn_w = [a for _, a in attn_pieces]
-        mlp_plan = [r for r, _ in mlp_pieces]
-        mlp_w = [a.reshape(-1, 9, rpd, D) for _, a in mlp_pieces]
     else:
-        attn_plan = [None]
-        attn_w = [natural_order(attn_pieces, me, count).reshape(D, 3 * D)]
-        both = natural_order(mlp_pieces, me, count).reshape(count, 9, rpd, D)
-        mlp_plan = [None] * 3
-        mlp_w = [both[:, 0].reshape(D, D), both[:, 1:5].transpose(1, 0, 2, 3).reshape(4, D, 512), both[:, 5:].reshape(128, 16, D)]
+        attn_plan = [None] * 2
+        both = natural_order(attn_pieces, me, count).reshape(count, -1)
+        attn_w = [both[:, : 3 * D * rpd].reshape(D, 3 * D), jnp.pad(both[:, 3 * D * rpd :].astype(f32).reshape(12, D), ((0, 4), (0, 0)))]
 
     bias = rel_bias(jnp.pad(rel_table.T * LOG2E, ((0, 0), (0, RP - RELN))))
     reg = regions.reshape(windows, CELLS)
@@ -691,31 +742,61 @@
     allowed = jnp.pad(allowed, ((0, 0), (0, KP - CELLS), (0, LANES - CELLS)), constant_values=NEG)
     vld = validity.astype(f32).reshape(rows, 1)
 
-    oT, o, qT, kT, v, pT, h1T, w_full = attn_fwd(me_s, tokens, rowv, colv, allowed, bias, attn_plan, attn_w, rpd)
-    got = mlp(me_s, tokens, o, cotangent, vld, bf1, rowv, mlp_plan, mlp_w, rpd, direct, count, groups)
+    x = after(tokens, mlp_up)
+    oT, o, qT, kT, v, pT, h1T, w_full, rowv = attn_fwd(me_s, x, allowed, bias, attn_plan, attn_w, rpd, per, count)
+
+    held = after([a for _, a in mlp_pieces], o)
+    mlp_pieces = gather_core([(r, a) for (r, _), a in zip(mlp_pieces, held)], count)
+    if direct:
+        mlp_plan = [r for r, _ in mlp_pieces]
+        mlp_w = [a.reshape(-1, 9, rpd, D) for _, a in mlp_pieces]
+    else:
+        both = natural_order(mlp_pieces, me, count).reshape(count, 9, rpd, D)
+        mlp_plan = [None] * 3
+        mlp_w = [both[:, 0].reshape(D, D), both[:, 1:5].transpose(1, 0, 2, 3).reshape(4, D, 512), both[:, 5:].reshape(128, 16, D)]
+    got = mlp(me_s, tokens, o, cotangent, vld, rowv, mlp_plan, mlp_w, rpd, direct, count, groups)
     mid, dmid, e, vec_two, dbf1, branch_sq, p_full, v_full = got[:8]
     order = None
     if direct:
-        mlp_pk = got[8]
+        mlp_keep, mlp_send = got[8:]
     else:
         blocks = jnp.arange(count)
         where = place_of(blocks, groups)
         order = jnp.zeros((count,), jnp.int32).at[where].set(blocks.astype(jnp.int32)) ^ me
         dU = got[8].reshape(count, rpd, 4, 512).transpose(0, 2, 1, 3).reshape(count, 4 * rpd, 512)
-        mlp_pk = jnp.take(jnp.concatenate([dU, got[9].reshape(count, 4 * rpd, D)], axis=1), order, axis=0)
-    mlp_sum = scatter_sum(mlp_pk, groups, count)
-
+        pk = jnp.take(jnp.concatenate([dU, got[9].reshape(count, 4 * rpd, D)], axis=1), order, axis=0)
+        mlp_keep, mlp_send = pk[: count // 2], pk[count // 2 :]
+
+    other = swap(mlp_send, 1, count)
+    result, squares = finish(e, v_full, mid, tokens, vld, rowv, branch_sq)
+    other = after(other, result)
+    mlp_own, parts = split_sum([mlp_keep, other], groups[1])
+    mlp_got = send_parts(parts, groups[1], count)
+    dmid = after(dmid, parts)
     got = attn_bwd(me_s, dmid, p_full, oT, qT, kT, v, pT, h1T, rpd, direct, count, groups)
     dmT, score_sums, vec_one = got[:3]
     if direct:
-        attn_pk = got[3]
+        attn_keep, attn_send = got[3:]
     else:
         dW = got[3].reshape(count, rpd, 3, D).transpose(0, 2, 1, 3).reshape(count, 3 * rpd, D)
-        attn_pk = jnp.take(jnp.concatenate([dW, got[4].reshape(count, rpd, D)], axis=1), order, axis=0)
-    attn_sum = scatter_sum(attn_pk, groups, count)
+        pk = jnp.take(jnp.concatenate([dW, got[4].reshape(count, rpd, D)], axis=1), order, axis=0)
+        attn_keep, attn_send = pk[: count // 2], pk[count // 2 :]
+    mlp_got, attn_send, score_sums, dmT = lax.optimization_barrier((mlp_got, attn_send, score_sums, dmT))
+    other = swap(attn_send, 1, count)
+    attn_own, parts = split_sum([attn_keep, other], groups[1])
+    attn_got = send_parts(parts, groups[1], count)
+    mlp_terms = [mlp_own] + mlp_got
+    dmT = after(dmT, parts)
     grad_tokens, vec_in = grad_in(dmT, w_full, tokens, dmid, rowv)
-    table = rel_grad(score_sums)
-    result, squares = finish(e, v_full, mid, tokens, vld, rowv, branch_sq)
+    table = rel_grad(after(score_sums, parts))
+    attn_terms = [attn_own] + after(attn_got, grad_tokens)
+    for g in groups[2:]:
+        mlp_own, parts = split_sum(mlp_terms, g)
+        mlp_terms = [mlp_own] + send_parts(parts, g, count)
+        attn_own, parts = split_sum(attn_terms, g)
+        attn_terms = [attn_own] + send_parts(parts, g, count)
+    mlp_sum = sum(t[0].astype(f32) for t in mlp_terms)
+    attn_sum = sum(t[0].astype(f32) for t in attn_terms)
     small = jnp.concatenate(
         [
             vec_in[0:2],

time: 333 us -> 237 us (0.71)
  waiting for transfers between devices: 68.1 us -> 22.8 us
  local copies, waits for them, and re-layouts: 38.9 us -> 17 us
  Pallas kernels: 156 us -> 139 us
  starting transfers between devices: 52.9 us -> 44.8 us
  other arithmetic: 15.7 us -> 11.5 us
    ppermute x51 -> x41, waiting for transfers between devices: 68.1 us -> 22.8 us  [swap(): return lax.ppermute(x, AXES, [(i, i ^ mask) for i in range(count)])]
    pallas_call x3, Pallas kernels: 60.2 us -> 37.1 us  [the longest x1 25 us: attn_fwd(): pl.pallas_call(functools.partial(attn_fwd_body, plan=plan, rpd=rpd, per=p...]
    unnamed x68 -> x61, local copies, waits for them, and re-layouts: 18.4 us -> 3.56 us
    ppermute x51 -> x41, starting transfers between devices: 52.9 us -> 44.8 us  [swap(): return lax.ppermute(x, AXES, [(i, i ^ mask) for i in range(count)])]
    slice x7 -> x0, local copies, waits for them, and re-layouts: 6.29 us -> none  [the longest x2 5.46 us: scatter_sum(): cur = pk[:half].astype(f32) + swap(pk[half:], 1, count).astype(f32)]
    pallas_call x1, Pallas kernels: 6.49 us -> 10.2 us  [finish(): pl.pallas_call(finish_body, grid=(n,), in_specs=[pl.BlockSpec((GR, FF), l...]
  transfers between devices with their start and end apart: 51 -> 41, of which waited for: 22 -> 13; matrix products, arithmetic and copies ran while one was open for 10% -> 9% of each run, Pallas kernels for 22% -> 40%
where the time goes in v2:
time: 237 us; the launch traced here: 236 us
  Pallas kernels  139 us (59%)
  starting transfers between devices  44.8 us (19%)
  waiting for transfers between devices  22.8 us (10%)
  local copies, waits for them, and re-layouts  17 us (7%)
  other arithmetic  11.5 us (5%)
    pallas_call x1, Pallas kernels, mlp(): pl.pallas_call(functools.partial(mlp_body, plan=plan, rows=rows, owners=c...  45 us
    ppermute x41, starting transfers between devices, swap(): return lax.ppermute(x, AXES, [(i, i ^ mask) for i in range(count)])  44.8 us
    pallas_call x1, Pallas kernels, attn_bwd(): pl.pallas_call(functools.partial(attn_bwd_body, owners=count if owners el...  36.3 us
    pallas_call x1, Pallas kernels, attn_fwd(): pl.pallas_call(functools.partial(attn_fwd_body, plan=plan, rpd=rpd, per=p...  25 us
    ppermute x41, waiting for transfers between devices, swap(): return lax.ppermute(x, AXES, [(i, i ^ mask) for i in range(count)])  22.8 us
    pallas_call x1, Pallas kernels, finish(): pl.pallas_call(finish_body, grid=(n,), in_specs=[pl.BlockSpec((GR, FF), l...  10.2 us
    pallas_call x1, Pallas kernels, grad_in(): pl.pallas_call(grad_in_body, grid=(n,), in_specs=[pl.BlockSpec((3 * D, GL...  10.2 us
    pallas_call x1, Pallas kernels, rel_bias(): pl.pallas_call(rel_bias_body, out_shape=sds((HEADS, KP, LANES), f32), com...  7.36 us
  transfers between devices with their start and end apart: 41, of which 13 were waited for; matrix products, arithmetic and copies ran while one was open for 9% of the time, Pallas kernels for 40%

profile of v2, /device:TPU:0, one launch (start us, length us, event | category | flops | bytes accessed | tf_op | source)
XLA Modules:
  0.0 236.2 jit_solution(8131163554509226823)
XLA Ops:
  2.2 3.1 %collective-permute-start = (bf16[1,16,1664]{2,1,0:T(8,128)(2,1)S(1)}, bf16[1,16,1664]{2,1,0:T(8,128)(2,1)S(1)}, u32[]{:S(2)}, u32[]{:S(2)}) collective-permute-start(bf16[1,16,1664]{2,1,0:T(8,128)(2,1)S(1)} %maximum_bitcast_fusion), channel_id=1, source_target_pairs={{0,8},{1,9},{2,10},{3,11},{4,12},{5,13},{6,14},{7,15},{8,0},{9,1},... | collective-permute-start | bytes 159752 | tf_op jit(solution)/shard_map/ppermute | solution.py:64
  5.3 2.6 %collective-permute-start.1 = (bf16[1,16,1664]{2,1,0:T(8,128)(2,1)S(1)}, bf16[1,16,1664]{2,1,0:T(8,128)(2,1)S(1)}, u32[]{:S(2)}, u32[]{:S(2)}) collective-permute-start(bf16[1,16,1664]{2,1,0:T(8,128)(2,1)S(1)} %maximum_bitcast_fusion), channel_id=1, source_target_pairs={{0,16},{1,17},{2,18},{3,19},{4,20},{5,21},{6,22},{7,23},{8,24},{9,... | collective-permute-start | bytes 159752 | tf_op jit(solution)/shard_map/ppermute | solution.py:64
  11.4 2.5 %collective-permute-done.2 = bf16[1,16,1664]{2,1,0:T(8,128)(2,1)S(1)} collective-permute-done((bf16[1,16,1664]{2,1,0:T(8,128)(2,1)S(1)}, bf16[1,16,1664]{2,1,0:T(8,128)(2,1)S(1)}, u32[]{:S(2)}, u32[]{:S(2)}) %collective-permute-start.2) | collective-permute-done | bytes 53280 | tf_op jit(solution)/shard_map/ppermute | solution.py:64
  15.5 2.8 %collective-permute-start.5 = (bf16[1,144,512]{2,1,0:T(8,128)(2,1)S(1)}, bf16[1,144,512]{2,1,0:T(8,128)(2,1)S(1)}, u32[]{:S(2)}, u32[]{:S(2)}) collective-permute-start(bf16[1,144,512]{2,1,0:T(8,128)(2,1)S(1)} %bitcast.40), channel_id=1, source_target_pairs={{0,24},{1,25},{2,26},{3,27},{4,28},{5,29},{6,30},{7,31},{8,16},{9,... | collective-permute-start | bytes 442376 | tf_op jit(solution)/shard_map/ppermute | solution.py:64
  23.2 3.6 %collective-permute-done.4 = bf16[1,144,512]{2,1,0:T(8,128)(2,1)S(1)} collective-permute-done((bf16[1,144,512]{2,1,0:T(8,128)(2,1)S(1)}, bf16[1,144,512]{2,1,0:T(8,128)(2,1)S(1)}, u32[]{:S(2)}, u32[]{:S(2)}) %collective-permute-start.4) | collective-permute-done | bytes 147488 | tf_op jit(solution)/shard_map/ppermute | solution.py:64
  34.0 7.4 %rel_bias.1.bias_ref = f32[16,112,128]{2,1,0:T(8,128)} custom-call(f32[16,384]{1,0:T(8,128)} %pad.14.t_ref), custom_call_target="tpu_custom_call" | custom-call | flops 10000000 | bytes 100000 | tf_op jit(solution)/shard_map/rel_bias/pallas_call | solution.py:662
  42.0 25.0 %attn_fwd.1 = (bf16[512,2048]{1,0:T(8,128)(2,1)}, bf16[1600,512]{1,0:T(8,128)(2,1)}, bf16[512,2048]{1,0:T(8,128)(2,1)}, bf16[512,2048]{1,0:T(8,128)(2,1)}, bf16[...) custom-call(s32[1]{0:T(128)} %bitcast.me_ref, ...), custom_call_target="tpu_custom_call" | custom-call | flops 10000000 | bytes 100000 | tf_op jit(solution)/shard_map/attn_fwd/pallas_call | solution.py:236
  72.6 45.0 %mlp.1 = (f32[1600,512]{1,0:T(8,128)}, f32[1600,512]{1,0:T(8,128)}, bf16[1600,2048]{1,0:T(8,128)(2,1)}, f32[8,512]{1,0:T(8,128)}, f32[1,2048]{1,0:T(1,128)}, /*i...) custom-call(s32[1]{0:T(128)} %bitcast.me_ref, ...), custom_call_target="tpu_custom_call" | custom-call | flops 10000000 | bytes 100000 | tf_op jit(solution)/shard_map/mlp/pallas_call | solution.py:436
  118.0 10.2 %finish.1 = (bf16[1600,512]{1,0:T(8,128)(2,1)}, f32[8,512]{1,0:T(8,128)}) custom-call(bf16[1600,2048]{1,0:T(8,128)(2,1)} %get-tuple-element.64.e_ref, bf16[128,16,512]{2,1,0:T(8,128)(2,1)} %get-tuple-element.65.v_ref, f32[1600,512]{1,0:T(8,128)} %get-tuple-element.66.mid_ref, bf16[1600,512]{1,0:T(8,128)(2,1)} %x_ref.6, f32[1600,1]{1,0:T(8,128)} %reshape.161.vld_ref, ...), custom_call_target="tpu_custom_call" | custom-call | flops 10000000 | bytes 100000 | tf_op jit(solution)/shard_map/finish/pallas_call | solution.py:624
  128.2 3.1 %convert_add_fusion = (f32[4,128,512]{2,1,0:T(8,128)S(1)}, bf16[4,128,512]{2,1,0:T(8,128)(2,1)S(1)}, bf16[4,128,512]{2,1,0:T(8,128)(2,1)}, bf16[4,128,512]{2,1,0:T(8,128)(2,1)}) fusion(bf16[16,128,512]{2,1,0:T(8,128)(2,1)} %collective-permute-done.20, bf16[16,128,512]{2,1,0:T(8,128)(2,1)S(1)} %copy-done.1), kind=kLoop, calls=%fused_computation | loop fusion | flops 3932160 | bytes 6815744 | tf_op jit(solution)/shard_map/add | solution.py:107
  134.8 36.3 %attn_bwd.1 = (bf16[1536,2048]{1,0:T(8,128)(2,1)}, f32[16,112,128]{2,1,0:T(8,128)}, f32[8,1536]{1,0:T(8,128)}, bf16[16,64,512]{2,1,0:T(8,128)(2,1)}, bf16[16,64,512]{2,1,0:T(8,128)(2,1)}) custom-call(s32[1]{0:T(128)} %bitcast.me_ref, f32[1600,512]{1,0:T(8,128)} %get-tuple-element.73.dmid_ref, bf16[512,512]{1,0:T(8,128)(2,1)} %get-tuple-element.74.p_ref, ...), custom_call_target="tpu_custom_call" | custom-call | flops 10000000 | bytes 100000 | tf_op jit(solution)/shard_map/attn_bwd/pallas_call | solution.py:542
  173.8 1.9 fusion.8
  175.7 2.0 collective-permute-start.31
  177.9 2.2 collective-permute-start.33
  180.1 2.3 convert_add_fusion.1
  182.4 4.7 %rel_grad.1 = f32[16,384]{1,0:T(8,128)} custom-call(f32[16,112,128]{2,1,0:T(8,128)} %get-tuple-element.101.a_ref), custom_call_target="tpu_custom_call" | custom-call | flops 10000000 | bytes 100000 | tf_op jit(solution)/shard_map/rel_grad/pallas_call | solution.py:692
  187.9 10.2 %grad_in.1 = (f32[1600,512]{1,0:T(8,128)}, f32[8,512]{1,0:T(8,128)}) custom-call(bf16[1536,2048]{1,0:T(8,128)(2,1)} %get-tuple-element.87.dmT_ref, bf16[512,1536]{1,0:T(8,128)(2,1)} %get-tuple-element.88.w_ref, bf16[1600,512]{1,0:T(8,128)(2,1)} %x_ref.6, f32[1600,512]{1,0:T(8,128)} %get-tuple-element.73.dmid_ref, f32[16,512]{1,0:T(8,128)} %get-tuple-element.59.rowv_ref), custom_call_target="tpu_custom_call" | custom-call | flops 10000000 | bytes 100000 | tf_op jit(solution)/shard_map/grad_in/pallas_call | solution.py:590
  206.2 2.4 %collective-permute-done.37 = f32[32,512]{1,0:T(8,128)S(1)} collective-permute-done((f32[32,512]{1,0:T(8,128)S(1)}, f32[32,512]{1,0:T(8,128)S(1)}, u32[]{:S(2)}, u32[]{:S(2)}) %collective-permute-start.37) | collective-permute-done | bytes 65568 | tf_op jit(solution)/shard_map/ppermute | solution.py:64
  210.8 2.3 collective-permute-start.40
  215.7 2.5 %collective-permute-start.27 = (bf16[4,64,512]{2,1,0:T(8,128)(2,1)S(1)}, bf16[4,64,512]{2,1,0:T(8,128)(2,1)S(1)}, u32[]{:S(2)}, u32[]{:S(2)}) collective-permute-start(bf16[4,64,512]{2,1,0:T(8,128)(2,1)S(1)} %get-tuple-element.111), channel_id=1, source_target_pairs={{0,6},{1,7},{2,4},{3,5},{4,2},{5,3},{6,0},{7,1},{8,14},{9,15},{10,... | collective-permute-start | bytes 786440 | tf_op jit(solution)/shard_map/ppermute | solution.py:64
  219.5 3.8 %collective-permute-done.25 = bf16[4,64,512]{2,1,0:T(8,128)(2,1)S(1)} collective-permute-done((bf16[4,64,512]{2,1,0:T(8,128)(2,1)S(1)}, bf16[4,64,512]{2,1,0:T(8,128)(2,1)S(1)}, u32[]{:S(2)}, u32[]{:S(2)}) %collective-permute-start.25) | collective-permute-done | bytes 262176 | tf_op jit(solution)/shard_map/ppermute | solution.py:64
  223.3 3.1 %collective-permute-done.26 = bf16[4,64,512]{2,1,0:T(8,128)(2,1)S(1)} collective-permute-done((bf16[4,64,512]{2,1,0:T(8,128)(2,1)S(1)}, bf16[4,64,512]{2,1,0:T(8,128)(2,1)S(1)}, u32[]{:S(2)}, u32[]{:S(2)}) %collective-permute-start.26) | collective-permute-done | bytes 262176 | tf_op jit(solution)/shard_map/ppermute | solution.py:64
  228.6 2.3 collective-permute-start.30
  232.8 1.9 collective-permute-done.30
  (176 shorter events, 51.7 us)
Async XLA Ops:
  2.2 8.5 %collective-permute-start = (bf16[1,16,1664]{2,1,0:T(8,128)(2,1)S(1)}, bf16[1,16,1664]{2,1,0:T(8,128)(2,1)S(1)}, u32[]{:S(2)}, u32[]{:S(2)}) collective-permute-start(bf16[1,16,1664]{2,1,0:T(8,128)(2,1)S(1)} %maximum_bitcast_fusion), channel_id=1, source_target_pairs={{0,8},{1,9},{2,10},{3,11},{4,12},{5,13},{6,14},{7,15},{8,0},{9,1},... | collective-permute-start | bytes 159752 | tf_op jit(solution)/shard_map/ppermute | solution.py:64
  13.9 7.5 %collective-permute-start.3 = (bf16[1,144,512]{2,1,0:T(8,128)(2,1)S(1)}, bf16[1,144,512]{2,1,0:T(8,128)(2,1)S(1)}, u32[]{:S(2)}, u32[]{:S(2)}) collective-permute-start(bf16[1,144,512]{2,1,0:T(8,128)(2,1)S(1)} %bitcast.38), channel_id=1, source_target_pairs={{0,8},{1,9},{2,10},{3,11},{4,12},{5,13},{6,14},{7,15},{8,0},{9,1},... | collective-permute-start | bytes 442376 | tf_op jit(solution)/shard_map/ppermute | solution.py:64
  14.0 12.9 %collective-permute-start.4 = (bf16[1,144,512]{2,1,0:T(8,128)(2,1)S(1)}, bf16[1,144,512]{2,1,0:T(8,128)(2,1)S(1)}, u32[]{:S(2)}, u32[]{:S(2)}) collective-permute-start(bf16[1,144,512]{2,1,0:T(8,128)(2,1)S(1)} %bitcast.39), channel_id=1, source_target_pairs={{0,16},{1,17},{2,18},{3,19},{4,20},{5,21},{6,22},{7,23},{8,24},{9,... | collective-permute-start | bytes 442376 | tf_op jit(solution)/shard_map/ppermute | solution.py:64
  15.5 11.3 %collective-permute-start.5 = (bf16[1,144,512]{2,1,0:T(8,128)(2,1)S(1)}, bf16[1,144,512]{2,1,0:T(8,128)(2,1)S(1)}, u32[]{:S(2)}, u32[]{:S(2)}) collective-permute-start(bf16[1,144,512]{2,1,0:T(8,128)(2,1)S(1)} %bitcast.40), channel_id=1, source_target_pairs={{0,24},{1,25},{2,26},{3,27},{4,28},{5,29},{6,30},{7,31},{8,16},{9,... | collective-permute-start | bytes 442376 | tf_op jit(solution)/shard_map/ppermute | solution.py:64
  18.3 11.7 %collective-permute-start.6 = (bf16[4,16,1664]{2,1,0:T(8,128)(2,1)S(1)}, bf16[4,16,1664]{2,1,0:T(8,128)(2,1)S(1)}, u32[]{:S(2)}, u32[]{:S(2)}) collective-permute-start(bf16[4,16,1664]{2,1,0:T(8,128)(2,1)S(1)} %pad_maximum_fusion.2.refs_0_), channel_id=1, source_target_pairs={{0,2},{1,3},{2,0},{3,1},{4,6},{5,7},{6,4},{7,5},{8,10},{9,11},{10,... | collective-permute-start | bytes 638984 | tf_op jit(solution)/shard_map/ppermute | solution.py:64
  19.8 10.9 %collective-permute-start.7 = (bf16[4,16,1664]{2,1,0:T(8,128)(2,1)S(1)}, bf16[4,16,1664]{2,1,0:T(8,128)(2,1)S(1)}, u32[]{:S(2)}, u32[]{:S(2)}) collective-permute-start(bf16[4,16,1664]{2,1,0:T(8,128)(2,1)S(1)} %pad_maximum_fusion.2.refs_0_), channel_id=1, source_target_pairs={{0,4},{1,5},{2,6},{3,7},{4,0},{5,1},{6,2},{7,3},{8,12},{9,13},{10,... | collective-permute-start | bytes 638984 | tf_op jit(solution)/shard_map/ppermute | solution.py:64
  21.4 9.7 %collective-permute-start.8 = (bf16[4,16,1664]{2,1,0:T(8,128)(2,1)S(1)}, bf16[4,16,1664]{2,1,0:T(8,128)(2,1)S(1)}, u32[]{:S(2)}, u32[]{:S(2)}) collective-permute-start(bf16[4,16,1664]{2,1,0:T(8,128)(2,1)S(1)} %pad_maximum_fusion.2.refs_0_), channel_id=1, source_target_pairs={{0,6},{1,7},{2,4},{3,5},{4,2},{5,3},{6,0},{7,1},{8,14},{9,15},{10,... | collective-permute-start | bytes 638984 | tf_op jit(solution)/shard_map/ppermute | solution.py:64
  26.9 40.1 %collective-permute-start.13 = (bf16[4,144,512]{2,1,0:T(8,128)(2,1)S(1)}, bf16[4,144,512]{2,1,0:T(8,128)(2,1)S(1)}, u32[]{:S(2)}, u32[]{:S(2)}) collective-permute-start(bf16[4,144,512]{2,1,0:T(8,128)(2,1)S(1)} %pad_maximum_fusion), channel_id=1, source_target_pairs={{0,2},{1,3},{2,0},{3,1},{4,6},{5,7},{6,4},{7,5},{8,10},{9,11},{10,... | collective-permute-start | bytes 1769480 | tf_op jit(solution)/shard_map/ppermute | solution.py:64
  28.5 38.6 %collective-permute-start.14 = (bf16[4,144,512]{2,1,0:T(8,128)(2,1)S(1)}, bf16[4,144,512]{2,1,0:T(8,128)(2,1)S(1)}, u32[]{:S(2)}, u32[]{:S(2)}) collective-permute-start(bf16[4,144,512]{2,1,0:T(8,128)(2,1)S(1)} %pad_maximum_fusion), channel_id=1, source_target_pairs={{0,4},{1,5},{2,6},{3,7},{4,0},{5,1},{6,2},{7,3},{8,12},{9,13},{10,... | collective-permute-start | bytes 1769480 | tf_op jit(solution)/shard_map/ppermute | solution.py:64
  30.0 37.1 %collective-permute-start.15 = (bf16[4,144,512]{2,1,0:T(8,128)(2,1)S(1)}, bf16[4,144,512]{2,1,0:T(8,128)(2,1)S(1)}, u32[]{:S(2)}, u32[]{:S(2)}) collective-permute-start(bf16[4,144,512]{2,1,0:T(8,128)(2,1)S(1)} %pad_maximum_fusion), channel_id=1, source_target_pairs={{0,6},{1,7},{2,4},{3,5},{4,2},{5,3},{6,0},{7,1},{8,14},{9,15},{10,... | collective-permute-start | bytes 1769480 | tf_op jit(solution)/shard_map/ppermute | solution.py:64
  32.8 8.5 %collective-permute-start.11 = (bf16[4,16,1664]{2,1,0:T(8,128)(2,1)S(1)}, bf16[4,16,1664]{2,1,0:T(8,128)(2,1)S(1)}, u32[]{:S(2)}, u32[]{:S(2)}) collective-permute-start(bf16[4,16,1664]{2,1,0:T(8,128)(2,1)S(1)} %collective-permute-done.7.refs_2_), channel_id=1, source_target_pairs={{0,1},{1,0},{2,3},{3,2},{4,5},{5,4},{6,7},{7,6},{8,9},{9,8},{10,11... | collective-permute-start | bytes 638984 | tf_op jit(solution)/shard_map/ppermute | solution.py:64
  33.1 8.2 %collective-permute-start.12 = (bf16[4,16,1664]{2,1,0:T(8,128)(2,1)S(1)}, bf16[4,16,1664]{2,1,0:T(8,128)(2,1)}, u32[]{:S(2)}, u32[]{:S(2)}) collective-permute-start(bf16[4,16,1664]{2,1,0:T(8,128)(2,1)S(1)} %collective-permute-done.8.refs_3_), channel_id=1, source_target_pairs={{0,1},{1,0},{2,3},{3,2},{4,5},{5,4},{6,7},{7,6},{8,9},{9,8},{10,11... | collective-permute-start | bytes 638984 | tf_op jit(solution)/shard_map/ppermute | solution.py:64
  117.6 10.6 %collective-permute-start.20 = (bf16[16,128,512]{2,1,0:T(8,128)(2,1)}, bf16[16,128,512]{2,1,0:T(8,128)(2,1)}, u32[]{:S(2)}, u32[]{:S(2)}) collective-permute-start(bf16[16,128,512]{2,1,0:T(8,128)(2,1)} %get-tuple-element.70), channel_id=1, source_target_pairs={{0,1},{1,0},{2,3},{3,2},{4,5},{5,4},{6,7},{7,6},{8,9},{9,8},{10,11... | collective-permute-start | bytes 6291464 | tf_op jit(solution)/shard_map/ppermute | solution.py:64
  131.3 39.8 %collective-permute-start.21 = (bf16[4,128,512]{2,1,0:T(8,128)(2,1)}, bf16[4,128,512]{2,1,0:T(8,128)(2,1)S(1)}, u32[]{:S(2)}, u32[]{:S(2)}) collective-permute-start(bf16[4,128,512]{2,1,0:T(8,128)(2,1)} %get-tuple-element.106), channel_id=1, source_target_pairs={{0,2},{1,3},{2,0},{3,1},{4,6},{5,7},{6,4},{7,5},{8,10},{9,11},{10,... | collective-permute-start | bytes 1572872 | tf_op jit(solution)/shard_map/ppermute | solution.py:64
  132.7 38.4 %collective-permute-start.22 = (bf16[4,128,512]{2,1,0:T(8,128)(2,1)}, bf16[4,128,512]{2,1,0:T(8,128)(2,1)S(1)}, u32[]{:S(2)}, u32[]{:S(2)}) collective-permute-start(bf16[4,128,512]{2,1,0:T(8,128)(2,1)} %get-tuple-element.105), channel_id=1, source_target_pairs={{0,4},{1,5},{2,6},{3,7},{4,0},{5,1},{6,2},{7,3},{8,12},{9,13},{10,... | collective-permute-start | bytes 1572872 | tf_op jit(solution)/shard_map/ppermute | solution.py:64
  134.2 36.9 %collective-permute-start.23 = (bf16[4,128,512]{2,1,0:T(8,128)(2,1)S(1)}, bf16[4,128,512]{2,1,0:T(8,128)(2,1)}, u32[]{:S(2)}, u32[]{:S(2)}) collective-permute-start(bf16[4,128,512]{2,1,0:T(8,128)(2,1)S(1)} %get-tuple-element.104), channel_id=1, source_target_pairs={{0,6},{1,7},{2,4},{3,5},{4,2},{5,3},{6,0},{7,1},{8,14},{9,15},{10,... | collective-permute-start | bytes 1572872 | tf_op jit(solution)/shard_map/ppermute | solution.py:64
  171.2 8.9 %collective-permute-start.24 = (bf16[16,64,512]{2,1,0:T(8,128)(2,1)}, bf16[16,64,512]{2,1,0:T(8,128)(2,1)}, u32[]{:S(2)}, u32[]{:S(2)}) collective-permute-start(bf16[16,64,512]{2,1,0:T(8,128)(2,1)} %get-tuple-element.86), channel_id=1, source_target_pairs={{0,1},{1,0},{2,3},{3,2},{4,5},{5,4},{6,7},{7,6},{8,9},{9,8},{10,11... | collective-permute-start | bytes 3145736 | tf_op jit(solution)/shard_map/ppermute | solution.py:64
  175.7 27.8 %collective-permute-start.31 = (bf16[1,128,512]{2,1,0:T(8,128)(2,1)}, bf16[1,128,512]{2,1,0:T(8,128)(2,1)S(1)}, u32[]{:S(2)}, u32[]{:S(2)}) collective-permute-start(bf16[1,128,512]{2,1,0:T(8,128)(2,1)} %get-tuple-element.107), channel_id=1, source_target_pairs={{0,8},{1,9},{2,10},{3,11},{4,12},{5,13},{6,14},{7,15},{8,0},{9,1},... | collective-permute-start | bytes 393224 | tf_op jit(solution)/shard_map/ppermute | solution.py:64
  177.7 26.2 %collective-permute-start.32 = (bf16[1,128,512]{2,1,0:T(8,128)(2,1)}, bf16[1,128,512]{2,1,0:T(8,128)(2,1)}, u32[]{:S(2)}, u32[]{:S(2)}) collective-permute-start(bf16[1,128,512]{2,1,0:T(8,128)(2,1)} %get-tuple-element.109), channel_id=1, source_target_pairs={{0,16},{1,17},{2,18},{3,19},{4,20},{5,21},{6,22},{7,23},{8,24},{9,... | collective-permute-start | bytes 393224 | tf_op jit(solution)/shard_map/ppermute | solution.py:64
  177.9 26.1 %collective-permute-start.33 = (bf16[1,128,512]{2,1,0:T(8,128)(2,1)}, bf16[1,128,512]{2,1,0:T(8,128)(2,1)}, u32[]{:S(2)}, u32[]{:S(2)}) collective-permute-start(bf16[1,128,512]{2,1,0:T(8,128)(2,1)} %get-tuple-element.108), channel_id=1, source_target_pairs={{0,24},{1,25},{2,26},{3,27},{4,28},{5,29},{6,30},{7,31},{8,16},{9,... | collective-permute-start | bytes 393224 | tf_op jit(solution)/shard_map/ppermute | solution.py:64
  209.9 8.3 %collective-permute-start.39 = (f32[32,512]{1,0:T(8,128)S(1)}, f32[32,512]{1,0:T(8,128)S(1)}, u32[]{:S(2)}, u32[]{:S(2)}) collective-permute-start(f32[32,512]{1,0:T(8,128)S(1)} %add_add_fusion.1), channel_id=1, source_target_pairs={{0,16},{1,17},{2,18},{3,19},{4,20},{5,21},{6,22},{7,23},{8,24},{9,... | collective-permute-start | bytes 196616 | tf_op jit(solution)/shard_map/ppermute | solution.py:64
  214.6 8.6 %collective-permute-start.25 = (bf16[4,64,512]{2,1,0:T(8,128)(2,1)S(1)}, bf16[4,64,512]{2,1,0:T(8,128)(2,1)S(1)}, u32[]{:S(2)}, u32[]{:S(2)}) collective-permute-start(bf16[4,64,512]{2,1,0:T(8,128)(2,1)S(1)} %copy-done.13), channel_id=1, source_target_pairs={{0,2},{1,3},{2,0},{3,1},{4,6},{5,7},{6,4},{7,5},{8,10},{9,11},{10,... | collective-permute-start | bytes 786440 | tf_op jit(solution)/shard_map/ppermute | solution.py:64
  215.2 11.2 %collective-permute-start.26 = (bf16[4,64,512]{2,1,0:T(8,128)(2,1)S(1)}, bf16[4,64,512]{2,1,0:T(8,128)(2,1)S(1)}, u32[]{:S(2)}, u32[]{:S(2)}) collective-permute-start(bf16[4,64,512]{2,1,0:T(8,128)(2,1)S(1)} %copy-done.12), channel_id=1, source_target_pairs={{0,4},{1,5},{2,6},{3,7},{4,0},{5,1},{6,2},{7,3},{8,12},{9,13},{10,... | collective-permute-start | bytes 786440 | tf_op jit(solution)/shard_map/ppermute | solution.py:64
  215.7 10.7 %collective-permute-start.27 = (bf16[4,64,512]{2,1,0:T(8,128)(2,1)S(1)}, bf16[4,64,512]{2,1,0:T(8,128)(2,1)S(1)}, u32[]{:S(2)}, u32[]{:S(2)}) collective-permute-start(bf16[4,64,512]{2,1,0:T(8,128)(2,1)S(1)} %get-tuple-element.111), channel_id=1, source_target_pairs={{0,6},{1,7},{2,4},{3,5},{4,2},{5,3},{6,0},{7,1},{8,14},{9,15},{10,... | collective-permute-start | bytes 786440 | tf_op jit(solution)/shard_map/ppermute | solution.py:64
  (45 other events, 468.1 us)

commit v3 on v2

v3 whole, which is shorter than its diff:
```python
import functools

import jax
import jax.numpy as jnp
from jax import lax
from jax.experimental import pallas as pl
from jax.experimental.pallas import tpu as pltpu
from jax.sharding import PartitionSpec as P

D = 512
FF = 2048
HEADS = 16
HD = 32
WSIDE = 10
RELN = 361
CELLS = WSIDE * WSIDE
GW = 4
GR = GW * CELLS
KP = 112
LANES = 128
GL = GW * LANES
RP = 384
AXES = ("dp", "shard")
LOG2E = 1.4426950408889634
NEG = -1e9
RT2 = 0.7071067811865476
PHI = 0.3989422804014327
f32 = jnp.float32
bf16 = jnp.bfloat16
sds = jax.ShapeDtypeStruct


def nn(a, b):
    return lax.dot_general(a, b, (((1,), (0,)), ((), ())), preferred_element_type=f32)


def nt(a, b):
    return lax.dot_general(a, b, (((1,), (1,)), ((), ())), preferred_element_type=f32)


def whole(shape):
    return pl.BlockSpec(shape, lambda i: (0,) * len(shape))


def params(mib):
    return pltpu.CompilerParams(vmem_limit_bytes=mib * 2**20)


def bit_groups(count):
    bits = count.bit_length() - 1
    groups = [(0,)]
    at = 1
    while at < bits:
        groups.append(tuple(range(at, min(at + 2, bits))))
        at += 2
    return groups


def masks_of(group):
    return [sum(((v >> k) & 1) << b for k, b in enumerate(group)) for v in range(1, 1 << len(group))]


def swap(x, mask, count):
    return lax.ppermute(x, AXES, [(i, i ^ mask) for i in range(count)])


def place_of(rel, groups):
    pos = 0
    for g in groups:
        pos = pos * (1 << len(g)) + ((rel >> g[0]) & ((1 << len(g)) - 1))
    return pos


def after(values, *others):
    return lax.optimization_barrier((values, others))[0]


def gather_upper(x, groups, count):
    cur = x[None]
    rels = [0]
    for g in groups[:1:-1]:
        ms = masks_of(g)
        cur = jnp.concatenate([cur] + [swap(cur, m, count) for m in ms], axis=0)
        rels = [r ^ m for m in [0] + ms for r in rels]
    return rels, cur


def gather_plane(rels, cur, groups, count):
    return [(rels, cur)] + [([r ^ m for r in rels], swap(cur, m, count)) for m in masks_of(groups[1])]


def gather_core(pieces, count):
    return pieces + [([r ^ 1 for r in rels], swap(arr, 1, count)) for rels, arr in pieces]


def natural_order(pieces, me, count):
    rels = [r for rs, _ in pieces for r in rs]
    where = [0] * count
    for k, r in enumerate(rels):
        where[r] = k
    both = jnp.concatenate([a for _, a in pieces], axis=0)
    return jnp.take(both, jnp.asarray(where, jnp.int32)[jnp.arange(count) ^ me], axis=0)


def split_sum(terms, group):
    n = terms[0].shape[0] >> len(group)
    parts = [sum(t[k * n : (k + 1) * n].astype(f32) for t in terms) for k in range(1 << len(group))]
    return parts[0], [p.astype(bf16) for p in parts[1:]]


def send_parts(parts, group, count):
    return [swap(p, m, count) for p, m in zip(parts, masks_of(group))]


def total(x, groups, count):
    for g in groups:
        got = [x] + [swap(x, m, count) for m in masks_of(g)]
        while len(got) > 1:
            got = [got[k] + got[k + 1] for k in range(0, len(got), 2)]
        x = got[0]
    return x


def lay_vectors(raw, per, rowv_ref):
    unit = LANES // 2
    each = per // unit
    low = lax.broadcasted_iota(jnp.int32, (1, LANES), 1) < unit

    def half(c, high):
        owner, part = divmod(c, each)
        got = raw[owner, part // 2 : part // 2 + 1, :].astype(f32)
        return got if part % 2 == high else pltpu.roll(got, unit, 1)

    for m in range((8 * D + FF) // LANES):
        row, col = divmod(m * LANES, D)
        rowv_ref[row : row + 1, col : col + LANES] = jnp.where(low, half(2 * m, 0), half(2 * m + 1, 1))


def pad_window(rows):
    at = lax.broadcasted_iota(jnp.int32, (104, 1), 0)
    rows = jnp.where(at < CELLS, rows, 0.0)
    return jnp.concatenate([rows, jnp.zeros((LANES - 104, rows.shape[1]), f32)], axis=0).astype(bf16)


def head_lanes():
    return lax.broadcasted_iota(jnp.int32, (1, LANES), 1) // HD


def by_head(block):
    lane = head_lanes()
    return jnp.concatenate([jnp.where(lane == q, block, jnp.zeros_like(block)) for q in range(4)], axis=0)


def attn_fwd_body(me_ref, x_ref, mask_ref, bias_ref, *refs, plan, rpd, per):
    pieces = refs[: len(plan)]
    (oT_ref, o_ref, q_ref, kT_ref, v_ref, pT_ref, h1T_ref, w_ref, rowv_ref) = refs[len(plan) : len(plan) + 9]
    xs, h1p, qT, kn, vT, osc, raw, sem = refs[len(plan) + 9 :]

    @pl.when(pl.program_id(0) == 0)
    def _():
        copies = []
        for ref, rels in zip(pieces, plan):
            if rels is None:
                copies.append(pltpu.make_async_copy(ref, (w_ref, rowv_ref)[len(copies)], sem.at[len(copies)]))
                continue
            for t, r in enumerate(rels):
                at = pl.multiple_of((r ^ me_ref[0]) * rpd, rpd)
                copies.append(
                    pltpu.make_async_copy(
                        ref.at[t, :, pl.ds(0, 3 * D)], w_ref.at[pl.ds(at, rpd), :], sem.at[len(copies)]
                    )
                )
                copies.append(
                    pltpu.make_async_copy(ref.at[t, :, pl.ds(3 * D, LANES)], raw.at[r ^ me_ref[0]], sem.at[len(copies)])
                )
        for c in copies:
            c.start()
        for c in copies:
            c.wait()
        if plan[0] is not None:
            rowv_ref[12:16, :] = jnp.zeros((4, D), f32)
            lay_vectors(raw, per, rowv_ref)

    xs[0:GR, :] = x_ref[...].astype(f32)
    gain = rowv_ref[0:1, :]
    shift = rowv_ref[1:2, :]
    for w in range(GW):
        xw = xs[CELLS * w : CELLS * w + 104, :]
        c = xw - jnp.mean(xw, axis=-1, keepdims=True)
        var = jnp.mean(c * c, axis=-1, keepdims=True)
        h = pad_window(c * lax.rsqrt(var + 1e-5) * gain + shift)
        h1p[LANES * w : LANES * w + LANES, :] = h
        for a in range(D // LANES):
            h1T_ref[LANES * a : LANES * a + LANES, LANES * w : LANES * w + LANES] = h[:, LANES * a : LANES * a + LANES].T
    h1T_ref[D : D + 16, :] = jnp.ones((16, GL), bf16)
    hp = h1p[...]
    q_ref[...] = (nn(hp, w_ref[:, 0:D]) + rowv_ref[2:3, :]).astype(bf16)
    kn[...] = nn(hp, w_ref[:, D : 2 * D]).astype(bf16)
    v_ref[...] = (nn(hp, w_ref[:, 2 * D : 3 * D]) + rowv_ref[3:4, :]).astype(bf16)
    for src, dst in ((q_ref, qT), (kn, kT_ref), (v_ref, vT)):
        for w in range(GW):
            for a in range(D // LANES):
                rows, cols = slice(LANES * w, LANES * w + LANES), slice(LANES * a, LANES * a + LANES)
                dst[cols, rows] = src[rows, cols].T
    factor = HD**-0.5 * LOG2E

    def window(w, carry):
        start = pl.multiple_of(w * LANES, LANES)
        at = pl.ds(start, LANES)
        allowed = mask_ref[w]
        for g in range(4):
            cols = slice(LANES * g, LANES * g + LANES)
            s = nn(by_head(kn[pl.ds(start, KP), cols]), qT[cols, at])
            ps = []
            for q in range(4):
                h = 4 * g + q
                t = s[KP * q : KP * q + KP] * factor + bias_ref[h] + allowed
                e = jnp.exp2(t - jnp.max(t, axis=0, keepdims=True))
                p = (e * (1.0 / jnp.sum(e, axis=0, keepdims=True))).astype(bf16)
                pT_ref[w, h] = p
                ps.append(p)
            o = [nn(vT[LANES * g + HD * q : LANES * g + HD * q + HD, at][:, 0:KP], ps[q]) for q in range(4)]
            oT_ref[cols, at] = jnp.concatenate(o, axis=0).astype(bf16)
        return carry

    lax.fori_loop(0, GW, window, 0, unroll=4)
    for w in range(GW):
        for a in range(D // LANES):
            osc[CELLS * w : CELLS * w + 104, LANES * a : LANES * a + LANES] = (
                oT_ref[LANES * a : LANES * a + LANES, LANES * w : LANES * w + LANES].T[0:112].astype(f32)[0:104]
            )
    o_ref[...] = osc[0:GR, :].astype(bf16)


def any_specs(n):
    return [pl.BlockSpec(memory_space=pl.ANY)] * n


SMEM = pl.BlockSpec(memory_space=pltpu.SMEM)


def attn_fwd(me, x, allowed, bias, plan, pieces, rpd, per, count):
    n = x.shape[0] // GR
    copies = sum(1 if r is None else 2 * len(r) for r in plan)
    rb = pl.BlockSpec((GR, D), lambda i: (i, 0))
    tb = pl.BlockSpec((D, GL), lambda i: (0, i))
    pb = pl.BlockSpec((GL, D), lambda i: (i, 0))
    return pl.pallas_call(
        functools.partial(attn_fwd_body, plan=plan, rpd=rpd, per=per),
        grid=(n,),
        in_specs=[SMEM, rb, pl.BlockSpec((GW, KP, LANES), lambda i: (i, 0, 0)), whole((HEADS, KP, LANES))]
        + any_specs(len(pieces)),
        out_specs=[
            tb,
            rb,
            pb,
            tb,
            pb,
            pl.BlockSpec((GW, HEADS, KP, LANES), lambda i: (i, 0, 0, 0)),
            pl.BlockSpec((D + 16, GL), lambda i: (0, i)),
            whole((D, 3 * D)),
            whole((16, D)),
        ],
        out_shape=[
            sds((D, n * GL), bf16),
            sds((n * GR, D), bf16),
            sds((n * GL, D), bf16),
            sds((D, n * GL), bf16),
            sds((n * GL, D), bf16),
            sds((n * GW, HEADS, KP, LANES), bf16),
            sds((D + 16, n * GL), bf16),
            sds((D, 3 * D), bf16),
            sds((16, D), f32),
        ],
        scratch_shapes=[
            pltpu.VMEM((GR + 8, D), f32),
            pltpu.VMEM((GL, D), bf16),
            pltpu.VMEM((D, GL), bf16),
            pltpu.VMEM((GL, D), bf16),
            pltpu.VMEM((D, GL), bf16),
            pltpu.VMEM((GR + 8, D), f32),
            pltpu.VMEM((count, max(rpd, 16), LANES), bf16),
            pltpu.SemaphoreType.DMA((copies,)),
        ],
        compiler_params=params(60),
        cost_estimate=pl.CostEstimate(flops=10**7, bytes_accessed=10**5, transcendentals=0),
        name="attn_fwd",
    )(me, x, allowed, bias, *pieces)


def mlp_body(me_ref, vld_ref, rowv_ref, x_any, o_any, g_any, *refs, plan, rows, owners, rpd, groups):
    pieces = refs[: len(plan)]
    refs = refs[len(plan) :]
    res_any, dmid_any, p_any, first_any, second_any, vec_ref, dbf1_ref, st_ref = refs[:8]
    xb, ob, gp, gT, h2, h2T, mid, dh2, es, dus, u4, vv, pp, res, pk, sem, sem_x, sem_o, sem_p, sem_g, sem_du, sem_dv, sem_r, sem_m = refs[8:]
    j = pl.program_id(0)
    last = FF // 512 - 1
    padded = h2.shape[0]
    blocks = rows // GR
    me = me_ref[0]
    proj_bias = rowv_ref[4:5, :]
    gain = rowv_ref[5:6, :]
    shift = rowv_ref[6:7, :]

    def weights():
        first, later = [], []
        count = 0
        for ref, rels in zip(pieces, plan):
            if rels is None:
                dst = (pp, u4, vv)[count]
                (first if count == 0 else later).append(pltpu.make_async_copy(ref, dst, sem.at[count]))
                count += 1
                continue
            for t, r in enumerate(rels):
                at = pl.ds(pl.multiple_of((r ^ me) * rpd, rpd), rpd)
                first.append(pltpu.make_async_copy(ref.at[t, 0], pp.at[at, :], sem.at[count]))
                later.append(pltpu.make_async_copy(ref.at[t, pl.ds(1, 4)], u4.at[:, at, :], sem.at[count + 1]))
                to = vv.at[pl.ds(pl.multiple_of((r ^ me) * 4, 4), 4)]
                later.append(pltpu.make_async_copy(ref.at[t, pl.ds(5, 4)], to, sem.at[count + 2]))
                count += 3
        return first, later

    def rows_of(k):
        return pl.ds(k * GR, GR)

    def grads_out(j):
        if not owners:
            cols = pl.ds(pl.multiple_of(j * 512, 512), 512)
            return [
                pltpu.make_async_copy(pk.at[0], first_any.at[:, cols], sem_du.at[j, 0]),
                pltpu.make_async_copy(pk.at[1], second_any.at[cols, :], sem_du.at[j, 1]),
            ]
        at = pl.ds(pl.multiple_of(j * rpd, rpd), rpd)
        low = pl.ds(4 * rpd, 4 * rpd)
        out = []
        for c, to in enumerate((first_any, second_any)):
            out.append(pltpu.make_async_copy(pk.at[c, :, at, :], to.at[:, at, :], sem_du.at[j, c]))
            for m in range(256 // (4 * rpd)):
                pos = place_of((j * (256 // (4 * rpd)) + m) ^ (me >> 1), [tuple(b - 1 for b in g) for g in groups[1:]])
                n = 2 * m + c
                out.append(pltpu.make_async_copy(pk.at[c, pos, low, :], to.at[pos, low, :], sem_dv.at[j, n]))
        return out

    @pl.when(j == 0)
    def _():
        first, later = weights()
        ins = []
        for c in first:
            c.start()
        for k in range(blocks):
            ins.append(pltpu.make_async_copy(x_any.at[rows_of(k)], xb.at[rows_of(k)], sem_x.at[k]))
            ins.append(pltpu.make_async_copy(o_any.at[rows_of(k)], ob.at[rows_of(k)], sem_o.at[k]))
        load_g = pltpu.make_async_copy(g_any, gp.at[pl.ds(0, rows)], sem_g.at[0])
        for c in ins + [load_g] + later:
            c.start()
        h2[rows:padded, :] = jnp.zeros((padded - rows, D), bf16)
        gp[rows:padded, :] = jnp.zeros((padded - rows, D), bf16)
        dh2[...] = jnp.zeros_like(dh2)
        for c in first:
            c.wait()
        store_p = pltpu.make_async_copy(pp, p_any, sem_p.at[0])
        store_p.start()
        squares = jnp.zeros((1, D), f32)
        for k in range(blocks):
            at = slice(k * GR, k * GR + GR)
            ins[2 * k].wait()
            ins[2 * k + 1].wait()
            a = nn(ob[at, :], pp[...]) + proj_bias
            squares = squares + jnp.sum(a * a * vld_ref[at, :], axis=0, keepdims=True)
            m = xb[at, :].astype(f32) + a
            mid[at, :] = m
            c = m - jnp.mean(m, axis=-1, keepdims=True)
            var = jnp.mean(c * c, axis=-1, keepdims=True)
            h2[at, :] = (c * lax.rsqrt(var + 1e-5) * gain + shift).astype(bf16)
        st_ref[...] = jnp.zeros_like(st_ref)
        st_ref[1:2, :] = squares
        load_g.wait()

        def turn(k, carry):
            at = pl.ds(pl.multiple_of(k * LANES, LANES), LANES)
            for a in range(D // LANES):
                cols = slice(LANES * a, LANES * a + LANES)
                h2T[cols, at] = h2[at, cols].T
                gT[cols, at] = gp[at, cols].T
            return carry

        lax.fori_loop(0, padded // LANES, turn, 0)
        for c in later:
            c.wait()
        store_p.wait()

    u = nn(h2[...], u4[j]) + rowv_ref[pl.ds(8 + j, 1), :]
    de = nt(gp[...], vv[pl.ds(pl.multiple_of(32 * j, 32), 32)].reshape(512, D))
    cdf = 0.5 * lax.erf(u * RT2) + 0.5
    es[j] = (u * cdf).astype(bf16)
    du = de * (cdf + u * (PHI * jnp.exp2(u * u * (-0.5 * LOG2E))))
    dus[...] = du.astype(bf16)
    dbf1_ref[pl.ds(j, 1), :] = jnp.sum(du, axis=0, keepdims=True)
    dh2[...] += nt(dus[...], u4[j])
    dU = nn(h2T[...], dus[...]).astype(bf16)
    dV = nn(gT[...], es[j]).astype(bf16).T
    if owners:
        at = pl.ds(pl.multiple_of(j * rpd, rpd), rpd)
        for k in range(owners):
            pk[(k ^ me) & 1, place_of(k ^ me, groups[1:]), at, :] = dU[rpd * k : rpd * k + rpd]
        per = 512 // (4 * rpd)
        for k in range(per):
            rel = (j * per + k) ^ me
            pk[rel & 1, place_of(rel, groups[1:]), 4 * rpd : 8 * rpd, :] = dV[4 * rpd * k : 4 * rpd * k + 4 * rpd]
        for c in grads_out(j):
            c.start()
    else:
        pk[0] = dU
        pk[1] = dV
        for c in grads_out(j):
            c.start()
        for c in grads_out(j):
            c.wait()

    @pl.when(j == last)
    def _():
        zero = jnp.zeros((1, D), f32)
        sums = [zero] * 4
        stats = [zero] * 5
        outs = []
        for k in range(blocks):
            at = slice(k * GR, k * GR + GR)
            m = mid[at, :]
            c = m - jnp.mean(m, axis=-1, keepdims=True)
            rs = lax.rsqrt(jnp.mean(c * c, axis=-1, keepdims=True) + 1e-5)
            xh = c * rs
            d = dh2[at, :]
            dx = d * gain
            dxx = d * xh
            m1 = jnp.mean(dx, axis=-1, keepdims=True)
            m2 = jnp.mean(dxx * gain, axis=-1, keepdims=True)
            grad = gp[at, :].astype(f32)
            dm = grad + (dx - m1 - xh * m2) * rs
            dh2[at, :] = dm
            outs.append(pltpu.make_async_copy(dh2.at[rows_of(k)], dmid_any.at[rows_of(k)], sem_m.at[k]))
            outs[-1].start()
            terms = (dm.astype(bf16).astype(f32), dxx, d, grad)
            sums = [a + jnp.sum(t, axis=0, keepdims=True) for a, t in zip(sums, terms)]
            f = rowv_ref[7:8, :]
            for b in range(4):
                f = f + nn(es[b, at, :], vv[32 * b : 32 * b + 32].reshape(512, D))
            out = m + f
            res[at, :] = out.astype(bf16)
            outs.append(pltpu.make_async_copy(res.at[rows_of(k)], res_any.at[rows_of(k)], sem_r.at[k]))
            outs[-1].start()
            vl = vld_ref[at, :]
            x = xb[at, :].astype(f32)
            terms = (x * x * vl, m * m * vl, f * f * vl, out * out * vl, jnp.broadcast_to(vl, (GR, D)))
            stats = [a + jnp.sum(t, axis=0, keepdims=True) for a, t in zip(stats, terms)]
        for q in range(4):
            vec_ref[q : q + 1, :] = sums[q]
        vec_ref[4:8, :] = jnp.zeros((4, D), f32)
        dbf1_ref[4:8, :] = jnp.zeros((4, D), f32)
        for q, t in zip((0, 2, 3, 4, 5), stats):
            st_ref[q : q + 1, :] = t
        if owners:
            for step in range(last + 1):
                outs += grads_out(step)
        for c in outs:
            c.wait()


def mlp(me, x, o, g, vld, rowv, plan, pieces, rpd, owners, count, groups):
    rows = x.shape[0]
    blocks = rows // GR
    steps = FF // 512
    padded = -(-rows // LANES) * LANES
    copies = sum(1 if r is None else 3 * len(r) for r in plan)
    if owners:
        grad_shapes = [sds((count // 2, 8 * rpd, 512), bf16)] * 2
        pk = (2, count // 2, 8 * rpd, 512)
    else:
        grad_shapes = [sds((D, FF), bf16), sds((FF, D), bf16)]
        pk = (2, 512, 512)
    dma = pltpu.SemaphoreType.DMA
    return pl.pallas_call(
        functools.partial(mlp_body, plan=plan, rows=rows, owners=count if owners else 0, rpd=rpd, groups=groups),
        grid=(steps,),
        in_specs=[SMEM, whole((rows, 1)), whole((16, D))] + any_specs(3 + len(pieces)),
        out_specs=any_specs(5) + [whole((8, D))] * 3,
        out_shape=[sds((rows, D), bf16), sds((rows, D), f32), sds((D, D), bf16)] + grad_shapes + [sds((8, D), f32)] * 3,
        scratch_shapes=[
            pltpu.VMEM((rows, D), bf16),
            pltpu.VMEM((rows, D), bf16),
            pltpu.VMEM((padded, D), bf16),
            pltpu.VMEM((D, padded), bf16),
            pltpu.VMEM((padded, D), bf16),
            pltpu.VMEM((D, padded), bf16),
            pltpu.VMEM((rows, D), f32),
            pltpu.VMEM((padded, D), f32),
            pltpu.VMEM((steps, padded, 512), bf16),
            pltpu.VMEM((padded, 512), bf16),
            pltpu.VMEM((steps, D, 512), bf16),
            pltpu.VMEM((FF // 16, 16, D), bf16),
            pltpu.VMEM((D, D), bf16),
            pltpu.VMEM((rows, D), bf16),
            pltpu.VMEM(pk, bf16),
            dma((copies,)),
            dma((blocks,)),
            dma((blocks,)),
            dma((1,)),
            dma((1,)),
            dma((steps, 2)),
            dma((steps, max(1, 512 // (4 * rpd)))),
            dma((blocks,)),
            dma((blocks,)),
        ],
        compiler_params=params(62),
        cost_estimate=pl.CostEstimate(flops=10**7, bytes_accessed=10**5, transcendentals=0),
        name="mlp",
    )(me, vld, rowv, x, o, g, *pieces)


def attn_bwd_body(me_ref, dmid_ref, p_ref, oT_ref, q_ref, kT_ref, v_ref, pT_ref, h1T_ref, *refs, owners, rpd, groups):
    dm_ref, acc_ref, vec_ref = refs[:3]
    grads = refs[3:-6]
    xs, dap, don, doT, dw, dproj = refs[-6:]
    i = pl.program_id(0)

    @pl.when(i == 0)
    def _():
        acc_ref[...] = jnp.zeros_like(acc_ref)
        dw[...] = jnp.zeros_like(dw)
        dproj[...] = jnp.zeros_like(dproj)

    xs[0:GR, :] = dmid_ref[...]
    for w in range(GW):
        dap[LANES * w : LANES * w + LANES, :] = pad_window(xs[CELLS * w : CELLS * w + 104, :])
        dm_ref[LANES * w + KP : LANES * w + LANES, :] = jnp.zeros((LANES - KP, 3 * D), bf16)
    da = dap[...]
    don[...] = nt(da, p_ref[...]).astype(bf16)
    dproj[...] += nn(oT_ref[...], da)
    for w in range(GW):
        for a in range(D // LANES):
            rows, cols = slice(LANES * w, LANES * w + LANES), slice(LANES * a, LANES * a + LANES)
            doT[cols, rows] = don[rows, cols].T
    factor = HD**-0.5

    def window(w, carry):
        start = pl.multiple_of(w * LANES, LANES)
        at = pl.ds(start, LANES)
        keys = pl.ds(start, KP)
        for g in range(4):
            c0 = LANES * g
            cols = slice(c0, c0 + LANES)
            dp = nn(by_head(v_ref[keys, cols]), doT[cols, at])
            dss = []
            for q in range(4):
                h = 4 * g + q
                head = slice(HD * h, HD * h + HD)
                delta = jnp.sum(doT[head, at].astype(f32) * oT_ref[head, at].astype(f32), axis=0, keepdims=True)
                ds = pT_ref[w, h].astype(f32) * (dp[KP * q : KP * q + KP] - delta)
                acc_ref[h] += ds
                dss.append(ds.astype(bf16))
            dq = [nn(kT_ref[c0 + HD * q : c0 + HD * q + HD, at][:, 0:KP], dss[q]) for q in range(4)]
            dm_ref[at, cols] = (jnp.concatenate(dq, axis=0) * factor).astype(bf16).T
            dk = nn(jnp.concatenate(dss, axis=1), by_head(q_ref[at, cols])) * factor
            dm_ref[keys, D + c0 : D + c0 + LANES] = dk.astype(bf16)
            dv = nn(jnp.concatenate([pT_ref[w, 4 * g + q] for q in range(4)], axis=1), by_head(don[at, cols]))
            dm_ref[keys, 2 * D + c0 : 2 * D + c0 + LANES] = dv.astype(bf16)
        return carry

    lax.fori_loop(0, GW, window, 0, unroll=4)
    dw[...] += nn(h1T_ref[...], dm_ref[...])

    @pl.when(i == pl.num_programs(0) - 1)
    def _():
        if owners:
            me = me_ref[0]

            def store(flip):
                for k in range(owners):
                    to = grads[(k ^ flip) & 1]
                    pos = place_of(k ^ me, groups[1:])
                    for q in range(3):
                        to[pos, rpd * q : rpd * q + rpd, :] = dw[rpd * k : rpd * k + rpd, D * q : D * q + D].astype(bf16)
                    to[pos, 3 * rpd : 4 * rpd, :] = dproj[rpd * k : rpd * k + rpd, :].astype(bf16)

            pl.when(me & 1 == 0)(lambda: store(0))
            pl.when(me & 1 == 1)(lambda: store(1))
        else:
            grads[0][...] = dw[0:D, :].astype(bf16)
            grads[1][...] = dproj[...].astype(bf16)
        vec_ref[...] = dw[D : D + 8, :]


def attn_bwd(me, dmid, p, oT, q, kT, v, pT, h1T, rpd, owners, count, groups):
    n = dmid.shape[0] // GR

    def tb(r):
        return pl.BlockSpec((r, GL), lambda i: (0, i))

    pb = pl.BlockSpec((GL, D), lambda i: (i, 0))
    if owners:
        grad_shapes = [sds((count // 2, 4 * rpd, D), bf16)] * 2
    else:
        grad_shapes = [sds((D, 3 * D), bf16), sds((D, D), bf16)]
    return pl.pallas_call(
        functools.partial(attn_bwd_body, owners=count if owners else 0, rpd=rpd, groups=groups),
        grid=(n,),
        in_specs=[SMEM, pl.BlockSpec((GR, D), lambda i: (i, 0)), whole((D, D)), tb(D), pb, tb(D), pb, pl.BlockSpec((GW, HEADS, KP, LANES), lambda i: (i, 0, 0, 0)), tb(D + 16)],
        out_specs=[pl.BlockSpec((GL, 3 * D), lambda i: (i, 0)), whole((HEADS, KP, LANES)), whole((8, 3 * D))] + [whole(s.shape) for s in grad_shapes],
        out_shape=[sds((n * GL, 3 * D), bf16), sds((HEADS, KP, LANES), f32), sds((8, 3 * D), f32)] + grad_shapes,
        scratch_shapes=[
            pltpu.VMEM((GR + 8, D), f32),
            pltpu.VMEM((GL, D), bf16),
            pltpu.VMEM((GL, D), bf16),
            pltpu.VMEM((D, GL), bf16),
            pltpu.VMEM((D + 16, 3 * D), f32),
            pltpu.VMEM((D, D), f32),
        ],
        compiler_params=params(60),
        cost_estimate=pl.CostEstimate(flops=10**7, bytes_accessed=10**5, transcendentals=0),
        name="attn_bwd",
    )(me, dmid, p, oT, q, kT, v, pT, h1T)


def grad_in_body(dm_ref, w_ref, x_ref, dmid_ref, rowv_ref, tg_ref, vec_ref, dsc):
    dh = nt(dm_ref[...], w_ref[...])
    for w in range(GW):
        dsc[CELLS * w : CELLS * w + 104, :] = dh[LANES * w : LANES * w + 104]
    d = dsc[0:GR, :]
    x = x_ref[...].astype(f32)
    c = x - jnp.mean(x, axis=-1, keepdims=True)
    rs = lax.rsqrt(jnp.mean(c * c, axis=-1, keepdims=True) + 1e-5)
    xh = c * rs
    gain = rowv_ref[0:1, :]
    dx = d * gain
    dxx = d * xh
    m1 = jnp.mean(dx, axis=-1, keepdims=True)
    m2 = jnp.mean(dxx * gain, axis=-1, keepdims=True)
    tg_ref[...] = dmid_ref[...] + (dx - m1 - xh * m2) * rs

    @pl.when(pl.program_id(0) == 0)
    def _():
        vec_ref[...] = jnp.zeros_like(vec_ref)

    vec_ref[0:1, :] += jnp.sum(dxx, axis=0, keepdims=True)
    vec_ref[1:2, :] += jnp.sum(d, axis=0, keepdims=True)


def grad_in(dm, w, x, dmid, rowv):
    n = x.shape[0] // GR
    rb = pl.BlockSpec((GR, D), lambda i: (i, 0))
    return pl.pallas_call(
        grad_in_body,
        grid=(n,),
        in_specs=[pl.BlockSpec((GL, 3 * D), lambda i: (i, 0)), whole((D, 3 * D)), rb, rb, whole((16, D))],
        out_specs=[rb, whole((8, D))],
        out_shape=[sds((n * GR, D), f32), sds((8, D), f32)],
        scratch_shapes=[pltpu.VMEM((GR + 8, D), f32)],
        compiler_params=params(60),
        cost_estimate=pl.CostEstimate(flops=10**7, bytes_accessed=10**5, transcendentals=0),
        name="grad_in",
    )(dm, w, x, dmid, rowv)


def place_hits(shape, axis, rev=0):
    c = lax.broadcasted_iota(jnp.int32, shape, 1 - axis)
    code = jnp.where(c < CELLS, (2 * WSIDE - 1) * (c // WSIDE) + c % WSIDE, -1000)
    if rev:
        code = rev - code
    return jnp.where(code == lax.broadcasted_iota(jnp.int32, shape, axis), 1.0, 0.0).astype(bf16)


def rel_bias_body(t_ref, o_ref):
    keys = place_hits((KP, 192), 1)
    queries = place_hits((256, LANES), 0)

    def head(h, carry):
        row = pltpu.roll(jnp.broadcast_to(t_ref[pl.ds(h, 1), :], (8, RP)), 0, 1, stride=1, stride_axis=0)
        t = jnp.concatenate([pltpu.roll(row, (8 * k - 180) % RP, 1)[:, 0:256] for k in range(24)], axis=0)
        hi = t.astype(bf16)
        r = t - hi.astype(f32)
        md = r.astype(bf16)
        lo = (r - md.astype(f32)).astype(bf16)
        o_ref[h] = sum(nn(nn(keys, part).astype(bf16), queries) for part in (lo, md, hi))
        return carry

    lax.fori_loop(0, HEADS, head, 0, unroll=8)


def rel_bias(table):
    return pl.pallas_call(
        rel_bias_body,
        out_shape=sds((HEADS, KP, LANES), f32),
        compiler_params=params(60),
        cost_estimate=pl.CostEstimate(flops=10**7, bytes_accessed=10**5, transcendentals=0),
        name="rel_bias",
    )(table)


def rel_grad_body(a_ref, o_ref):
    keys = place_hits((192, KP), 0, 191)
    queries = place_hits((LANES, 256), 1)
    zero = jnp.zeros((8, RP - 256), f32)

    def head(h, carry):
        a = a_ref[h]
        hi = a.astype(bf16)
        lo = (a - hi.astype(f32)).astype(bf16)
        b = nn(nn(keys, hi).astype(bf16), queries) + nn(nn(keys, lo).astype(bf16), queries)
        t = jnp.zeros((8, RP), f32)
        for k in range(24):
            t = t + pltpu.roll(jnp.concatenate([b[8 * k : 8 * k + 8], zero], axis=1), (8 * k - 11) % RP, 1)
        t = pltpu.roll(t, 0, 1, stride=1, stride_axis=0)
        o_ref[pl.ds(h, 1), :] = jnp.sum(t, axis=0, keepdims=True)
        return carry

    lax.fori_loop(0, HEADS, head, 0, unroll=8)


def rel_grad(acc):
    return pl.pallas_call(
        rel_grad_body,
        out_shape=sds((HEADS, RP), f32),
        compiler_params=params(60),
        cost_estimate=pl.CostEstimate(flops=10**7, bytes_accessed=10**5, transcendentals=0),
        name="rel_grad",
    )(acc)


def shards(tokens, cotangent, regions, validity, qkv_weight, proj_weight, fc1_weight, fc2_weight, vectors, rel_table, *, count, inner):
    rows = tokens.shape[0]
    windows = rows // CELLS
    groups = bit_groups(count)
    rpd = D // count
    direct = rpd % 16 == 0
    me = lax.axis_index("dp") * inner + lax.axis_index("shard")
    me_s = me.astype(jnp.int32).reshape(1)

    per = vectors.shape[0]
    if direct:
        own = jnp.pad(vectors, (0, rpd * LANES - per)).reshape(rpd, LANES)
        own = jnp.concatenate([qkv_weight.reshape(rpd, 3 * D), own], axis=1)
    else:
        own = jnp.concatenate([qkv_weight, vectors]).reshape(1, -1)
    rels, attn_up = gather_upper(own, groups, count)
    packed = jnp.concatenate(
        [
            proj_weight.reshape(1, rpd, D),
            fc1_weight.reshape(rpd, 4, 512).transpose(1, 0, 2),
            fc2_weight.reshape(4, rpd, D),
        ],
        axis=0,
    )
    packed, table_in, valid_in = after((packed.reshape(9 * rpd, D), rel_table, validity), attn_up)
    attn_pieces = gather_plane(rels, attn_up, groups, count)
    _, mlp_up = gather_upper(packed, groups, count)

    bias = rel_bias(jnp.pad(table_in.T * LOG2E, ((0, 0), (0, RP - RELN))))
    reg = regions.reshape(windows, CELLS)
    val = valid_in.reshape(windows, CELLS)
    allowed = (reg[:, :, None] == reg[:, None, :]) & (val[:, :, None] == 1)
    allowed = jnp.where(allowed | jnp.eye(CELLS, dtype=jnp.bool_)[None], 0.0, NEG).astype(f32)
    allowed = jnp.pad(allowed, ((0, 0), (0, KP - CELLS), (0, LANES - CELLS)), constant_values=NEG)
    vld = valid_in.astype(f32).reshape(rows, 1)

    held, mlp_up = after(([a for _, a in attn_pieces], mlp_up), bias, allowed, vld)
    mlp_up = after(mlp_up, held)
    attn_pieces = gather_core([(r, a) for (r, _), a in zip(attn_pieces, held)], count)
    mlp_pieces = gather_plane(rels, mlp_up, groups, count)
    if direct:
        attn_plan = [r for r, _ in attn_pieces]
        attn_w = [a for _, a in attn_pieces]
    else:
        attn_plan = [None] * 2
        both = natural_order(attn_pieces, me, count).reshape(count, -1)
        attn_w = [both[:, : 3 * D * rpd].reshape(D, 3 * D), jnp.pad(both[:, 3 * D * rpd :].astype(f32).reshape(12, D), ((0, 4), (0, 0)))]

    x = after(tokens, mlp_up, vld)
    oT, o, q, kT, v, pT, h1T, w_full, rowv = attn_fwd(me_s, x, allowed, bias, attn_plan, attn_w, rpd, per, count)

    held = after([a for _, a in mlp_pieces], o)
    mlp_pieces = gather_core([(r, a) for (r, _), a in zip(mlp_pieces, held)], count)
    if direct:
        mlp_plan = [r for r, _ in mlp_pieces]
        mlp_w = [a.reshape(-1, 9, rpd, D) for _, a in mlp_pieces]
    else:
        both = natural_order(mlp_pieces, me, count).reshape(count, 9, rpd, D)
        mlp_plan = [None] * 3
        mlp_w = [both[:, 0].reshape(D, D), both[:, 1:5].transpose(1, 0, 2, 3).reshape(4, D, 512), both[:, 5:].reshape(128, 16, D)]
    result, dmid, p_full, mlp_keep, mlp_send, vec_two, dbf1, squares = mlp(
        me_s, tokens, o, cotangent, vld, rowv, mlp_plan, mlp_w, rpd, direct, count, groups
    )
    order = None
    if not direct:
        blocks = jnp.arange(count)
        where = place_of(blocks, groups)
        order = jnp.zeros((count,), jnp.int32).at[where].set(blocks.astype(jnp.int32)) ^ me
        dU = mlp_keep.reshape(count, rpd, 4, 512).transpose(0, 2, 1, 3).reshape(count, 4 * rpd, 512)
        pk = jnp.take(jnp.concatenate([dU, mlp_send.reshape(count, 4 * rpd, D)], axis=1), order, axis=0)
        mlp_keep, mlp_send = pk[: count // 2], pk[count // 2 :]

    other = swap(mlp_send, 1, count)
    mlp_own, parts = split_sum([mlp_keep, other], groups[1])
    mlp_got = send_parts(parts, groups[1], count)
    dmid = after(dmid, parts)
    got = attn_bwd(me_s, dmid, p_full, oT, q, kT, v, pT, h1T, rpd, direct, count, groups)
    dm, score_sums, vec_one = got[:3]
    if direct:
        attn_keep, attn_send = got[3:]
    else:
        dW = got[3].reshape(count, rpd, 3, D).transpose(0, 2, 1, 3).reshape(count, 3 * rpd, D)
        pk = jnp.take(jnp.concatenate([dW, got[4].reshape(count, rpd, D)], axis=1), order, axis=0)
        attn_keep, attn_send = pk[: count // 2], pk[count // 2 :]
    mlp_got, attn_send, score_sums, dm = lax.optimization_barrier((mlp_got, attn_send, score_sums, dm))
    other = swap(attn_send, 1, count)
    attn_own, parts = split_sum([attn_keep, other], groups[1])
    attn_got = send_parts(parts, groups[1], count)
    mlp_terms = [mlp_own] + mlp_got
    dm = after(dm, parts)
    grad_tokens, vec_in = grad_in(dm, w_full, tokens, dmid, rowv)
    table = rel_grad(after(score_sums, parts))
    attn_terms = [attn_own] + after(attn_got, grad_tokens)
    for g in groups[2:]:
        mlp_own, parts = split_sum(mlp_terms, g)
        mlp_terms = [mlp_own] + send_parts(parts, g, count)
        attn_own, parts = split_sum(attn_terms, g)
        attn_terms = [attn_own] + send_parts(parts, g, count)
    mlp_sum = sum(t[0].astype(f32) for t in mlp_terms)
    attn_sum = sum(t[0].astype(f32) for t in attn_terms)
    small = jnp.concatenate(
        [
            vec_in[0:2],
            vec_one[0:1, 0:D],
            vec_one[0:1, 2 * D : 3 * D],
            vec_two[0:4],
            dbf1[0:4],
            table.reshape(-1, D),
            squares,
        ],
        axis=0,
    )
    small = total(small, groups, count)
    length = vectors.shape[0]
    grad_vectors = lax.dynamic_slice(small[:12].reshape(-1), (me * length,), (length,))
    grad_table = small[12:24].reshape(HEADS, RP)[:, :RELN].T
    sums = jnp.sum(small[24:32], axis=1)
    stats = jnp.sqrt(sums[0:5] / sums[5] + 1e-06)
    return (
        result,
        grad_tokens,
        attn_sum[: 3 * rpd].reshape(3, rpd, D).transpose(1, 0, 2).reshape(-1),
        attn_sum[3 * rpd :].reshape(-1),
        mlp_sum[: 4 * rpd].reshape(4, rpd, 512).transpose(1, 0, 2).reshape(-1),
        mlp_sum[4 * rpd :].reshape(-1),
        grad_vectors,
        grad_table,
        stats,
    )


def solution(mesh):
    flat = P(AXES)
    tall = P(AXES, None)
    in_specs = (tall, tall, flat, flat, flat, flat, flat, flat, flat, P())
    out_specs = (tall, tall, flat, flat, flat, flat, flat, P(), P())
    inner = mesh.shape["shard"]
    body = functools.partial(shards, count=mesh.shape["dp"] * inner, inner=inner)
    return jax.shard_map(body, mesh=mesh, in_specs=in_specs, out_specs=out_specs, check_vma=False)
```

time: 237 us -> 208 us (0.88)
  Pallas kernels: 139 us -> 108 us
  waiting for transfers between devices: 22.8 us -> 26.3 us
  other arithmetic: 11.5 us -> 9.11 us
    pallas_call x2 -> x1, Pallas kernels: 20.4 us -> 9.4 us  [grad_in(): pl.pallas_call(grad_in_body, grid=(n,), in_specs=[pl.BlockSpec((GL, 3 * D...]
    pallas_call x1, Pallas kernels: 36.3 us -> 27.1 us  [attn_bwd(): pl.pallas_call(functools.partial(attn_bwd_body, owners=count if owners el...]
    pallas_call x1, Pallas kernels: 25 us -> 19.2 us  [attn_fwd(): pl.pallas_call(functools.partial(attn_fwd_body, plan=plan, rpd=rpd, per=p...]
    pallas_call x1, Pallas kernels: 45 us -> 40.1 us  [mlp(): pl.pallas_call(functools.partial(mlp_body, plan=plan, rows=rows, owners=c...]
    ppermute x41, waiting for transfers between devices: 22.8 us -> 26.3 us  [swap(): return lax.ppermute(x, AXES, [(i, i ^ mask) for i in range(count)])]
  transfers between devices with their start and end apart: 41 -> 41, of which waited for: 13 -> 18; matrix products, arithmetic and copies ran while one was open for 9% -> 9% of each run, Pallas kernels for 40% -> 33%
where the time goes in v3:
time: 208 us; the launch traced here: 207 us
  Pallas kernels  108 us (52%)
  starting transfers between devices  46.4 us (22%)
  waiting for transfers between devices  26.3 us (13%)
  local copies, waits for them, and re-layouts  16.1 us (8%)
  other arithmetic  9.11 us (4%)
    ppermute x41, starting transfers between devices, swap(): return lax.ppermute(x, AXES, [(i, i ^ mask) for i in range(count)])  46.4 us
    pallas_call x1, Pallas kernels, mlp(): pl.pallas_call(functools.partial(mlp_body, plan=plan, rows=rows, owners=c...  40.1 us
    pallas_call x1, Pallas kernels, attn_bwd(): pl.pallas_call(functools.partial(attn_bwd_body, owners=count if owners el...  27.1 us
    ppermute x41, waiting for transfers between devices, swap(): return lax.ppermute(x, AXES, [(i, i ^ mask) for i in range(count)])  26.3 us
    pallas_call x1, Pallas kernels, attn_fwd(): pl.pallas_call(functools.partial(attn_fwd_body, plan=plan, rpd=rpd, per=p...  19.2 us
    pallas_call x1, Pallas kernels, grad_in(): pl.pallas_call(grad_in_body, grid=(n,), in_specs=[pl.BlockSpec((GL, 3 * D...  9.4 us
    pallas_call x1, Pallas kernels, rel_bias(): pl.pallas_call(rel_bias_body, out_shape=sds((HEADS, KP, LANES), f32), com...  7.2 us
    pallas_call x1, Pallas kernels, rel_grad(): pl.pallas_call(rel_grad_body, out_shape=sds((HEADS, RP), f32), compiler_p...  4.73 us
  transfers between devices with their start and end apart: 41, of which 18 were waited for; matrix products, arithmetic and copies ran while one was open for 9% of the time, Pallas kernels for 33%

profile of v3, /device:TPU:0, one launch (start us, length us, event | category | flops | bytes accessed | tf_op | source)
XLA Modules:
  0.0 206.8 jit_solution(14674095932204907110)
XLA Ops:
  2.2 5.1 %collective-permute-start.2 = (bf16[1,16,1664]{2,1,0:T(8,128)(2,1)S(1)}, bf16[1,16,1664]{2,1,0:T(8,128)(2,1)S(1)}, u32[]{:S(2)}, u32[]{:S(2)}) collective-permute-start(bf16[1,16,1664]{2,1,0:T(8,128)(2,1)S(1)} %maximum_bitcast_fusion), channel_id=1, source_target_pairs={{0,24},{1,25},{2,26},{3,27},{4,28},{5,29},{6,30},{7,31},{8,16},{9,... | collective-permute-start | bytes 159752 | tf_op jit(solution)/shard_map/ppermute | solution.py:64
  12.4 3.1 %collective-permute-start.8 = (bf16[1,144,512]{2,1,0:T(8,128)(2,1)S(1)}, bf16[1,144,512]{2,1,0:T(8,128)(2,1)S(1)}, u32[]{:S(2)}, u32[]{:S(2)}) collective-permute-start(bf16[1,144,512]{2,1,0:T(8,128)(2,1)S(1)} %bitcast.38), channel_id=1, source_target_pairs={{0,24},{1,25},{2,26},{3,27},{4,28},{5,29},{6,30},{7,31},{8,16},{9,... | collective-permute-start | bytes 442376 | tf_op jit(solution)/shard_map/ppermute | solution.py:64
  16.9 2.4 %collective-permute-start.5 = (bf16[4,16,1664]{2,1,0:T(8,128)(2,1)S(1)}, bf16[4,16,1664]{2,1,0:T(8,128)(2,1)S(1)}, u32[]{:S(2)}, u32[]{:S(2)}) collective-permute-start(bf16[4,16,1664]{2,1,0:T(8,128)(2,1)S(1)} %pad_maximum_fusion.2.refs_0_), channel_id=1, source_target_pairs={{0,6},{1,7},{2,4},{3,5},{4,2},{5,3},{6,0},{7,1},{8,14},{9,15},{10,... | collective-permute-start | bytes 638984 | tf_op jit(solution)/shard_map/ppermute | solution.py:64
  24.2 7.2 %rel_bias.1.bias_ref = f32[16,112,128]{2,1,0:T(8,128)} custom-call(f32[16,384]{1,0:T(8,128)} %pad.13.t_ref), custom_call_target="tpu_custom_call" | custom-call | flops 10000000 | bytes 100000 | tf_op jit(solution)/shard_map/rel_bias/pallas_call | solution.py:689
  31.6 1.7 collective-permute-start.15
  38.9 19.2 %attn_fwd.1 = (bf16[512,2048]{1,0:T(8,128)(2,1)}, bf16[1600,512]{1,0:T(8,128)(2,1)}, bf16[2048,512]{1,0:T(8,128)(2,1)}, bf16[512,2048]{1,0:T(8,128)(2,1)}, bf16[...) custom-call(s32[1]{0:T(128)} %bitcast.me_ref, ...), custom_call_target="tpu_custom_call" | custom-call | flops 10000000 | bytes 100000 | tf_op jit(solution)/shard_map/attn_fwd/pallas_call | solution.py:248
  62.9 40.1 %mlp.1 = (bf16[1600,512]{1,0:T(8,128)(2,1)}, f32[1600,512]{1,0:T(8,128)}, bf16[512,512]{1,0:T(8,128)(2,1)}, bf16[16,128,512]{2,1,0:T(8,128)(2,1)}, bf16[16,128,5...) custom-call(s32[1]{0:T(128)} %bitcast.me_ref, f32[1600,1]{1,0:T(8,128)} %copy.25.vld_ref, ...), custom_call_target="tpu_custom_call" | custom-call | flops 10000000 | bytes 100000 | tf_op jit(solution)/shard_map/mlp/pallas_call | solution.py:481
  103.2 4.2 %collective-permute-done.20 = bf16[16,128,512]{2,1,0:T(8,128)(2,1)S(1)} collective-permute-done((bf16[16,128,512]{2,1,0:T(8,128)(2,1)}, bf16[16,128,512]{2,1,0:T(8,128)(2,1)S(1)}, u32[]{:S(2)}, u32[]{:S(2)}) %collective-permute-start.20) | collective-permute-done | bytes 2097184 | tf_op jit(solution)/shard_map/ppermute | solution.py:64
  107.4 2.9 %convert_add_fusion = (f32[4,128,512]{2,1,0:T(8,128)S(1)}, bf16[4,128,512]{2,1,0:T(8,128)(2,1)}, bf16[4,128,512]{2,1,0:T(8,128)(2,1)S(1)}, bf16[4,128,512]{2,1,0:T(8,128)(2,1)S(1)}) fusion(bf16[16,128,512]{2,1,0:T(8,128)(2,1)S(1)} %collective-permute-done.20, bf16[16,128,512]{2,1,0:T(8,128)(2,1)} %get-tuple-element.76), kind=kLoop, calls=%fused_computation | loop fusion | flops 3932160 | bytes 6815744 | tf_op jit(solution)/shard_map/add | solution.py:107
  110.4 1.6 collective-permute-start.23
  113.9 27.1 %attn_bwd.1 = (bf16[2048,1536]{1,0:T(8,128)(2,1)}, f32[16,112,128]{2,1,0:T(8,128)}, f32[8,1536]{1,0:T(8,128)}, bf16[16,64,512]{2,1,0:T(8,128)(2,1)}, bf16[16,64,512]{2,1,0:T(8,128)(2,1)}) custom-call(s32[1]{0:T(128)} %bitcast.me_ref, f32[1600,512]{1,0:T(8,128)} %get-tuple-element.79.dmid_ref, bf16[512,512]{1,0:T(8,128)(2,1)} %get-tuple-element.80.p_ref, ...), custom_call_target="tpu_custom_call" | custom-call | flops 10000000 | bytes 100000 | tf_op jit(solution)/shard_map/attn_bwd/pallas_call | solution.py:603
  142.8 5.0 %collective-permute-start.31 = (bf16[1,128,512]{2,1,0:T(8,128)(2,1)}, bf16[1,128,512]{2,1,0:T(8,128)(2,1)}, u32[]{:S(2)}, u32[]{:S(2)}) collective-permute-start(bf16[1,128,512]{2,1,0:T(8,128)(2,1)} %get-tuple-element.113), channel_id=1, source_target_pairs={{0,8},{1,9},{2,10},{3,11},{4,12},{5,13},{6,14},{7,15},{8,0},{9,1},... | collective-permute-start | bytes 393224 | tf_op jit(solution)/shard_map/ppermute | solution.py:64
  147.9 2.5 %collective-permute-start.33 = (bf16[1,128,512]{2,1,0:T(8,128)(2,1)}, bf16[1,128,512]{2,1,0:T(8,128)(2,1)}, u32[]{:S(2)}, u32[]{:S(2)}) collective-permute-start(bf16[1,128,512]{2,1,0:T(8,128)(2,1)} %get-tuple-element.114), channel_id=1, source_target_pairs={{0,24},{1,25},{2,26},{3,27},{4,28},{5,29},{6,30},{7,31},{8,16},{9,... | collective-permute-start | bytes 393224 | tf_op jit(solution)/shard_map/ppermute | solution.py:64
  151.5 9.4 %grad_in.1 = (f32[1600,512]{1,0:T(8,128)}, f32[8,512]{1,0:T(8,128)}) custom-call(bf16[2048,1536]{1,0:T(8,128)(2,1)} %get-tuple-element.93.dm_ref, bf16[512,1536]{1,0:T(8,128)(2,1)} %get-tuple-element.94.w_ref, bf16[1600,512]{1,0:T(8,128)(2,1)} %x_ref.2, f32[1600,512]{1,0:T(8,128)} %get-tuple-element.79.dmid_ref, f32[16,512]{1,0:T(8,128)} %get-tuple-element.69.rowv_ref), custom_call_target="tpu_custom_call" | custom-call | flops 10000000 | bytes 100000 | tf_op jit(solution)/shard_map/grad_in/pallas_call | solution.py:650
  161.6 4.7 %rel_grad.1 = f32[16,384]{1,0:T(8,128)} custom-call(f32[16,112,128]{2,1,0:T(8,128)} %get-tuple-element.107.a_ref), custom_call_target="tpu_custom_call" | custom-call | flops 10000000 | bytes 100000 | tf_op jit(solution)/shard_map/rel_grad/pallas_call | solution.py:719
  168.6 1.5 collective-permute-start.37
  175.2 1.5 collective-permute-start.40
  176.8 1.9 collective-permute-start.39
  181.2 2.2 %collective-permute-start.27 = (bf16[4,64,512]{2,1,0:T(8,128)(2,1)}, bf16[4,64,512]{2,1,0:T(8,128)(2,1)S(1)}, u32[]{:S(2)}, u32[]{:S(2)}) collective-permute-start(bf16[4,64,512]{2,1,0:T(8,128)(2,1)} %get-tuple-element.117), channel_id=1, source_target_pairs={{0,6},{1,7},{2,4},{3,5},{4,2},{5,3},{6,0},{7,1},{8,14},{9,15},{10,... | collective-permute-start | bytes 786440 | tf_op jit(solution)/shard_map/ppermute | solution.py:64
  186.1 5.5 %collective-permute-done.27 = bf16[4,64,512]{2,1,0:T(8,128)(2,1)S(1)} collective-permute-done((bf16[4,64,512]{2,1,0:T(8,128)(2,1)}, bf16[4,64,512]{2,1,0:T(8,128)(2,1)S(1)}, u32[]{:S(2)}, u32[]{:S(2)}) %collective-permute-start.27) | collective-permute-done | bytes 262176 | tf_op jit(solution)/shard_map/ppermute | solution.py:64
  191.5 3.6 %collective-permute-done.26 = bf16[4,64,512]{2,1,0:T(8,128)(2,1)S(1)} collective-permute-done((bf16[4,64,512]{2,1,0:T(8,128)(2,1)}, bf16[4,64,512]{2,1,0:T(8,128)(2,1)S(1)}, u32[]{:S(2)}, u32[]{:S(2)}) %collective-permute-start.26) | collective-permute-done | bytes 262176 | tf_op jit(solution)/shard_map/ppermute | solution.py:64
  196.3 2.5 %collective-permute-start.30 = (bf16[1,64,512]{2,1,0:T(8,128)(2,1)S(1)}, bf16[1,64,512]{2,1,0:T(8,128)(2,1)S(1)}, u32[]{:S(2)}, u32[]{:S(2)}) collective-permute-start(bf16[1,64,512]{2,1,0:T(8,128)(2,1)S(1)} %get-tuple-element.121), channel_id=1, source_target_pairs={{0,24},{1,25},{2,26},{3,27},{4,28},{5,29},{6,30},{7,31},{8,16},{9,... | collective-permute-start | bytes 196616 | tf_op jit(solution)/shard_map/ppermute | solution.py:64
  200.6 2.6 %collective-permute-done.30 = bf16[1,64,512]{2,1,0:T(8,128)(2,1)S(1)} collective-permute-done((bf16[1,64,512]{2,1,0:T(8,128)(2,1)S(1)}, bf16[1,64,512]{2,1,0:T(8,128)(2,1)S(1)}, u32[]{:S(2)}, u32[]{:S(2)}) %collective-permute-start.30) | collective-permute-done | bytes 65568 | tf_op jit(solution)/shard_map/ppermute | solution.py:64
  203.2 2.0 collective-permute-done.29
  (154 shorter events, 45.9 us)
Async XLA Ops:
  2.2 9.4 %collective-permute-start.2 = (bf16[1,16,1664]{2,1,0:T(8,128)(2,1)S(1)}, bf16[1,16,1664]{2,1,0:T(8,128)(2,1)S(1)}, u32[]{:S(2)}, u32[]{:S(2)}) collective-permute-start(bf16[1,16,1664]{2,1,0:T(8,128)(2,1)S(1)} %maximum_bitcast_fusion), channel_id=1, source_target_pairs={{0,24},{1,25},{2,26},{3,27},{4,28},{5,29},{6,30},{7,31},{8,16},{9,... | collective-permute-start | bytes 159752 | tf_op jit(solution)/shard_map/ppermute | solution.py:64
  12.4 8.7 %collective-permute-start.8 = (bf16[1,144,512]{2,1,0:T(8,128)(2,1)S(1)}, bf16[1,144,512]{2,1,0:T(8,128)(2,1)S(1)}, u32[]{:S(2)}, u32[]{:S(2)}) collective-permute-start(bf16[1,144,512]{2,1,0:T(8,128)(2,1)S(1)} %bitcast.38), channel_id=1, source_target_pairs={{0,24},{1,25},{2,26},{3,27},{4,28},{5,29},{6,30},{7,31},{8,16},{9,... | collective-permute-start | bytes 442376 | tf_op jit(solution)/shard_map/ppermute | solution.py:64
  15.5 15.9 %collective-permute-start.7 = (bf16[1,144,512]{2,1,0:T(8,128)(2,1)S(1)}, bf16[1,144,512]{2,1,0:T(8,128)(2,1)S(1)}, u32[]{:S(2)}, u32[]{:S(2)}) collective-permute-start(bf16[1,144,512]{2,1,0:T(8,128)(2,1)S(1)} %bitcast.39), channel_id=1, source_target_pairs={{0,16},{1,17},{2,18},{3,19},{4,20},{5,21},{6,22},{7,23},{8,24},{9,... | collective-permute-start | bytes 442376 | tf_op jit(solution)/shard_map/ppermute | solution.py:64
  15.5 15.9 %collective-permute-start.6 = (bf16[1,144,512]{2,1,0:T(8,128)(2,1)S(1)}, bf16[1,144,512]{2,1,0:T(8,128)(2,1)S(1)}, u32[]{:S(2)}, u32[]{:S(2)}) collective-permute-start(bf16[1,144,512]{2,1,0:T(8,128)(2,1)S(1)} %bitcast.40), channel_id=1, source_target_pairs={{0,8},{1,9},{2,10},{3,11},{4,12},{5,13},{6,14},{7,15},{8,0},{9,1},... | collective-permute-start | bytes 442376 | tf_op jit(solution)/shard_map/ppermute | solution.py:64
  16.9 14.6 %collective-permute-start.5 = (bf16[4,16,1664]{2,1,0:T(8,128)(2,1)S(1)}, bf16[4,16,1664]{2,1,0:T(8,128)(2,1)S(1)}, u32[]{:S(2)}, u32[]{:S(2)}) collective-permute-start(bf16[4,16,1664]{2,1,0:T(8,128)(2,1)S(1)} %pad_maximum_fusion.2.refs_0_), channel_id=1, source_target_pairs={{0,6},{1,7},{2,4},{3,5},{4,2},{5,3},{6,0},{7,1},{8,14},{9,15},{10,... | collective-permute-start | bytes 638984 | tf_op jit(solution)/shard_map/ppermute | solution.py:64
  19.3 12.2 %collective-permute-start.4 = (bf16[4,16,1664]{2,1,0:T(8,128)(2,1)S(1)}, bf16[4,16,1664]{2,1,0:T(8,128)(2,1)S(1)}, u32[]{:S(2)}, u32[]{:S(2)}) collective-permute-start(bf16[4,16,1664]{2,1,0:T(8,128)(2,1)S(1)} %pad_maximum_fusion.2.refs_0_), channel_id=1, source_target_pairs={{0,4},{1,5},{2,6},{3,7},{4,0},{5,1},{6,2},{7,3},{8,12},{9,13},{10,... | collective-permute-start | bytes 638984 | tf_op jit(solution)/shard_map/ppermute | solution.py:64
  21.2 10.4 %collective-permute-start.3 = (bf16[4,16,1664]{2,1,0:T(8,128)(2,1)S(1)}, bf16[4,16,1664]{2,1,0:T(8,128)(2,1)S(1)}, u32[]{:S(2)}, u32[]{:S(2)}) collective-permute-start(bf16[4,16,1664]{2,1,0:T(8,128)(2,1)S(1)} %pad_maximum_fusion.2.refs_0_), channel_id=1, source_target_pairs={{0,2},{1,3},{2,0},{3,1},{4,6},{5,7},{6,4},{7,5},{8,10},{9,11},{10,... | collective-permute-start | bytes 638984 | tf_op jit(solution)/shard_map/ppermute | solution.py:64
  31.6 26.5 %collective-permute-start.15 = (bf16[4,144,512]{2,1,0:T(8,128)(2,1)S(1)}, bf16[4,144,512]{2,1,0:T(8,128)(2,1)S(1)}, u32[]{:S(2)}, u32[]{:S(2)}) collective-permute-start(bf16[4,144,512]{2,1,0:T(8,128)(2,1)S(1)} %pad_maximum_fusion), channel_id=1, source_target_pairs={{0,6},{1,7},{2,4},{3,5},{4,2},{5,3},{6,0},{7,1},{8,14},{9,15},{10,... | collective-permute-start | bytes 1769480 | tf_op jit(solution)/shard_map/ppermute | solution.py:64
  33.3 24.8 %collective-permute-start.14 = (bf16[4,144,512]{2,1,0:T(8,128)(2,1)S(1)}, bf16[4,144,512]{2,1,0:T(8,128)(2,1)S(1)}, u32[]{:S(2)}, u32[]{:S(2)}) collective-permute-start(bf16[4,144,512]{2,1,0:T(8,128)(2,1)S(1)} %pad_maximum_fusion), channel_id=1, source_target_pairs={{0,4},{1,5},{2,6},{3,7},{4,0},{5,1},{6,2},{7,3},{8,12},{9,13},{10,... | collective-permute-start | bytes 1769480 | tf_op jit(solution)/shard_map/ppermute | solution.py:64
  33.8 24.3 %collective-permute-start.13 = (bf16[4,144,512]{2,1,0:T(8,128)(2,1)S(1)}, bf16[4,144,512]{2,1,0:T(8,128)(2,1)S(1)}, u32[]{:S(2)}, u32[]{:S(2)}) collective-permute-start(bf16[4,144,512]{2,1,0:T(8,128)(2,1)S(1)} %pad_maximum_fusion), channel_id=1, source_target_pairs={{0,2},{1,3},{2,0},{3,1},{4,6},{5,7},{6,4},{7,5},{8,10},{9,11},{10,... | collective-permute-start | bytes 1769480 | tf_op jit(solution)/shard_map/ppermute | solution.py:64
  110.4 30.6 %collective-permute-start.23 = (bf16[4,128,512]{2,1,0:T(8,128)(2,1)}, bf16[4,128,512]{2,1,0:T(8,128)(2,1)S(1)}, u32[]{:S(2)}, u32[]{:S(2)}) collective-permute-start(bf16[4,128,512]{2,1,0:T(8,128)(2,1)} %get-tuple-element.110), channel_id=1, source_target_pairs={{0,6},{1,7},{2,4},{3,5},{4,2},{5,3},{6,0},{7,1},{8,14},{9,15},{10,... | collective-permute-start | bytes 1572872 | tf_op jit(solution)/shard_map/ppermute | solution.py:64
  112.0 29.0 %collective-permute-start.22 = (bf16[4,128,512]{2,1,0:T(8,128)(2,1)S(1)}, bf16[4,128,512]{2,1,0:T(8,128)(2,1)S(1)}, u32[]{:S(2)}, u32[]{:S(2)}) collective-permute-start(bf16[4,128,512]{2,1,0:T(8,128)(2,1)S(1)} %get-tuple-element.111), channel_id=1, source_target_pairs={{0,4},{1,5},{2,6},{3,7},{4,0},{5,1},{6,2},{7,3},{8,12},{9,13},{10,... | collective-permute-start | bytes 1572872 | tf_op jit(solution)/shard_map/ppermute | solution.py:64
  112.5 28.5 %collective-permute-start.21 = (bf16[4,128,512]{2,1,0:T(8,128)(2,1)S(1)}, bf16[4,128,512]{2,1,0:T(8,128)(2,1)S(1)}, u32[]{:S(2)}, u32[]{:S(2)}) collective-permute-start(bf16[4,128,512]{2,1,0:T(8,128)(2,1)S(1)} %get-tuple-element.112), channel_id=1, source_target_pairs={{0,2},{1,3},{2,0},{3,1},{4,6},{5,7},{6,4},{7,5},{8,10},{9,11},{10,... | collective-permute-start | bytes 1572872 | tf_op jit(solution)/shard_map/ppermute | solution.py:64
  141.0 9.4 %collective-permute-start.24 = (bf16[16,64,512]{2,1,0:T(8,128)(2,1)}, bf16[16,64,512]{2,1,0:T(8,128)(2,1)S(1)}, u32[]{:S(2)}, u32[]{:S(2)}) collective-permute-start(bf16[16,64,512]{2,1,0:T(8,128)(2,1)} %get-tuple-element.92), channel_id=1, source_target_pairs={{0,1},{1,0},{2,3},{3,2},{4,5},{5,4},{6,7},{7,6},{8,9},{9,8},{10,11... | collective-permute-start | bytes 3145736 | tf_op jit(solution)/shard_map/ppermute | solution.py:64
  142.8 27.8 %collective-permute-start.31 = (bf16[1,128,512]{2,1,0:T(8,128)(2,1)}, bf16[1,128,512]{2,1,0:T(8,128)(2,1)}, u32[]{:S(2)}, u32[]{:S(2)}) collective-permute-start(bf16[1,128,512]{2,1,0:T(8,128)(2,1)} %get-tuple-element.113), channel_id=1, source_target_pairs={{0,8},{1,9},{2,10},{3,11},{4,12},{5,13},{6,14},{7,15},{8,0},{9,1},... | collective-permute-start | bytes 393224 | tf_op jit(solution)/shard_map/ppermute | solution.py:64
  147.9 24.3 %collective-permute-start.33 = (bf16[1,128,512]{2,1,0:T(8,128)(2,1)}, bf16[1,128,512]{2,1,0:T(8,128)(2,1)}, u32[]{:S(2)}, u32[]{:S(2)}) collective-permute-start(bf16[1,128,512]{2,1,0:T(8,128)(2,1)} %get-tuple-element.114), channel_id=1, source_target_pairs={{0,24},{1,25},{2,26},{3,27},{4,28},{5,29},{6,30},{7,31},{8,16},{9,... | collective-permute-start | bytes 393224 | tf_op jit(solution)/shard_map/ppermute | solution.py:64
  150.3 21.8 %collective-permute-start.32 = (bf16[1,128,512]{2,1,0:T(8,128)(2,1)}, bf16[1,128,512]{2,1,0:T(8,128)(2,1)}, u32[]{:S(2)}, u32[]{:S(2)}) collective-permute-start(bf16[1,128,512]{2,1,0:T(8,128)(2,1)} %get-tuple-element.115), channel_id=1, source_target_pairs={{0,16},{1,17},{2,18},{3,19},{4,20},{5,21},{6,22},{7,23},{8,24},{9,... | collective-permute-start | bytes 393224 | tf_op jit(solution)/shard_map/ppermute | solution.py:64
  175.2 8.7 %collective-permute-start.40 = (f32[32,512]{1,0:T(8,128)S(1)}, f32[32,512]{1,0:T(8,128)S(1)}, u32[]{:S(2)}, u32[]{:S(2)}) collective-permute-start(f32[32,512]{1,0:T(8,128)S(1)} %add_add_fusion.1), channel_id=1, source_target_pairs={{0,24},{1,25},{2,26},{3,27},{4,28},{5,29},{6,30},{7,31},{8,16},{9,... | collective-permute-start | bytes 196616 | tf_op jit(solution)/shard_map/ppermute | solution.py:64
  176.8 8.0 %collective-permute-start.39 = (f32[32,512]{1,0:T(8,128)S(1)}, f32[32,512]{1,0:T(8,128)S(1)}, u32[]{:S(2)}, u32[]{:S(2)}) collective-permute-start(f32[32,512]{1,0:T(8,128)S(1)} %add_add_fusion.1), channel_id=1, source_target_pairs={{0,16},{1,17},{2,18},{3,19},{4,20},{5,21},{6,22},{7,23},{8,24},{9,... | collective-permute-start | bytes 196616 | tf_op jit(solution)/shard_map/ppermute | solution.py:64
  181.2 10.4 %collective-permute-start.27 = (bf16[4,64,512]{2,1,0:T(8,128)(2,1)}, bf16[4,64,512]{2,1,0:T(8,128)(2,1)S(1)}, u32[]{:S(2)}, u32[]{:S(2)}) collective-permute-start(bf16[4,64,512]{2,1,0:T(8,128)(2,1)} %get-tuple-element.117), channel_id=1, source_target_pairs={{0,6},{1,7},{2,4},{3,5},{4,2},{5,3},{6,0},{7,1},{8,14},{9,15},{10,... | collective-permute-start | bytes 786440 | tf_op jit(solution)/shard_map/ppermute | solution.py:64
  183.4 11.8 %collective-permute-start.26 = (bf16[4,64,512]{2,1,0:T(8,128)(2,1)}, bf16[4,64,512]{2,1,0:T(8,128)(2,1)S(1)}, u32[]{:S(2)}, u32[]{:S(2)}) collective-permute-start(bf16[4,64,512]{2,1,0:T(8,128)(2,1)} %get-tuple-element.118), channel_id=1, source_target_pairs={{0,4},{1,5},{2,6},{3,7},{4,0},{5,1},{6,2},{7,3},{8,12},{9,13},{10,... | collective-permute-start | bytes 786440 | tf_op jit(solution)/shard_map/ppermute | solution.py:64
  183.9 11.3 %collective-permute-start.25 = (bf16[4,64,512]{2,1,0:T(8,128)(2,1)S(1)}, bf16[4,64,512]{2,1,0:T(8,128)(2,1)S(1)}, u32[]{:S(2)}, u32[]{:S(2)}) collective-permute-start(bf16[4,64,512]{2,1,0:T(8,128)(2,1)S(1)} %get-tuple-element.119), channel_id=1, source_target_pairs={{0,2},{1,3},{2,0},{3,1},{4,6},{5,7},{6,4},{7,5},{8,10},{9,11},{10,... | collective-permute-start | bytes 786440 | tf_op jit(solution)/shard_map/ppermute | solution.py:64
  196.3 6.9 %collective-permute-start.30 = (bf16[1,64,512]{2,1,0:T(8,128)(2,1)S(1)}, bf16[1,64,512]{2,1,0:T(8,128)(2,1)S(1)}, u32[]{:S(2)}, u32[]{:S(2)}) collective-permute-start(bf16[1,64,512]{2,1,0:T(8,128)(2,1)S(1)} %get-tuple-element.121), channel_id=1, source_target_pairs={{0,24},{1,25},{2,26},{3,27},{4,28},{5,29},{6,30},{7,31},{8,16},{9,... | collective-permute-start | bytes 196616 | tf_op jit(solution)/shard_map/ppermute | solution.py:64
  198.8 6.5 %collective-permute-start.29 = (bf16[1,64,512]{2,1,0:T(8,128)(2,1)S(1)}, bf16[1,64,512]{2,1,0:T(8,128)(2,1)S(1)}, u32[]{:S(2)}, u32[]{:S(2)}) collective-permute-start(bf16[1,64,512]{2,1,0:T(8,128)(2,1)S(1)} %get-tuple-element.122), channel_id=1, source_target_pairs={{0,16},{1,17},{2,18},{3,19},{4,20},{5,21},{6,22},{7,23},{8,24},{9,... | collective-permute-start | bytes 196616 | tf_op jit(solution)/shard_map/ppermute | solution.py:64
  (35 other events, 274.5 us)

commit v4 on v3

--- a/solution.py
+++ b/solution.py
@@ -75,10 +75,12 @@
     return lax.optimization_barrier((values, others))[0]
 
 
-def gather_upper(x, groups, count):
+def gather_upper(x, groups, count, *others):
     cur = x[None]
     rels = [0]
-    for g in groups[:1:-1]:
+    for k, g in enumerate(groups[:1:-1]):
+        if k and others:
+            cur = after(cur, *others)
         ms = masks_of(g)
         cur = jnp.concatenate([cur] + [swap(cur, m, count) for m in ms], axis=0)
         rels = [r ^ m for m in [0] + ms for r in rels]
@@ -112,15 +114,6 @@
     return [swap(p, m, count) for p, m in zip(parts, masks_of(group))]
 
 
-def total(x, groups, count):
-    for g in groups:
-        got = [x] + [swap(x, m, count) for m in masks_of(g)]
-        while len(got) > 1:
-            got = [got[k] + got[k + 1] for k in range(0, len(got), 2)]
-        x = got[0]
-    return x
-
-
 def lay_vectors(raw, per, rowv_ref):
     unit = LANES // 2
     each = per // unit
@@ -151,10 +144,10 @@
     return jnp.concatenate([jnp.where(lane == q, block, jnp.zeros_like(block)) for q in range(4)], axis=0)
 
 
-def attn_fwd_body(me_ref, x_ref, mask_ref, bias_ref, *refs, plan, rpd, per):
+def attn_fwd_body(me_ref, x_ref, code_ref, bias_ref, *refs, plan, rpd, per):
     pieces = refs[: len(plan)]
-    (oT_ref, o_ref, q_ref, kT_ref, v_ref, pT_ref, h1T_ref, w_ref, rowv_ref) = refs[len(plan) : len(plan) + 9]
-    xs, h1p, qT, kn, vT, osc, raw, sem = refs[len(plan) + 9 :]
+    (oT_ref, o_ref, q_ref, kT_ref, v_ref, pT_ref, xT_ref, vld_ref, w_ref, rowv_ref) = refs[len(plan) : len(plan) + 10]
+    xs, h1p, qT, kn, vT, osc, vsc, mask_ref, raw, sem = refs[len(plan) + 10 :]
 
     @pl.when(pl.program_id(0) == 0)
     def _():
@@ -188,11 +181,21 @@
         xw = xs[CELLS * w : CELLS * w + 104, :]
         c = xw - jnp.mean(xw, axis=-1, keepdims=True)
         var = jnp.mean(c * c, axis=-1, keepdims=True)
-        h = pad_window(c * lax.rsqrt(var + 1e-5) * gain + shift)
-        h1p[LANES * w : LANES * w + LANES, :] = h
+        xh = c * lax.rsqrt(var + 1e-5)
+        h1p[LANES * w : LANES * w + LANES, :] = pad_window(xh * gain + shift)
+        xh = pad_window(xh)
         for a in range(D // LANES):
-            h1T_ref[LANES * a : LANES * a + LANES, LANES * w : LANES * w + LANES] = h[:, LANES * a : LANES * a + LANES].T
-    h1T_ref[D : D + 16, :] = jnp.ones((16, GL), bf16)
+            xT_ref[LANES * a : LANES * a + LANES, LANES * w : LANES * w + LANES] = xh[:, LANES * a : LANES * a + LANES].T
+    xT_ref[D : D + 16, :] = jnp.ones((16, GL), bf16)
+    turned = code_ref[0].T
+    keys = lax.broadcasted_iota(jnp.int32, (KP, LANES), 0)
+    same = (keys == lax.broadcasted_iota(jnp.int32, (KP, LANES), 1)) & (keys < CELLS)
+    for w in range(GW):
+        of_key = turned[:, GW + w : GW + w + 1]
+        equal = jnp.broadcast_to(of_key[0:KP], (KP, LANES)) == jnp.broadcast_to(code_ref[0, w : w + 1, :], (KP, LANES))
+        mask_ref[w] = jnp.where(equal | same, 0.0, NEG)
+        vsc[CELLS * w : CELLS * w + 104, :] = jnp.broadcast_to(jnp.where(of_key[0:104] >= 0.0, 1.0, 0.0), (104, LANES))
+    vld_ref[...] = vsc[0:GR, :]
     hp = h1p[...]
     q_ref[...] = (nn(hp, w_ref[:, 0:D]) + rowv_ref[2:3, :]).astype(bf16)
     kn[...] = nn(hp, w_ref[:, D : 2 * D]).astype(bf16)
@@ -239,7 +242,7 @@
 SMEM = pl.BlockSpec(memory_space=pltpu.SMEM)
 
 
-def attn_fwd(me, x, allowed, bias, plan, pieces, rpd, per, count):
+def attn_fwd(me, x, codes, bias, plan, pieces, rpd, per, count):
     n = x.shape[0] // GR
     copies = sum(1 if r is None else 2 * len(r) for r in plan)
     rb = pl.BlockSpec((GR, D), lambda i: (i, 0))
@@ -248,7 +251,7 @@
     return pl.pallas_call(
         functools.partial(attn_fwd_body, plan=plan, rpd=rpd, per=per),
         grid=(n,),
-        in_specs=[SMEM, rb, pl.BlockSpec((GW, KP, LANES), lambda i: (i, 0, 0)), whole((HEADS, KP, LANES))]
+        in_specs=[SMEM, rb, pl.BlockSpec((1, 2 * GW, LANES), lambda i: (i, 0, 0)), whole((HEADS, KP, LANES))]
         + any_specs(len(pieces)),
         out_specs=[
             tb,
@@ -258,6 +261,7 @@
             pb,
             pl.BlockSpec((GW, HEADS, KP, LANES), lambda i: (i, 0, 0, 0)),
             pl.BlockSpec((D + 16, GL), lambda i: (0, i)),
+            pl.BlockSpec((GR, LANES), lambda i: (i, 0)),
             whole((D, 3 * D)),
             whole((16, D)),
         ],
@@ -269,6 +273,7 @@
             sds((n * GL, D), bf16),
             sds((n * GW, HEADS, KP, LANES), bf16),
             sds((D + 16, n * GL), bf16),
+            sds((n * GR, LANES), f32),
             sds((D, 3 * D), bf16),
             sds((16, D), f32),
         ],
@@ -279,13 +284,15 @@
             pltpu.VMEM((GL, D), bf16),
             pltpu.VMEM((D, GL), bf16),
             pltpu.VMEM((GR + 8, D), f32),
+            pltpu.VMEM((GR + 8, LANES), f32),
+            pltpu.VMEM((GW, KP, LANES), f32),
             pltpu.VMEM((count, max(rpd, 16), LANES), bf16),
             pltpu.SemaphoreType.DMA((copies,)),
         ],
         compiler_params=params(60),
         cost_estimate=pl.CostEstimate(flops=10**7, bytes_accessed=10**5, transcendentals=0),
         name="attn_fwd",
-    )(me, x, allowed, bias, *pieces)
+    )(me, x, codes, bias, *pieces)
 
 
 def mlp_body(me_ref, vld_ref, rowv_ref, x_any, o_any, g_any, *refs, plan, rows, owners, rpd, groups):
@@ -355,6 +362,9 @@
             c.start()
         h2[rows:padded, :] = jnp.zeros((padded - rows, D), bf16)
         gp[rows:padded, :] = jnp.zeros((padded - rows, D), bf16)
+        dus[rows:padded, :] = jnp.zeros((padded - rows, 512), bf16)
+        for q in range(FF // 512):
+            es[q, rows:padded, :] = jnp.zeros((padded - rows, 512), bf16)
         dh2[...] = jnp.zeros_like(dh2)
         for c in first:
             c.wait()
@@ -366,7 +376,7 @@
             ins[2 * k].wait()
             ins[2 * k + 1].wait()
             a = nn(ob[at, :], pp[...]) + proj_bias
-            squares = squares + jnp.sum(a * a * vld_ref[at, :], axis=0, keepdims=True)
+            squares = squares + jnp.sum(a * a * vld_ref[at, 0:1], axis=0, keepdims=True)
             m = xb[at, :].astype(f32) + a
             mid[at, :] = m
             c = m - jnp.mean(m, axis=-1, keepdims=True)
@@ -389,14 +399,28 @@
             c.wait()
         store_p.wait()
 
-    u = nn(h2[...], u4[j]) + rowv_ref[pl.ds(8 + j, 1), :]
-    de = nt(gp[...], vv[pl.ds(pl.multiple_of(32 * j, 32), 32)].reshape(512, D))
-    cdf = 0.5 * lax.erf(u * RT2) + 0.5
-    es[j] = (u * cdf).astype(bf16)
-    du = de * (cdf + u * (PHI * jnp.exp2(u * u * (-0.5 * LOG2E))))
-    dus[...] = du.astype(bf16)
-    dbf1_ref[pl.ds(j, 1), :] = jnp.sum(du, axis=0, keepdims=True)
-    dh2[...] += nt(dus[...], u4[j])
+    up = u4[j]
+    down = vv[pl.ds(pl.multiple_of(32 * j, 32), 32)].reshape(512, D)
+    up_bias = rowv_ref[pl.ds(8 + j, 1), :]
+
+    def products(k):
+        at = slice(k * GR, k * GR + GR)
+        return nn(h2[at, :], up) + up_bias, nt(gp[at, :], down)
+
+    up_sum = jnp.zeros((1, 512), f32)
+    ahead = products(0)
+    for k in range(blocks):
+        u, de = ahead
+        if k + 1 < blocks:
+            ahead = products(k + 1)
+        at = slice(k * GR, k * GR + GR)
+        cdf = 0.5 * lax.erf(u * RT2) + 0.5
+        es[j, at, :] = (u * cdf).astype(bf16)
+        du = de * (cdf + u * (PHI * jnp.exp2(u * u * (-0.5 * LOG2E))))
+        dus[at, :] = du.astype(bf16)
+        up_sum = up_sum + jnp.sum(du, axis=0, keepdims=True)
+        dh2[at, :] += nt(dus[at, :], up)
+    dbf1_ref[pl.ds(j, 1), :] = up_sum
     dU = nn(h2T[...], dus[...]).astype(bf16)
     dV = nn(gT[...], es[j]).astype(bf16).T
     if owners:
@@ -448,7 +472,7 @@
             res[at, :] = out.astype(bf16)
             outs.append(pltpu.make_async_copy(res.at[rows_of(k)], res_any.at[rows_of(k)], sem_r.at[k]))
             outs[-1].start()
-            vl = vld_ref[at, :]
+            vl = vld_ref[at, 0:1]
             x = xb[at, :].astype(f32)
             terms = (x * x * vl, m * m * vl, f * f * vl, out * out * vl, jnp.broadcast_to(vl, (GR, D)))
             stats = [a + jnp.sum(t, axis=0, keepdims=True) for a, t in zip(stats, terms)]
@@ -481,7 +505,7 @@
     return pl.pallas_call(
         functools.partial(mlp_body, plan=plan, rows=rows, owners=count if owners else 0, rpd=rpd, groups=groups),
         grid=(steps,),
-        in_specs=[SMEM, whole((rows, 1)), whole((16, D))] + any_specs(3 + len(pieces)),
+        in_specs=[SMEM, whole((rows, LANES)), whole((16, D))] + any_specs(3 + len(pieces)),
         out_specs=any_specs(5) + [whole((8, D))] * 3,
         out_shape=[sds((rows, D), bf16), sds((rows, D), f32), sds((D, D), bf16)] + grad_shapes + [sds((8, D), f32)] * 3,
         scratch_shapes=[
@@ -492,7 +516,7 @@
             pltpu.VMEM((padded, D), bf16),
             pltpu.VMEM((D, padded), bf16),
             pltpu.VMEM((rows, D), f32),
-            pltpu.VMEM((padded, D), f32),
+            pltpu.VMEM((rows, D), f32),
             pltpu.VMEM((steps, padded, 512), bf16),
             pltpu.VMEM((padded, 512), bf16),
             pltpu.VMEM((steps, D, 512), bf16),
@@ -516,7 +540,7 @@
     )(me, vld, rowv, x, o, g, *pieces)
 
 
-def attn_bwd_body(me_ref, dmid_ref, p_ref, oT_ref, q_ref, kT_ref, v_ref, pT_ref, h1T_ref, *refs, owners, rpd, groups):
+def attn_bwd_body(me_ref, dmid_ref, p_ref, oT_ref, q_ref, kT_ref, v_ref, pT_ref, xT_ref, w_ref, rowv_ref, *refs, owners, rpd, groups):
     dm_ref, acc_ref, vec_ref = refs[:3]
     grads = refs[3:-6]
     xs, dap, don, doT, dw, dproj = refs[-6:]
@@ -566,31 +590,44 @@
         return carry
 
     lax.fori_loop(0, GW, window, 0, unroll=4)
-    dw[...] += nn(h1T_ref[...], dm_ref[...])
+    dw[...] += nn(xT_ref[...], dm_ref[...])
 
     @pl.when(i == pl.num_programs(0) - 1)
     def _():
+        s = dw[D : D + 1, :]
+        vec_ref[...] = jnp.zeros_like(vec_ref)
+        vec_ref[0:1, :] = s
+        for a in range(D // LANES):
+            rows = slice(LANES * a, LANES * a + LANES)
+            col = rowv_ref[0:8, rows].T
+            x = dw[rows, :]
+            wt = w_ref[rows, :].astype(f32)
+            by_gain = jnp.broadcast_to(jnp.sum(wt * x, axis=1, keepdims=True), (LANES, LANES)).T
+            by_shift = jnp.broadcast_to(jnp.sum(wt * s, axis=1, keepdims=True), (LANES, LANES)).T
+            vec_ref[1:2, rows] = by_gain[0:1]
+            vec_ref[2:3, rows] = by_shift[0:1]
+            dw[rows, :] = col[:, 0:1] * x + col[:, 1:2] * s
         if owners:
             me = me_ref[0]
-
-            def store(flip):
-                for k in range(owners):
-                    to = grads[(k ^ flip) & 1]
-                    pos = place_of(k ^ me, groups[1:])
+            for k in range(owners):
+                rel = k ^ me
+                pos = place_of(rel, groups[1:])
+                mine = slice(rpd * k, rpd * k + rpd)
+
+                def store(to, mine=mine, pos=pos):
                     for q in range(3):
-                        to[pos, rpd * q : rpd * q + rpd, :] = dw[rpd * k : rpd * k + rpd, D * q : D * q + D].astype(bf16)
-                    to[pos, 3 * rpd : 4 * rpd, :] = dproj[rpd * k : rpd * k + rpd, :].astype(bf16)
-
-            pl.when(me & 1 == 0)(lambda: store(0))
-            pl.when(me & 1 == 1)(lambda: store(1))
+                        to[pos, rpd * q : rpd * q + rpd, :] = dw[mine, D * q : D * q + D].astype(bf16)
+                    to[pos, 3 * rpd : 4 * rpd, :] = dproj[mine, :].astype(bf16)
+
+                pl.when(rel & 1 == 0)(functools.partial(store, grads[0]))
+                pl.when(rel & 1 == 1)(functools.partial(store, grads[1]))
         else:
             grads[0][...] = dw[0:D, :].astype(bf16)
             grads[1][...] = dproj[...].astype(bf16)
-        vec_ref[...] = dw[D : D + 8, :]
-
-
-def attn_bwd(me, dmid, p, oT, q, kT, v, pT, h1T, rpd, owners, count, groups):
-    n = dmid.shape[0] // GR
+
+
+def attn_bwd(me, dmid, p, oT, q, kT, v, pT, xT, w, rowv, rpd, owners, count, groups):
+    n = q.shape[0] // GL
 
     def tb(r):
         return pl.BlockSpec((r, GL), lambda i: (0, i))
@@ -603,7 +640,7 @@
     return pl.pallas_call(
         functools.partial(attn_bwd_body, owners=count if owners else 0, rpd=rpd, groups=groups),
         grid=(n,),
-        in_specs=[SMEM, pl.BlockSpec((GR, D), lambda i: (i, 0)), whole((D, D)), tb(D), pb, tb(D), pb, pl.BlockSpec((GW, HEADS, KP, LANES), lambda i: (i, 0, 0, 0)), tb(D + 16)],
+        in_specs=[SMEM, pl.BlockSpec((GR, D), lambda i: (i, 0)), whole((D, D)), tb(D), pb, tb(D), pb, pl.BlockSpec((GW, HEADS, KP, LANES), lambda i: (i, 0, 0, 0)), tb(D + 16), whole((D, 3 * D)), whole((16, D))],
         out_specs=[pl.BlockSpec((GL, 3 * D), lambda i: (i, 0)), whole((HEADS, KP, LANES)), whole((8, 3 * D))] + [whole(s.shape) for s in grad_shapes],
         out_shape=[sds((n * GL, 3 * D), bf16), sds((HEADS, KP, LANES), f32), sds((8, 3 * D), f32)] + grad_shapes,
         scratch_shapes=[
@@ -617,31 +654,21 @@
         compiler_params=params(60),
         cost_estimate=pl.CostEstimate(flops=10**7, bytes_accessed=10**5, transcendentals=0),
         name="attn_bwd",
-    )(me, dmid, p, oT, q, kT, v, pT, h1T)
-
-
-def grad_in_body(dm_ref, w_ref, x_ref, dmid_ref, rowv_ref, tg_ref, vec_ref, dsc):
+    )(me, dmid, p, oT, q, kT, v, pT, xT, w, rowv)
+
+
+def grad_in_body(dm_ref, w_ref, x_ref, dmid_ref, rowv_ref, tg_ref, dsc):
     dh = nt(dm_ref[...], w_ref[...])
     for w in range(GW):
         dsc[CELLS * w : CELLS * w + 104, :] = dh[LANES * w : LANES * w + 104]
-    d = dsc[0:GR, :]
     x = x_ref[...].astype(f32)
     c = x - jnp.mean(x, axis=-1, keepdims=True)
     rs = lax.rsqrt(jnp.mean(c * c, axis=-1, keepdims=True) + 1e-5)
     xh = c * rs
-    gain = rowv_ref[0:1, :]
-    dx = d * gain
-    dxx = d * xh
+    dx = dsc[0:GR, :] * rowv_ref[0:1, :]
     m1 = jnp.mean(dx, axis=-1, keepdims=True)
-    m2 = jnp.mean(dxx * gain, axis=-1, keepdims=True)
+    m2 = jnp.mean(dx * xh, axis=-1, keepdims=True)
     tg_ref[...] = dmid_ref[...] + (dx - m1 - xh * m2) * rs
-
-    @pl.when(pl.program_id(0) == 0)
-    def _():
-        vec_ref[...] = jnp.zeros_like(vec_ref)
-
-    vec_ref[0:1, :] += jnp.sum(dxx, axis=0, keepdims=True)
-    vec_ref[1:2, :] += jnp.sum(d, axis=0, keepdims=True)
 
 
 def grad_in(dm, w, x, dmid, rowv):
@@ -651,13 +678,138 @@
         grad_in_body,
         grid=(n,),
         in_specs=[pl.BlockSpec((GL, 3 * D), lambda i: (i, 0)), whole((D, 3 * D)), rb, rb, whole((16, D))],
-        out_specs=[rb, whole((8, D))],
-        out_shape=[sds((n * GR, D), f32), sds((8, D), f32)],
+        out_specs=rb,
+        out_shape=sds((n * GR, D), f32),
         scratch_shapes=[pltpu.VMEM((GR + 8, D), f32)],
         compiler_params=params(60),
         cost_estimate=pl.CostEstimate(flops=10**7, bytes_accessed=10**5, transcendentals=0),
         name="grad_in",
     )(dm, w, x, dmid, rowv)
+
+
+SMALL = 24
+
+
+def two_terms(x):
+    hi = x.astype(bf16).astype(f32)
+    return jnp.concatenate([hi, x - hi], axis=0).astype(bf16)
+
+
+def one_term(x):
+    x = x.astype(f32)
+    return x[0:SMALL] + x[SMALL : 2 * SMALL]
+
+
+def fold_body(*refs, first, terms, parts):
+    ins, outs = refs[: 2 * terms if first else terms + 1], refs[2 * terms if first else terms + 1 :]
+    nb, rows = ins[0].shape[0], ins[0].shape[1]
+    n = nb // (parts + 1)
+    if first:
+        small = ins[2][...] + ins[3][...]
+    else:
+        got = [one_term(ins[1][...])] + [one_term(r[nb * rows :, :]) for r in ins[2:]]
+        while len(got) > 1:
+            got = [got[k] + got[k + 1] for k in range(0, len(got), 2)]
+        small = got[0]
+    for p in range(parts + 1):
+        at = slice(p * n, p * n + n)
+        total = ins[0][at].astype(f32)
+        if first:
+            total = total + ins[1][at].astype(f32)
+        else:
+            for r in ins[2:]:
+                total = total + r[p * n * rows : (p + 1) * n * rows, :].astype(f32).reshape(n, rows, D)
+        if p == 0:
+            outs[0][...] = total
+            outs[1][...] = two_terms(small)
+        else:
+            outs[p + 1][0 : n * rows, :] = total.reshape(n * rows, D).astype(bf16)
+            outs[p + 1][n * rows :, :] = two_terms(small)
+
+
+def fold(arrays, parts, first=False):
+    terms = 2 if first else len(arrays) - 1
+    nb, rows = arrays[0].shape[:2]
+    n = nb // (parts + 1)
+    return pl.pallas_call(
+        functools.partial(fold_body, first=first, terms=terms, parts=parts),
+        out_shape=[sds((n, rows, D), f32), sds((2 * SMALL, D), bf16)] + [sds((n * rows + 2 * SMALL, D), bf16)] * parts,
+        compiler_params=params(16),
+        cost_estimate=pl.CostEstimate(flops=10**6, bytes_accessed=10**5, transcendentals=0),
+        name="fold",
+    )(*arrays)
+
+
+def spread(o_ref, block, width, at):
+    each = width // LANES
+    for b in range(block.shape[1] // LANES):
+        o_ref[pl.ds(at // LANES + b, block.shape[0], stride=each), :] = block[:, LANES * b : LANES * b + LANES]
+
+
+def attn_last_body(me_ref, own_ref, kept_ref, *refs, rpd, per):
+    got_refs, (qkv_ref, proj_ref, vec_ref, table_ref, stats_ref, lines) = refs[:-6], refs[-6:]
+    rows = 4 * rpd
+    total = own_ref[0]
+    for r in got_refs:
+        total = total + r[0:rows, :].astype(f32)
+    for q in range(3):
+        spread(qkv_ref, total[rpd * q : rpd * q + rpd], 3 * D, D * q)
+    spread(proj_ref, total[3 * rpd : rows], D, 0)
+    got = [one_term(kept_ref[...])] + [one_term(r[rows:, :]) for r in got_refs]
+    while len(got) > 1:
+        got = [got[k] + got[k + 1] for k in range(0, len(got), 2)]
+    small = got[0]
+    for k in range(8):
+        for a in range(4):
+            lines[4 * k + a : 4 * k + a + 1, :] = small[k : k + 1, LANES * a : LANES * a + LANES]
+    lines[32:48, :] = small[8:24, RP:D]
+    if per % 64:
+        vec_ref[...] = lines[...]
+    else:
+        low = lax.broadcasted_iota(jnp.int32, (1, LANES), 1) < 64
+        for p in range(0, per // 64, 2):
+            halves = []
+            for k in range(2):
+                c = me_ref[0] * (per // 64) + min(p + k, per // 64 - 1)
+                line = lines[pl.ds(c >> 1, 1), :]
+                halves.append(jnp.where(c & 1 == k, line, pltpu.roll(line, 64, 1)))
+            vec_ref[p // 2 : p // 2 + 1, :] = jnp.where(low, halves[0], halves[1])
+    turned = small[8:24, 0:RP].T
+    table_ref[...] = turned[0:RELN]
+    line = turned[RELN : RELN + 1]
+    stats_ref[...] = jnp.sqrt(line / line[:, 5:6] + 1e-06)
+
+
+def attn_last(me, arrays, rpd, per):
+    lines = -(-per // LANES) if per % 64 == 0 else 48
+    return pl.pallas_call(
+        functools.partial(attn_last_body, rpd=rpd, per=per),
+        in_specs=[SMEM] + [pl.BlockSpec(memory_space=pltpu.VMEM)] * len(arrays),
+        out_shape=[sds((12 * rpd, LANES), f32), sds((4 * rpd, LANES), f32), sds((lines, LANES), f32), sds((RELN, HEADS), f32), sds((1, HEADS), f32)],
+        scratch_shapes=[pltpu.VMEM((48, LANES), f32)],
+        compiler_params=params(16),
+        cost_estimate=pl.CostEstimate(flops=10**6, bytes_accessed=10**5, transcendentals=0),
+        name="attn_last",
+    )(me, *arrays)
+
+
+def mlp_last_body(own_ref, *refs, rpd):
+    total = own_ref[0]
+    for r in refs[:-2]:
+        total = total + r[0].astype(f32)
+    for q in range(4):
+        spread(refs[-2], total[rpd * q : rpd * q + rpd], FF, 512 * q)
+    spread(refs[-1], total[4 * rpd :], D, 0)
+
+
+def mlp_last(arrays, rpd):
+    return pl.pallas_call(
+        functools.partial(mlp_last_body, rpd=rpd),
+        out_shape=[sds((16 * rpd, LANES), f32)] * 2,
+        compiler_params=params(16),
+        cost_estimate=pl.CostEstimate(flops=10**6, bytes_accessed=10**5, transcendentals=0),
+        name="mlp_last",
+    )(*arrays)
 
 
 def place_hits(shape, axis, rev=0):
@@ -676,10 +828,10 @@
         row = pltpu.roll(jnp.broadcast_to(t_ref[pl.ds(h, 1), :], (8, RP)), 0, 1, stride=1, stride_axis=0)
         t = jnp.concatenate([pltpu.roll(row, (8 * k - 180) % RP, 1)[:, 0:256] for k in range(24)], axis=0)
         hi = t.astype(bf16)
-        r = t - hi.astype(f32)
-        md = r.astype(bf16)
-        lo = (r - md.astype(f32)).astype(bf16)
-        o_ref[h] = sum(nn(nn(keys, part).astype(bf16), queries) for part in (lo, md, hi))
+        lo = (t - hi.astype(f32)).astype(bf16)
+        b = nn(jnp.concatenate([hi, lo], axis=0), queries).astype(bf16)
+        b = nn(keys, jnp.concatenate([b[0:192], b[192:384]], axis=1))
+        o_ref[h] = b[:, 0:LANES] + b[:, LANES : 2 * LANES]
         return carry
 
     lax.fori_loop(0, HEADS, head, 0, unroll=8)
@@ -689,46 +841,57 @@
     return pl.pallas_call(
         rel_bias_body,
         out_shape=sds((HEADS, KP, LANES), f32),
-        compiler_params=params(60),
+        compiler_params=params(16),
         cost_estimate=pl.CostEstimate(flops=10**7, bytes_accessed=10**5, transcendentals=0),
         name="rel_bias",
     )(table)
 
 
-def rel_grad_body(a_ref, o_ref):
+def rel_grad_body(a_ref, one_ref, two_ref, up_ref, squares_ref, o_ref):
     keys = place_hits((192, KP), 0, 191)
     queries = place_hits((LANES, 256), 1)
     zero = jnp.zeros((8, RP - 256), f32)
+    o_ref[0:2, :] = one_ref[1:3, 0:D]
+    o_ref[2:3, :] = one_ref[0:1, 0:D]
+    o_ref[3:4, :] = one_ref[0:1, 2 * D : 3 * D]
+    o_ref[4:8, :] = two_ref[0:4, :]
 
     def head(h, carry):
         a = a_ref[h]
         hi = a.astype(bf16)
         lo = (a - hi.astype(f32)).astype(bf16)
-        b = nn(nn(keys, hi).astype(bf16), queries) + nn(nn(keys, lo).astype(bf16), queries)
+        b = nn(keys, jnp.concatenate([hi, lo], axis=1)).astype(bf16)
+        b = nn(jnp.concatenate([b[:, 0:LANES], b[:, LANES : 2 * LANES]], axis=0), queries)
+        b = b[0:192] + b[192:384]
         t = jnp.zeros((8, RP), f32)
         for k in range(24):
             t = t + pltpu.roll(jnp.concatenate([b[8 * k : 8 * k + 8], zero], axis=1), (8 * k - 11) % RP, 1)
         t = pltpu.roll(t, 0, 1, stride=1, stride_axis=0)
-        o_ref[pl.ds(h, 1), :] = jnp.sum(t, axis=0, keepdims=True)
+        o_ref[pl.ds(8 + h, 1), 0:RP] = jnp.sum(t, axis=0, keepdims=True)
         return carry
 
-    lax.fori_loop(0, HEADS, head, 0, unroll=8)
-
-
-def rel_grad(acc):
+    lax.fori_loop(0, HEADS, head, 0, unroll=16)
+    for k in range(4):
+        for a in range(4):
+            o_ref[8 + 4 * k + a : 9 + 4 * k + a, RP:D] = up_ref[k : k + 1, LANES * a : LANES * a + LANES]
+    for k in range(6):
+        o_ref[8 + k : 9 + k, RELN : RELN + 1] = jnp.sum(squares_ref[k : k + 1, :], axis=1, keepdims=True)
+
+
+def rel_grad(acc, one, two, up, squares):
     return pl.pallas_call(
         rel_grad_body,
-        out_shape=sds((HEADS, RP), f32),
-        compiler_params=params(60),
+        out_shape=sds((SMALL, D), f32),
+        compiler_params=params(16),
         cost_estimate=pl.CostEstimate(flops=10**7, bytes_accessed=10**5, transcendentals=0),
         name="rel_grad",
-    )(acc)
+    )(acc, one, two, up, squares)
 
 
 def shards(tokens, cotangent, regions, validity, qkv_weight, proj_weight, fc1_weight, fc2_weight, vectors, rel_table, *, count, inner):
     rows = tokens.shape[0]
-    windows = rows // CELLS
     groups = bit_groups(count)
+    single = groups[:2] + [(b,) for g in groups[2:] for b in g]
     rpd = D // count
     direct = rpd % 16 == 0
     me = lax.axis_index("dp") * inner + lax.axis_index("shard")
@@ -749,22 +912,20 @@
         ],
         axis=0,
     )
-    packed, table_in, valid_in = after((packed.reshape(9 * rpd, D), rel_table, validity), attn_up)
+    packed = packed.reshape(9 * rpd, D)
     attn_pieces = gather_plane(rels, attn_up, groups, count)
-    _, mlp_up = gather_upper(packed, groups, count)
+    table_in = after(rel_table, attn_up)
+    mlp_rels, mlp_up = gather_upper(packed, single, count, attn_up)
 
     bias = rel_bias(jnp.pad(table_in.T * LOG2E, ((0, 0), (0, RP - RELN))))
-    reg = regions.reshape(windows, CELLS)
-    val = valid_in.reshape(windows, CELLS)
-    allowed = (reg[:, :, None] == reg[:, None, :]) & (val[:, :, None] == 1)
-    allowed = jnp.where(allowed | jnp.eye(CELLS, dtype=jnp.bool_)[None], 0.0, NEG).astype(f32)
-    allowed = jnp.pad(allowed, ((0, 0), (0, KP - CELLS), (0, LANES - CELLS)), constant_values=NEG)
-    vld = valid_in.astype(f32).reshape(rows, 1)
-
-    held, mlp_up = after(([a for _, a in attn_pieces], mlp_up), bias, allowed, vld)
+    reg = regions.reshape(-1, GW, CELLS).astype(f32)
+    key_code = jnp.where(validity.reshape(-1, GW, CELLS) == 1, reg, -2.0)
+    codes = jnp.pad(jnp.concatenate([reg, key_code], axis=1), ((0, 0), (0, 0), (0, LANES - CELLS)), constant_values=-3.0)
+
+    held, mlp_up = after(([a for _, a in attn_pieces], mlp_up), bias, codes)
     mlp_up = after(mlp_up, held)
     attn_pieces = gather_core([(r, a) for (r, _), a in zip(attn_pieces, held)], count)
-    mlp_pieces = gather_plane(rels, mlp_up, groups, count)
+    mlp_pieces = gather_plane(mlp_rels, mlp_up, groups, count)
     if direct:
         attn_plan = [r for r, _ in attn_pieces]
         attn_w = [a for _, a in attn_pieces]
@@ -773,8 +934,8 @@
         both = natural_order(attn_pieces, me, count).reshape(count, -1)
         attn_w = [both[:, : 3 * D * rpd].reshape(D, 3 * D), jnp.pad(both[:, 3 * D * rpd :].astype(f32).reshape(12, D), ((0, 4), (0, 0)))]
 
-    x = after(tokens, mlp_up, vld)
-    oT, o, q, kT, v, pT, h1T, w_full, rowv = attn_fwd(me_s, x, allowed, bias, attn_plan, attn_w, rpd, per, count)
+    x = after(tokens, mlp_up)
+    oT, o, q, kT, v, pT, xT, vld, w_full, rowv = attn_fwd(me_s, x, codes, bias, attn_plan, attn_w, rpd, per, count)
 
     held = after([a for _, a in mlp_pieces], o)
     mlp_pieces = gather_core([(r, a) for (r, _), a in zip(mlp_pieces, held)], count)
@@ -786,22 +947,23 @@
         mlp_plan = [None] * 3
         mlp_w = [both[:, 0].reshape(D, D), both[:, 1:5].transpose(1, 0, 2, 3).reshape(4, D, 512), both[:, 5:].reshape(128, 16, D)]
     result, dmid, p_full, mlp_keep, mlp_send, vec_two, dbf1, squares = mlp(
-        me_s, tokens, o, cotangent, vld, rowv, mlp_plan, mlp_w, rpd, direct, count, groups
+        me_s, tokens, o, cotangent, vld, rowv, mlp_plan, mlp_w, rpd, direct, count, single
     )
     order = None
     if not direct:
         blocks = jnp.arange(count)
-        where = place_of(blocks, groups)
-        order = jnp.zeros((count,), jnp.int32).at[where].set(blocks.astype(jnp.int32)) ^ me
+        order, mlp_order = (
+            jnp.zeros((count,), jnp.int32).at[place_of(blocks, way)].set(blocks.astype(jnp.int32)) ^ me for way in (groups, single)
+        )
         dU = mlp_keep.reshape(count, rpd, 4, 512).transpose(0, 2, 1, 3).reshape(count, 4 * rpd, 512)
-        pk = jnp.take(jnp.concatenate([dU, mlp_send.reshape(count, 4 * rpd, D)], axis=1), order, axis=0)
+        pk = jnp.take(jnp.concatenate([dU, mlp_send.reshape(count, 4 * rpd, D)], axis=1), mlp_order, axis=0)
         mlp_keep, mlp_send = pk[: count // 2], pk[count // 2 :]
 
     other = swap(mlp_send, 1, count)
     mlp_own, parts = split_sum([mlp_keep, other], groups[1])
     mlp_got = send_parts(parts, groups[1], count)
     dmid = after(dmid, parts)
-    got = attn_bwd(me_s, dmid, p_full, oT, q, kT, v, pT, h1T, rpd, direct, count, groups)
+    got = attn_bwd(me_s, dmid, p_full, oT, q, kT, v, pT, xT, w_full, rowv, rpd, direct, count, groups)
     dm, score_sums, vec_one = got[:3]
     if direct:
         attn_keep, attn_send = got[3:]
@@ -810,49 +972,47 @@
         pk = jnp.take(jnp.concatenate([dW, got[4].reshape(count, rpd, D)], axis=1), order, axis=0)
         attn_keep, attn_send = pk[: count // 2], pk[count // 2 :]
     mlp_got, attn_send, score_sums, dm = lax.optimization_barrier((mlp_got, attn_send, score_sums, dm))
+
     other = swap(attn_send, 1, count)
-    attn_own, parts = split_sum([attn_keep, other], groups[1])
-    attn_got = send_parts(parts, groups[1], count)
     mlp_terms = [mlp_own] + mlp_got
-    dm = after(dm, parts)
-    grad_tokens, vec_in = grad_in(dm, w_full, tokens, dmid, rowv)
-    table = rel_grad(after(score_sums, parts))
-    attn_terms = [attn_own] + after(attn_got, grad_tokens)
-    for g in groups[2:]:
+    for g in single[2:3]:
         mlp_own, parts = split_sum(mlp_terms, g)
         mlp_terms = [mlp_own] + send_parts(parts, g, count)
-        attn_own, parts = split_sum(attn_terms, g)
-        attn_terms = [attn_own] + send_parts(parts, g, count)
-    mlp_sum = sum(t[0].astype(f32) for t in mlp_terms)
-    attn_sum = sum(t[0].astype(f32) for t in attn_terms)
-    small = jnp.concatenate(
-        [
-            vec_in[0:2],
-            vec_one[0:1, 0:D],
-            vec_one[0:1, 2 * D : 3 * D],
-            vec_two[0:4],
-            dbf1[0:4],
-            table.reshape(-1, D),
-            squares,
-        ],
-        axis=0,
-    )
-    small = total(small, groups, count)
-    length = vectors.shape[0]
-    grad_vectors = lax.dynamic_slice(small[:12].reshape(-1), (me * length,), (length,))
-    grad_table = small[12:24].reshape(HEADS, RP)[:, :RELN].T
-    sums = jnp.sum(small[24:32], axis=1)
-    stats = jnp.sqrt(sums[0:5] / sums[5] + 1e-06)
+        score_sums = after(score_sums, parts)
+    small = rel_grad(score_sums, vec_one, vec_two, dbf1, squares)
+    other = after(other, small)
+    levels = [len(masks_of(g)) for g in groups[1:]]
+    out = fold([attn_keep, other, small, swap(small, 1, count)], levels[0], first=True)
+    for k, g in enumerate(groups[1:]):
+        own, kept, parts = out[0], out[1], out[2:]
+        sent = send_parts(parts, g, count)
+        if k == 0:
+            dm = after(dm, parts)
+            grad_tokens = grad_in(dm, w_full, tokens, dmid, rowv)
+            sent, mlp_terms = after((sent, mlp_terms), grad_tokens)
+            for up in single[3:]:
+                mlp_own, parts = split_sum(mlp_terms, up)
+                mlp_terms = [mlp_own] + send_parts(parts, up, count)
+        if k + 1 < len(levels):
+            out = fold([own, kept] + sent, levels[k + 1])
+            mlp_terms = after(mlp_terms, out)
+    grad_fc1, grad_fc2 = mlp_last(mlp_terms, rpd)
+    sent = after(sent, grad_fc1)
+    grad_qkv, grad_proj, grad_vectors, grad_table, stats = attn_last(me_s, [own, kept] + sent, rpd, per)
+    if per % 64 == 0:
+        grad_vectors = grad_vectors.reshape(-1)[:per]
+    else:
+        grad_vectors = lax.dynamic_slice(grad_vectors.reshape(-1), (me * per,), (per,))
     return (
         result,
         grad_tokens,
-        attn_sum[: 3 * rpd].reshape(3, rpd, D).transpose(1, 0, 2).reshape(-1),
-        attn_sum[3 * rpd :].reshape(-1),
-        mlp_sum[: 4 * rpd].reshape(4, rpd, 512).transpose(1, 0, 2).reshape(-1),
-        mlp_sum[4 * rpd :].reshape(-1),
+        grad_qkv.reshape(-1),
+        grad_proj.reshape(-1),
+        grad_fc1.reshape(-1),
+        grad_fc2.reshape(-1),
         grad_vectors,
         grad_table,
-        stats,
+        stats[0, 0:5],
     )
 
 

time: 208 us -> 188 us (0.904)
  starting transfers between devices: 46.4 us -> 33.4 us
  local copies, waits for them, and re-layouts: 16.1 us -> 8.83 us
  waiting for transfers between devices: 26.3 us -> 33.1 us
  other arithmetic: 9.11 us -> 5.6 us
  Pallas kernels: 108 us -> 105 us
    ppermute x41 -> x33, starting transfers between devices: 46.4 us -> 33.4 us  [swap(): return lax.ppermute(x, AXES, [(i, i ^ mask) for i in range(count)])]
    ppermute x41 -> x33, waiting for transfers between devices: 26.3 us -> 33.1 us  [swap(): return lax.ppermute(x, AXES, [(i, i ^ mask) for i in range(count)])]
    pallas_call x1, Pallas kernels: 7.2 us -> 4.31 us  [rel_bias(): pl.pallas_call(rel_bias_body, out_shape=sds((HEADS, KP, LANES), f32), com...]
    reshape x8 -> x0, local copies, waits for them, and re-layouts: 2.86 us -> none  [the longest x2 1.26 us: shards(): vld = valid_in.astype(f32).reshape(rows, 1)]
    slice x7 -> x0, local copies, waits for them, and re-layouts: 2.16 us -> none  [the longest x1 0.83 us: shards(): vec_one[0:1, 2 * D:3 * D]]
    pallas_call x1 -> x5, Pallas kernels: 4.73 us -> 4.36 us  [the longest x1 2.41 us: rel_grad(): pl.pallas_call(rel_grad_body, out_shape=sds((SMALL, D), f32), compiler_pa...]
  transfers between devices with their start and end apart: 41 -> 33, of which waited for: 18 -> 19; matrix products, arithmetic and copies ran while one was open for 9% -> 3% of each run, Pallas kernels for 33% -> 35%
where the time goes in v4:
time: 188 us; the launch traced here: 187 us
  Pallas kernels  105 us (56%)
  starting transfers between devices  33.4 us (18%)
  waiting for transfers between devices  33.1 us (18%)
  local copies, waits for them, and re-layouts  8.83 us (5%)
  other arithmetic  5.6 us (3%)
    pallas_call x1, Pallas kernels, mlp(): pl.pallas_call(functools.partial(mlp_body, plan=plan, rows=rows, owners=c...  38.8 us
    ppermute x33, starting transfers between devices, swap(): return lax.ppermute(x, AXES, [(i, i ^ mask) for i in range(count)])  33.4 us
    ppermute x33, waiting for transfers between devices, swap(): return lax.ppermute(x, AXES, [(i, i ^ mask) for i in range(count)])  33.1 us
    pallas_call x1, Pallas kernels, attn_bwd(): pl.pallas_call(functools.partial(attn_bwd_body, owners=count if owners el...  28.9 us
    pallas_call x1, Pallas kernels, attn_fwd(): pl.pallas_call(functools.partial(attn_fwd_body, plan=plan, rpd=rpd, per=p...  19.8 us
    pallas_call x1, Pallas kernels, grad_in(): pl.pallas_call(grad_in_body, grid=(n,), in_specs=[pl.BlockSpec((GL, 3 * D...  9.2 us
    pallas_call x1, Pallas kernels, rel_bias(): pl.pallas_call(rel_bias_body, out_shape=sds((HEADS, KP, LANES), f32), com...  4.31 us
    unnamed x45, local copies, waits for them, and re-layouts  3.93 us
  transfers between devices with their start and end apart: 33, of which 19 were waited for; matrix products, arithmetic and copies ran while one was open for 3% of the time, Pallas kernels for 35%

profile of v4, /device:TPU:0, one launch (start us, length us, event | category | flops | bytes accessed | tf_op | source)
XLA Modules:
  0.0 187.3 jit_solution(4499284947322447565)
XLA Ops:
  2.2 5.1 %collective-permute-start.2 = (bf16[1,16,1664]{2,1,0:T(8,128)(2,1)S(1)}, bf16[1,16,1664]{2,1,0:T(8,128)(2,1)S(1)}, u32[]{:S(2)}, u32[]{:S(2)}) collective-permute-start(bf16[1,16,1664]{2,1,0:T(8,128)(2,1)S(1)} %maximum_bitcast_fusion), channel_id=1, source_target_pairs={{0,24},{1,25},{2,26},{3,27},{4,28},{5,29},{6,30},{7,31},{8,16},{9,... | collective-permute-start | bytes 159752 | tf_op jit(solution)/shard_map/ppermute | solution.py:64
  10.8 2.4 %collective-permute-start.6 = (bf16[1,144,512]{2,1,0:T(8,128)(2,1)S(1)}, bf16[1,144,512]{2,1,0:T(8,128)(2,1)S(1)}, u32[]{:S(2)}, u32[]{:S(2)}) collective-permute-start(bf16[1,144,512]{2,1,0:T(8,128)(2,1)S(1)} %bitcast.26), channel_id=1, source_target_pairs={{0,16},{1,17},{2,18},{3,19},{4,20},{5,21},{6,22},{7,23},{8,24},{9,... | collective-permute-start | bytes 442376 | tf_op jit(solution)/shard_map/ppermute | solution.py:64
  14.8 5.1 %collective-permute-done.6 = bf16[1,144,512]{2,1,0:T(8,128)(2,1)S(1)} collective-permute-done((bf16[1,144,512]{2,1,0:T(8,128)(2,1)S(1)}, bf16[1,144,512]{2,1,0:T(8,128)(2,1)S(1)}, u32[]{:S(2)}, u32[]{:S(2)}) %collective-permute-start.6) | collective-permute-done | bytes 147488 | tf_op jit(solution)/shard_map/ppermute | solution.py:64
  21.0 2.4 %collective-permute-start.5 = (bf16[4,16,1664]{2,1,0:T(8,128)(2,1)S(1)}, bf16[4,16,1664]{2,1,0:T(8,128)(2,1)S(1)}, u32[]{:S(2)}, u32[]{:S(2)}) collective-permute-start(bf16[4,16,1664]{2,1,0:T(8,128)(2,1)S(1)} %pad_maximum_fusion.3.refs_0_), channel_id=1, source_target_pairs={{0,6},{1,7},{2,4},{3,5},{4,2},{5,3},{6,0},{7,1},{8,14},{9,15},{10,... | collective-permute-start | bytes 638984 | tf_op jit(solution)/shard_map/ppermute | solution.py:64
  24.5 4.3 %rel_bias.1.bias_ref = f32[16,112,128]{2,1,0:T(8,128)S(1)} custom-call(f32[16,384]{1,0:T(8,128)S(1)} %pad.13.t_ref), custom_call_target="tpu_custom_call" | custom-call | flops 10000000 | bytes 100000 | tf_op jit(solution)/shard_map/rel_bias/pallas_call | solution.py:841
  30.1 3.2 %collective-permute-done.4.refs_2_ = bf16[4,16,1664]{2,1,0:T(8,128)(2,1)S(1)} collective-permute-done((bf16[4,16,1664]{2,1,0:T(8,128)(2,1)S(1)}, bf16[4,16,1664]{2,1,0:T(8,128)(2,1)S(1)}, u32[]{:S(2)}, u32[]{:S(2)}) %collective-permute-start.4) | collective-permute-done | bytes 213024 | tf_op jit(solution)/shard_map/ppermute | solution.py:64
  33.5 1.7 collective-permute-start.14
  41.0 19.8 %attn_fwd.1 = (bf16[512,2048]{1,0:T(8,128)(2,1)}, bf16[1600,512]{1,0:T(8,128)(2,1)}, bf16[2048,512]{1,0:T(8,128)(2,1)}, bf16[512,2048]{1,0:T(8,128)(2,1)}, bf16[...) custom-call(s32[1]{0:T(128)} %bitcast.me_ref, ...), custom_call_target="tpu_custom_call" | custom-call | flops 10000000 | bytes 100000 | tf_op jit(solution)/shard_map/attn_fwd/pallas_call | solution.py:251
  60.9 1.3 collective-permute-done.13
  67.7 38.8 %mlp.1 = (bf16[1600,512]{1,0:T(8,128)(2,1)}, f32[1600,512]{1,0:T(8,128)}, bf16[512,512]{1,0:T(8,128)(2,1)}, bf16[16,128,512]{2,1,0:T(8,128)(2,1)}, bf16[16,128,5...) custom-call(s32[1]{0:T(128)} %bitcast.me_ref, ...), custom_call_target="tpu_custom_call" | custom-call | flops 10000000 | bytes 100000 | tf_op jit(solution)/shard_map/mlp/pallas_call | solution.py:505
  106.7 4.2 %collective-permute-done.19 = bf16[16,128,512]{2,1,0:T(8,128)(2,1)S(1)} collective-permute-done((bf16[16,128,512]{2,1,0:T(8,128)(2,1)}, bf16[16,128,512]{2,1,0:T(8,128)(2,1)S(1)}, u32[]{:S(2)}, u32[]{:S(2)}) %collective-permute-start.19) | collective-permute-done | bytes 2097184 | tf_op jit(solution)/shard_map/ppermute | solution.py:64
  110.9 3.0 %convert_add_fusion = (f32[4,128,512]{2,1,0:T(8,128)S(1)}, bf16[4,128,512]{2,1,0:T(8,128)(2,1)}, bf16[4,128,512]{2,1,0:T(8,128)(2,1)S(1)}, bf16[4,128,512]{2,1,0:T(8,128)(2,1)S(1)}) fusion(bf16[16,128,512]{2,1,0:T(8,128)(2,1)S(1)} %collective-permute-done.19, bf16[16,128,512]{2,1,0:T(8,128)(2,1)} %get-tuple-element.99), kind=kLoop, calls=%fused_computation | loop fusion | flops 3932160 | bytes 6815744 | tf_op jit(solution)/shard_map/add | solution.py:109
  113.9 1.4 collective-permute-start.22
  115.3 1.5 collective-permute-start.21
  117.4 28.9 %attn_bwd.1 = (bf16[2048,1536]{1,0:T(8,128)(2,1)}, f32[16,112,128]{2,1,0:T(8,128)}, f32[8,1536]{1,0:T(8,128)}, bf16[16,64,512]{2,1,0:T(8,128)(2,1)}, bf16[16,64,512]{2,1,0:T(8,128)(2,1)}) custom-call(s32[1]{0:T(128)} %bitcast.me_ref, f32[1600,512]{1,0:T(8,128)} %get-tuple-element.102.dmid_ref, bf16[512,512]{1,0:T(8,128)(2,1)} %get-tuple-element.103.p_ref, ...), custom_call_target="tpu_custom_call" | custom-call | flops 10000000 | bytes 100000 | tf_op jit(solution)/shard_map/attn_bwd/pallas_call | solution.py:640
  147.5 2.4 %rel_grad.1.refs_2_ = f32[24,512]{1,0:T(8,128)S(1)} custom-call(f32[16,112,128]{2,1,0:T(8,128)S(1)} %copy-done.2, f32[8,1536]{1,0:T(8,128)S(1)} %copy-done.3, f32[8,512]{1,0:T(8,128)S(1)} %copy-done.4, f32[8,512]{1,0:T(8,128)S(1)} %copy-done.5, f32[8,512]{1,0:T(8,128)S(1)} %copy-done.6), custom_call_target="tpu_custom_call" | custom-call | flops 10000000 | bytes 100000 | tf_op jit(solution)/shard_map/rel_grad/pallas_call | solution.py:882
  151.4 1.5 collective-permute-start.25
  153.5 1.5 collective-permute-start.27
  155.7 9.2 %grad_in.1 = f32[1600,512]{1,0:T(8,128)} custom-call(bf16[2048,1536]{1,0:T(8,128)(2,1)} %get-tuple-element.130.dm_ref, bf16[512,1536]{1,0:T(8,128)(2,1)} %get-tuple-element.110.w_ref, bf16[1600,512]{1,0:T(8,128)(2,1)} %x_ref.2, f32[1600,512]{1,0:T(8,128)} %get-tuple-element.102.dmid_ref, f32[16,512]{1,0:T(8,128)} %get-tuple-element.92.rowv_ref), custom_call_target="tpu_custom_call" | custom-call | flops 10000000 | bytes 100000 | tf_op jit(solution)/shard_map/grad_in/pallas_call | solution.py:677
  164.9 3.8 %collective-permute-done.26.refs_3_ = bf16[304,512]{1,0:T(8,128)(2,1)S(1)} collective-permute-done((bf16[304,512]{1,0:T(8,128)(2,1)S(1)}, bf16[304,512]{1,0:T(8,128)(2,1)S(1)}, u32[]{:S(2)}, u32[]{:S(2)}) %collective-permute-start.26) | collective-permute-done | bytes 311328 | tf_op jit(solution)/shard_map/ppermute | solution.py:64
  168.8 3.4 %collective-permute-start.32 = (bf16[1,128,512]{2,1,0:T(8,128)(2,1)S(1)}, bf16[1,128,512]{2,1,0:T(8,128)(2,1)S(1)}, u32[]{:S(2)}, u32[]{:S(2)}) collective-permute-start(bf16[1,128,512]{2,1,0:T(8,128)(2,1)S(1)} %get-tuple-element.188), channel_id=1, source_target_pairs={{0,16},{1,17},{2,18},{3,19},{4,20},{5,21},{6,22},{7,23},{8,24},{9,... | collective-permute-start | bytes 393224 | tf_op jit(solution)/shard_map/ppermute | solution.py:64
  172.8 4.0 %collective-permute-start.31 = (bf16[112,512]{1,0:T(8,128)(2,1)S(1)}, bf16[112,512]{1,0:T(8,128)(2,1)S(1)}, u32[]{:S(2)}, u32[]{:S(2)}) collective-permute-start(bf16[112,512]{1,0:T(8,128)(2,1)S(1)} %get-tuple-element.140), channel_id=1, source_target_pairs={{0,24},{1,25},{2,26},{3,27},{4,28},{5,29},{6,30},{7,31},{8,16},{9,... | collective-permute-start | bytes 344072 | tf_op jit(solution)/shard_map/ppermute | solution.py:64
  176.9 5.9 %collective-permute-done.32.refs_0_ = bf16[1,128,512]{2,1,0:T(8,128)(2,1)S(1)} collective-permute-done((bf16[1,128,512]{2,1,0:T(8,128)(2,1)S(1)}, bf16[1,128,512]{2,1,0:T(8,128)(2,1)S(1)}, u32[]{:S(2)}, u32[]{:S(2)}) %collective-permute-start.32) | collective-permute-done | bytes 131104 | tf_op jit(solution)/shard_map/ppermute | solution.py:64
  183.5 1.7 collective-permute-done.30.refs_1_
  (121 shorter events, 29.5 us)
Async XLA Ops:
  2.2 12.5 %collective-permute-start.2 = (bf16[1,16,1664]{2,1,0:T(8,128)(2,1)S(1)}, bf16[1,16,1664]{2,1,0:T(8,128)(2,1)S(1)}, u32[]{:S(2)}, u32[]{:S(2)}) collective-permute-start(bf16[1,16,1664]{2,1,0:T(8,128)(2,1)S(1)} %maximum_bitcast_fusion), channel_id=1, source_target_pairs={{0,24},{1,25},{2,26},{3,27},{4,28},{5,29},{6,30},{7,31},{8,16},{9,... | collective-permute-start | bytes 159752 | tf_op jit(solution)/shard_map/ppermute | solution.py:64
  7.3 7.4 %collective-permute-start.1 = (bf16[1,16,1664]{2,1,0:T(8,128)(2,1)S(1)}, bf16[1,16,1664]{2,1,0:T(8,128)(2,1)S(1)}, u32[]{:S(2)}, u32[]{:S(2)}) collective-permute-start(bf16[1,16,1664]{2,1,0:T(8,128)(2,1)S(1)} %maximum_bitcast_fusion), channel_id=1, source_target_pairs={{0,16},{1,17},{2,18},{3,19},{4,20},{5,21},{6,22},{7,23},{8,24},{9,... | collective-permute-start | bytes 159752 | tf_op jit(solution)/shard_map/ppermute | solution.py:64
  7.3 7.5 %collective-permute-start = (bf16[1,16,1664]{2,1,0:T(8,128)(2,1)S(1)}, bf16[1,16,1664]{2,1,0:T(8,128)(2,1)S(1)}, u32[]{:S(2)}, u32[]{:S(2)}) collective-permute-start(bf16[1,16,1664]{2,1,0:T(8,128)(2,1)S(1)} %maximum_bitcast_fusion), channel_id=1, source_target_pairs={{0,8},{1,9},{2,10},{3,11},{4,12},{5,13},{6,14},{7,15},{8,0},{9,1},... | collective-permute-start | bytes 159752 | tf_op jit(solution)/shard_map/ppermute | solution.py:64
  10.8 9.2 %collective-permute-start.6 = (bf16[1,144,512]{2,1,0:T(8,128)(2,1)S(1)}, bf16[1,144,512]{2,1,0:T(8,128)(2,1)S(1)}, u32[]{:S(2)}, u32[]{:S(2)}) collective-permute-start(bf16[1,144,512]{2,1,0:T(8,128)(2,1)S(1)} %bitcast.26), channel_id=1, source_target_pairs={{0,16},{1,17},{2,18},{3,19},{4,20},{5,21},{6,22},{7,23},{8,24},{9,... | collective-permute-start | bytes 442376 | tf_op jit(solution)/shard_map/ppermute | solution.py:64
  20.0 9.8 %collective-permute-start.7 = (bf16[2,144,512]{2,1,0:T(8,128)(2,1)S(1)}, bf16[2,144,512]{2,1,0:T(8,128)(2,1)S(1)}, u32[]{:S(2)}, u32[]{:S(2)}) collective-permute-start(bf16[2,144,512]{2,1,0:T(8,128)(2,1)S(1)} %pad_maximum_fusion.1), channel_id=1, source_target_pairs={{0,8},{1,9},{2,10},{3,11},{4,12},{5,13},{6,14},{7,15},{8,0},{9,1},... | collective-permute-start | bytes 884744 | tf_op jit(solution)/shard_map/ppermute | solution.py:64
  21.0 9.1 %collective-permute-start.5 = (bf16[4,16,1664]{2,1,0:T(8,128)(2,1)S(1)}, bf16[4,16,1664]{2,1,0:T(8,128)(2,1)S(1)}, u32[]{:S(2)}, u32[]{:S(2)}) collective-permute-start(bf16[4,16,1664]{2,1,0:T(8,128)(2,1)S(1)} %pad_maximum_fusion.3.refs_0_), channel_id=1, source_target_pairs={{0,6},{1,7},{2,4},{3,5},{4,2},{5,3},{6,0},{7,1},{8,14},{9,15},{10,... | collective-permute-start | bytes 638984 | tf_op jit(solution)/shard_map/ppermute | solution.py:64
  23.5 9.9 %collective-permute-start.4 = (bf16[4,16,1664]{2,1,0:T(8,128)(2,1)S(1)}, bf16[4,16,1664]{2,1,0:T(8,128)(2,1)S(1)}, u32[]{:S(2)}, u32[]{:S(2)}) collective-permute-start(bf16[4,16,1664]{2,1,0:T(8,128)(2,1)S(1)} %pad_maximum_fusion.3.refs_0_), channel_id=1, source_target_pairs={{0,4},{1,5},{2,6},{3,7},{4,0},{5,1},{6,2},{7,3},{8,12},{9,13},{10,... | collective-permute-start | bytes 638984 | tf_op jit(solution)/shard_map/ppermute | solution.py:64
  24.0 9.5 %collective-permute-start.3 = (bf16[4,16,1664]{2,1,0:T(8,128)(2,1)S(1)}, bf16[4,16,1664]{2,1,0:T(8,128)(2,1)S(1)}, u32[]{:S(2)}, u32[]{:S(2)}) collective-permute-start(bf16[4,16,1664]{2,1,0:T(8,128)(2,1)S(1)} %pad_maximum_fusion.3.refs_0_), channel_id=1, source_target_pairs={{0,2},{1,3},{2,0},{3,1},{4,6},{5,7},{6,4},{7,5},{8,10},{9,11},{10,... | collective-permute-start | bytes 638984 | tf_op jit(solution)/shard_map/ppermute | solution.py:64
  33.5 27.4 %collective-permute-start.14 = (bf16[4,144,512]{2,1,0:T(8,128)(2,1)S(1)}, bf16[4,144,512]{2,1,0:T(8,128)(2,1)S(1)}, u32[]{:S(2)}, u32[]{:S(2)}) collective-permute-start(bf16[4,144,512]{2,1,0:T(8,128)(2,1)S(1)} %pad_maximum_fusion), channel_id=1, source_target_pairs={{0,6},{1,7},{2,4},{3,5},{4,2},{5,3},{6,0},{7,1},{8,14},{9,15},{10,... | collective-permute-start | bytes 1769480 | tf_op jit(solution)/shard_map/ppermute | solution.py:64
  35.2 27.0 %collective-permute-start.13 = (bf16[4,144,512]{2,1,0:T(8,128)(2,1)S(1)}, bf16[4,144,512]{2,1,0:T(8,128)(2,1)S(1)}, u32[]{:S(2)}, u32[]{:S(2)}) collective-permute-start(bf16[4,144,512]{2,1,0:T(8,128)(2,1)S(1)} %pad_maximum_fusion), channel_id=1, source_target_pairs={{0,4},{1,5},{2,6},{3,7},{4,0},{5,1},{6,2},{7,3},{8,12},{9,13},{10,... | collective-permute-start | bytes 1769480 | tf_op jit(solution)/shard_map/ppermute | solution.py:64
  36.4 25.9 %collective-permute-start.12 = (bf16[4,144,512]{2,1,0:T(8,128)(2,1)S(1)}, bf16[4,144,512]{2,1,0:T(8,128)(2,1)S(1)}, u32[]{:S(2)}, u32[]{:S(2)}) collective-permute-start(bf16[4,144,512]{2,1,0:T(8,128)(2,1)S(1)} %pad_maximum_fusion), channel_id=1, source_target_pairs={{0,2},{1,3},{2,0},{3,1},{4,6},{5,7},{6,4},{7,5},{8,10},{9,11},{10,... | collective-permute-start | bytes 1769480 | tf_op jit(solution)/shard_map/ppermute | solution.py:64
  62.9 4.0 %collective-permute-start.18 = (bf16[4,144,512]{2,1,0:T(8,128)(2,1)S(1)}, bf16[4,144,512]{2,1,0:T(8,128)(2,1)S(1)}, u32[]{:S(2)}, u32[]{:S(2)}) collective-permute-start(bf16[4,144,512]{2,1,0:T(8,128)(2,1)S(1)} %collective-permute-done.14), channel_id=1, source_target_pairs={{0,1},{1,0},{2,3},{3,2},{4,5},{5,4},{6,7},{7,6},{8,9},{9,8},{10,11... | collective-permute-start | bytes 1769480 | tf_op jit(solution)/shard_map/ppermute | solution.py:64
  106.5 4.4 %collective-permute-start.19 = (bf16[16,128,512]{2,1,0:T(8,128)(2,1)}, bf16[16,128,512]{2,1,0:T(8,128)(2,1)S(1)}, u32[]{:S(2)}, u32[]{:S(2)}) collective-permute-start(bf16[16,128,512]{2,1,0:T(8,128)(2,1)} %get-tuple-element.100), channel_id=1, source_target_pairs={{0,1},{1,0},{2,3},{3,2},{4,5},{5,4},{6,7},{7,6},{8,9},{9,8},{10,11... | collective-permute-start | bytes 6291464 | tf_op jit(solution)/shard_map/ppermute | solution.py:64
  113.9 32.4 %collective-permute-start.22 = (bf16[4,128,512]{2,1,0:T(8,128)(2,1)}, bf16[4,128,512]{2,1,0:T(8,128)(2,1)S(1)}, u32[]{:S(2)}, u32[]{:S(2)}) collective-permute-start(bf16[4,128,512]{2,1,0:T(8,128)(2,1)} %get-tuple-element.183), channel_id=1, source_target_pairs={{0,6},{1,7},{2,4},{3,5},{4,2},{5,3},{6,0},{7,1},{8,14},{9,15},{10,... | collective-permute-start | bytes 1572872 | tf_op jit(solution)/shard_map/ppermute | solution.py:64
  115.3 31.0 %collective-permute-start.21 = (bf16[4,128,512]{2,1,0:T(8,128)(2,1)S(1)}, bf16[4,128,512]{2,1,0:T(8,128)(2,1)S(1)}, u32[]{:S(2)}, u32[]{:S(2)}) collective-permute-start(bf16[4,128,512]{2,1,0:T(8,128)(2,1)S(1)} %get-tuple-element.184), channel_id=1, source_target_pairs={{0,4},{1,5},{2,6},{3,7},{4,0},{5,1},{6,2},{7,3},{8,12},{9,13},{10,... | collective-permute-start | bytes 1572872 | tf_op jit(solution)/shard_map/ppermute | solution.py:64
  116.8 29.5 %collective-permute-start.20 = (bf16[4,128,512]{2,1,0:T(8,128)(2,1)S(1)}, bf16[4,128,512]{2,1,0:T(8,128)(2,1)S(1)}, u32[]{:S(2)}, u32[]{:S(2)}) collective-permute-start(bf16[4,128,512]{2,1,0:T(8,128)(2,1)S(1)} %get-tuple-element.185), channel_id=1, source_target_pairs={{0,2},{1,3},{2,0},{3,1},{4,6},{5,7},{6,4},{7,5},{8,10},{9,11},{10,... | collective-permute-start | bytes 1572872 | tf_op jit(solution)/shard_map/ppermute | solution.py:64
  151.4 13.5 %collective-permute-start.25 = (bf16[304,512]{1,0:T(8,128)(2,1)S(1)}, bf16[304,512]{1,0:T(8,128)(2,1)S(1)}, u32[]{:S(2)}, u32[]{:S(2)}) collective-permute-start(bf16[304,512]{1,0:T(8,128)(2,1)S(1)} %get-tuple-element.127), channel_id=1, source_target_pairs={{0,2},{1,3},{2,0},{3,1},{4,6},{5,7},{6,4},{7,5},{8,10},{9,11},{10,... | collective-permute-start | bytes 933896 | tf_op jit(solution)/shard_map/ppermute | solution.py:64
  152.9 15.8 %collective-permute-start.26 = (bf16[304,512]{1,0:T(8,128)(2,1)S(1)}, bf16[304,512]{1,0:T(8,128)(2,1)S(1)}, u32[]{:S(2)}, u32[]{:S(2)}) collective-permute-start(bf16[304,512]{1,0:T(8,128)(2,1)S(1)} %get-tuple-element.128), channel_id=1, source_target_pairs={{0,4},{1,5},{2,6},{3,7},{4,0},{5,1},{6,2},{7,3},{8,12},{9,13},{10,... | collective-permute-start | bytes 933896 | tf_op jit(solution)/shard_map/ppermute | solution.py:64
  153.5 15.3 %collective-permute-start.27 = (bf16[304,512]{1,0:T(8,128)(2,1)S(1)}, bf16[304,512]{1,0:T(8,128)(2,1)S(1)}, u32[]{:S(2)}, u32[]{:S(2)}) collective-permute-start(bf16[304,512]{1,0:T(8,128)(2,1)S(1)} %get-tuple-element.129), channel_id=1, source_target_pairs={{0,6},{1,7},{2,4},{3,5},{4,2},{5,3},{6,0},{7,1},{8,14},{9,15},{10,... | collective-permute-start | bytes 933896 | tf_op jit(solution)/shard_map/ppermute | solution.py:64
  155.0 9.9 %collective-permute-start.28 = (bf16[2,128,512]{2,1,0:T(8,128)(2,1)S(1)}, bf16[2,128,512]{2,1,0:T(8,128)(2,1)S(1)}, u32[]{:S(2)}, u32[]{:S(2)}) collective-permute-start(bf16[2,128,512]{2,1,0:T(8,128)(2,1)S(1)} %get-tuple-element.187), channel_id=1, source_target_pairs={{0,8},{1,9},{2,10},{3,11},{4,12},{5,13},{6,14},{7,15},{8,0},{9,1},... | collective-permute-start | bytes 786440 | tf_op jit(solution)/shard_map/ppermute | solution.py:64
  168.8 13.9 %collective-permute-start.32 = (bf16[1,128,512]{2,1,0:T(8,128)(2,1)S(1)}, bf16[1,128,512]{2,1,0:T(8,128)(2,1)S(1)}, u32[]{:S(2)}, u32[]{:S(2)}) collective-permute-start(bf16[1,128,512]{2,1,0:T(8,128)(2,1)S(1)} %get-tuple-element.188), channel_id=1, source_target_pairs={{0,16},{1,17},{2,18},{3,19},{4,20},{5,21},{6,22},{7,23},{8,24},{9,... | collective-permute-start | bytes 393224 | tf_op jit(solution)/shard_map/ppermute | solution.py:64
  172.4 11.1 %collective-permute-start.29 = (bf16[112,512]{1,0:T(8,128)(2,1)S(1)}, bf16[112,512]{1,0:T(8,128)(2,1)S(1)}, u32[]{:S(2)}, u32[]{:S(2)}) collective-permute-start(bf16[112,512]{1,0:T(8,128)(2,1)S(1)} %get-tuple-element.138), channel_id=1, source_target_pairs={{0,8},{1,9},{2,10},{3,11},{4,12},{5,13},{6,14},{7,15},{8,0},{9,1},... | collective-permute-start | bytes 344072 | tf_op jit(solution)/shard_map/ppermute | solution.py:64
  172.8 12.4 %collective-permute-start.30 = (bf16[112,512]{1,0:T(8,128)(2,1)S(1)}, bf16[112,512]{1,0:T(8,128)(2,1)S(1)}, u32[]{:S(2)}, u32[]{:S(2)}) collective-permute-start(bf16[112,512]{1,0:T(8,128)(2,1)S(1)} %get-tuple-element.139), channel_id=1, source_target_pairs={{0,16},{1,17},{2,18},{3,19},{4,20},{5,21},{6,22},{7,23},{8,24},{9,... | collective-permute-start | bytes 344072 | tf_op jit(solution)/shard_map/ppermute | solution.py:64
  172.8 12.4 %collective-permute-start.31 = (bf16[112,512]{1,0:T(8,128)(2,1)S(1)}, bf16[112,512]{1,0:T(8,128)(2,1)S(1)}, u32[]{:S(2)}, u32[]{:S(2)}) collective-permute-start(bf16[112,512]{1,0:T(8,128)(2,1)S(1)} %get-tuple-element.140), channel_id=1, source_target_pairs={{0,24},{1,25},{2,26},{3,27},{4,28},{5,29},{6,30},{7,31},{8,16},{9,... | collective-permute-start | bytes 344072 | tf_op jit(solution)/shard_map/ppermute | solution.py:64
  (31 other events, 166.3 us)

commit v5 on v4

--- a/solution.py
+++ b/solution.py
@@ -95,6 +95,11 @@
     return pieces + [([r ^ 1 for r in rels], swap(arr, 1, count)) for rels, arr in pieces]
 
 
+def hold(pieces, *others):
+    held = after([a for _, a in pieces[1:]], *others)
+    return pieces[:1] + [(r, a) for (r, _), a in zip(pieces[1:], held)]
+
+
 def natural_order(pieces, me, count):
     rels = [r for rs, _ in pieces for r in rs]
     where = [0] * count
@@ -102,12 +107,6 @@
         where[r] = k
     both = jnp.concatenate([a for _, a in pieces], axis=0)
     return jnp.take(both, jnp.asarray(where, jnp.int32)[jnp.arange(count) ^ me], axis=0)
-
-
-def split_sum(terms, group):
-    n = terms[0].shape[0] >> len(group)
-    parts = [sum(t[k * n : (k + 1) * n].astype(f32) for t in terms) for k in range(1 << len(group))]
-    return parts[0], [p.astype(bf16) for p in parts[1:]]
 
 
 def send_parts(parts, group, count):
@@ -688,16 +687,23 @@
 
 
 SMALL = 24
-
-
-def two_terms(x):
-    hi = x.astype(bf16).astype(f32)
-    return jnp.concatenate([hi, x - hi], axis=0).astype(bf16)
-
-
-def one_term(x):
-    x = x.astype(f32)
-    return x[0:SMALL] + x[SMALL : 2 * SMALL]
+SENT = 32
+
+
+def to_send(small):
+    lane = lax.broadcasted_iota(jnp.int32, small.shape, 1)
+    lane = jnp.where(lax.broadcasted_iota(jnp.int32, small.shape, 0) >= 8, lane, -1)
+    small = jnp.where(lane == RELN, small + pltpu.roll(small, D - 1, 1), small)
+    hi = small.astype(bf16).astype(f32)
+    small = jnp.where(lane == RELN + 1, pltpu.roll(small - hi, 1, 1), hi)
+    return jnp.concatenate([small, jnp.zeros((SENT - SMALL, D), f32)], axis=0).astype(bf16)
+
+
+def sent_sums(terms):
+    got = [t.astype(f32)[0:SMALL] for t in terms]
+    while len(got) > 1:
+        got = [got[k] + got[k + 1] for k in range(0, len(got), 2)]
+    return got[0]
 
 
 def fold_body(*refs, first, terms, parts):
@@ -707,10 +713,7 @@
     if first:
         small = ins[2][...] + ins[3][...]
     else:
-        got = [one_term(ins[1][...])] + [one_term(r[nb * rows :, :]) for r in ins[2:]]
-        while len(got) > 1:
-            got = [got[k] + got[k + 1] for k in range(0, len(got), 2)]
-        small = got[0]
+        small = sent_sums([ins[1][...]] + [r[nb * rows :, :] for r in ins[2:]])
     for p in range(parts + 1):
         at = slice(p * n, p * n + n)
         total = ins[0][at].astype(f32)
@@ -721,10 +724,10 @@
                 total = total + r[p * n * rows : (p + 1) * n * rows, :].astype(f32).reshape(n, rows, D)
         if p == 0:
             outs[0][...] = total
-            outs[1][...] = two_terms(small)
+            outs[1][...] = to_send(small)
         else:
             outs[p + 1][0 : n * rows, :] = total.reshape(n * rows, D).astype(bf16)
-            outs[p + 1][n * rows :, :] = two_terms(small)
+            outs[p + 1][n * rows :, :] = to_send(small)
 
 
 def fold(arrays, parts, first=False):
@@ -733,11 +736,51 @@
     n = nb // (parts + 1)
     return pl.pallas_call(
         functools.partial(fold_body, first=first, terms=terms, parts=parts),
-        out_shape=[sds((n, rows, D), f32), sds((2 * SMALL, D), bf16)] + [sds((n * rows + 2 * SMALL, D), bf16)] * parts,
+        out_shape=[sds((n, rows, D), f32), sds((SENT, D), bf16)] + [sds((n * rows + SENT, D), bf16)] * parts,
         compiler_params=params(16),
         cost_estimate=pl.CostEstimate(flops=10**6, bytes_accessed=10**5, transcendentals=0),
         name="fold",
     )(*arrays)
+
+
+def add_body(*refs, terms, later):
+    ins, outs = refs[:terms], refs[terms : -2] if later else refs[terms:]
+    n = outs[0].shape[0]
+    copies = []
+    if later:
+        buf, sem = refs[-2:]
+        for p in range(len(outs)):
+            at = pl.ds(p * n, n)
+            copies.append(pltpu.make_async_copy(ins[0].at[at], buf.at[at], sem.at[p]))
+        for c in copies:
+            c.start()
+        ins = (buf,) + ins[1:]
+    for p, out in enumerate(outs):
+        if later:
+            copies[p].wait()
+        at = slice(p * n, p * n + n)
+        total = ins[0][at].astype(f32)
+        for r in ins[1:]:
+            total = total + r[at].astype(f32)
+        out[...] = total.astype(out.dtype)
+
+
+def add_split(terms, group, later=False):
+    parts = len(masks_of(group))
+    first = terms[0]
+    n = first.shape[0] // (parts + 1)
+    shape = (n,) + first.shape[1:]
+    vmem = pl.BlockSpec(memory_space=pltpu.VMEM)
+    out = pl.pallas_call(
+        functools.partial(add_body, terms=len(terms), later=later),
+        in_specs=[pl.BlockSpec(memory_space=pl.ANY) if later else vmem] + [vmem] * (len(terms) - 1),
+        out_shape=[sds(shape, f32)] + [sds(shape, bf16)] * parts,
+        scratch_shapes=[pltpu.VMEM(first.shape, first.dtype), pltpu.SemaphoreType.DMA((parts + 1,))] if later else [],
+        compiler_params=params(16),
+        cost_estimate=pl.CostEstimate(flops=10**6, bytes_accessed=10**5, transcendentals=0),
+        name="add_split",
+    )(*terms)
+    return out[0], out[1:]
 
 
 def spread(o_ref, block, width, at):
@@ -755,10 +798,7 @@
     for q in range(3):
         spread(qkv_ref, total[rpd * q : rpd * q + rpd], 3 * D, D * q)
     spread(proj_ref, total[3 * rpd : rows], D, 0)
-    got = [one_term(kept_ref[...])] + [one_term(r[rows:, :]) for r in got_refs]
-    while len(got) > 1:
-        got = [got[k] + got[k + 1] for k in range(0, len(got), 2)]
-    small = got[0]
+    small = sent_sums([kept_ref[...]] + [r[rows:, :] for r in got_refs])
     for k in range(8):
         for a in range(4):
             lines[4 * k + a : 4 * k + a + 1, :] = small[k : k + 1, LANES * a : LANES * a + LANES]
@@ -776,7 +816,7 @@
             vec_ref[p // 2 : p // 2 + 1, :] = jnp.where(low, halves[0], halves[1])
     turned = small[8:24, 0:RP].T
     table_ref[...] = turned[0:RELN]
-    line = turned[RELN : RELN + 1]
+    line = turned[RELN : RELN + 1] + turned[RELN + 1 : RELN + 2]
     stats_ref[...] = jnp.sqrt(line / line[:, 5:6] + 1e-06)
 
 
@@ -842,7 +882,7 @@
         rel_bias_body,
         out_shape=sds((HEADS, KP, LANES), f32),
         compiler_params=params(16),
-        cost_estimate=pl.CostEstimate(flops=10**7, bytes_accessed=10**5, transcendentals=0),
+        cost_estimate=pl.CostEstimate(flops=2 * 10**10, bytes_accessed=10**6, transcendentals=0),
         name="rel_bias",
     )(table)
 
@@ -876,6 +916,7 @@
             o_ref[8 + 4 * k + a : 9 + 4 * k + a, RP:D] = up_ref[k : k + 1, LANES * a : LANES * a + LANES]
     for k in range(6):
         o_ref[8 + k : 9 + k, RELN : RELN + 1] = jnp.sum(squares_ref[k : k + 1, :], axis=1, keepdims=True)
+        o_ref[8 + k : 9 + k, RELN + 1 : RELN + 2] = jnp.zeros((1, 1), f32)
 
 
 def rel_grad(acc, one, two, up, squares):
@@ -922,9 +963,9 @@
     key_code = jnp.where(validity.reshape(-1, GW, CELLS) == 1, reg, -2.0)
     codes = jnp.pad(jnp.concatenate([reg, key_code], axis=1), ((0, 0), (0, 0), (0, LANES - CELLS)), constant_values=-3.0)
 
-    held, mlp_up = after(([a for _, a in attn_pieces], mlp_up), bias, codes)
-    mlp_up = after(mlp_up, held)
-    attn_pieces = gather_core([(r, a) for (r, _), a in zip(attn_pieces, held)], count)
+    attn_pieces = hold(attn_pieces, bias, codes)
+    mlp_up = after(mlp_up, bias, codes, [a for _, a in attn_pieces])
+    attn_pieces = gather_core(attn_pieces, count)
     mlp_pieces = gather_plane(mlp_rels, mlp_up, groups, count)
     if direct:
         attn_plan = [r for r, _ in attn_pieces]
@@ -937,8 +978,7 @@
     x = after(tokens, mlp_up)
     oT, o, q, kT, v, pT, xT, vld, w_full, rowv = attn_fwd(me_s, x, codes, bias, attn_plan, attn_w, rpd, per, count)
 
-    held = after([a for _, a in mlp_pieces], o)
-    mlp_pieces = gather_core([(r, a) for (r, _), a in zip(mlp_pieces, held)], count)
+    mlp_pieces = gather_core(hold(mlp_pieces, o), count)
     if direct:
         mlp_plan = [r for r, _ in mlp_pieces]
         mlp_w = [a.reshape(-1, 9, rpd, D) for _, a in mlp_pieces]
@@ -960,7 +1000,7 @@
         mlp_keep, mlp_send = pk[: count // 2], pk[count // 2 :]
 
     other = swap(mlp_send, 1, count)
-    mlp_own, parts = split_sum([mlp_keep, other], groups[1])
+    mlp_own, parts = add_split([mlp_keep, other], groups[1], later=True)
     mlp_got = send_parts(parts, groups[1], count)
     dmid = after(dmid, parts)
     got = attn_bwd(me_s, dmid, p_full, oT, q, kT, v, pT, xT, w_full, rowv, rpd, direct, count, groups)
@@ -976,7 +1016,7 @@
     other = swap(attn_send, 1, count)
     mlp_terms = [mlp_own] + mlp_got
     for g in single[2:3]:
-        mlp_own, parts = split_sum(mlp_terms, g)
+        mlp_own, parts = add_split(mlp_terms, g)
         mlp_terms = [mlp_own] + send_parts(parts, g, count)
         score_sums = after(score_sums, parts)
     small = rel_grad(score_sums, vec_one, vec_two, dbf1, squares)
@@ -987,12 +1027,13 @@
         own, kept, parts = out[0], out[1], out[2:]
         sent = send_parts(parts, g, count)
         if k == 0:
+            mlp_terms = after(mlp_terms, parts)
+            for up in single[3:]:
+                mlp_own, parts = add_split(mlp_terms, up)
+                mlp_terms = [mlp_own] + send_parts(parts, up, count)
             dm = after(dm, parts)
             grad_tokens = grad_in(dm, w_full, tokens, dmid, rowv)
             sent, mlp_terms = after((sent, mlp_terms), grad_tokens)
-            for up in single[3:]:
-                mlp_own, parts = split_sum(mlp_terms, up)
-                mlp_terms = [mlp_own] + send_parts(parts, up, count)
         if k + 1 < len(levels):
             out = fold([own, kept] + sent, levels[k + 1])
             mlp_terms = after(mlp_terms, out)

time: 188 us -> 177 us (0.941)
  waiting for transfers between devices: 33.1 us -> 19.3 us
  other arithmetic: 5.6 us -> 3.05 us
  starting transfers between devices: 33.4 us -> 35.8 us
  Pallas kernels: 105 us -> 107 us
    ppermute x33, waiting for transfers between devices: 33.1 us -> 19.3 us  [swap(): return lax.ppermute(x, AXES, [(i, i ^ mask) for i in range(count)])]
    add x2 -> x0, other arithmetic: 3.23 us -> none  [split_sum(): sum((t[k * n:(k + 1) * n].astype(f32) for t in terms))]
    ppermute x33, starting transfers between devices: 33.4 us -> 35.8 us  [swap(): return lax.ppermute(x, AXES, [(i, i ^ mask) for i in range(count)])]
    unnamed x45 -> x47, local copies, waits for them, and re-layouts: 3.93 us -> 4.79 us
  transfers between devices with their start and end apart: 33 -> 33, of which waited for: 19 -> 16; matrix products, arithmetic and copies ran while one was open for 3% -> 3% of each run, Pallas kernels for 35% -> 38%
where the time goes in v5:
time: 177 us; the launch traced here: 176 us
  Pallas kernels  107 us (60%)
  starting transfers between devices  35.8 us (20%)
  waiting for transfers between devices  19.3 us (11%)
  local copies, waits for them, and re-layouts  9.68 us (5%)
  other arithmetic  3.05 us (2%)
    pallas_call x1, Pallas kernels, mlp(): pl.pallas_call(functools.partial(mlp_body, plan=plan, rows=rows, owners=c...  38.6 us
    ppermute x33, starting transfers between devices, swap(): return lax.ppermute(x, AXES, [(i, i ^ mask) for i in range(count)])  35.8 us
    pallas_call x1, Pallas kernels, attn_bwd(): pl.pallas_call(functools.partial(attn_bwd_body, owners=count if owners el...  28.9 us
    pallas_call x1, Pallas kernels, attn_fwd(): pl.pallas_call(functools.partial(attn_fwd_body, plan=plan, rpd=rpd, per=p...  19.8 us
    ppermute x33, waiting for transfers between devices, swap(): return lax.ppermute(x, AXES, [(i, i ^ mask) for i in range(count)])  19.3 us
    pallas_call x1, Pallas kernels, grad_in(): pl.pallas_call(grad_in_body, grid=(n,), in_specs=[pl.BlockSpec((GL, 3 * D...  9.2 us
    unnamed x47, local copies, waits for them, and re-layouts  4.79 us
    pallas_call x1, Pallas kernels, rel_bias(): pl.pallas_call(rel_bias_body, out_shape=sds((HEADS, KP, LANES), f32), com...  4.31 us
  transfers between devices with their start and end apart: 33, of which 16 were waited for; matrix products, arithmetic and copies ran while one was open for 3% of the time, Pallas kernels for 38%

profile of v5, /device:TPU:0, one launch (start us, length us, event | category | flops | bytes accessed | tf_op | source)
XLA Modules:
  0.0 175.9 jit_solution(12544597114555144241)
XLA Ops:
  2.2 5.1 %collective-permute-start.3 = (bf16[1,16,1664]{2,1,0:T(8,128)(2,1)S(1)}, bf16[1,16,1664]{2,1,0:T(8,128)(2,1)S(1)}, u32[]{:S(2)}, u32[]{:S(2)}) collective-permute-start(bf16[1,16,1664]{2,1,0:T(8,128)(2,1)S(1)} %maximum_bitcast_fusion), channel_id=1, source_target_pairs={{0,24},{1,25},{2,26},{3,27},{4,28},{5,29},{6,30},{7,31},{8,16},{9,... | collective-permute-start | bytes 159752 | tf_op jit(solution)/shard_map/ppermute | solution.py:64
  10.8 2.4 %collective-permute-start = (bf16[1,144,512]{2,1,0:T(8,128)(2,1)S(1)}, bf16[1,144,512]{2,1,0:T(8,128)(2,1)S(1)}, u32[]{:S(2)}, u32[]{:S(2)}) collective-permute-start(bf16[1,144,512]{2,1,0:T(8,128)(2,1)S(1)} %bitcast.26), channel_id=1, source_target_pairs={{0,16},{1,17},{2,18},{3,19},{4,20},{5,21},{6,22},{7,23},{8,24},{9,... | collective-permute-start | bytes 442376 | tf_op jit(solution)/shard_map/ppermute | solution.py:64
  15.4 2.5 %collective-permute-start.7 = (bf16[4,16,1664]{2,1,0:T(8,128)(2,1)S(1)}, bf16[4,16,1664]{2,1,0:T(8,128)(2,1)S(1)}, u32[]{:S(2)}, u32[]{:S(2)}) collective-permute-start(bf16[4,16,1664]{2,1,0:T(8,128)(2,1)S(1)} %pad_maximum_fusion.3.refs_0_), channel_id=1, source_target_pairs={{0,6},{1,7},{2,4},{3,5},{4,2},{5,3},{6,0},{7,1},{8,14},{9,15},{10,... | collective-permute-start | bytes 638984 | tf_op jit(solution)/shard_map/ppermute | solution.py:64
  20.0 1.9 %collective-permute-start.4 = (bf16[2,144,512]{2,1,0:T(8,128)(2,1)S(1)}, bf16[2,144,512]{2,1,0:T(8,128)(2,1)S(1)}, u32[]{:S(2)}, u32[]{:S(2)}) collective-permute-start(bf16[2,144,512]{2,1,0:T(8,128)(2,1)S(1)} %pad_maximum_fusion.1), channel_id=1, source_target_pairs={{0,8},{1,9},{2,10},{3,11},{4,12},{5,13},{6,14},{7,15},{8,0},{9,1},... | collective-permute-start | bytes 884744 | tf_op jit(solution)/shard_map/ppermute | solution.py:64
  21.9 4.3 %rel_bias.1.bias_ref = f32[16,112,128]{2,1,0:T(8,128)S(1)} custom-call(f32[16,384]{1,0:T(8,128)S(1)} %pad.13.t_ref), custom_call_target="tpu_custom_call" | custom-call | flops 20000000000 | bytes 1000000 | tf_op jit(solution)/shard_map/rel_bias/pallas_call | solution.py:881
  28.1 2.5 %collective-permute-start.14 = (bf16[4,144,512]{2,1,0:T(8,128)(2,1)S(1)}, bf16[4,144,512]{2,1,0:T(8,128)(2,1)S(1)}, u32[]{:S(2)}, u32[]{:S(2)}) collective-permute-start(bf16[4,144,512]{2,1,0:T(8,128)(2,1)S(1)} %pad_maximum_fusion), channel_id=1, source_target_pairs={{0,6},{1,7},{2,4},{3,5},{4,2},{5,3},{6,0},{7,1},{8,14},{9,15},{10,... | collective-permute-start | bytes 1769480 | tf_op jit(solution)/shard_map/ppermute | solution.py:64
  35.7 19.8 %attn_fwd.1 = (bf16[512,2048]{1,0:T(8,128)(2,1)}, bf16[1600,512]{1,0:T(8,128)(2,1)}, bf16[2048,512]{1,0:T(8,128)(2,1)}, bf16[512,2048]{1,0:T(8,128)(2,1)}, bf16[...) custom-call(s32[1]{0:T(128)} %bitcast.me_ref, ...), custom_call_target="tpu_custom_call" | custom-call | flops 10000000 | bytes 100000 | tf_op jit(solution)/shard_map/attn_fwd/pallas_call | solution.py:250
  56.7 1.5 collective-permute-done.16
  60.7 38.6 %mlp.1 = (bf16[1600,512]{1,0:T(8,128)(2,1)}, f32[1600,512]{1,0:T(8,128)}, bf16[512,512]{1,0:T(8,128)(2,1)}, bf16[16,128,512]{2,1,0:T(8,128)(2,1)}, bf16[16,128,5...) custom-call(s32[1]{0:T(128)} %bitcast.me_ref, ...), custom_call_target="tpu_custom_call" | custom-call | flops 10000000 | bytes 100000 | tf_op jit(solution)/shard_map/mlp/pallas_call | solution.py:504
  99.5 4.2 %collective-permute-done.19.refs_1_ = bf16[16,128,512]{2,1,0:T(8,128)(2,1)S(1)} collective-permute-done((bf16[16,128,512]{2,1,0:T(8,128)(2,1)}, bf16[16,128,512]{2,1,0:T(8,128)(2,1)S(1)}, u32[]{:S(2)}, u32[]{:S(2)}) %collective-permute-start.19) | collective-permute-done | bytes 2097184 | tf_op jit(solution)/shard_map/ppermute | solution.py:64
  103.7 1.6 copy-done
  105.3 1.3 add_split.3
  106.7 1.5 collective-permute-start.20
  108.2 1.1 collective-permute-start.21
  110.2 28.9 %attn_bwd.1 = (bf16[2048,1536]{1,0:T(8,128)(2,1)}, f32[16,112,128]{2,1,0:T(8,128)}, f32[8,1536]{1,0:T(8,128)}, bf16[16,64,512]{2,1,0:T(8,128)(2,1)}, bf16[16,64,512]{2,1,0:T(8,128)(2,1)}) custom-call(s32[1]{0:T(128)} %bitcast.me_ref, f32[1600,512]{1,0:T(8,128)} %get-tuple-element.109.dmid_ref, bf16[512,512]{1,0:T(8,128)(2,1)} %get-tuple-element.110.p_ref, ...), custom_call_target="tpu_custom_call" | custom-call | flops 10000000 | bytes 100000 | tf_op jit(solution)/shard_map/attn_bwd/pallas_call | solution.py:639
  139.5 1.6 collective-permute-start.23
  141.2 2.4 %rel_grad.1.refs_2_ = f32[24,512]{1,0:T(8,128)S(1)} custom-call(f32[16,112,128]{2,1,0:T(8,128)S(1)} %copy-done.3, f32[8,1536]{1,0:T(8,128)S(1)} %copy-done.4, f32[8,512]{1,0:T(8,128)S(1)} %copy-done.5, f32[8,512]{1,0:T(8,128)S(1)} %copy-done.6, f32[8,512]{1,0:T(8,128)S(1)} %copy-done.7), custom_call_target="tpu_custom_call" | custom-call | flops 10000000 | bytes 100000 | tf_op jit(solution)/shard_map/rel_grad/pallas_call | solution.py:923
  143.8 1.0 collective-permute-done.25.refs_3_
  145.3 1.5 collective-permute-start.26
  147.6 1.3 collective-permute-start.28
  148.9 3.2 %collective-permute-start.29 = (bf16[1,128,512]{2,1,0:T(8,128)(2,1)S(1)}, bf16[1,128,512]{2,1,0:T(8,128)(2,1)S(1)}, u32[]{:S(2)}, u32[]{:S(2)}) collective-permute-start(bf16[1,128,512]{2,1,0:T(8,128)(2,1)S(1)} %get-tuple-element.142), channel_id=1, source_target_pairs={{0,16},{1,17},{2,18},{3,19},{4,20},{5,21},{6,22},{7,23},{8,24},{9,... | collective-permute-start | bytes 393224 | tf_op jit(solution)/shard_map/ppermute | solution.py:64
  152.1 9.2 %grad_in.1 = f32[1600,512]{1,0:T(8,128)} custom-call(bf16[2048,1536]{1,0:T(8,128)(2,1)} %get-tuple-element.143.dm_ref, bf16[512,1536]{1,0:T(8,128)(2,1)} %get-tuple-element.117.w_ref, bf16[1600,512]{1,0:T(8,128)(2,1)} %x_ref.2, f32[1600,512]{1,0:T(8,128)} %get-tuple-element.109.dmid_ref, f32[16,512]{1,0:T(8,128)} %get-tuple-element.97.rowv_ref), custom_call_target="tpu_custom_call" | custom-call | flops 10000000 | bytes 100000 | tf_op jit(solution)/shard_map/grad_in/pallas_call | solution.py:676
  162.9 3.2 %collective-permute-start.31 = (bf16[96,512]{1,0:T(8,128)(2,1)S(1)}, bf16[96,512]{1,0:T(8,128)(2,1)S(1)}, u32[]{:S(2)}, u32[]{:S(2)}) collective-permute-start(bf16[96,512]{1,0:T(8,128)(2,1)S(1)} %get-tuple-element.153), channel_id=1, source_target_pairs={{0,16},{1,17},{2,18},{3,19},{4,20},{5,21},{6,22},{7,23},{8,24},{9,... | collective-permute-start | bytes 294920 | tf_op jit(solution)/shard_map/ppermute | solution.py:64
  168.0 5.8 %collective-permute-done.31.refs_1_ = bf16[96,512]{1,0:T(8,128)(2,1)S(1)} collective-permute-done((bf16[96,512]{1,0:T(8,128)(2,1)S(1)}, bf16[96,512]{1,0:T(8,128)(2,1)S(1)}, u32[]{:S(2)}, u32[]{:S(2)}) %collective-permute-start.31) | collective-permute-done | bytes 98336 | tf_op jit(solution)/shard_map/ppermute | solution.py:64
  (123 shorter events, 28.5 us)
Async XLA Ops:
  2.2 13.2 %collective-permute-start.3 = (bf16[1,16,1664]{2,1,0:T(8,128)(2,1)S(1)}, bf16[1,16,1664]{2,1,0:T(8,128)(2,1)S(1)}, u32[]{:S(2)}, u32[]{:S(2)}) collective-permute-start(bf16[1,16,1664]{2,1,0:T(8,128)(2,1)S(1)} %maximum_bitcast_fusion), channel_id=1, source_target_pairs={{0,24},{1,25},{2,26},{3,27},{4,28},{5,29},{6,30},{7,31},{8,16},{9,... | collective-permute-start | bytes 159752 | tf_op jit(solution)/shard_map/ppermute | solution.py:64
  7.3 8.1 %collective-permute-start.2 = (bf16[1,16,1664]{2,1,0:T(8,128)(2,1)S(1)}, bf16[1,16,1664]{2,1,0:T(8,128)(2,1)S(1)}, u32[]{:S(2)}, u32[]{:S(2)}) collective-permute-start(bf16[1,16,1664]{2,1,0:T(8,128)(2,1)S(1)} %maximum_bitcast_fusion), channel_id=1, source_target_pairs={{0,16},{1,17},{2,18},{3,19},{4,20},{5,21},{6,22},{7,23},{8,24},{9,... | collective-permute-start | bytes 159752 | tf_op jit(solution)/shard_map/ppermute | solution.py:64
  7.3 8.1 %collective-permute-start.1 = (bf16[1,16,1664]{2,1,0:T(8,128)(2,1)S(1)}, bf16[1,16,1664]{2,1,0:T(8,128)(2,1)S(1)}, u32[]{:S(2)}, u32[]{:S(2)}) collective-permute-start(bf16[1,16,1664]{2,1,0:T(8,128)(2,1)S(1)} %maximum_bitcast_fusion), channel_id=1, source_target_pairs={{0,8},{1,9},{2,10},{3,11},{4,12},{5,13},{6,14},{7,15},{8,0},{9,1},... | collective-permute-start | bytes 159752 | tf_op jit(solution)/shard_map/ppermute | solution.py:64
  10.8 9.2 %collective-permute-start = (bf16[1,144,512]{2,1,0:T(8,128)(2,1)S(1)}, bf16[1,144,512]{2,1,0:T(8,128)(2,1)S(1)}, u32[]{:S(2)}, u32[]{:S(2)}) collective-permute-start(bf16[1,144,512]{2,1,0:T(8,128)(2,1)S(1)} %bitcast.26), channel_id=1, source_target_pairs={{0,16},{1,17},{2,18},{3,19},{4,20},{5,21},{6,22},{7,23},{8,24},{9,... | collective-permute-start | bytes 442376 | tf_op jit(solution)/shard_map/ppermute | solution.py:64
  15.4 11.7 %collective-permute-start.7 = (bf16[4,16,1664]{2,1,0:T(8,128)(2,1)S(1)}, bf16[4,16,1664]{2,1,0:T(8,128)(2,1)S(1)}, u32[]{:S(2)}, u32[]{:S(2)}) collective-permute-start(bf16[4,16,1664]{2,1,0:T(8,128)(2,1)S(1)} %pad_maximum_fusion.3.refs_0_), channel_id=1, source_target_pairs={{0,6},{1,7},{2,4},{3,5},{4,2},{5,3},{6,0},{7,1},{8,14},{9,15},{10,... | collective-permute-start | bytes 638984 | tf_op jit(solution)/shard_map/ppermute | solution.py:64
  17.9 9.2 %collective-permute-start.6 = (bf16[4,16,1664]{2,1,0:T(8,128)(2,1)S(1)}, bf16[4,16,1664]{2,1,0:T(8,128)(2,1)S(1)}, u32[]{:S(2)}, u32[]{:S(2)}) collective-permute-start(bf16[4,16,1664]{2,1,0:T(8,128)(2,1)S(1)} %pad_maximum_fusion.3.refs_0_), channel_id=1, source_target_pairs={{0,4},{1,5},{2,6},{3,7},{4,0},{5,1},{6,2},{7,3},{8,12},{9,13},{10,... | collective-permute-start | bytes 638984 | tf_op jit(solution)/shard_map/ppermute | solution.py:64
  18.4 8.8 %collective-permute-start.5 = (bf16[4,16,1664]{2,1,0:T(8,128)(2,1)S(1)}, bf16[4,16,1664]{2,1,0:T(8,128)(2,1)S(1)}, u32[]{:S(2)}, u32[]{:S(2)}) collective-permute-start(bf16[4,16,1664]{2,1,0:T(8,128)(2,1)S(1)} %pad_maximum_fusion.3.refs_0_), channel_id=1, source_target_pairs={{0,2},{1,3},{2,0},{3,1},{4,6},{5,7},{6,4},{7,5},{8,10},{9,11},{10,... | collective-permute-start | bytes 638984 | tf_op jit(solution)/shard_map/ppermute | solution.py:64
  20.0 8.1 %collective-permute-start.4 = (bf16[2,144,512]{2,1,0:T(8,128)(2,1)S(1)}, bf16[2,144,512]{2,1,0:T(8,128)(2,1)S(1)}, u32[]{:S(2)}, u32[]{:S(2)}) collective-permute-start(bf16[2,144,512]{2,1,0:T(8,128)(2,1)S(1)} %pad_maximum_fusion.1), channel_id=1, source_target_pairs={{0,8},{1,9},{2,10},{3,11},{4,12},{5,13},{6,14},{7,15},{8,0},{9,1},... | collective-permute-start | bytes 884744 | tf_op jit(solution)/shard_map/ppermute | solution.py:64
  28.1 27.4 %collective-permute-start.14 = (bf16[4,144,512]{2,1,0:T(8,128)(2,1)S(1)}, bf16[4,144,512]{2,1,0:T(8,128)(2,1)S(1)}, u32[]{:S(2)}, u32[]{:S(2)}) collective-permute-start(bf16[4,144,512]{2,1,0:T(8,128)(2,1)S(1)} %pad_maximum_fusion), channel_id=1, source_target_pairs={{0,6},{1,7},{2,4},{3,5},{4,2},{5,3},{6,0},{7,1},{8,14},{9,15},{10,... | collective-permute-start | bytes 1769480 | tf_op jit(solution)/shard_map/ppermute | solution.py:64
  30.7 24.9 %collective-permute-start.13 = (bf16[4,144,512]{2,1,0:T(8,128)(2,1)S(1)}, bf16[4,144,512]{2,1,0:T(8,128)(2,1)S(1)}, u32[]{:S(2)}, u32[]{:S(2)}) collective-permute-start(bf16[4,144,512]{2,1,0:T(8,128)(2,1)S(1)} %pad_maximum_fusion), channel_id=1, source_target_pairs={{0,4},{1,5},{2,6},{3,7},{4,0},{5,1},{6,2},{7,3},{8,12},{9,13},{10,... | collective-permute-start | bytes 1769480 | tf_op jit(solution)/shard_map/ppermute | solution.py:64
  31.2 25.0 %collective-permute-start.12 = (bf16[4,144,512]{2,1,0:T(8,128)(2,1)S(1)}, bf16[4,144,512]{2,1,0:T(8,128)(2,1)S(1)}, u32[]{:S(2)}, u32[]{:S(2)}) collective-permute-start(bf16[4,144,512]{2,1,0:T(8,128)(2,1)S(1)} %pad_maximum_fusion), channel_id=1, source_target_pairs={{0,2},{1,3},{2,0},{3,1},{4,6},{5,7},{6,4},{7,5},{8,10},{9,11},{10,... | collective-permute-start | bytes 1769480 | tf_op jit(solution)/shard_map/ppermute | solution.py:64
  34.6 22.0 %collective-permute-start.15 = (bf16[4,144,512]{2,1,0:T(8,128)(2,1)S(1)}, bf16[4,144,512]{2,1,0:T(8,128)(2,1)S(1)}, u32[]{:S(2)}, u32[]{:S(2)}) collective-permute-start(bf16[4,144,512]{2,1,0:T(8,128)(2,1)S(1)} %pad_maximum_fusion), channel_id=1, source_target_pairs={{0,1},{1,0},{2,3},{3,2},{4,5},{5,4},{6,7},{7,6},{8,9},{9,8},{10,11... | collective-permute-start | bytes 1769480 | tf_op jit(solution)/shard_map/ppermute | solution.py:64
  106.7 32.5 %collective-permute-start.20 = (bf16[4,128,512]{2,1,0:T(8,128)(2,1)}, bf16[4,128,512]{2,1,0:T(8,128)(2,1)S(1)}, u32[]{:S(2)}, u32[]{:S(2)}) collective-permute-start(bf16[4,128,512]{2,1,0:T(8,128)(2,1)} %get-tuple-element.105), channel_id=1, source_target_pairs={{0,2},{1,3},{2,0},{3,1},{4,6},{5,7},{6,4},{7,5},{8,10},{9,11},{10,... | collective-permute-start | bytes 1572872 | tf_op jit(solution)/shard_map/ppermute | solution.py:64
  108.2 31.0 %collective-permute-start.21 = (bf16[4,128,512]{2,1,0:T(8,128)(2,1)S(1)}, bf16[4,128,512]{2,1,0:T(8,128)(2,1)S(1)}, u32[]{:S(2)}, u32[]{:S(2)}) collective-permute-start(bf16[4,128,512]{2,1,0:T(8,128)(2,1)S(1)} %get-tuple-element.106), channel_id=1, source_target_pairs={{0,4},{1,5},{2,6},{3,7},{4,0},{5,1},{6,2},{7,3},{8,12},{9,13},{10,... | collective-permute-start | bytes 1572872 | tf_op jit(solution)/shard_map/ppermute | solution.py:64
  109.2 30.0 %collective-permute-start.22 = (bf16[4,128,512]{2,1,0:T(8,128)(2,1)S(1)}, bf16[4,128,512]{2,1,0:T(8,128)(2,1)S(1)}, u32[]{:S(2)}, u32[]{:S(2)}) collective-permute-start(bf16[4,128,512]{2,1,0:T(8,128)(2,1)S(1)} %get-tuple-element.107), channel_id=1, source_target_pairs={{0,6},{1,7},{2,4},{3,5},{4,2},{5,3},{6,0},{7,1},{8,14},{9,15},{10,... | collective-permute-start | bytes 1572872 | tf_op jit(solution)/shard_map/ppermute | solution.py:64
  139.2 4.6 %collective-permute-start.24 = (bf16[16,64,512]{2,1,0:T(8,128)(2,1)}, bf16[16,64,512]{2,1,0:T(8,128)(2,1)S(1)}, u32[]{:S(2)}, u32[]{:S(2)}) collective-permute-start(bf16[16,64,512]{2,1,0:T(8,128)(2,1)} %get-tuple-element.129), channel_id=1, source_target_pairs={{0,1},{1,0},{2,3},{3,2},{4,5},{5,4},{6,7},{7,6},{8,9},{9,8},{10,11... | collective-permute-start | bytes 3145736 | tf_op jit(solution)/shard_map/ppermute | solution.py:64
  139.5 9.4 %collective-permute-start.23 = (bf16[2,128,512]{2,1,0:T(8,128)(2,1)S(1)}, bf16[2,128,512]{2,1,0:T(8,128)(2,1)S(1)}, u32[]{:S(2)}, u32[]{:S(2)}) collective-permute-start(bf16[2,128,512]{2,1,0:T(8,128)(2,1)S(1)} %get-tuple-element.127), channel_id=1, source_target_pairs={{0,8},{1,9},{2,10},{3,11},{4,12},{5,13},{6,14},{7,15},{8,0},{9,1},... | collective-permute-start | bytes 786440 | tf_op jit(solution)/shard_map/ppermute | solution.py:64
  145.3 16.0 %collective-permute-start.26 = (bf16[288,512]{1,0:T(8,128)(2,1)S(1)}, bf16[288,512]{1,0:T(8,128)(2,1)S(1)}, u32[]{:S(2)}, u32[]{:S(2)}) collective-permute-start(bf16[288,512]{1,0:T(8,128)(2,1)S(1)} %get-tuple-element.137), channel_id=1, source_target_pairs={{0,2},{1,3},{2,0},{3,1},{4,6},{5,7},{6,4},{7,5},{8,10},{9,11},{10,... | collective-permute-start | bytes 884744 | tf_op jit(solution)/shard_map/ppermute | solution.py:64
  146.8 15.2 %collective-permute-start.27 = (bf16[288,512]{1,0:T(8,128)(2,1)S(1)}, bf16[288,512]{1,0:T(8,128)(2,1)S(1)}, u32[]{:S(2)}, u32[]{:S(2)}) collective-permute-start(bf16[288,512]{1,0:T(8,128)(2,1)S(1)} %get-tuple-element.138), channel_id=1, source_target_pairs={{0,4},{1,5},{2,6},{3,7},{4,0},{5,1},{6,2},{7,3},{8,12},{9,13},{10,... | collective-permute-start | bytes 884744 | tf_op jit(solution)/shard_map/ppermute | solution.py:64
  147.6 14.4 %collective-permute-start.28 = (bf16[288,512]{1,0:T(8,128)(2,1)S(1)}, bf16[288,512]{1,0:T(8,128)(2,1)S(1)}, u32[]{:S(2)}, u32[]{:S(2)}) collective-permute-start(bf16[288,512]{1,0:T(8,128)(2,1)S(1)} %get-tuple-element.139), channel_id=1, source_target_pairs={{0,6},{1,7},{2,4},{3,5},{4,2},{5,3},{6,0},{7,1},{8,14},{9,15},{10,... | collective-permute-start | bytes 884744 | tf_op jit(solution)/shard_map/ppermute | solution.py:64
  148.9 12.4 %collective-permute-start.29 = (bf16[1,128,512]{2,1,0:T(8,128)(2,1)S(1)}, bf16[1,128,512]{2,1,0:T(8,128)(2,1)S(1)}, u32[]{:S(2)}, u32[]{:S(2)}) collective-permute-start(bf16[1,128,512]{2,1,0:T(8,128)(2,1)S(1)} %get-tuple-element.142), channel_id=1, source_target_pairs={{0,16},{1,17},{2,18},{3,19},{4,20},{5,21},{6,22},{7,23},{8,24},{9,... | collective-permute-start | bytes 393224 | tf_op jit(solution)/shard_map/ppermute | solution.py:64
  162.2 5.8 %collective-permute-start.30 = (bf16[96,512]{1,0:T(8,128)(2,1)S(1)}, bf16[96,512]{1,0:T(8,128)(2,1)S(1)}, u32[]{:S(2)}, u32[]{:S(2)}) collective-permute-start(bf16[96,512]{1,0:T(8,128)(2,1)S(1)} %get-tuple-element.152), channel_id=1, source_target_pairs={{0,8},{1,9},{2,10},{3,11},{4,12},{5,13},{6,14},{7,15},{8,0},{9,1},... | collective-permute-start | bytes 294920 | tf_op jit(solution)/shard_map/ppermute | solution.py:64
  162.9 10.9 %collective-permute-start.31 = (bf16[96,512]{1,0:T(8,128)(2,1)S(1)}, bf16[96,512]{1,0:T(8,128)(2,1)S(1)}, u32[]{:S(2)}, u32[]{:S(2)}) collective-permute-start(bf16[96,512]{1,0:T(8,128)(2,1)S(1)} %get-tuple-element.153), channel_id=1, source_target_pairs={{0,16},{1,17},{2,18},{3,19},{4,20},{5,21},{6,22},{7,23},{8,24},{9,... | collective-permute-start | bytes 294920 | tf_op jit(solution)/shard_map/ppermute | solution.py:64
  166.1 7.7 %collective-permute-start.32 = (bf16[96,512]{1,0:T(8,128)(2,1)S(1)}, bf16[96,512]{1,0:T(8,128)(2,1)S(1)}, u32[]{:S(2)}, u32[]{:S(2)}) collective-permute-start(bf16[96,512]{1,0:T(8,128)(2,1)S(1)} %get-tuple-element.154), channel_id=1, source_target_pairs={{0,24},{1,25},{2,26},{3,27},{4,28},{5,29},{6,30},{7,31},{8,16},{9,... | collective-permute-start | bytes 294920 | tf_op jit(solution)/shard_map/ppermute | solution.py:64
  (32 other events, 128.5 us)

commit v6 on v5

--- a/solution.py
+++ b/solution.py
@@ -36,6 +36,10 @@
 
 def nt(a, b):
     return lax.dot_general(a, b, (((1,), (1,)), ((), ())), preferred_element_type=f32)
+
+
+def tn(a, b):
+    return lax.dot_general(a, b, (((0,), (0,)), ((), ())), preferred_element_type=f32)
 
 
 def whole(shape):
@@ -297,8 +301,8 @@
 def mlp_body(me_ref, vld_ref, rowv_ref, x_any, o_any, g_any, *refs, plan, rows, owners, rpd, groups):
     pieces = refs[: len(plan)]
     refs = refs[len(plan) :]
-    res_any, dmid_any, p_any, first_any, second_any, vec_ref, dbf1_ref, st_ref = refs[:8]
-    xb, ob, gp, gT, h2, h2T, mid, dh2, es, dus, u4, vv, pp, res, pk, sem, sem_x, sem_o, sem_p, sem_g, sem_du, sem_dv, sem_r, sem_m = refs[8:]
+    res_any, dmid_any, p_any, first_any, second_any, third_ref, vec_ref, dbf1_ref, st_ref = refs[:9]
+    xb, ob, gp, gT, h2, h2T, mid, dh2, es, dus, u4, vv, pp, res, pk, sem, sem_x, sem_o, sem_p, sem_g, sem_du, sem_dv, sem_dp, sem_r, sem_m = refs[9:]
     j = pl.program_id(0)
     last = FF // 512 - 1
     padded = h2.shape[0]
@@ -446,6 +450,7 @@
         sums = [zero] * 4
         stats = [zero] * 5
         outs = []
+        proj = jnp.zeros((D, D), f32)
         for k in range(blocks):
             at = slice(k * GR, k * GR + GR)
             m = mid[at, :]
@@ -462,7 +467,9 @@
             dh2[at, :] = dm
             outs.append(pltpu.make_async_copy(dh2.at[rows_of(k)], dmid_any.at[rows_of(k)], sem_m.at[k]))
             outs[-1].start()
-            terms = (dm.astype(bf16).astype(f32), dxx, d, grad)
+            da = dm.astype(bf16)
+            proj = proj + tn(ob[at, :], da)
+            terms = (da.astype(f32), dxx, d, grad)
             sums = [a + jnp.sum(t, axis=0, keepdims=True) for a, t in zip(sums, terms)]
             f = rowv_ref[7:8, :]
             for b in range(4):
@@ -482,8 +489,18 @@
         for q, t in zip((0, 2, 3, 4, 5), stats):
             st_ref[q : q + 1, :] = t
         if owners:
+            proj = proj.astype(bf16)
+            at = pl.ds(8 * rpd, rpd)
+            for k in range(owners):
+                pk[(k ^ me) & 1, place_of(k ^ me, groups[1:]), at, :] = proj[rpd * k : rpd * k + rpd]
+            third_ref[...] = jnp.zeros_like(third_ref)
+            for c, to in enumerate((first_any, second_any)):
+                outs.append(pltpu.make_async_copy(pk.at[c, :, at, :], to.at[:, at, :], sem_dp.at[c]))
+                outs[-1].start()
             for step in range(last + 1):
                 outs += grads_out(step)
+        else:
+            third_ref[...] = proj
         for c in outs:
             c.wait()
 
@@ -495,17 +512,17 @@
     padded = -(-rows // LANES) * LANES
     copies = sum(1 if r is None else 3 * len(r) for r in plan)
     if owners:
-        grad_shapes = [sds((count // 2, 8 * rpd, 512), bf16)] * 2
-        pk = (2, count // 2, 8 * rpd, 512)
+        grad_shapes = [sds((count // 2, 9 * rpd, 512), bf16)] * 2 + [sds((8, LANES), f32)]
+        pk = (2, count // 2, 9 * rpd, 512)
     else:
-        grad_shapes = [sds((D, FF), bf16), sds((FF, D), bf16)]
+        grad_shapes = [sds((D, FF), bf16), sds((FF, D), bf16), sds((D, D), f32)]
         pk = (2, 512, 512)
     dma = pltpu.SemaphoreType.DMA
     return pl.pallas_call(
         functools.partial(mlp_body, plan=plan, rows=rows, owners=count if owners else 0, rpd=rpd, groups=groups),
         grid=(steps,),
         in_specs=[SMEM, whole((rows, LANES)), whole((16, D))] + any_specs(3 + len(pieces)),
-        out_specs=any_specs(5) + [whole((8, D))] * 3,
+        out_specs=any_specs(5) + [whole(grad_shapes[2].shape)] + [whole((8, D))] * 3,
         out_shape=[sds((rows, D), bf16), sds((rows, D), f32), sds((D, D), bf16)] + grad_shapes + [sds((8, D), f32)] * 3,
         scratch_shapes=[
             pltpu.VMEM((rows, D), bf16),
@@ -530,26 +547,28 @@
             dma((1,)),
             dma((steps, 2)),
             dma((steps, max(1, 512 // (4 * rpd)))),
+            dma((2,)),
             dma((blocks,)),
             dma((blocks,)),
         ],
-        compiler_params=params(62),
+        compiler_params=params(52),
         cost_estimate=pl.CostEstimate(flops=10**7, bytes_accessed=10**5, transcendentals=0),
         name="mlp",
     )(me, vld, rowv, x, o, g, *pieces)
 
 
-def attn_bwd_body(me_ref, dmid_ref, p_ref, oT_ref, q_ref, kT_ref, v_ref, pT_ref, xT_ref, w_ref, rowv_ref, *refs, owners, rpd, groups):
+def attn_bwd_body(me_ref, dmid_ref, p_ref, oT_ref, q_ref, kT_ref, v_ref, pT_ref, xT_ref, w_any, rowv_ref, *refs, owners, rpd, groups):
     dm_ref, acc_ref, vec_ref = refs[:3]
-    grads = refs[3:-6]
-    xs, dap, don, doT, dw, dproj = refs[-6:]
+    grads = refs[3:-7]
+    xs, dap, don, doT, dw, w_ref, sem_w = refs[-7:]
     i = pl.program_id(0)
+    load_w = pltpu.make_async_copy(w_any, w_ref, sem_w.at[0])
 
     @pl.when(i == 0)
     def _():
+        load_w.start()
         acc_ref[...] = jnp.zeros_like(acc_ref)
         dw[...] = jnp.zeros_like(dw)
-        dproj[...] = jnp.zeros_like(dproj)
 
     xs[0:GR, :] = dmid_ref[...]
     for w in range(GW):
@@ -557,7 +576,6 @@
         dm_ref[LANES * w + KP : LANES * w + LANES, :] = jnp.zeros((LANES - KP, 3 * D), bf16)
     da = dap[...]
     don[...] = nt(da, p_ref[...]).astype(bf16)
-    dproj[...] += nn(oT_ref[...], da)
     for w in range(GW):
         for a in range(D // LANES):
             rows, cols = slice(LANES * w, LANES * w + LANES), slice(LANES * a, LANES * a + LANES)
@@ -593,6 +611,7 @@
 
     @pl.when(i == pl.num_programs(0) - 1)
     def _():
+        load_w.wait()
         s = dw[D : D + 1, :]
         vec_ref[...] = jnp.zeros_like(vec_ref)
         vec_ref[0:1, :] = s
@@ -616,13 +635,11 @@
                 def store(to, mine=mine, pos=pos):
                     for q in range(3):
                         to[pos, rpd * q : rpd * q + rpd, :] = dw[mine, D * q : D * q + D].astype(bf16)
-                    to[pos, 3 * rpd : 4 * rpd, :] = dproj[mine, :].astype(bf16)
 
                 pl.when(rel & 1 == 0)(functools.partial(store, grads[0]))
                 pl.when(rel & 1 == 1)(functools.partial(store, grads[1]))
         else:
             grads[0][...] = dw[0:D, :].astype(bf16)
-            grads[1][...] = dproj[...].astype(bf16)
 
 
 def attn_bwd(me, dmid, p, oT, q, kT, v, pT, xT, w, rowv, rpd, owners, count, groups):
@@ -633,13 +650,13 @@
 
     pb = pl.BlockSpec((GL, D), lambda i: (i, 0))
     if owners:
-        grad_shapes = [sds((count // 2, 4 * rpd, D), bf16)] * 2
+        grad_shapes = [sds((count // 2, 3 * rpd, D), bf16)] * 2
     else:
-        grad_shapes = [sds((D, 3 * D), bf16), sds((D, D), bf16)]
+        grad_shapes = [sds((D, 3 * D), bf16)]
     return pl.pallas_call(
         functools.partial(attn_bwd_body, owners=count if owners else 0, rpd=rpd, groups=groups),
         grid=(n,),
-        in_specs=[SMEM, pl.BlockSpec((GR, D), lambda i: (i, 0)), whole((D, D)), tb(D), pb, tb(D), pb, pl.BlockSpec((GW, HEADS, KP, LANES), lambda i: (i, 0, 0, 0)), tb(D + 16), whole((D, 3 * D)), whole((16, D))],
+        in_specs=[SMEM, pl.BlockSpec((GR, D), lambda i: (i, 0)), whole((D, D)), tb(D), pb, tb(D), pb, pl.BlockSpec((GW, HEADS, KP, LANES), lambda i: (i, 0, 0, 0)), tb(D + 16), pl.BlockSpec(memory_space=pl.ANY), whole((16, D))],
         out_specs=[pl.BlockSpec((GL, 3 * D), lambda i: (i, 0)), whole((HEADS, KP, LANES)), whole((8, 3 * D))] + [whole(s.shape) for s in grad_shapes],
         out_shape=[sds((n * GL, 3 * D), bf16), sds((HEADS, KP, LANES), f32), sds((8, 3 * D), f32)] + grad_shapes,
         scratch_shapes=[
@@ -648,7 +665,8 @@
             pltpu.VMEM((GL, D), bf16),
             pltpu.VMEM((D, GL), bf16),
             pltpu.VMEM((D + 16, 3 * D), f32),
-            pltpu.VMEM((D, D), f32),
+            pltpu.VMEM((D, 3 * D), bf16),
+            pltpu.SemaphoreType.DMA((1,)),
         ],
         compiler_params=params(60),
         cost_estimate=pl.CostEstimate(flops=10**7, bytes_accessed=10**5, transcendentals=0),
@@ -773,7 +791,7 @@
     vmem = pl.BlockSpec(memory_space=pltpu.VMEM)
     out = pl.pallas_call(
         functools.partial(add_body, terms=len(terms), later=later),
-        in_specs=[pl.BlockSpec(memory_space=pl.ANY) if later else vmem] + [vmem] * (len(terms) - 1),
+        in_specs=[pl.BlockSpec(memory_space=pltpu.HBM) if later else vmem] + [vmem] * (len(terms) - 1),
         out_shape=[sds(shape, f32)] + [sds(shape, bf16)] * parts,
         scratch_shapes=[pltpu.VMEM(first.shape, first.dtype), pltpu.SemaphoreType.DMA((parts + 1,))] if later else [],
         compiler_params=params(16),
@@ -790,14 +808,13 @@
 
 
 def attn_last_body(me_ref, own_ref, kept_ref, *refs, rpd, per):
-    got_refs, (qkv_ref, proj_ref, vec_ref, table_ref, stats_ref, lines) = refs[:-6], refs[-6:]
-    rows = 4 * rpd
+    got_refs, (qkv_ref, vec_ref, table_ref, stats_ref, lines) = refs[:-5], refs[-5:]
+    rows = own_ref.shape[1]
     total = own_ref[0]
     for r in got_refs:
         total = total + r[0:rows, :].astype(f32)
     for q in range(3):
         spread(qkv_ref, total[rpd * q : rpd * q + rpd], 3 * D, D * q)
-    spread(proj_ref, total[3 * rpd : rows], D, 0)
     small = sent_sums([kept_ref[...]] + [r[rows:, :] for r in got_refs])
     for k in range(8):
         for a in range(4):
@@ -814,9 +831,10 @@
                 line = lines[pl.ds(c >> 1, 1), :]
                 halves.append(jnp.where(c & 1 == k, line, pltpu.roll(line, 64, 1)))
             vec_ref[p // 2 : p // 2 + 1, :] = jnp.where(low, halves[0], halves[1])
-    turned = small[8:24, 0:RP].T
-    table_ref[...] = turned[0:RELN]
-    line = turned[RELN : RELN + 1] + turned[RELN + 1 : RELN + 2]
+    table_ref[...] = small[8:24, 0:RELN]
+    turned = small[8:24, RP - LANES : RP].T
+    at = RELN - (RP - LANES)
+    line = turned[at : at + 1] + turned[at + 1 : at + 2]
     stats_ref[...] = jnp.sqrt(line / line[:, 5:6] + 1e-06)
 
 
@@ -825,7 +843,7 @@
     return pl.pallas_call(
         functools.partial(attn_last_body, rpd=rpd, per=per),
         in_specs=[SMEM] + [pl.BlockSpec(memory_space=pltpu.VMEM)] * len(arrays),
-        out_shape=[sds((12 * rpd, LANES), f32), sds((4 * rpd, LANES), f32), sds((lines, LANES), f32), sds((RELN, HEADS), f32), sds((1, HEADS), f32)],
+        out_shape=[sds((12 * rpd, LANES), f32), sds((lines, LANES), f32), sds((HEADS, RELN), f32), sds((1, HEADS), f32)],
         scratch_shapes=[pltpu.VMEM((48, LANES), f32)],
         compiler_params=params(16),
         cost_estimate=pl.CostEstimate(flops=10**6, bytes_accessed=10**5, transcendentals=0),
@@ -835,17 +853,18 @@
 
 def mlp_last_body(own_ref, *refs, rpd):
     total = own_ref[0]
-    for r in refs[:-2]:
+    for r in refs[:-3]:
         total = total + r[0].astype(f32)
     for q in range(4):
-        spread(refs[-2], total[rpd * q : rpd * q + rpd], FF, 512 * q)
-    spread(refs[-1], total[4 * rpd :], D, 0)
+        spread(refs[-3], total[rpd * q : rpd * q + rpd], FF, 512 * q)
+    spread(refs[-2], total[4 * rpd : 8 * rpd], D, 0)
+    spread(refs[-1], total[8 * rpd :], D, 0)
 
 
 def mlp_last(arrays, rpd):
     return pl.pallas_call(
         functools.partial(mlp_last_body, rpd=rpd),
-        out_shape=[sds((16 * rpd, LANES), f32)] * 2,
+        out_shape=[sds((16 * rpd, LANES), f32)] * 2 + [sds((4 * rpd, LANES), f32)],
         compiler_params=params(16),
         cost_estimate=pl.CostEstimate(flops=10**6, bytes_accessed=10**5, transcendentals=0),
         name="mlp_last",
@@ -945,15 +964,10 @@
     else:
         own = jnp.concatenate([qkv_weight, vectors]).reshape(1, -1)
     rels, attn_up = gather_upper(own, groups, count)
+    up_rows = fc1_weight.reshape(rpd, FF)
     packed = jnp.concatenate(
-        [
-            proj_weight.reshape(1, rpd, D),
-            fc1_weight.reshape(rpd, 4, 512).transpose(1, 0, 2),
-            fc2_weight.reshape(4, rpd, D),
-        ],
-        axis=0,
+        [proj_weight.reshape(rpd, D)] + [up_rows[:, 512 * q : 512 * q + 512] for q in range(4)] + [fc2_weight.reshape(4 * rpd, D)], axis=0
     )
-    packed = packed.reshape(9 * rpd, D)
     attn_pieces = gather_plane(rels, attn_up, groups, count)
     table_in = after(rel_table, attn_up)
     mlp_rels, mlp_up = gather_upper(packed, single, count, attn_up)
@@ -986,7 +1000,7 @@
         both = natural_order(mlp_pieces, me, count).reshape(count, 9, rpd, D)
         mlp_plan = [None] * 3
         mlp_w = [both[:, 0].reshape(D, D), both[:, 1:5].transpose(1, 0, 2, 3).reshape(4, D, 512), both[:, 5:].reshape(128, 16, D)]
-    result, dmid, p_full, mlp_keep, mlp_send, vec_two, dbf1, squares = mlp(
+    result, dmid, p_full, mlp_keep, mlp_send, dproj, vec_two, dbf1, squares = mlp(
         me_s, tokens, o, cotangent, vld, rowv, mlp_plan, mlp_w, rpd, direct, count, single
     )
     order = None
@@ -996,7 +1010,8 @@
             jnp.zeros((count,), jnp.int32).at[place_of(blocks, way)].set(blocks.astype(jnp.int32)) ^ me for way in (groups, single)
         )
         dU = mlp_keep.reshape(count, rpd, 4, 512).transpose(0, 2, 1, 3).reshape(count, 4 * rpd, 512)
-        pk = jnp.take(jnp.concatenate([dU, mlp_send.reshape(count, 4 * rpd, D)], axis=1), mlp_order, axis=0)
+        pk = [dU, mlp_send.reshape(count, 4 * rpd, D), dproj.astype(bf16).reshape(count, rpd, D)]
+        pk = jnp.take(jnp.concatenate(pk, axis=1), mlp_order, axis=0)
         mlp_keep, mlp_send = pk[: count // 2], pk[count // 2 :]
 
     other = swap(mlp_send, 1, count)
@@ -1009,7 +1024,7 @@
         attn_keep, attn_send = got[3:]
     else:
         dW = got[3].reshape(count, rpd, 3, D).transpose(0, 2, 1, 3).reshape(count, 3 * rpd, D)
-        pk = jnp.take(jnp.concatenate([dW, got[4].reshape(count, rpd, D)], axis=1), order, axis=0)
+        pk = jnp.take(jnp.pad(dW, ((0, 0), (0, rpd), (0, 0))), order, axis=0)
         attn_keep, attn_send = pk[: count // 2], pk[count // 2 :]
     mlp_got, attn_send, score_sums, dm = lax.optimization_barrier((mlp_got, attn_send, score_sums, dm))
 
@@ -1037,9 +1052,9 @@
         if k + 1 < len(levels):
             out = fold([own, kept] + sent, levels[k + 1])
             mlp_terms = after(mlp_terms, out)
-    grad_fc1, grad_fc2 = mlp_last(mlp_terms, rpd)
+    grad_fc1, grad_fc2, grad_proj = mlp_last(mlp_terms, rpd)
     sent = after(sent, grad_fc1)
-    grad_qkv, grad_proj, grad_vectors, grad_table, stats = attn_last(me_s, [own, kept] + sent, rpd, per)
+    grad_qkv, grad_vectors, grad_table, stats = attn_last(me_s, [own, kept] + sent, rpd, per)
     if per % 64 == 0:
         grad_vectors = grad_vectors.reshape(-1)[:per]
     else:
@@ -1052,7 +1067,7 @@
         grad_fc1.reshape(-1),
         grad_fc2.reshape(-1),
         grad_vectors,
-        grad_table,
+        grad_table.T,
         stats[0, 0:5],
     )
 

time: 177 us -> 173 us (0.977)
  Pallas kernels: 107 us -> 105 us
    unnamed x47 -> x43, local copies, waits for them, and re-layouts: 4.79 us -> 4 us
  transfers between devices with their start and end apart: 33 -> 33, of which waited for: 16 -> 16; matrix products, arithmetic and copies ran while one was open for 3% -> 3% of each run, Pallas kernels for 38% -> 37%
where the time goes in v6:
time: 173 us; the launch traced here: 172 us
  Pallas kernels  105 us (61%)
  starting transfers between devices  35.6 us (21%)
  waiting for transfers between devices  18.8 us (11%)
  local copies, waits for them, and re-layouts  8.76 us (5%)
  other arithmetic  2.89 us (2%)
    pallas_call x1, Pallas kernels, mlp(): pl.pallas_call(functools.partial(mlp_body, plan=plan, rows=rows, owners=c...  37.9 us
    ppermute x33, starting transfers between devices, swap(): return lax.ppermute(x, AXES, [(i, i ^ mask) for i in range(count)])  35.6 us
    pallas_call x1, Pallas kernels, attn_bwd(): pl.pallas_call(functools.partial(attn_bwd_body, owners=count if owners el...  27.3 us
    pallas_call x1, Pallas kernels, attn_fwd(): pl.pallas_call(functools.partial(attn_fwd_body, plan=plan, rpd=rpd, per=p...  19.9 us
    ppermute x33, waiting for transfers between devices, swap(): return lax.ppermute(x, AXES, [(i, i ^ mask) for i in range(count)])  18.8 us
    pallas_call x1, Pallas kernels, grad_in(): pl.pallas_call(grad_in_body, grid=(n,), in_specs=[pl.BlockSpec((GL, 3 * D...  9.2 us
    pallas_call x1, Pallas kernels, rel_bias(): pl.pallas_call(rel_bias_body, out_shape=sds((HEADS, KP, LANES), f32), com...  4.31 us
    unnamed x43, local copies, waits for them, and re-layouts  4 us
  transfers between devices with their start and end apart: 33, of which 16 were waited for; matrix products, arithmetic and copies ran while one was open for 3% of the time, Pallas kernels for 37%

profile of v6, /device:TPU:0, one launch (start us, length us, event | category | flops | bytes accessed | tf_op | source)
XLA Modules:
  0.0 172.4 jit_solution(11446709705173879750)
XLA Ops:
  2.2 5.1 %collective-permute-start.3 = (bf16[1,16,1664]{2,1,0:T(8,128)(2,1)S(1)}, bf16[1,16,1664]{2,1,0:T(8,128)(2,1)S(1)}, u32[]{:S(2)}, u32[]{:S(2)}) collective-permute-start(bf16[1,16,1664]{2,1,0:T(8,128)(2,1)S(1)} %maximum_bitcast_fusion), channel_id=1, source_target_pairs={{0,24},{1,25},{2,26},{3,27},{4,28},{5,29},{6,30},{7,31},{8,16},{9,... | collective-permute-start | bytes 159752 | tf_op jit(solution)/shard_map/ppermute | solution.py:68
  10.5 2.4 %collective-permute-start = (bf16[1,144,512]{2,1,0:T(8,128)(2,1)S(1)}, bf16[1,144,512]{2,1,0:T(8,128)(2,1)S(1)}, u32[]{:S(2)}, u32[]{:S(2)}) collective-permute-start(bf16[1,144,512]{2,1,0:T(8,128)(2,1)S(1)} %bitcast.32), channel_id=1, source_target_pairs={{0,16},{1,17},{2,18},{3,19},{4,20},{5,21},{6,22},{7,23},{8,24},{9,... | collective-permute-start | bytes 442376 | tf_op jit(solution)/shard_map/ppermute | solution.py:68
  15.2 2.5 %collective-permute-start.7 = (bf16[4,16,1664]{2,1,0:T(8,128)(2,1)S(1)}, bf16[4,16,1664]{2,1,0:T(8,128)(2,1)S(1)}, u32[]{:S(2)}, u32[]{:S(2)}) collective-permute-start(bf16[4,16,1664]{2,1,0:T(8,128)(2,1)S(1)} %pad_maximum_fusion.2.refs_0_), channel_id=1, source_target_pairs={{0,6},{1,7},{2,4},{3,5},{4,2},{5,3},{6,0},{7,1},{8,14},{9,15},{10,... | collective-permute-start | bytes 638984 | tf_op jit(solution)/shard_map/ppermute | solution.py:68
  19.7 1.9 %collective-permute-start.4 = (bf16[2,144,512]{2,1,0:T(8,128)(2,1)S(1)}, bf16[2,144,512]{2,1,0:T(8,128)(2,1)S(1)}, u32[]{:S(2)}, u32[]{:S(2)}) collective-permute-start(bf16[2,144,512]{2,1,0:T(8,128)(2,1)S(1)} %pad_maximum_fusion.1), channel_id=1, source_target_pairs={{0,8},{1,9},{2,10},{3,11},{4,12},{5,13},{6,14},{7,15},{8,0},{9,1},... | collective-permute-start | bytes 884744 | tf_op jit(solution)/shard_map/ppermute | solution.py:68
  21.6 4.3 %rel_bias.1.bias_ref = f32[16,112,128]{2,1,0:T(8,128)S(1)} custom-call(f32[16,384]{1,0:T(8,128)S(1)} %pad.13.t_ref), custom_call_target="tpu_custom_call" | custom-call | flops 20000000000 | bytes 1000000 | tf_op jit(solution)/shard_map/rel_bias/pallas_call | solution.py:900
  27.9 2.5 %collective-permute-start.14 = (bf16[4,144,512]{2,1,0:T(8,128)(2,1)S(1)}, bf16[4,144,512]{2,1,0:T(8,128)(2,1)S(1)}, u32[]{:S(2)}, u32[]{:S(2)}) collective-permute-start(bf16[4,144,512]{2,1,0:T(8,128)(2,1)S(1)} %pad_maximum_fusion), channel_id=1, source_target_pairs={{0,6},{1,7},{2,4},{3,5},{4,2},{5,3},{6,0},{7,1},{8,14},{9,15},{10,... | collective-permute-start | bytes 1769480 | tf_op jit(solution)/shard_map/ppermute | solution.py:68
  35.6 19.9 %attn_fwd.1 = (bf16[512,2048]{1,0:T(8,128)(2,1)}, bf16[1600,512]{1,0:T(8,128)(2,1)}, bf16[2048,512]{1,0:T(8,128)(2,1)}, bf16[512,2048]{1,0:T(8,128)(2,1)}, bf16[...) custom-call(s32[1]{0:T(128)} %bitcast.me_ref, ...), custom_call_target="tpu_custom_call" | custom-call | flops 10000000 | bytes 100000 | tf_op jit(solution)/shard_map/attn_fwd/pallas_call | solution.py:254
  56.4 1.5 collective-permute-done.16
  61.2 37.9 %mlp.1 = (bf16[1600,512]{1,0:T(8,128)(2,1)}, f32[1600,512]{1,0:T(8,128)}, bf16[512,512]{1,0:T(8,128)(2,1)S(1)}, bf16[16,144,512]{2,1,0:T(8,128)(2,1)}, bf16[16,1...) custom-call(s32[1]{0:T(128)} %bitcast.me_ref, ...), custom_call_target="tpu_custom_call" | custom-call | flops 10000000 | bytes 100000 | tf_op jit(solution)/shard_map/mlp/pallas_call | solution.py:521
  99.3 4.6 %collective-permute-done.19.refs_1_ = bf16[16,144,512]{2,1,0:T(8,128)(2,1)S(1)} collective-permute-done((bf16[16,144,512]{2,1,0:T(8,128)(2,1)}, bf16[16,144,512]{2,1,0:T(8,128)(2,1)S(1)}, u32[]{:S(2)}, u32[]{:S(2)}) %collective-permute-start.19) | collective-permute-done | bytes 2359328 | tf_op jit(solution)/shard_map/ppermute | solution.py:68
  103.9 1.7 copy-done
  105.6 2.0 %add_split.3 = (f32[4,144,512]{2,1,0:T(8,128)S(1)}, bf16[4,144,512]{2,1,0:T(8,128)(2,1)}, bf16[4,144,512]{2,1,0:T(8,128)(2,1)}, bf16[4,144,512]{2,1,0:T(8,128)(2,1)S(1)}) custom-call(bf16[16,144,512]{2,1,0:T(8,128)(2,1)S(1)} %copy-done, bf16[16,144,512]{2,1,0:T(8,128)(2,1)S(1)} %collective-permute-done.19.refs_1_), custom_call_target="tpu_custom_call" | custom-call | flops 1000000 | bytes 100000 | tf_op jit(solution)/shard_map/add_split/pallas_call | solution.py:792
  107.5 1.5 collective-permute-start.20
  109.0 1.2 collective-permute-start.21
  111.1 27.3 %attn_bwd.1 = (bf16[2048,1536]{1,0:T(8,128)(2,1)}, f32[16,112,128]{2,1,0:T(8,128)}, f32[8,1536]{1,0:T(8,128)}, bf16[16,48,512]{2,1,0:T(8,128)(2,1)}, bf16[16,48,512]{2,1,0:T(8,128)(2,1)}) custom-call(s32[1]{0:T(128)} %bitcast.me_ref, f32[1600,512]{1,0:T(8,128)} %get-tuple-element.109.dmid_ref, bf16[512,512]{1,0:T(8,128)(2,1)} %copy-done.4, ...), custom_call_target="tpu_custom_call" | custom-call | flops 10000000 | bytes 100000 | tf_op jit(solution)/shard_map/attn_bwd/pallas_call | solution.py:656
  138.8 1.6 collective-permute-start.23
  140.4 2.4 %rel_grad.1.refs_2_ = f32[24,512]{1,0:T(8,128)S(1)} custom-call(f32[16,112,128]{2,1,0:T(8,128)S(1)} %copy-done.2, f32[8,1536]{1,0:T(8,128)S(1)} %copy-done.6, f32[8,512]{1,0:T(8,128)S(1)} %get-tuple-element.133.two_ref, f32[8,512]{1,0:T(8,128)S(1)} %get-tuple-element.134.up_ref, f32[8,512]{1,0:T(8,128)S(1)} %get-tuple-element.135.squares_ref), custom_call_target="tpu_custom_call" | custom-call | flops 10000000 | bytes 100000 | tf_op jit(solution)/shard_map/rel_grad/pallas_call | solution.py:942
  144.5 1.4 collective-permute-start.26
  146.9 1.1 collective-permute-start.28
  148.3 3.3 %collective-permute-start.29 = (bf16[1,144,512]{2,1,0:T(8,128)(2,1)S(1)}, bf16[1,144,512]{2,1,0:T(8,128)(2,1)S(1)}, u32[]{:S(2)}, u32[]{:S(2)}) collective-permute-start(bf16[1,144,512]{2,1,0:T(8,128)(2,1)S(1)} %get-tuple-element.142), channel_id=1, source_target_pairs={{0,16},{1,17},{2,18},{3,19},{4,20},{5,21},{6,22},{7,23},{8,24},{9,... | collective-permute-start | bytes 442376 | tf_op jit(solution)/shard_map/ppermute | solution.py:68
  151.7 9.2 %grad_in.1 = f32[1600,512]{1,0:T(8,128)} custom-call(bf16[2048,1536]{1,0:T(8,128)(2,1)} %get-tuple-element.143.dm_ref, bf16[512,1536]{1,0:T(8,128)(2,1)} %get-tuple-element.117.w_any.w_ref, bf16[1600,512]{1,0:T(8,128)(2,1)} %x_ref.2, f32[1600,512]{1,0:T(8,128)} %get-tuple-element.109.dmid_ref, f32[16,512]{1,0:T(8,128)} %get-tuple-element.97.rowv_ref), custom_call_target="tpu_custom_call" | custom-call | flops 10000000 | bytes 100000 | tf_op jit(solution)/shard_map/grad_in/pallas_call | solution.py:694
  161.1 1.5 collective-permute-start.30
  162.9 2.7 %collective-permute-start.32 = (bf16[80,512]{1,0:T(8,128)(2,1)S(1)}, bf16[80,512]{1,0:T(8,128)(2,1)S(1)}, u32[]{:S(2)}, u32[]{:S(2)}) collective-permute-start(bf16[80,512]{1,0:T(8,128)(2,1)S(1)} %get-tuple-element.154), channel_id=1, source_target_pairs={{0,24},{1,25},{2,26},{3,27},{4,28},{5,29},{6,30},{7,31},{8,16},{9,... | collective-permute-start | bytes 245768 | tf_op jit(solution)/shard_map/ppermute | solution.py:68
  166.3 4.8 %collective-permute-done.31.refs_1_ = bf16[80,512]{1,0:T(8,128)(2,1)S(1)} collective-permute-done((bf16[80,512]{1,0:T(8,128)(2,1)S(1)}, bf16[80,512]{1,0:T(8,128)(2,1)S(1)}, u32[]{:S(2)}, u32[]{:S(2)}) %collective-permute-start.31) | collective-permute-done | bytes 81952 | tf_op jit(solution)/shard_map/ppermute | solution.py:68
  (117 shorter events, 27.1 us)
Async XLA Ops:
  2.2 12.9 %collective-permute-start.3 = (bf16[1,16,1664]{2,1,0:T(8,128)(2,1)S(1)}, bf16[1,16,1664]{2,1,0:T(8,128)(2,1)S(1)}, u32[]{:S(2)}, u32[]{:S(2)}) collective-permute-start(bf16[1,16,1664]{2,1,0:T(8,128)(2,1)S(1)} %maximum_bitcast_fusion), channel_id=1, source_target_pairs={{0,24},{1,25},{2,26},{3,27},{4,28},{5,29},{6,30},{7,31},{8,16},{9,... | collective-permute-start | bytes 159752 | tf_op jit(solution)/shard_map/ppermute | solution.py:68
  7.3 7.8 %collective-permute-start.2 = (bf16[1,16,1664]{2,1,0:T(8,128)(2,1)S(1)}, bf16[1,16,1664]{2,1,0:T(8,128)(2,1)S(1)}, u32[]{:S(2)}, u32[]{:S(2)}) collective-permute-start(bf16[1,16,1664]{2,1,0:T(8,128)(2,1)S(1)} %maximum_bitcast_fusion), channel_id=1, source_target_pairs={{0,16},{1,17},{2,18},{3,19},{4,20},{5,21},{6,22},{7,23},{8,24},{9,... | collective-permute-start | bytes 159752 | tf_op jit(solution)/shard_map/ppermute | solution.py:68
  7.3 7.8 %collective-permute-start.1 = (bf16[1,16,1664]{2,1,0:T(8,128)(2,1)S(1)}, bf16[1,16,1664]{2,1,0:T(8,128)(2,1)S(1)}, u32[]{:S(2)}, u32[]{:S(2)}) collective-permute-start(bf16[1,16,1664]{2,1,0:T(8,128)(2,1)S(1)} %maximum_bitcast_fusion), channel_id=1, source_target_pairs={{0,8},{1,9},{2,10},{3,11},{4,12},{5,13},{6,14},{7,15},{8,0},{9,1},... | collective-permute-start | bytes 159752 | tf_op jit(solution)/shard_map/ppermute | solution.py:68
  10.5 9.2 %collective-permute-start = (bf16[1,144,512]{2,1,0:T(8,128)(2,1)S(1)}, bf16[1,144,512]{2,1,0:T(8,128)(2,1)S(1)}, u32[]{:S(2)}, u32[]{:S(2)}) collective-permute-start(bf16[1,144,512]{2,1,0:T(8,128)(2,1)S(1)} %bitcast.32), channel_id=1, source_target_pairs={{0,16},{1,17},{2,18},{3,19},{4,20},{5,21},{6,22},{7,23},{8,24},{9,... | collective-permute-start | bytes 442376 | tf_op jit(solution)/shard_map/ppermute | solution.py:68
  15.2 10.8 %collective-permute-start.7 = (bf16[4,16,1664]{2,1,0:T(8,128)(2,1)S(1)}, bf16[4,16,1664]{2,1,0:T(8,128)(2,1)S(1)}, u32[]{:S(2)}, u32[]{:S(2)}) collective-permute-start(bf16[4,16,1664]{2,1,0:T(8,128)(2,1)S(1)} %pad_maximum_fusion.2.refs_0_), channel_id=1, source_target_pairs={{0,6},{1,7},{2,4},{3,5},{4,2},{5,3},{6,0},{7,1},{8,14},{9,15},{10,... | collective-permute-start | bytes 638984 | tf_op jit(solution)/shard_map/ppermute | solution.py:68
  17.7 9.2 %collective-permute-start.6 = (bf16[4,16,1664]{2,1,0:T(8,128)(2,1)S(1)}, bf16[4,16,1664]{2,1,0:T(8,128)(2,1)S(1)}, u32[]{:S(2)}, u32[]{:S(2)}) collective-permute-start(bf16[4,16,1664]{2,1,0:T(8,128)(2,1)S(1)} %pad_maximum_fusion.2.refs_0_), channel_id=1, source_target_pairs={{0,4},{1,5},{2,6},{3,7},{4,0},{5,1},{6,2},{7,3},{8,12},{9,13},{10,... | collective-permute-start | bytes 638984 | tf_op jit(solution)/shard_map/ppermute | solution.py:68
  18.2 8.8 %collective-permute-start.5 = (bf16[4,16,1664]{2,1,0:T(8,128)(2,1)S(1)}, bf16[4,16,1664]{2,1,0:T(8,128)(2,1)S(1)}, u32[]{:S(2)}, u32[]{:S(2)}) collective-permute-start(bf16[4,16,1664]{2,1,0:T(8,128)(2,1)S(1)} %pad_maximum_fusion.2.refs_0_), channel_id=1, source_target_pairs={{0,2},{1,3},{2,0},{3,1},{4,6},{5,7},{6,4},{7,5},{8,10},{9,11},{10,... | collective-permute-start | bytes 638984 | tf_op jit(solution)/shard_map/ppermute | solution.py:68
  19.7 8.1 %collective-permute-start.4 = (bf16[2,144,512]{2,1,0:T(8,128)(2,1)S(1)}, bf16[2,144,512]{2,1,0:T(8,128)(2,1)S(1)}, u32[]{:S(2)}, u32[]{:S(2)}) collective-permute-start(bf16[2,144,512]{2,1,0:T(8,128)(2,1)S(1)} %pad_maximum_fusion.1), channel_id=1, source_target_pairs={{0,8},{1,9},{2,10},{3,11},{4,12},{5,13},{6,14},{7,15},{8,0},{9,1},... | collective-permute-start | bytes 884744 | tf_op jit(solution)/shard_map/ppermute | solution.py:68
  27.9 27.6 %collective-permute-start.14 = (bf16[4,144,512]{2,1,0:T(8,128)(2,1)S(1)}, bf16[4,144,512]{2,1,0:T(8,128)(2,1)S(1)}, u32[]{:S(2)}, u32[]{:S(2)}) collective-permute-start(bf16[4,144,512]{2,1,0:T(8,128)(2,1)S(1)} %pad_maximum_fusion), channel_id=1, source_target_pairs={{0,6},{1,7},{2,4},{3,5},{4,2},{5,3},{6,0},{7,1},{8,14},{9,15},{10,... | collective-permute-start | bytes 1769480 | tf_op jit(solution)/shard_map/ppermute | solution.py:68
  30.4 25.1 %collective-permute-start.13 = (bf16[4,144,512]{2,1,0:T(8,128)(2,1)S(1)}, bf16[4,144,512]{2,1,0:T(8,128)(2,1)S(1)}, u32[]{:S(2)}, u32[]{:S(2)}) collective-permute-start(bf16[4,144,512]{2,1,0:T(8,128)(2,1)S(1)} %pad_maximum_fusion), channel_id=1, source_target_pairs={{0,4},{1,5},{2,6},{3,7},{4,0},{5,1},{6,2},{7,3},{8,12},{9,13},{10,... | collective-permute-start | bytes 1769480 | tf_op jit(solution)/shard_map/ppermute | solution.py:68
  30.9 25.0 %collective-permute-start.12 = (bf16[4,144,512]{2,1,0:T(8,128)(2,1)S(1)}, bf16[4,144,512]{2,1,0:T(8,128)(2,1)S(1)}, u32[]{:S(2)}, u32[]{:S(2)}) collective-permute-start(bf16[4,144,512]{2,1,0:T(8,128)(2,1)S(1)} %pad_maximum_fusion), channel_id=1, source_target_pairs={{0,2},{1,3},{2,0},{3,1},{4,6},{5,7},{6,4},{7,5},{8,10},{9,11},{10,... | collective-permute-start | bytes 1769480 | tf_op jit(solution)/shard_map/ppermute | solution.py:68
  34.4 22.0 %collective-permute-start.15 = (bf16[4,144,512]{2,1,0:T(8,128)(2,1)S(1)}, bf16[4,144,512]{2,1,0:T(8,128)(2,1)}, u32[]{:S(2)}, u32[]{:S(2)}) collective-permute-start(bf16[4,144,512]{2,1,0:T(8,128)(2,1)S(1)} %pad_maximum_fusion), channel_id=1, source_target_pairs={{0,1},{1,0},{2,3},{3,2},{4,5},{5,4},{6,7},{7,6},{8,9},{9,8},{10,11... | collective-permute-start | bytes 1769480 | tf_op jit(solution)/shard_map/ppermute | solution.py:68
  99.1 4.8 %collective-permute-start.19 = (bf16[16,144,512]{2,1,0:T(8,128)(2,1)}, bf16[16,144,512]{2,1,0:T(8,128)(2,1)S(1)}, u32[]{:S(2)}, u32[]{:S(2)}) collective-permute-start(bf16[16,144,512]{2,1,0:T(8,128)(2,1)} %get-tuple-element.104), channel_id=1, source_target_pairs={{0,1},{1,0},{2,3},{3,2},{4,5},{5,4},{6,7},{7,6},{8,9},{9,8},{10,11... | collective-permute-start | bytes 7077896 | tf_op jit(solution)/shard_map/ppermute | solution.py:68
  107.5 30.9 %collective-permute-start.20 = (bf16[4,144,512]{2,1,0:T(8,128)(2,1)}, bf16[4,144,512]{2,1,0:T(8,128)(2,1)S(1)}, u32[]{:S(2)}, u32[]{:S(2)}) collective-permute-start(bf16[4,144,512]{2,1,0:T(8,128)(2,1)} %get-tuple-element.105), channel_id=1, source_target_pairs={{0,2},{1,3},{2,0},{3,1},{4,6},{5,7},{6,4},{7,5},{8,10},{9,11},{10,... | collective-permute-start | bytes 1769480 | tf_op jit(solution)/shard_map/ppermute | solution.py:68
  109.0 29.5 %collective-permute-start.21 = (bf16[4,144,512]{2,1,0:T(8,128)(2,1)}, bf16[4,144,512]{2,1,0:T(8,128)(2,1)S(1)}, u32[]{:S(2)}, u32[]{:S(2)}) collective-permute-start(bf16[4,144,512]{2,1,0:T(8,128)(2,1)} %get-tuple-element.106), channel_id=1, source_target_pairs={{0,4},{1,5},{2,6},{3,7},{4,0},{5,1},{6,2},{7,3},{8,12},{9,13},{10,... | collective-permute-start | bytes 1769480 | tf_op jit(solution)/shard_map/ppermute | solution.py:68
  110.2 28.2 %collective-permute-start.22 = (bf16[4,144,512]{2,1,0:T(8,128)(2,1)S(1)}, bf16[4,144,512]{2,1,0:T(8,128)(2,1)S(1)}, u32[]{:S(2)}, u32[]{:S(2)}) collective-permute-start(bf16[4,144,512]{2,1,0:T(8,128)(2,1)S(1)} %get-tuple-element.107), channel_id=1, source_target_pairs={{0,6},{1,7},{2,4},{3,5},{4,2},{5,3},{6,0},{7,1},{8,14},{9,15},{10,... | collective-permute-start | bytes 1769480 | tf_op jit(solution)/shard_map/ppermute | solution.py:68
  138.8 9.5 %collective-permute-start.23 = (bf16[2,144,512]{2,1,0:T(8,128)(2,1)S(1)}, bf16[2,144,512]{2,1,0:T(8,128)(2,1)S(1)}, u32[]{:S(2)}, u32[]{:S(2)}) collective-permute-start(bf16[2,144,512]{2,1,0:T(8,128)(2,1)S(1)} %get-tuple-element.127), channel_id=1, source_target_pairs={{0,8},{1,9},{2,10},{3,11},{4,12},{5,13},{6,14},{7,15},{8,0},{9,1},... | collective-permute-start | bytes 884744 | tf_op jit(solution)/shard_map/ppermute | solution.py:68
  144.5 16.4 %collective-permute-start.26 = (bf16[224,512]{1,0:T(8,128)(2,1)S(1)}, bf16[224,512]{1,0:T(8,128)(2,1)S(1)}, u32[]{:S(2)}, u32[]{:S(2)}) collective-permute-start(bf16[224,512]{1,0:T(8,128)(2,1)S(1)} %get-tuple-element.137), channel_id=1, source_target_pairs={{0,2},{1,3},{2,0},{3,1},{4,6},{5,7},{6,4},{7,5},{8,10},{9,11},{10,... | collective-permute-start | bytes 688136 | tf_op jit(solution)/shard_map/ppermute | solution.py:68
  145.9 14.9 %collective-permute-start.27 = (bf16[224,512]{1,0:T(8,128)(2,1)S(1)}, bf16[224,512]{1,0:T(8,128)(2,1)S(1)}, u32[]{:S(2)}, u32[]{:S(2)}) collective-permute-start(bf16[224,512]{1,0:T(8,128)(2,1)S(1)} %get-tuple-element.138), channel_id=1, source_target_pairs={{0,4},{1,5},{2,6},{3,7},{4,0},{5,1},{6,2},{7,3},{8,12},{9,13},{10,... | collective-permute-start | bytes 688136 | tf_op jit(solution)/shard_map/ppermute | solution.py:68
  146.9 14.0 %collective-permute-start.28 = (bf16[224,512]{1,0:T(8,128)(2,1)S(1)}, bf16[224,512]{1,0:T(8,128)(2,1)S(1)}, u32[]{:S(2)}, u32[]{:S(2)}) collective-permute-start(bf16[224,512]{1,0:T(8,128)(2,1)S(1)} %get-tuple-element.139), channel_id=1, source_target_pairs={{0,6},{1,7},{2,4},{3,5},{4,2},{5,3},{6,0},{7,1},{8,14},{9,15},{10,... | collective-permute-start | bytes 688136 | tf_op jit(solution)/shard_map/ppermute | solution.py:68
  148.3 12.5 %collective-permute-start.29 = (bf16[1,144,512]{2,1,0:T(8,128)(2,1)S(1)}, bf16[1,144,512]{2,1,0:T(8,128)(2,1)S(1)}, u32[]{:S(2)}, u32[]{:S(2)}) collective-permute-start(bf16[1,144,512]{2,1,0:T(8,128)(2,1)S(1)} %get-tuple-element.142), channel_id=1, source_target_pairs={{0,16},{1,17},{2,18},{3,19},{4,20},{5,21},{6,22},{7,23},{8,24},{9,... | collective-permute-start | bytes 442376 | tf_op jit(solution)/shard_map/ppermute | solution.py:68
  161.1 5.2 %collective-permute-start.30 = (bf16[80,512]{1,0:T(8,128)(2,1)S(1)}, bf16[80,512]{1,0:T(8,128)(2,1)S(1)}, u32[]{:S(2)}, u32[]{:S(2)}) collective-permute-start(bf16[80,512]{1,0:T(8,128)(2,1)S(1)} %get-tuple-element.152), channel_id=1, source_target_pairs={{0,8},{1,9},{2,10},{3,11},{4,12},{5,13},{6,14},{7,15},{8,0},{9,1},... | collective-permute-start | bytes 245768 | tf_op jit(solution)/shard_map/ppermute | solution.py:68
  162.6 8.6 %collective-permute-start.31 = (bf16[80,512]{1,0:T(8,128)(2,1)S(1)}, bf16[80,512]{1,0:T(8,128)(2,1)S(1)}, u32[]{:S(2)}, u32[]{:S(2)}) collective-permute-start(bf16[80,512]{1,0:T(8,128)(2,1)S(1)} %get-tuple-element.153), channel_id=1, source_target_pairs={{0,16},{1,17},{2,18},{3,19},{4,20},{5,21},{6,22},{7,23},{8,24},{9,... | collective-permute-start | bytes 245768 | tf_op jit(solution)/shard_map/ppermute | solution.py:68
  162.9 8.3 %collective-permute-start.32 = (bf16[80,512]{1,0:T(8,128)(2,1)S(1)}, bf16[80,512]{1,0:T(8,128)(2,1)S(1)}, u32[]{:S(2)}, u32[]{:S(2)}) collective-permute-start(bf16[80,512]{1,0:T(8,128)(2,1)S(1)} %get-tuple-element.154), channel_id=1, source_target_pairs={{0,24},{1,25},{2,26},{3,27},{4,28},{5,29},{6,30},{7,31},{8,16},{9,... | collective-permute-start | bytes 245768 | tf_op jit(solution)/shard_map/ppermute | solution.py:68
  (28 other events, 104.4 us)

commit v7 on v6

--- a/solution.py
+++ b/solution.py
@@ -194,8 +194,10 @@
     keys = lax.broadcasted_iota(jnp.int32, (KP, LANES), 0)
     same = (keys == lax.broadcasted_iota(jnp.int32, (KP, LANES), 1)) & (keys < CELLS)
     for w in range(GW):
-        of_key = turned[:, GW + w : GW + w + 1]
-        equal = jnp.broadcast_to(of_key[0:KP], (KP, LANES)) == jnp.broadcast_to(code_ref[0, w : w + 1, :], (KP, LANES))
+        of_key = turned[:, w : w + 1]
+        region = code_ref[0, w : w + 1, :]
+        region = jnp.where(region < 0.0, region + 16.0, region)
+        equal = jnp.broadcast_to(of_key[0:KP], (KP, LANES)) == jnp.broadcast_to(region, (KP, LANES))
         mask_ref[w] = jnp.where(equal | same, 0.0, NEG)
         vsc[CELLS * w : CELLS * w + 104, :] = jnp.broadcast_to(jnp.where(of_key[0:104] >= 0.0, 1.0, 0.0), (104, LANES))
     vld_ref[...] = vsc[0:GR, :]
@@ -761,21 +763,10 @@
     )(*arrays)
 
 
-def add_body(*refs, terms, later):
-    ins, outs = refs[:terms], refs[terms : -2] if later else refs[terms:]
+def add_body(*refs, terms):
+    ins, outs = refs[:terms], refs[terms:]
     n = outs[0].shape[0]
-    copies = []
-    if later:
-        buf, sem = refs[-2:]
-        for p in range(len(outs)):
-            at = pl.ds(p * n, n)
-            copies.append(pltpu.make_async_copy(ins[0].at[at], buf.at[at], sem.at[p]))
-        for c in copies:
-            c.start()
-        ins = (buf,) + ins[1:]
     for p, out in enumerate(outs):
-        if later:
-            copies[p].wait()
         at = slice(p * n, p * n + n)
         total = ins[0][at].astype(f32)
         for r in ins[1:]:
@@ -783,18 +774,13 @@
         out[...] = total.astype(out.dtype)
 
 
-def add_split(terms, group, later=False):
+def add_split(terms, group):
     parts = len(masks_of(group))
-    first = terms[0]
-    n = first.shape[0] // (parts + 1)
-    shape = (n,) + first.shape[1:]
-    vmem = pl.BlockSpec(memory_space=pltpu.VMEM)
+    shape = (terms[0].shape[0] // (parts + 1),) + terms[0].shape[1:]
     out = pl.pallas_call(
-        functools.partial(add_body, terms=len(terms), later=later),
-        in_specs=[pl.BlockSpec(memory_space=pltpu.HBM) if later else vmem] + [vmem] * (len(terms) - 1),
+        functools.partial(add_body, terms=len(terms)),
         out_shape=[sds(shape, f32)] + [sds(shape, bf16)] * parts,
-        scratch_shapes=[pltpu.VMEM(first.shape, first.dtype), pltpu.SemaphoreType.DMA((parts + 1,))] if later else [],
-        compiler_params=params(16),
+        compiler_params=params(24),
         cost_estimate=pl.CostEstimate(flops=10**6, bytes_accessed=10**5, transcendentals=0),
         name="add_split",
     )(*terms)
@@ -973,9 +959,8 @@
     mlp_rels, mlp_up = gather_upper(packed, single, count, attn_up)
 
     bias = rel_bias(jnp.pad(table_in.T * LOG2E, ((0, 0), (0, RP - RELN))))
-    reg = regions.reshape(-1, GW, CELLS).astype(f32)
-    key_code = jnp.where(validity.reshape(-1, GW, CELLS) == 1, reg, -2.0)
-    codes = jnp.pad(jnp.concatenate([reg, key_code], axis=1), ((0, 0), (0, 0), (0, LANES - CELLS)), constant_values=-3.0)
+    codes = jnp.where(validity == 1, regions, regions - 16).astype(f32).reshape(-1, GW, CELLS)
+    codes = jnp.pad(codes, ((0, 0), (0, 8 - GW), (0, LANES - CELLS)), constant_values=-100.0)
 
     attn_pieces = hold(attn_pieces, bias, codes)
     mlp_up = after(mlp_up, bias, codes, [a for _, a in attn_pieces])
@@ -1015,7 +1000,7 @@
         mlp_keep, mlp_send = pk[: count // 2], pk[count // 2 :]
 
     other = swap(mlp_send, 1, count)
-    mlp_own, parts = add_split([mlp_keep, other], groups[1], later=True)
+    mlp_own, parts = add_split([mlp_keep, other], groups[1])
     mlp_got = send_parts(parts, groups[1], count)
     dmid = after(dmid, parts)
     got = attn_bwd(me_s, dmid, p_full, oT, q, kT, v, pT, xT, w_full, rowv, rpd, direct, count, groups)

time: 173 us -> 172 us (level)
  transfers between devices with their start and end apart: 33 -> 33, of which waited for: 16 -> 15; matrix products, arithmetic and copies ran while one was open for 3% -> 3% of each run, Pallas kernels for 37% -> 38%
where the time goes in v7:
time: 172 us
  Pallas kernels  105 us (61%)
  starting transfers between devices  35.2 us (20%)
  waiting for transfers between devices  19.9 us (12%)
  local copies, waits for them, and re-layouts  9.28 us (5%)
    pallas_call x1, Pallas kernels, mlp(): pl.pallas_call(functools.partial(mlp_body, plan=plan, rows=rows, owners=c...  37.9 us
    ppermute x33, starting transfers between devices, swap(): return lax.ppermute(x, AXES, [(i, i ^ mask) for i in range(count)])  35.2 us
    pallas_call x1, Pallas kernels, attn_bwd(): pl.pallas_call(functools.partial(attn_bwd_body, owners=count if owners el...  27.3 us
    ppermute x33, waiting for transfers between devices, swap(): return lax.ppermute(x, AXES, [(i, i ^ mask) for i in range(count)])  19.9 us
    pallas_call x1, Pallas kernels, attn_fwd(): pl.pallas_call(functools.partial(attn_fwd_body, plan=plan, rpd=rpd, per=p...  19.9 us
    pallas_call x1, Pallas kernels, grad_in(): pl.pallas_call(grad_in_body, grid=(n,), in_specs=[pl.BlockSpec((GL, 3 * D...  9.2 us
    pallas_call x1, Pallas kernels, rel_bias(): pl.pallas_call(rel_bias_body, out_shape=sds((HEADS, KP, LANES), f32), com...  4.31 us
    unnamed x43, local copies, waits for them, and re-layouts  4 us
  transfers between devices with their start and end apart: 33, of which 15 were waited for; matrix products, arithmetic and copies ran while one was open for 3% of the time, Pallas kernels for 38%

profile of v7, /device:TPU:0, one launch (start us, length us, event | category | flops | bytes accessed | tf_op | source)
XLA Modules:
  0.0 171.7 jit_solution(553869166943394563)
XLA Ops:
  2.2 5.1 %collective-permute-start.3 = (bf16[1,16,1664]{2,1,0:T(8,128)(2,1)S(1)}, bf16[1,16,1664]{2,1,0:T(8,128)(2,1)S(1)}, u32[]{:S(2)}, u32[]{:S(2)}) collective-permute-start(bf16[1,16,1664]{2,1,0:T(8,128)(2,1)S(1)} %maximum_bitcast_fusion), channel_id=1, source_target_pairs={{0,24},{1,25},{2,26},{3,27},{4,28},{5,29},{6,30},{7,31},{8,16},{9,... | collective-permute-start | bytes 159752 | tf_op jit(solution)/shard_map/ppermute | solution.py:68
  10.5 2.4 %collective-permute-start = (bf16[1,144,512]{2,1,0:T(8,128)(2,1)S(1)}, bf16[1,144,512]{2,1,0:T(8,128)(2,1)S(1)}, u32[]{:S(2)}, u32[]{:S(2)}) collective-permute-start(bf16[1,144,512]{2,1,0:T(8,128)(2,1)S(1)} %bitcast.32), channel_id=1, source_target_pairs={{0,16},{1,17},{2,18},{3,19},{4,20},{5,21},{6,22},{7,23},{8,24},{9,... | collective-permute-start | bytes 442376 | tf_op jit(solution)/shard_map/ppermute | solution.py:68
  14.4 2.5 %collective-permute-start.7 = (bf16[4,16,1664]{2,1,0:T(8,128)(2,1)S(1)}, bf16[4,16,1664]{2,1,0:T(8,128)(2,1)S(1)}, u32[]{:S(2)}, u32[]{:S(2)}) collective-permute-start(bf16[4,16,1664]{2,1,0:T(8,128)(2,1)S(1)} %pad_maximum_fusion.2.refs_0_), channel_id=1, source_target_pairs={{0,6},{1,7},{2,4},{3,5},{4,2},{5,3},{6,0},{7,1},{8,14},{9,15},{10,... | collective-permute-start | bytes 638984 | tf_op jit(solution)/shard_map/ppermute | solution.py:68
  20.8 4.3 %rel_bias.1.bias_ref = f32[16,112,128]{2,1,0:T(8,128)S(1)} custom-call(f32[16,384]{1,0:T(8,128)S(1)} %pad.13.t_ref), custom_call_target="tpu_custom_call" | custom-call | flops 20000000000 | bytes 1000000 | tf_op jit(solution)/shard_map/rel_bias/pallas_call | solution.py:886
  26.2 1.7 collective-permute-done.4
  27.9 2.5 %collective-permute-start.14 = (bf16[4,144,512]{2,1,0:T(8,128)(2,1)S(1)}, bf16[4,144,512]{2,1,0:T(8,128)(2,1)S(1)}, u32[]{:S(2)}, u32[]{:S(2)}) collective-permute-start(bf16[4,144,512]{2,1,0:T(8,128)(2,1)S(1)} %pad_maximum_fusion), channel_id=1, source_target_pairs={{0,6},{1,7},{2,4},{3,5},{4,2},{5,3},{6,0},{7,1},{8,14},{9,15},{10,... | collective-permute-start | bytes 1769480 | tf_op jit(solution)/shard_map/ppermute | solution.py:68
  35.6 19.9 %attn_fwd.1 = (bf16[512,2048]{1,0:T(8,128)(2,1)}, bf16[1600,512]{1,0:T(8,128)(2,1)}, bf16[2048,512]{1,0:T(8,128)(2,1)}, bf16[512,2048]{1,0:T(8,128)(2,1)}, bf16[...) custom-call(s32[1]{0:T(128)} %bitcast.me_ref, ...), custom_call_target="tpu_custom_call" | custom-call | flops 10000000 | bytes 100000 | tf_op jit(solution)/shard_map/attn_fwd/pallas_call | solution.py:256
  56.3 1.3 collective-permute-done.16
  60.8 37.9 %mlp.1 = (bf16[1600,512]{1,0:T(8,128)(2,1)}, f32[1600,512]{1,0:T(8,128)}, bf16[512,512]{1,0:T(8,128)(2,1)S(1)}, bf16[16,144,512]{2,1,0:T(8,128)(2,1)}, bf16[16,1...) custom-call(s32[1]{0:T(128)} %bitcast.me_ref, ...), custom_call_target="tpu_custom_call" | custom-call | flops 10000000 | bytes 100000 | tf_op jit(solution)/shard_map/mlp/pallas_call | solution.py:523
  99.0 4.5 %collective-permute-done.19.refs_1_ = bf16[16,144,512]{2,1,0:T(8,128)(2,1)S(1)} collective-permute-done((bf16[16,144,512]{2,1,0:T(8,128)(2,1)}, bf16[16,144,512]{2,1,0:T(8,128)(2,1)S(1)}, u32[]{:S(2)}, u32[]{:S(2)}) %collective-permute-start.19) | collective-permute-done | bytes 2359328 | tf_op jit(solution)/shard_map/ppermute | solution.py:68
  103.5 1.7 copy-done
  105.2 1.3 add_split.3
  106.5 1.5 collective-permute-start.20
  108.0 1.5 collective-permute-start.21
  110.0 27.3 %attn_bwd.1 = (bf16[2048,1536]{1,0:T(8,128)(2,1)}, f32[16,112,128]{2,1,0:T(8,128)}, f32[8,1536]{1,0:T(8,128)}, bf16[16,48,512]{2,1,0:T(8,128)(2,1)}, bf16[16,48,512]{2,1,0:T(8,128)(2,1)}) custom-call(s32[1]{0:T(128)} %bitcast.me_ref, f32[1600,512]{1,0:T(8,128)} %get-tuple-element.109.dmid_ref, bf16[512,512]{1,0:T(8,128)(2,1)} %copy-done.4, ...), custom_call_target="tpu_custom_call" | custom-call | flops 10000000 | bytes 100000 | tf_op jit(solution)/shard_map/attn_bwd/pallas_call | solution.py:658
  137.7 1.3 collective-permute-start.23
  139.0 2.4 %rel_grad.1.refs_2_ = f32[24,512]{1,0:T(8,128)S(1)} custom-call(f32[16,112,128]{2,1,0:T(8,128)S(1)} %copy-done.2, f32[8,1536]{1,0:T(8,128)S(1)} %copy-done.6, f32[8,512]{1,0:T(8,128)S(1)} %get-tuple-element.133.two_ref, f32[8,512]{1,0:T(8,128)S(1)} %get-tuple-element.134.up_ref, f32[8,512]{1,0:T(8,128)S(1)} %get-tuple-element.135.squares_ref), custom_call_target="tpu_custom_call" | custom-call | flops 10000000 | bytes 100000 | tf_op jit(solution)/shard_map/rel_grad/pallas_call | solution.py:928
  143.1 1.6 collective-permute-start.26
  144.6 1.5 collective-permute-start.27
  147.2 3.7 %collective-permute-start.29 = (bf16[1,144,512]{2,1,0:T(8,128)(2,1)S(1)}, bf16[1,144,512]{2,1,0:T(8,128)(2,1)S(1)}, u32[]{:S(2)}, u32[]{:S(2)}) collective-permute-start(bf16[1,144,512]{2,1,0:T(8,128)(2,1)S(1)} %get-tuple-element.142), channel_id=1, source_target_pairs={{0,16},{1,17},{2,18},{3,19},{4,20},{5,21},{6,22},{7,23},{8,24},{9,... | collective-permute-start | bytes 442376 | tf_op jit(solution)/shard_map/ppermute | solution.py:68
  150.9 9.2 %grad_in.1 = f32[1600,512]{1,0:T(8,128)} custom-call(bf16[2048,1536]{1,0:T(8,128)(2,1)} %get-tuple-element.143.dm_ref, bf16[512,1536]{1,0:T(8,128)(2,1)} %get-tuple-element.117.w_any.w_ref, bf16[1600,512]{1,0:T(8,128)(2,1)} %x_ref.2, f32[1600,512]{1,0:T(8,128)} %get-tuple-element.109.dmid_ref, f32[16,512]{1,0:T(8,128)} %get-tuple-element.97.rowv_ref), custom_call_target="tpu_custom_call" | custom-call | flops 10000000 | bytes 100000 | tf_op jit(solution)/shard_map/grad_in/pallas_call | solution.py:696
  160.4 1.5 collective-permute-start.30
  162.1 2.7 %collective-permute-start.32 = (bf16[80,512]{1,0:T(8,128)(2,1)S(1)}, bf16[80,512]{1,0:T(8,128)(2,1)S(1)}, u32[]{:S(2)}, u32[]{:S(2)}) collective-permute-start(bf16[80,512]{1,0:T(8,128)(2,1)S(1)} %get-tuple-element.154), channel_id=1, source_target_pairs={{0,24},{1,25},{2,26},{3,27},{4,28},{5,29},{6,30},{7,31},{8,16},{9,... | collective-permute-start | bytes 245768 | tf_op jit(solution)/shard_map/ppermute | solution.py:68
  165.6 4.8 %collective-permute-done.31.refs_1_ = bf16[80,512]{1,0:T(8,128)(2,1)S(1)} collective-permute-done((bf16[80,512]{1,0:T(8,128)(2,1)S(1)}, bf16[80,512]{1,0:T(8,128)(2,1)S(1)}, u32[]{:S(2)}, u32[]{:S(2)}) %collective-permute-start.31) | collective-permute-done | bytes 81952 | tf_op jit(solution)/shard_map/ppermute | solution.py:68
  (114 shorter events, 26.7 us)
Async XLA Ops:
  2.2 12.1 %collective-permute-start.3 = (bf16[1,16,1664]{2,1,0:T(8,128)(2,1)S(1)}, bf16[1,16,1664]{2,1,0:T(8,128)(2,1)S(1)}, u32[]{:S(2)}, u32[]{:S(2)}) collective-permute-start(bf16[1,16,1664]{2,1,0:T(8,128)(2,1)S(1)} %maximum_bitcast_fusion), channel_id=1, source_target_pairs={{0,24},{1,25},{2,26},{3,27},{4,28},{5,29},{6,30},{7,31},{8,16},{9,... | collective-permute-start | bytes 159752 | tf_op jit(solution)/shard_map/ppermute | solution.py:68
  7.3 7.0 %collective-permute-start.2 = (bf16[1,16,1664]{2,1,0:T(8,128)(2,1)S(1)}, bf16[1,16,1664]{2,1,0:T(8,128)(2,1)S(1)}, u32[]{:S(2)}, u32[]{:S(2)}) collective-permute-start(bf16[1,16,1664]{2,1,0:T(8,128)(2,1)S(1)} %maximum_bitcast_fusion), channel_id=1, source_target_pairs={{0,16},{1,17},{2,18},{3,19},{4,20},{5,21},{6,22},{7,23},{8,24},{9,... | collective-permute-start | bytes 159752 | tf_op jit(solution)/shard_map/ppermute | solution.py:68
  7.3 7.0 %collective-permute-start.1 = (bf16[1,16,1664]{2,1,0:T(8,128)(2,1)S(1)}, bf16[1,16,1664]{2,1,0:T(8,128)(2,1)S(1)}, u32[]{:S(2)}, u32[]{:S(2)}) collective-permute-start(bf16[1,16,1664]{2,1,0:T(8,128)(2,1)S(1)} %maximum_bitcast_fusion), channel_id=1, source_target_pairs={{0,8},{1,9},{2,10},{3,11},{4,12},{5,13},{6,14},{7,15},{8,0},{9,1},... | collective-permute-start | bytes 159752 | tf_op jit(solution)/shard_map/ppermute | solution.py:68
  10.5 9.2 %collective-permute-start = (bf16[1,144,512]{2,1,0:T(8,128)(2,1)S(1)}, bf16[1,144,512]{2,1,0:T(8,128)(2,1)S(1)}, u32[]{:S(2)}, u32[]{:S(2)}) collective-permute-start(bf16[1,144,512]{2,1,0:T(8,128)(2,1)S(1)} %bitcast.32), channel_id=1, source_target_pairs={{0,16},{1,17},{2,18},{3,19},{4,20},{5,21},{6,22},{7,23},{8,24},{9,... | collective-permute-start | bytes 442376 | tf_op jit(solution)/shard_map/ppermute | solution.py:68
  14.4 10.8 %collective-permute-start.7 = (bf16[4,16,1664]{2,1,0:T(8,128)(2,1)S(1)}, bf16[4,16,1664]{2,1,0:T(8,128)(2,1)S(1)}, u32[]{:S(2)}, u32[]{:S(2)}) collective-permute-start(bf16[4,16,1664]{2,1,0:T(8,128)(2,1)S(1)} %pad_maximum_fusion.2.refs_0_), channel_id=1, source_target_pairs={{0,6},{1,7},{2,4},{3,5},{4,2},{5,3},{6,0},{7,1},{8,14},{9,15},{10,... | collective-permute-start | bytes 638984 | tf_op jit(solution)/shard_map/ppermute | solution.py:68
  16.9 9.2 %collective-permute-start.6 = (bf16[4,16,1664]{2,1,0:T(8,128)(2,1)S(1)}, bf16[4,16,1664]{2,1,0:T(8,128)(2,1)S(1)}, u32[]{:S(2)}, u32[]{:S(2)}) collective-permute-start(bf16[4,16,1664]{2,1,0:T(8,128)(2,1)S(1)} %pad_maximum_fusion.2.refs_0_), channel_id=1, source_target_pairs={{0,4},{1,5},{2,6},{3,7},{4,0},{5,1},{6,2},{7,3},{8,12},{9,13},{10,... | collective-permute-start | bytes 638984 | tf_op jit(solution)/shard_map/ppermute | solution.py:68
  17.4 8.8 %collective-permute-start.5 = (bf16[4,16,1664]{2,1,0:T(8,128)(2,1)S(1)}, bf16[4,16,1664]{2,1,0:T(8,128)(2,1)S(1)}, u32[]{:S(2)}, u32[]{:S(2)}) collective-permute-start(bf16[4,16,1664]{2,1,0:T(8,128)(2,1)S(1)} %pad_maximum_fusion.2.refs_0_), channel_id=1, source_target_pairs={{0,2},{1,3},{2,0},{3,1},{4,6},{5,7},{6,4},{7,5},{8,10},{9,11},{10,... | collective-permute-start | bytes 638984 | tf_op jit(solution)/shard_map/ppermute | solution.py:68
  19.7 8.1 %collective-permute-start.4 = (bf16[2,144,512]{2,1,0:T(8,128)(2,1)S(1)}, bf16[2,144,512]{2,1,0:T(8,128)(2,1)S(1)}, u32[]{:S(2)}, u32[]{:S(2)}) collective-permute-start(bf16[2,144,512]{2,1,0:T(8,128)(2,1)S(1)} %pad_maximum_fusion.1), channel_id=1, source_target_pairs={{0,8},{1,9},{2,10},{3,11},{4,12},{5,13},{6,14},{7,15},{8,0},{9,1},... | collective-permute-start | bytes 884744 | tf_op jit(solution)/shard_map/ppermute | solution.py:68
  27.9 27.5 %collective-permute-start.14 = (bf16[4,144,512]{2,1,0:T(8,128)(2,1)S(1)}, bf16[4,144,512]{2,1,0:T(8,128)(2,1)S(1)}, u32[]{:S(2)}, u32[]{:S(2)}) collective-permute-start(bf16[4,144,512]{2,1,0:T(8,128)(2,1)S(1)} %pad_maximum_fusion), channel_id=1, source_target_pairs={{0,6},{1,7},{2,4},{3,5},{4,2},{5,3},{6,0},{7,1},{8,14},{9,15},{10,... | collective-permute-start | bytes 1769480 | tf_op jit(solution)/shard_map/ppermute | solution.py:68
  30.4 25.0 %collective-permute-start.13 = (bf16[4,144,512]{2,1,0:T(8,128)(2,1)S(1)}, bf16[4,144,512]{2,1,0:T(8,128)(2,1)S(1)}, u32[]{:S(2)}, u32[]{:S(2)}) collective-permute-start(bf16[4,144,512]{2,1,0:T(8,128)(2,1)S(1)} %pad_maximum_fusion), channel_id=1, source_target_pairs={{0,4},{1,5},{2,6},{3,7},{4,0},{5,1},{6,2},{7,3},{8,12},{9,13},{10,... | collective-permute-start | bytes 1769480 | tf_op jit(solution)/shard_map/ppermute | solution.py:68
  30.9 24.6 %collective-permute-start.12 = (bf16[4,144,512]{2,1,0:T(8,128)(2,1)S(1)}, bf16[4,144,512]{2,1,0:T(8,128)(2,1)S(1)}, u32[]{:S(2)}, u32[]{:S(2)}) collective-permute-start(bf16[4,144,512]{2,1,0:T(8,128)(2,1)S(1)} %pad_maximum_fusion), channel_id=1, source_target_pairs={{0,2},{1,3},{2,0},{3,1},{4,6},{5,7},{6,4},{7,5},{8,10},{9,11},{10,... | collective-permute-start | bytes 1769480 | tf_op jit(solution)/shard_map/ppermute | solution.py:68
  34.4 21.9 %collective-permute-start.15 = (bf16[4,144,512]{2,1,0:T(8,128)(2,1)S(1)}, bf16[4,144,512]{2,1,0:T(8,128)(2,1)}, u32[]{:S(2)}, u32[]{:S(2)}) collective-permute-start(bf16[4,144,512]{2,1,0:T(8,128)(2,1)S(1)} %pad_maximum_fusion), channel_id=1, source_target_pairs={{0,1},{1,0},{2,3},{3,2},{4,5},{5,4},{6,7},{7,6},{8,9},{9,8},{10,11... | collective-permute-start | bytes 1769480 | tf_op jit(solution)/shard_map/ppermute | solution.py:68
  98.7 4.8 %collective-permute-start.19 = (bf16[16,144,512]{2,1,0:T(8,128)(2,1)}, bf16[16,144,512]{2,1,0:T(8,128)(2,1)S(1)}, u32[]{:S(2)}, u32[]{:S(2)}) collective-permute-start(bf16[16,144,512]{2,1,0:T(8,128)(2,1)} %get-tuple-element.104), channel_id=1, source_target_pairs={{0,1},{1,0},{2,3},{3,2},{4,5},{5,4},{6,7},{7,6},{8,9},{9,8},{10,11... | collective-permute-start | bytes 7077896 | tf_op jit(solution)/shard_map/ppermute | solution.py:68
  106.5 30.9 %collective-permute-start.20 = (bf16[4,144,512]{2,1,0:T(8,128)(2,1)}, bf16[4,144,512]{2,1,0:T(8,128)(2,1)S(1)}, u32[]{:S(2)}, u32[]{:S(2)}) collective-permute-start(bf16[4,144,512]{2,1,0:T(8,128)(2,1)} %get-tuple-element.105), channel_id=1, source_target_pairs={{0,2},{1,3},{2,0},{3,1},{4,6},{5,7},{6,4},{7,5},{8,10},{9,11},{10,... | collective-permute-start | bytes 1769480 | tf_op jit(solution)/shard_map/ppermute | solution.py:68
  108.0 29.4 %collective-permute-start.21 = (bf16[4,144,512]{2,1,0:T(8,128)(2,1)}, bf16[4,144,512]{2,1,0:T(8,128)(2,1)S(1)}, u32[]{:S(2)}, u32[]{:S(2)}) collective-permute-start(bf16[4,144,512]{2,1,0:T(8,128)(2,1)} %get-tuple-element.106), channel_id=1, source_target_pairs={{0,4},{1,5},{2,6},{3,7},{4,0},{5,1},{6,2},{7,3},{8,12},{9,13},{10,... | collective-permute-start | bytes 1769480 | tf_op jit(solution)/shard_map/ppermute | solution.py:68
  109.5 27.9 %collective-permute-start.22 = (bf16[4,144,512]{2,1,0:T(8,128)(2,1)S(1)}, bf16[4,144,512]{2,1,0:T(8,128)(2,1)S(1)}, u32[]{:S(2)}, u32[]{:S(2)}) collective-permute-start(bf16[4,144,512]{2,1,0:T(8,128)(2,1)S(1)} %get-tuple-element.107), channel_id=1, source_target_pairs={{0,6},{1,7},{2,4},{3,5},{4,2},{5,3},{6,0},{7,1},{8,14},{9,15},{10,... | collective-permute-start | bytes 1769480 | tf_op jit(solution)/shard_map/ppermute | solution.py:68
  137.7 9.5 %collective-permute-start.23 = (bf16[2,144,512]{2,1,0:T(8,128)(2,1)S(1)}, bf16[2,144,512]{2,1,0:T(8,128)(2,1)S(1)}, u32[]{:S(2)}, u32[]{:S(2)}) collective-permute-start(bf16[2,144,512]{2,1,0:T(8,128)(2,1)S(1)} %get-tuple-element.127), channel_id=1, source_target_pairs={{0,8},{1,9},{2,10},{3,11},{4,12},{5,13},{6,14},{7,15},{8,0},{9,1},... | collective-permute-start | bytes 884744 | tf_op jit(solution)/shard_map/ppermute | solution.py:68
  143.1 17.1 %collective-permute-start.26 = (bf16[224,512]{1,0:T(8,128)(2,1)S(1)}, bf16[224,512]{1,0:T(8,128)(2,1)S(1)}, u32[]{:S(2)}, u32[]{:S(2)}) collective-permute-start(bf16[224,512]{1,0:T(8,128)(2,1)S(1)} %get-tuple-element.137), channel_id=1, source_target_pairs={{0,2},{1,3},{2,0},{3,1},{4,6},{5,7},{6,4},{7,5},{8,10},{9,11},{10,... | collective-permute-start | bytes 688136 | tf_op jit(solution)/shard_map/ppermute | solution.py:68
  144.6 15.5 %collective-permute-start.27 = (bf16[224,512]{1,0:T(8,128)(2,1)S(1)}, bf16[224,512]{1,0:T(8,128)(2,1)S(1)}, u32[]{:S(2)}, u32[]{:S(2)}) collective-permute-start(bf16[224,512]{1,0:T(8,128)(2,1)S(1)} %get-tuple-element.138), channel_id=1, source_target_pairs={{0,4},{1,5},{2,6},{3,7},{4,0},{5,1},{6,2},{7,3},{8,12},{9,13},{10,... | collective-permute-start | bytes 688136 | tf_op jit(solution)/shard_map/ppermute | solution.py:68
  146.2 14.0 %collective-permute-start.28 = (bf16[224,512]{1,0:T(8,128)(2,1)S(1)}, bf16[224,512]{1,0:T(8,128)(2,1)S(1)}, u32[]{:S(2)}, u32[]{:S(2)}) collective-permute-start(bf16[224,512]{1,0:T(8,128)(2,1)S(1)} %get-tuple-element.139), channel_id=1, source_target_pairs={{0,6},{1,7},{2,4},{3,5},{4,2},{5,3},{6,0},{7,1},{8,14},{9,15},{10,... | collective-permute-start | bytes 688136 | tf_op jit(solution)/shard_map/ppermute | solution.py:68
  147.2 12.9 %collective-permute-start.29 = (bf16[1,144,512]{2,1,0:T(8,128)(2,1)S(1)}, bf16[1,144,512]{2,1,0:T(8,128)(2,1)S(1)}, u32[]{:S(2)}, u32[]{:S(2)}) collective-permute-start(bf16[1,144,512]{2,1,0:T(8,128)(2,1)S(1)} %get-tuple-element.142), channel_id=1, source_target_pairs={{0,16},{1,17},{2,18},{3,19},{4,20},{5,21},{6,22},{7,23},{8,24},{9,... | collective-permute-start | bytes 442376 | tf_op jit(solution)/shard_map/ppermute | solution.py:68
  160.4 5.2 %collective-permute-start.30 = (bf16[80,512]{1,0:T(8,128)(2,1)S(1)}, bf16[80,512]{1,0:T(8,128)(2,1)S(1)}, u32[]{:S(2)}, u32[]{:S(2)}) collective-permute-start(bf16[80,512]{1,0:T(8,128)(2,1)S(1)} %get-tuple-element.152), channel_id=1, source_target_pairs={{0,8},{1,9},{2,10},{3,11},{4,12},{5,13},{6,14},{7,15},{8,0},{9,1},... | collective-permute-start | bytes 245768 | tf_op jit(solution)/shard_map/ppermute | solution.py:68
  161.8 8.6 %collective-permute-start.31 = (bf16[80,512]{1,0:T(8,128)(2,1)S(1)}, bf16[80,512]{1,0:T(8,128)(2,1)S(1)}, u32[]{:S(2)}, u32[]{:S(2)}) collective-permute-start(bf16[80,512]{1,0:T(8,128)(2,1)S(1)} %get-tuple-element.153), channel_id=1, source_target_pairs={{0,16},{1,17},{2,18},{3,19},{4,20},{5,21},{6,22},{7,23},{8,24},{9,... | collective-permute-start | bytes 245768 | tf_op jit(solution)/shard_map/ppermute | solution.py:68
  162.1 8.3 %collective-permute-start.32 = (bf16[80,512]{1,0:T(8,128)(2,1)S(1)}, bf16[80,512]{1,0:T(8,128)(2,1)S(1)}, u32[]{:S(2)}, u32[]{:S(2)}) collective-permute-start(bf16[80,512]{1,0:T(8,128)(2,1)S(1)} %get-tuple-element.154), channel_id=1, source_target_pairs={{0,24},{1,25},{2,26},{3,27},{4,28},{5,29},{6,30},{7,31},{8,16},{9,... | collective-permute-start | bytes 245768 | tf_op jit(solution)/shard_map/ppermute | solution.py:68
  (28 other events, 105.7 us)

commit v8 on v7

--- a/solution.py
+++ b/solution.py
@@ -399,7 +399,7 @@
                 gT[cols, at] = gp[at, cols].T
             return carry
 
-        lax.fori_loop(0, padded // LANES, turn, 0)
+        lax.fori_loop(0, padded // LANES, turn, 0, unroll=True)
         for c in later:
             c.wait()
         store_p.wait()

time: 172 us -> 172 us (level)
  no operation moved by 1% of the time
where the time goes in v8:
time: 172 us; the launch traced here: 171 us
  Pallas kernels  104 us (60%)
  starting transfers between devices  35.2 us (20%)
  waiting for transfers between devices  19.9 us (12%)
  local copies, waits for them, and re-layouts  9.28 us (5%)
    pallas_call x1, Pallas kernels, mlp(): pl.pallas_call(functools.partial(mlp_body, plan=plan, rows=rows, owners=c...  37.2 us
    ppermute x33, starting transfers between devices, swap(): return lax.ppermute(x, AXES, [(i, i ^ mask) for i in range(count)])  35.2 us
    pallas_call x1, Pallas kernels, attn_bwd(): pl.pallas_call(functools.partial(attn_bwd_body, owners=count if owners el...  27.3 us
    ppermute x33, waiting for transfers between devices, swap(): return lax.ppermute(x, AXES, [(i, i ^ mask) for i in range(count)])  19.9 us
    pallas_call x1, Pallas kernels, attn_fwd(): pl.pallas_call(functools.partial(attn_fwd_body, plan=plan, rpd=rpd, per=p...  19.9 us
    pallas_call x1, Pallas kernels, grad_in(): pl.pallas_call(grad_in_body, grid=(n,), in_specs=[pl.BlockSpec((GL, 3 * D...  9.2 us
    pallas_call x1, Pallas kernels, rel_bias(): pl.pallas_call(rel_bias_body, out_shape=sds((HEADS, KP, LANES), f32), com...  4.31 us
    unnamed x43, local copies, waits for them, and re-layouts  4 us
  transfers between devices with their start and end apart: 33, of which 15 were waited for; matrix products, arithmetic and copies ran while one was open for 3% of the time, Pallas kernels for 38%

profile of v8, /device:TPU:0, one launch (start us, length us, event | category | flops | bytes accessed | tf_op | source)
XLA Modules:
  0.0 171.0 jit_solution(2633809742508503331)
XLA Ops:
  2.2 5.1 %collective-permute-start.3 = (bf16[1,16,1664]{2,1,0:T(8,128)(2,1)S(1)}, bf16[1,16,1664]{2,1,0:T(8,128)(2,1)S(1)}, u32[]{:S(2)}, u32[]{:S(2)}) collective-permute-start(bf16[1,16,1664]{2,1,0:T(8,128)(2,1)S(1)} %maximum_bitcast_fusion), channel_id=1, source_target_pairs={{0,24},{1,25},{2,26},{3,27},{4,28},{5,29},{6,30},{7,31},{8,16},{9,... | collective-permute-start | bytes 159752 | tf_op jit(solution)/shard_map/ppermute | solution.py:68
  10.5 2.4 %collective-permute-start = (bf16[1,144,512]{2,1,0:T(8,128)(2,1)S(1)}, bf16[1,144,512]{2,1,0:T(8,128)(2,1)S(1)}, u32[]{:S(2)}, u32[]{:S(2)}) collective-permute-start(bf16[1,144,512]{2,1,0:T(8,128)(2,1)S(1)} %bitcast.32), channel_id=1, source_target_pairs={{0,16},{1,17},{2,18},{3,19},{4,20},{5,21},{6,22},{7,23},{8,24},{9,... | collective-permute-start | bytes 442376 | tf_op jit(solution)/shard_map/ppermute | solution.py:68
  14.4 2.5 %collective-permute-start.7 = (bf16[4,16,1664]{2,1,0:T(8,128)(2,1)S(1)}, bf16[4,16,1664]{2,1,0:T(8,128)(2,1)S(1)}, u32[]{:S(2)}, u32[]{:S(2)}) collective-permute-start(bf16[4,16,1664]{2,1,0:T(8,128)(2,1)S(1)} %pad_maximum_fusion.2.refs_0_), channel_id=1, source_target_pairs={{0,6},{1,7},{2,4},{3,5},{4,2},{5,3},{6,0},{7,1},{8,14},{9,15},{10,... | collective-permute-start | bytes 638984 | tf_op jit(solution)/shard_map/ppermute | solution.py:68
  20.8 4.3 %rel_bias.1.bias_ref = f32[16,112,128]{2,1,0:T(8,128)S(1)} custom-call(f32[16,384]{1,0:T(8,128)S(1)} %pad.13.t_ref), custom_call_target="tpu_custom_call" | custom-call | flops 20000000000 | bytes 1000000 | tf_op jit(solution)/shard_map/rel_bias/pallas_call | solution.py:886
  26.2 1.7 collective-permute-done.4
  27.9 2.5 %collective-permute-start.14 = (bf16[4,144,512]{2,1,0:T(8,128)(2,1)S(1)}, bf16[4,144,512]{2,1,0:T(8,128)(2,1)S(1)}, u32[]{:S(2)}, u32[]{:S(2)}) collective-permute-start(bf16[4,144,512]{2,1,0:T(8,128)(2,1)S(1)} %pad_maximum_fusion), channel_id=1, source_target_pairs={{0,6},{1,7},{2,4},{3,5},{4,2},{5,3},{6,0},{7,1},{8,14},{9,15},{10,... | collective-permute-start | bytes 1769480 | tf_op jit(solution)/shard_map/ppermute | solution.py:68
  35.6 19.9 %attn_fwd.1 = (bf16[512,2048]{1,0:T(8,128)(2,1)}, bf16[1600,512]{1,0:T(8,128)(2,1)}, bf16[2048,512]{1,0:T(8,128)(2,1)}, bf16[512,2048]{1,0:T(8,128)(2,1)}, bf16[...) custom-call(s32[1]{0:T(128)} %bitcast.me_ref, ...), custom_call_target="tpu_custom_call" | custom-call | flops 10000000 | bytes 100000 | tf_op jit(solution)/shard_map/attn_fwd/pallas_call | solution.py:256
  56.3 1.3 collective-permute-done.16
  60.8 37.2 %mlp.1 = (bf16[1600,512]{1,0:T(8,128)(2,1)}, f32[1600,512]{1,0:T(8,128)}, bf16[512,512]{1,0:T(8,128)(2,1)S(1)}, bf16[16,144,512]{2,1,0:T(8,128)(2,1)}, bf16[16,1...) custom-call(s32[1]{0:T(128)} %bitcast.me_ref, ...), custom_call_target="tpu_custom_call" | custom-call | flops 10000000 | bytes 100000 | tf_op jit(solution)/shard_map/mlp/pallas_call | solution.py:523
  98.3 4.5 %collective-permute-done.19.refs_1_ = bf16[16,144,512]{2,1,0:T(8,128)(2,1)S(1)} collective-permute-done((bf16[16,144,512]{2,1,0:T(8,128)(2,1)}, bf16[16,144,512]{2,1,0:T(8,128)(2,1)S(1)}, u32[]{:S(2)}, u32[]{:S(2)}) %collective-permute-start.19) | collective-permute-done | bytes 2359328 | tf_op jit(solution)/shard_map/ppermute | solution.py:68
  102.9 1.7 copy-done
  104.5 1.3 add_split.3
  105.8 1.5 collective-permute-start.20
  107.3 1.5 collective-permute-start.21
  109.3 27.3 %attn_bwd.1 = (bf16[2048,1536]{1,0:T(8,128)(2,1)}, f32[16,112,128]{2,1,0:T(8,128)}, f32[8,1536]{1,0:T(8,128)}, bf16[16,48,512]{2,1,0:T(8,128)(2,1)}, bf16[16,48,512]{2,1,0:T(8,128)(2,1)}) custom-call(s32[1]{0:T(128)} %bitcast.me_ref, f32[1600,512]{1,0:T(8,128)} %get-tuple-element.109.dmid_ref, bf16[512,512]{1,0:T(8,128)(2,1)} %copy-done.4, ...), custom_call_target="tpu_custom_call" | custom-call | flops 10000000 | bytes 100000 | tf_op jit(solution)/shard_map/attn_bwd/pallas_call | solution.py:658
  137.1 1.3 collective-permute-start.23
  138.4 2.4 %rel_grad.1.refs_2_ = f32[24,512]{1,0:T(8,128)S(1)} custom-call(f32[16,112,128]{2,1,0:T(8,128)S(1)} %copy-done.2, f32[8,1536]{1,0:T(8,128)S(1)} %copy-done.6, f32[8,512]{1,0:T(8,128)S(1)} %get-tuple-element.133.two_ref, f32[8,512]{1,0:T(8,128)S(1)} %get-tuple-element.134.up_ref, f32[8,512]{1,0:T(8,128)S(1)} %get-tuple-element.135.squares_ref), custom_call_target="tpu_custom_call" | custom-call | flops 10000000 | bytes 100000 | tf_op jit(solution)/shard_map/rel_grad/pallas_call | solution.py:928
  142.4 1.6 collective-permute-start.26
  144.0 1.5 collective-permute-start.27
  146.6 3.7 %collective-permute-start.29 = (bf16[1,144,512]{2,1,0:T(8,128)(2,1)S(1)}, bf16[1,144,512]{2,1,0:T(8,128)(2,1)S(1)}, u32[]{:S(2)}, u32[]{:S(2)}) collective-permute-start(bf16[1,144,512]{2,1,0:T(8,128)(2,1)S(1)} %get-tuple-element.142), channel_id=1, source_target_pairs={{0,16},{1,17},{2,18},{3,19},{4,20},{5,21},{6,22},{7,23},{8,24},{9,... | collective-permute-start | bytes 442376 | tf_op jit(solution)/shard_map/ppermute | solution.py:68
  150.3 9.2 %grad_in.1 = f32[1600,512]{1,0:T(8,128)} custom-call(bf16[2048,1536]{1,0:T(8,128)(2,1)} %get-tuple-element.143.dm_ref, bf16[512,1536]{1,0:T(8,128)(2,1)} %get-tuple-element.117.w_any.w_ref, bf16[1600,512]{1,0:T(8,128)(2,1)} %x_ref.2, f32[1600,512]{1,0:T(8,128)} %get-tuple-element.109.dmid_ref, f32[16,512]{1,0:T(8,128)} %get-tuple-element.97.rowv_ref), custom_call_target="tpu_custom_call" | custom-call | flops 10000000 | bytes 100000 | tf_op jit(solution)/shard_map/grad_in/pallas_call | solution.py:696
  159.7 1.5 collective-permute-start.30
  161.5 2.7 %collective-permute-start.32 = (bf16[80,512]{1,0:T(8,128)(2,1)S(1)}, bf16[80,512]{1,0:T(8,128)(2,1)S(1)}, u32[]{:S(2)}, u32[]{:S(2)}) collective-permute-start(bf16[80,512]{1,0:T(8,128)(2,1)S(1)} %get-tuple-element.154), channel_id=1, source_target_pairs={{0,24},{1,25},{2,26},{3,27},{4,28},{5,29},{6,30},{7,31},{8,16},{9,... | collective-permute-start | bytes 245768 | tf_op jit(solution)/shard_map/ppermute | solution.py:68
  164.9 4.8 %collective-permute-done.31.refs_1_ = bf16[80,512]{1,0:T(8,128)(2,1)S(1)} collective-permute-done((bf16[80,512]{1,0:T(8,128)(2,1)S(1)}, bf16[80,512]{1,0:T(8,128)(2,1)S(1)}, u32[]{:S(2)}, u32[]{:S(2)}) %collective-permute-start.31) | collective-permute-done | bytes 81952 | tf_op jit(solution)/shard_map/ppermute | solution.py:68
  (114 shorter events, 26.7 us)
Async XLA Ops:
  2.2 12.1 %collective-permute-start.3 = (bf16[1,16,1664]{2,1,0:T(8,128)(2,1)S(1)}, bf16[1,16,1664]{2,1,0:T(8,128)(2,1)S(1)}, u32[]{:S(2)}, u32[]{:S(2)}) collective-permute-start(bf16[1,16,1664]{2,1,0:T(8,128)(2,1)S(1)} %maximum_bitcast_fusion), channel_id=1, source_target_pairs={{0,24},{1,25},{2,26},{3,27},{4,28},{5,29},{6,30},{7,31},{8,16},{9,... | collective-permute-start | bytes 159752 | tf_op jit(solution)/shard_map/ppermute | solution.py:68
  7.3 7.0 %collective-permute-start.2 = (bf16[1,16,1664]{2,1,0:T(8,128)(2,1)S(1)}, bf16[1,16,1664]{2,1,0:T(8,128)(2,1)S(1)}, u32[]{:S(2)}, u32[]{:S(2)}) collective-permute-start(bf16[1,16,1664]{2,1,0:T(8,128)(2,1)S(1)} %maximum_bitcast_fusion), channel_id=1, source_target_pairs={{0,16},{1,17},{2,18},{3,19},{4,20},{5,21},{6,22},{7,23},{8,24},{9,... | collective-permute-start | bytes 159752 | tf_op jit(solution)/shard_map/ppermute | solution.py:68
  7.3 7.0 %collective-permute-start.1 = (bf16[1,16,1664]{2,1,0:T(8,128)(2,1)S(1)}, bf16[1,16,1664]{2,1,0:T(8,128)(2,1)S(1)}, u32[]{:S(2)}, u32[]{:S(2)}) collective-permute-start(bf16[1,16,1664]{2,1,0:T(8,128)(2,1)S(1)} %maximum_bitcast_fusion), channel_id=1, source_target_pairs={{0,8},{1,9},{2,10},{3,11},{4,12},{5,13},{6,14},{7,15},{8,0},{9,1},... | collective-permute-start | bytes 159752 | tf_op jit(solution)/shard_map/ppermute | solution.py:68
  10.5 9.2 %collective-permute-start = (bf16[1,144,512]{2,1,0:T(8,128)(2,1)S(1)}, bf16[1,144,512]{2,1,0:T(8,128)(2,1)S(1)}, u32[]{:S(2)}, u32[]{:S(2)}) collective-permute-start(bf16[1,144,512]{2,1,0:T(8,128)(2,1)S(1)} %bitcast.32), channel_id=1, source_target_pairs={{0,16},{1,17},{2,18},{3,19},{4,20},{5,21},{6,22},{7,23},{8,24},{9,... | collective-permute-start | bytes 442376 | tf_op jit(solution)/shard_map/ppermute | solution.py:68
  14.4 10.8 %collective-permute-start.7 = (bf16[4,16,1664]{2,1,0:T(8,128)(2,1)S(1)}, bf16[4,16,1664]{2,1,0:T(8,128)(2,1)S(1)}, u32[]{:S(2)}, u32[]{:S(2)}) collective-permute-start(bf16[4,16,1664]{2,1,0:T(8,128)(2,1)S(1)} %pad_maximum_fusion.2.refs_0_), channel_id=1, source_target_pairs={{0,6},{1,7},{2,4},{3,5},{4,2},{5,3},{6,0},{7,1},{8,14},{9,15},{10,... | collective-permute-start | bytes 638984 | tf_op jit(solution)/shard_map/ppermute | solution.py:68
  16.9 9.2 %collective-permute-start.6 = (bf16[4,16,1664]{2,1,0:T(8,128)(2,1)S(1)}, bf16[4,16,1664]{2,1,0:T(8,128)(2,1)S(1)}, u32[]{:S(2)}, u32[]{:S(2)}) collective-permute-start(bf16[4,16,1664]{2,1,0:T(8,128)(2,1)S(1)} %pad_maximum_fusion.2.refs_0_), channel_id=1, source_target_pairs={{0,4},{1,5},{2,6},{3,7},{4,0},{5,1},{6,2},{7,3},{8,12},{9,13},{10,... | collective-permute-start | bytes 638984 | tf_op jit(solution)/shard_map/ppermute | solution.py:68
  17.4 8.8 %collective-permute-start.5 = (bf16[4,16,1664]{2,1,0:T(8,128)(2,1)S(1)}, bf16[4,16,1664]{2,1,0:T(8,128)(2,1)S(1)}, u32[]{:S(2)}, u32[]{:S(2)}) collective-permute-start(bf16[4,16,1664]{2,1,0:T(8,128)(2,1)S(1)} %pad_maximum_fusion.2.refs_0_), channel_id=1, source_target_pairs={{0,2},{1,3},{2,0},{3,1},{4,6},{5,7},{6,4},{7,5},{8,10},{9,11},{10,... | collective-permute-start | bytes 638984 | tf_op jit(solution)/shard_map/ppermute | solution.py:68
  19.7 8.1 %collective-permute-start.4 = (bf16[2,144,512]{2,1,0:T(8,128)(2,1)S(1)}, bf16[2,144,512]{2,1,0:T(8,128)(2,1)S(1)}, u32[]{:S(2)}, u32[]{:S(2)}) collective-permute-start(bf16[2,144,512]{2,1,0:T(8,128)(2,1)S(1)} %pad_maximum_fusion.1), channel_id=1, source_target_pairs={{0,8},{1,9},{2,10},{3,11},{4,12},{5,13},{6,14},{7,15},{8,0},{9,1},... | collective-permute-start | bytes 884744 | tf_op jit(solution)/shard_map/ppermute | solution.py:68
  27.9 27.5 %collective-permute-start.14 = (bf16[4,144,512]{2,1,0:T(8,128)(2,1)S(1)}, bf16[4,144,512]{2,1,0:T(8,128)(2,1)S(1)}, u32[]{:S(2)}, u32[]{:S(2)}) collective-permute-start(bf16[4,144,512]{2,1,0:T(8,128)(2,1)S(1)} %pad_maximum_fusion), channel_id=1, source_target_pairs={{0,6},{1,7},{2,4},{3,5},{4,2},{5,3},{6,0},{7,1},{8,14},{9,15},{10,... | collective-permute-start | bytes 1769480 | tf_op jit(solution)/shard_map/ppermute | solution.py:68
  30.4 25.0 %collective-permute-start.13 = (bf16[4,144,512]{2,1,0:T(8,128)(2,1)S(1)}, bf16[4,144,512]{2,1,0:T(8,128)(2,1)S(1)}, u32[]{:S(2)}, u32[]{:S(2)}) collective-permute-start(bf16[4,144,512]{2,1,0:T(8,128)(2,1)S(1)} %pad_maximum_fusion), channel_id=1, source_target_pairs={{0,4},{1,5},{2,6},{3,7},{4,0},{5,1},{6,2},{7,3},{8,12},{9,13},{10,... | collective-permute-start | bytes 1769480 | tf_op jit(solution)/shard_map/ppermute | solution.py:68
  30.9 24.6 %collective-permute-start.12 = (bf16[4,144,512]{2,1,0:T(8,128)(2,1)S(1)}, bf16[4,144,512]{2,1,0:T(8,128)(2,1)S(1)}, u32[]{:S(2)}, u32[]{:S(2)}) collective-permute-start(bf16[4,144,512]{2,1,0:T(8,128)(2,1)S(1)} %pad_maximum_fusion), channel_id=1, source_target_pairs={{0,2},{1,3},{2,0},{3,1},{4,6},{5,7},{6,4},{7,5},{8,10},{9,11},{10,... | collective-permute-start | bytes 1769480 | tf_op jit(solution)/shard_map/ppermute | solution.py:68
  34.4 21.9 %collective-permute-start.15 = (bf16[4,144,512]{2,1,0:T(8,128)(2,1)S(1)}, bf16[4,144,512]{2,1,0:T(8,128)(2,1)}, u32[]{:S(2)}, u32[]{:S(2)}) collective-permute-start(bf16[4,144,512]{2,1,0:T(8,128)(2,1)S(1)} %pad_maximum_fusion), channel_id=1, source_target_pairs={{0,1},{1,0},{2,3},{3,2},{4,5},{5,4},{6,7},{7,6},{8,9},{9,8},{10,11... | collective-permute-start | bytes 1769480 | tf_op jit(solution)/shard_map/ppermute | solution.py:68
  98.0 4.8 %collective-permute-start.19 = (bf16[16,144,512]{2,1,0:T(8,128)(2,1)}, bf16[16,144,512]{2,1,0:T(8,128)(2,1)S(1)}, u32[]{:S(2)}, u32[]{:S(2)}) collective-permute-start(bf16[16,144,512]{2,1,0:T(8,128)(2,1)} %get-tuple-element.104), channel_id=1, source_target_pairs={{0,1},{1,0},{2,3},{3,2},{4,5},{5,4},{6,7},{7,6},{8,9},{9,8},{10,11... | collective-permute-start | bytes 7077896 | tf_op jit(solution)/shard_map/ppermute | solution.py:68
  105.8 30.9 %collective-permute-start.20 = (bf16[4,144,512]{2,1,0:T(8,128)(2,1)}, bf16[4,144,512]{2,1,0:T(8,128)(2,1)S(1)}, u32[]{:S(2)}, u32[]{:S(2)}) collective-permute-start(bf16[4,144,512]{2,1,0:T(8,128)(2,1)} %get-tuple-element.105), channel_id=1, source_target_pairs={{0,2},{1,3},{2,0},{3,1},{4,6},{5,7},{6,4},{7,5},{8,10},{9,11},{10,... | collective-permute-start | bytes 1769480 | tf_op jit(solution)/shard_map/ppermute | solution.py:68
  107.3 29.4 %collective-permute-start.21 = (bf16[4,144,512]{2,1,0:T(8,128)(2,1)}, bf16[4,144,512]{2,1,0:T(8,128)(2,1)S(1)}, u32[]{:S(2)}, u32[]{:S(2)}) collective-permute-start(bf16[4,144,512]{2,1,0:T(8,128)(2,1)} %get-tuple-element.106), channel_id=1, source_target_pairs={{0,4},{1,5},{2,6},{3,7},{4,0},{5,1},{6,2},{7,3},{8,12},{9,13},{10,... | collective-permute-start | bytes 1769480 | tf_op jit(solution)/shard_map/ppermute | solution.py:68
  108.8 27.9 %collective-permute-start.22 = (bf16[4,144,512]{2,1,0:T(8,128)(2,1)S(1)}, bf16[4,144,512]{2,1,0:T(8,128)(2,1)S(1)}, u32[]{:S(2)}, u32[]{:S(2)}) collective-permute-start(bf16[4,144,512]{2,1,0:T(8,128)(2,1)S(1)} %get-tuple-element.107), channel_id=1, source_target_pairs={{0,6},{1,7},{2,4},{3,5},{4,2},{5,3},{6,0},{7,1},{8,14},{9,15},{10,... | collective-permute-start | bytes 1769480 | tf_op jit(solution)/shard_map/ppermute | solution.py:68
  137.1 9.5 %collective-permute-start.23 = (bf16[2,144,512]{2,1,0:T(8,128)(2,1)S(1)}, bf16[2,144,512]{2,1,0:T(8,128)(2,1)S(1)}, u32[]{:S(2)}, u32[]{:S(2)}) collective-permute-start(bf16[2,144,512]{2,1,0:T(8,128)(2,1)S(1)} %get-tuple-element.127), channel_id=1, source_target_pairs={{0,8},{1,9},{2,10},{3,11},{4,12},{5,13},{6,14},{7,15},{8,0},{9,1},... | collective-permute-start | bytes 884744 | tf_op jit(solution)/shard_map/ppermute | solution.py:68
  142.4 17.1 %collective-permute-start.26 = (bf16[224,512]{1,0:T(8,128)(2,1)S(1)}, bf16[224,512]{1,0:T(8,128)(2,1)S(1)}, u32[]{:S(2)}, u32[]{:S(2)}) collective-permute-start(bf16[224,512]{1,0:T(8,128)(2,1)S(1)} %get-tuple-element.137), channel_id=1, source_target_pairs={{0,2},{1,3},{2,0},{3,1},{4,6},{5,7},{6,4},{7,5},{8,10},{9,11},{10,... | collective-permute-start | bytes 688136 | tf_op jit(solution)/shard_map/ppermute | solution.py:68
  144.0 15.5 %collective-permute-start.27 = (bf16[224,512]{1,0:T(8,128)(2,1)S(1)}, bf16[224,512]{1,0:T(8,128)(2,1)S(1)}, u32[]{:S(2)}, u32[]{:S(2)}) collective-permute-start(bf16[224,512]{1,0:T(8,128)(2,1)S(1)} %get-tuple-element.138), channel_id=1, source_target_pairs={{0,4},{1,5},{2,6},{3,7},{4,0},{5,1},{6,2},{7,3},{8,12},{9,13},{10,... | collective-permute-start | bytes 688136 | tf_op jit(solution)/shard_map/ppermute | solution.py:68
  145.5 14.0 %collective-permute-start.28 = (bf16[224,512]{1,0:T(8,128)(2,1)S(1)}, bf16[224,512]{1,0:T(8,128)(2,1)S(1)}, u32[]{:S(2)}, u32[]{:S(2)}) collective-permute-start(bf16[224,512]{1,0:T(8,128)(2,1)S(1)} %get-tuple-element.139), channel_id=1, source_target_pairs={{0,6},{1,7},{2,4},{3,5},{4,2},{5,3},{6,0},{7,1},{8,14},{9,15},{10,... | collective-permute-start | bytes 688136 | tf_op jit(solution)/shard_map/ppermute | solution.py:68
  146.6 12.9 %collective-permute-start.29 = (bf16[1,144,512]{2,1,0:T(8,128)(2,1)S(1)}, bf16[1,144,512]{2,1,0:T(8,128)(2,1)S(1)}, u32[]{:S(2)}, u32[]{:S(2)}) collective-permute-start(bf16[1,144,512]{2,1,0:T(8,128)(2,1)S(1)} %get-tuple-element.142), channel_id=1, source_target_pairs={{0,16},{1,17},{2,18},{3,19},{4,20},{5,21},{6,22},{7,23},{8,24},{9,... | collective-permute-start | bytes 442376 | tf_op jit(solution)/shard_map/ppermute | solution.py:68
  159.7 5.2 %collective-permute-start.30 = (bf16[80,512]{1,0:T(8,128)(2,1)S(1)}, bf16[80,512]{1,0:T(8,128)(2,1)S(1)}, u32[]{:S(2)}, u32[]{:S(2)}) collective-permute-start(bf16[80,512]{1,0:T(8,128)(2,1)S(1)} %get-tuple-element.152), channel_id=1, source_target_pairs={{0,8},{1,9},{2,10},{3,11},{4,12},{5,13},{6,14},{7,15},{8,0},{9,1},... | collective-permute-start | bytes 245768 | tf_op jit(solution)/shard_map/ppermute | solution.py:68
  161.2 8.6 %collective-permute-start.31 = (bf16[80,512]{1,0:T(8,128)(2,1)S(1)}, bf16[80,512]{1,0:T(8,128)(2,1)S(1)}, u32[]{:S(2)}, u32[]{:S(2)}) collective-permute-start(bf16[80,512]{1,0:T(8,128)(2,1)S(1)} %get-tuple-element.153), channel_id=1, source_target_pairs={{0,16},{1,17},{2,18},{3,19},{4,20},{5,21},{6,22},{7,23},{8,24},{9,... | collective-permute-start | bytes 245768 | tf_op jit(solution)/shard_map/ppermute | solution.py:68
  161.5 8.3 %collective-permute-start.32 = (bf16[80,512]{1,0:T(8,128)(2,1)S(1)}, bf16[80,512]{1,0:T(8,128)(2,1)S(1)}, u32[]{:S(2)}, u32[]{:S(2)}) collective-permute-start(bf16[80,512]{1,0:T(8,128)(2,1)S(1)} %get-tuple-element.154), channel_id=1, source_target_pairs={{0,24},{1,25},{2,26},{3,27},{4,28},{5,29},{6,30},{7,31},{8,16},{9,... | collective-permute-start | bytes 245768 | tf_op jit(solution)/shard_map/ppermute | solution.py:68
  (28 other events, 105.7 us)
